TPU v7x, 32 devices: a whole 2x2x4 slice. The times are simulated.
32 devices in a mesh: row: 8 (over z, x), col: 4 (over y, core).
Axes of the slice: x: 2, y: 2, z: 4, core: 2. Of those that a mesh axis runs over, the one named last changes fastest.
Arguments:
- front: float32 [12, 8, 24, 4, 128, 128], P(None, 'row', None, 'col'), may hold values from -6 to 6
- child_tiles: float32 [512, 128, 128], P(('row', 'col')), may hold values from -6 to 6
- tile_dest: int32 [512, 1], P(('row', 'col')), may hold values from 0 to 31; in each aligned block of 16 rows (0 to 15, 16 to 31, ...) no two rows name the same one
- tile_slot: int32 [512], P(('row', 'col')), may hold values from 0 to 287
- tile_count: int32 [32], P(('row', 'col')), may hold values from 12 to 16, as said below
- diag_inverses: float32 [2, 256, 256], replicated, as said below
Outputs:
- factored: float32 [12, 8, 24, 4, 128, 128], P(None, 'row', None, 'col')
Inputs may be any that keep to these rules, and one draw needn't show every extreme that they name: Among the 16 slots of one device, no two name the same device in tile_dest, live or not; every device is named by some slot. `tile_count`: some device has all 16 slots live. `diag_inverses`: each matrix is upper triangular with a positive diagonal; it is given as it is and need not match any diagonal block of the front.
All inputs are finite; a program needn't handle non-finite values.
Results may differ from a plain program's by a relative error of at most 0.000068.
Values sent between devices are 32-bit elements; how exact they have to be, the bound alone decides.
No kernel may reach another device: no remote copies, remote signals or barrier semaphores. Data moves between devices by JAX's collectives and lax.ppermute only.
A program may use at most 128 MiB of HBM per device.

v0:
```python
import functools

import jax
import jax.numpy as jnp
from jax import lax
from jax.experimental import pallas as pl
from jax.experimental.pallas import tpu as pltpu
from jax.sharding import PartitionSpec as P

TILE = 128
PANEL = 256
WIDTH = 2 * PANEL
NOTE = 8
VMEM = 56 * 1024 * 1024
NT = (((1,), (1,)), ((), ()))
NN = (((1,), (0,)), ((), ()))
BOTH = ("row", "col")


def halves(value):
    high = value.astype(jnp.bfloat16)
    low = (value - high.astype(jnp.float32)).astype(jnp.bfloat16)
    return high, low


def product(left, right, dims):
    dot = functools.partial(
        lax.dot_general, dimension_numbers=dims, preferred_element_type=jnp.float32
    )
    return dot(left[0], right[0]) + (dot(left[0], right[1]) + dot(left[1], right[0]))


def whole_spec(array):
    rank = len(array.shape)
    return pl.BlockSpec(array.shape, lambda *_: (0,) * rank)


def columns_kernel(
    place, row_of, col_of, front_ref, incoming_ref, out_ref, lead_ref, *rest
):
    *parts, tile_ref, sem = rest
    my_row, my_col = place[0], place[1]
    out_ref[...] = front_ref[:, 0, 0, 0]

    @pl.loop(0, incoming_ref.shape[0])
    def _(s):
        @pl.when(col_of[s] == 0)
        def _():
            copy = pltpu.make_async_copy(incoming_ref.at[s, pl.ds(0, TILE)], tile_ref, sem)
            copy.start()
            copy.wait()
            out_ref[row_of[s]] = out_ref[row_of[s]] + tile_ref[...]

    lead_ref[...] = jnp.zeros_like(lead_ref)
    for r in range(2):
        for c in range(2):

            @pl.when(jnp.logical_and(my_row == 2 + r, my_col == c))
            def _():
                lead_ref[r, c] = out_ref[0]

    count = len(parts)
    for j, part_ref in enumerate(parts):
        group = part_ref.shape[0]
        part_ref[...] = out_ref[pl.ds(lax.rem(my_col + j, count) * group, group)]


def assemble_columns(front, incoming, place, row_of, col_of, parts):
    rows = front.shape[0]
    shapes = [(rows, TILE, TILE), (2, 2, TILE, TILE)] + [(rows // parts, TILE, TILE)] * parts
    out_shape = [jax.ShapeDtypeStruct(shape, jnp.float32) for shape in shapes]
    return pl.pallas_call(
        columns_kernel,
        grid_spec=pltpu.PrefetchScalarGridSpec(
            num_scalar_prefetch=3,
            grid=(1,),
            in_specs=[
                pl.BlockSpec((rows, 1, 1, 1, TILE, TILE), lambda i, *_: (0, 0, 0, 0, 0, 0)),
                pl.BlockSpec(memory_space=pl.ANY),
            ],
            out_specs=[whole_spec(a) for a in out_shape],
            scratch_shapes=[pltpu.VMEM((TILE, TILE), jnp.float32), pltpu.SemaphoreType.DMA],
        ),
        out_shape=out_shape,
        compiler_params=pltpu.CompilerParams(vmem_limit_bytes=VMEM),
        name="panel_columns",
    )(place, row_of, col_of, front, incoming)


def row_panels_kernel(
    place, t0, t1, t2, t3, lead_ref, diag_ref,
    pair_ref, mine_ref, small_high_ref, small_low_ref, tiles_ref,
):
    step = pl.program_id(0)
    my_row, my_col = place[0], place[1]
    group = t0.shape[0]
    height = group * TILE

    @pl.when(step == 0)
    def _():
        inverse_one = halves(diag_ref[0])
        lead = jnp.concatenate(
            [jnp.concatenate([lead_ref[i, 0], lead_ref[i, 1]], axis=1) for i in range(2)], axis=0
        )
        lead = halves(product(halves(lead), inverse_one, NN))
        inverse_two = halves(diag_ref[1])
        for index, pair in enumerate((inverse_one, lead, inverse_two)):
            small_high_ref[index] = pair[0]
            small_low_ref[index] = pair[1]

    for i, tile_ref in enumerate((t0, t1, t2, t3)):
        tiles_ref[jnp.bitwise_xor(my_col, i)] = tile_ref[...]
    small = [(small_high_ref[i], small_low_ref[i]) for i in range(3)]
    columns = [tiles_ref[c].reshape(height, TILE) for c in range(4)]
    tile_row = lax.broadcasted_iota(jnp.int32, (height, PANEL), 0) // TILE
    first = jnp.logical_and(step == 0, tile_row == 0)
    above_one = jnp.logical_and(first, my_row < 2)
    above_two = jnp.logical_and(first, my_row < 4)
    one = product(halves(jnp.concatenate(columns[:2], axis=1)), small[0], NN)
    one_pair = halves(jnp.where(above_one, 0.0, one))
    field = jnp.concatenate(columns[2:], axis=1) - product(one_pair, small[1], NT)
    two = jnp.where(above_one, 0.0, product(halves(field), small[2], NN))
    two_pair = halves(jnp.where(above_two, 0.0, two))
    for i in range(2):
        pair_ref[:, i * WIDTH : i * WIDTH + PANEL] = one_pair[i]
        pair_ref[:, i * WIDTH + PANEL : (i + 1) * WIDTH] = two_pair[i]
    pieces = (one[:, :TILE], one[:, TILE:], two[:, :TILE], two[:, TILE:])
    for c in range(4):

        @pl.when(my_col == c)
        def _():
            mine_ref[...] = pieces[c].reshape(group, TILE, TILE)


def row_panels(tiles, lead, diag, place):
    rows = tiles[0].shape[0]
    group = rows // 3
    height = group * TILE
    out_shape = [
        jax.ShapeDtypeStruct((rows * TILE, 2 * WIDTH), jnp.bfloat16),
        jax.ShapeDtypeStruct((rows, TILE, TILE), jnp.float32),
        jax.ShapeDtypeStruct((3, PANEL, PANEL), jnp.bfloat16),
        jax.ShapeDtypeStruct((3, PANEL, PANEL), jnp.bfloat16),
    ]
    strip = pl.BlockSpec((group, TILE, TILE), lambda i, *_: (i, 0, 0))
    return pl.pallas_call(
        row_panels_kernel,
        grid_spec=pltpu.PrefetchScalarGridSpec(
            num_scalar_prefetch=1,
            grid=(3,),
            in_specs=[strip] * 4 + [whole_spec(lead), whole_spec(diag)],
            out_specs=[
                pl.BlockSpec((height, 2 * WIDTH), lambda i, *_: (i, 0)),
                strip,
                whole_spec(out_shape[2]),
                whole_spec(out_shape[3]),
            ],
            scratch_shapes=[pltpu.VMEM((4, group, TILE, TILE), jnp.float32)],
        ),
        out_shape=out_shape,
        compiler_params=pltpu.CompilerParams(vmem_limit_bytes=VMEM),
        name="row_panels",
    )(place, *tiles, lead, diag)


def trailing_kernel(
    n_pieces, columns, places, order, starts, front_one, front_two, pair_ref, small_high_ref,
    small_low_ref, incoming_ref, mine_ref, *rest,
):
    piece_refs = rest[:n_pieces]
    out_ref, right_high, right_low, buffer, sems = rest[-5:]
    step, steps = pl.program_id(0), pl.num_programs(0)
    group = piece_refs[0].shape[1]
    count = n_pieces * group
    rows = front_one.shape[0]
    slot = lax.rem(step, 2)

    def copy_of(at_step, j):
        at_slot = lax.rem(at_step, 2)
        index = jnp.minimum(2 * at_step, count - 2) + j
        return pltpu.make_async_copy(
            buffer.at[at_slot, j], out_ref.at[:, 0, columns[index], 0], sems.at[at_slot, j]
        )

    def each_copy(at_step, act):
        for j in range(2):
            if count % 2 and j == 0:
                pl.when(at_step < steps - 1)(lambda: act(copy_of(at_step, 0)))
            else:
                act(copy_of(at_step, j))

    @pl.when(step == 0)
    def _():
        small = [(small_high_ref[i], small_low_ref[i]) for i in range(3)]
        for p, piece in enumerate(piece_refs):
            columns_here = [piece[places[4 * p + c]].reshape(group * TILE, TILE) for c in range(4)]
            one = product(halves(jnp.concatenate(columns_here[:2], axis=1)), small[0], NN)
            field = jnp.concatenate(columns_here[2:], axis=1)
            field = field - product(halves(one), small[1], NT)
            two = product(halves(field), small[2], NN)
            for i, panel in enumerate((one, two)):
                high, low = halves(panel.T)
                span = slice(p * group * TILE, (p + 1) * group * TILE)
                right_high[i * PANEL : (i + 1) * PANEL, span] = high
                right_low[i * PANEL : (i + 1) * PANEL, span] = low

    @pl.when(step >= 2)
    def _():
        each_copy(step - 2, lambda copy: copy.wait())

    start = jnp.minimum(2 * step, count - 2)
    lanes = pl.ds(pl.multiple_of(start * TILE, TILE), 2 * TILE)
    right = (right_high[:, lanes], right_low[:, lanes])
    update = product((pair_ref[:, :WIDTH], pair_ref[:, WIDTH:]), right, NN)
    for j, front_ref in enumerate((front_one, front_two)):
        part = update[:, j * TILE : (j + 1) * TILE].reshape(rows, TILE, TILE)
        buffer[slot, j] = front_ref[:, 0, 0, 0] - part
        b = columns[start + j]

        @pl.when(b == 0)
        def _():
            buffer[slot, j] = mine_ref[...]

        @pl.when(b > 0)
        def _():
            @pl.loop(starts[b], starts[b + 1])
            def _(i):
                s, a = order[2 * i], order[2 * i + 1]
                buffer[slot, j, a] = buffer[slot, j, a] + incoming_ref[s, :TILE]

    each_copy(step, lambda copy: copy.start())

    @pl.when(step == steps - 1)
    def _():
        @pl.when(step >= 1)
        def _():
            each_copy(step - 1, lambda copy: copy.wait())

        each_copy(step, lambda copy: copy.wait())


def trailing(front, pieces, columns, places, panels, incoming, order, starts, before):
    rows = front.shape[0]
    pair, mine, small_high, small_low = panels
    group = pieces[0].shape[1]
    count = len(pieces) * group
    steps = (count + 1) // 2

    def strip(j):
        def index(i, columns, *_):
            return (0, 0, columns[jnp.minimum(2 * i, count - 2) + j], 0, 0, 0)

        return pl.BlockSpec((rows, 1, 1, 1, TILE, TILE), index)

    operands = [pair, small_high, small_low, incoming, mine, *pieces]
    in_specs = [strip(0), strip(1), *[whole_spec(a) for a in operands]]
    operands = [front, front, *operands]
    aliases = {}
    if before is not None:
        operands.append(before)
        in_specs.append(pl.BlockSpec(memory_space=pl.ANY))
        aliases = {len(operands) + 3: 0}
    height = rows * TILE
    return pl.pallas_call(
        functools.partial(trailing_kernel, len(pieces)),
        grid_spec=pltpu.PrefetchScalarGridSpec(
            num_scalar_prefetch=4,
            grid=(steps,),
            in_specs=in_specs,
            out_specs=pl.BlockSpec(memory_space=pl.ANY),
            scratch_shapes=[
                pltpu.VMEM((WIDTH, count * TILE), jnp.bfloat16),
                pltpu.VMEM((WIDTH, count * TILE), jnp.bfloat16),
                pltpu.VMEM((2, 2, rows, TILE, TILE), jnp.float32),
                pltpu.SemaphoreType.DMA((2, 2)),
            ],
        ),
        out_shape=jax.ShapeDtypeStruct(front.shape, jnp.float32),
        input_output_aliases=aliases,
        compiler_params=pltpu.CompilerParams(vmem_limit_bytes=VMEM),
        cost_estimate=pl.CostEstimate(
            flops=count * 2 * height * TILE * WIDTH * 3,
            bytes_accessed=count * 2 * height * TILE * 4,
            transcendentals=0,
        ),
        name="trailing",
    )(columns, places, order, starts, *operands)


def spread_lead(lead, n_row, n_col):
    lead = lead + lax.ppermute(
        lead, BOTH, [(r * n_col + c, r * n_col + 1 - c) for r in (2, 3) for c in (0, 1)]
    )
    lead = lead + lax.ppermute(
        lead, BOTH, [(r * n_col + c, (5 - r) * n_col + c) for r in (2, 3) for c in (0, 1)]
    )
    lead = lead + lax.ppermute(
        lead, BOTH, [(r * n_col + c, r * n_col + c + 2) for r in (2, 3) for c in (0, 1)]
    )
    below = lax.ppermute(lead, "row", [(2, 0), (3, 1)])
    for r in range(4, n_row, 2):
        lead = lead + lax.ppermute(lead, "row", [(r - 2, r), (r - 1, r + 1)])
    return lead + below


def body(front, child_tiles, tile_dest, tile_slot, tile_count, diag_inverses):
    n_row = lax.axis_size("row")
    n_col = lax.axis_size("col")
    my_row = lax.axis_index("row").astype(jnp.int32)
    my_col = lax.axis_index("col").astype(jnp.int32)
    rows_here, cols_here = (front.shape[0], front.shape[2])
    slots = child_tiles.shape[0]
    devices = n_row * n_col
    assert n_col == 4 and n_row % 4 == 0 and rows_here % 3 == 0
    place = jnp.stack([my_row, my_col])

    numbers = jnp.arange(slots, dtype=jnp.int32)
    live = numbers < tile_count[0]
    dest = tile_dest[:, 0]
    hits = (dest[None, :] == jnp.arange(devices, dtype=jnp.int32)[:, None]) & live[None, :]
    picked = jnp.sum(jnp.where(hits, numbers[None, :], 0), axis=1)
    slot_out = jnp.sum(jnp.where(hits, tile_slot[None, :] + 1, 0), axis=1) - 1
    notes = jnp.broadcast_to(
        slot_out.astype(jnp.float32)[:, None, None], (devices, NOTE, TILE)
    )
    outgoing = jnp.concatenate([jnp.take(child_tiles, picked, axis=0), notes], axis=1)
    incoming = lax.all_to_all(outgoing, BOTH, split_axis=0, concat_axis=0, tiled=True)
    slot_in = incoming[:, TILE, 0].astype(jnp.int32)
    row_of = jnp.where(slot_in >= 0, slot_in // cols_here, 0)
    col_of = jnp.where(slot_in >= 0, slot_in % cols_here, -1)
    sources = jnp.arange(devices, dtype=jnp.int32)
    key = jnp.where(slot_in >= 0, col_of, cols_here) * devices + sources
    rank = jnp.sum((key[None, :] < key[:, None]).astype(jnp.int32), axis=1)
    at = rank[None, :] == sources[:, None]
    order = jnp.stack(
        [jnp.sum(jnp.where(at, v[None, :], 0), axis=1) for v in (sources, row_of)], axis=1
    ).reshape(-1)
    edges = jnp.arange(cols_here + 1, dtype=jnp.int32) * devices
    starts = jnp.sum((key[None, :] < edges[:, None]).astype(jnp.int32), axis=1)

    ring = rows_here % n_col == 0
    mine, lead, *parts = assemble_columns(
        front, incoming, place, row_of, col_of, n_col if ring else 1
    )

    sets = n_row // n_col
    if ring:
        arrived = []
        for j, part in enumerate(parts):
            pairs = [
                (r * n_col + c, ((r // n_col) * n_col + (c + j) % n_col) * n_col + r % n_col)
                for r in range(n_row)
                for c in range(n_col)
            ]
            arrived.append(lax.ppermute(part, BOTH, pairs))
        piece = jnp.stack(arrived)
        circle = list(range(0, n_row, 2)) + list(range(n_row - 1, 0, -2))
        spot = jnp.asarray([circle.index(r) for r in range(n_row)], jnp.int32)[my_row]
        up = [(circle[i], circle[(i + 1) % n_row]) for i in range(n_row)]
        down = [(b, a) for a, b in up]
        rounds = [[(piece, 0)]]
        ahead = behind = piece
        for step in range(1, n_row // 2):
            ahead = lax.ppermute(ahead, "row", up)
            behind = lax.ppermute(behind, "row", down)
            rounds.append([(ahead, -step), (behind, step)])
        last = jnp.concatenate(
            [lax.ppermute(ahead[:2], "row", up), lax.ppermute(behind[2:], "row", down)]
        )
        rounds.append([(last, n_row // 2)])
        rounds = [rounds[0] + rounds[1]] + rounds[2:]

        def described(shift):
            origin = jnp.asarray(circle, jnp.int32)[(spot + shift + n_row) % n_row]
            part, group = origin % n_col, rows_here // n_col
            row = part * group + jnp.arange(group, dtype=jnp.int32)
            places = (part - jnp.arange(n_col, dtype=jnp.int32) + n_col) % n_col
            return row * sets + origin // n_col, places

    else:
        pairs = [
            (r * n_col + c, ((r // n_col) * n_col + c) * n_col + r % n_col)
            for r in range(n_row)
            for c in range(n_col)
        ]
        moved = lax.all_gather(lax.ppermute(mine, BOTH, pairs), "row", axis=0, tiled=False)
        rounds = [[(moved[h * n_col : (h + 1) * n_col], h)] for h in range(sets)]

        def described(h):
            row = jnp.arange(rows_here, dtype=jnp.int32)
            return row * sets + h, jnp.arange(n_col, dtype=jnp.int32)

    lead = spread_lead(lead, n_row, n_col)
    near = lax.ppermute(mine, "col", [(c, c ^ 1) for c in range(n_col)])
    far = lax.ppermute(mine, "col", [(c, c ^ 2) for c in range(n_col)])
    other = lax.ppermute(far, "col", [(c, c ^ 1) for c in range(n_col)])
    panels = row_panels([mine, near, far, other], lead, diag_inverses, place)

    out = None
    for entries in rounds:
        described_here = [described(shift) for _, shift in entries]
        columns = jnp.concatenate([d[0] for d in described_here])
        places = jnp.concatenate([d[1] for d in described_here])
        pieces = [p for p, _ in entries]
        out = trailing(front, pieces, columns, places, panels, incoming, order, starts, out)
    return out


def solution(mesh):
    return jax.shard_map(
        body,
        mesh=mesh,
        in_specs=(
            P(None, "row", None, "col", None, None),
            P(BOTH, None, None),
            P(BOTH, None),
            P(BOTH),
            P(BOTH),
            P(),
        ),
        out_specs=P(None, "row", None, "col", None, None),
        check_vma=False,
    )
```

profile of v0, /device:TPU:0, one launch (start us, length us, event | category | flops | bytes accessed | tf_op | source)
XLA Modules:
  0.0 211.8 jit_solution(12111164502193046199)
XLA Ops:
  0.8 0.7 broadcast_add_fusion
  1.4 0.7 select_reduce_fusion.3
  2.2 0.7 gather_fusion
  2.9 0.2 broadcast_select_fusion
  3.1 0.1 broadcast_in_dim.73
  3.2 1.5 pad_maximum_fusion
  4.8 7.3 %all-to-all-start = ((f32[32,136,128]{2,1,0:T(8,128)}), f32[32,136,128]{2,1,0:T(8,128)S(1)}, u32[]{:S(2)}, u32[]{:S(2)}) async-start(f32[32,136,128]{2,1,0:T(8,128)} %pad_maximum_fusion), calls=%async_computation | async-start | bytes 4456448 | tf_op jit(solution)/shard_map/all_to_all | solution.py:327
  12.1 0.6 dynamic_slice.27
  17.2 0.7 fusion.13
  30.4 0.6 pad_add_fusion.1.place
  31.1 32.6 %all-to-all-done.incoming_ref = f32[32,136,128]{2,1,0:T(8,128)S(1)} async-done(((f32[32,136,128]{2,1,0:T(8,128)}), f32[32,136,128]{2,1,0:T(8,128)S(1)}, u32[]{:S(2)}, u32[]{:S(2)}) %all-to-all-start) | async-done | bytes 2228256 | tf_op jit(solution)/shard_map/all_to_all | solution.py:327
  63.7 1.2 remainder_reduce_fusion
  64.9 1.2 compare_reduce_fusion
  66.2 0.6 iota_add_fusion
  66.8 4.5 %panel_columns.1 = (f32[12,128,128]{2,1,0:T(8,128)}, f32[2,2,128,128]{3,2,1,0:T(8,128)}, f32[3,128,128]{2,1,0:T(8,128)}, f32[3,128,128]{2,1,0:T(8,128)}, f32[3,128,128]{2,1,0:T(8,128)}, /*index=5*/f32[3,128,128]{2,1,0:T(8,128)}) custom-call(s32[2]{0:T(128)} %pad_add_fusion.1.place, s32[32]{0:T(128)} %get-tuple-element.35.row_of, ...), custom_call_target="tpu_custom_call" | custom-call | tf_op jit(solution)/shard_map/panel_columns/pallas_call | solution.py:72
  71.2 1.6 collective-permute-start.9
  72.8 0.9 collective-permute-start.10
  73.8 2.4 %collective-permute-start.11 = (f32[3,128,128]{2,1,0:T(8,128)}, f32[3,128,128]{2,1,0:T(8,128)S(1)}, u32[]{:S(2)}, u32[]{:S(2)}) collective-permute-start(f32[3,128,128]{2,1,0:T(8,128)} %get-tuple-element.23), channel_id=1, source_target_pairs={{0,8},{1,12},{2,0},{3,4},{4,9},{5,13},{6,1},{7,5},{8,10},{9,14},{1... | collective-permute-start | bytes 589832 | tf_op jit(solution)/shard_map/ppermute | solution.py:355
  76.2 0.3 collective-permute-start.12
  76.5 0.7 collective-permute-start.3
  77.2 0.6 and_select_fusion.9.places
  78.4 0.0 collective-permute-done.9
  78.4 3.1 %collective-permute-done.10 = f32[3,128,128]{2,1,0:T(8,128)S(1)} collective-permute-done((f32[3,128,128]{2,1,0:T(8,128)}, f32[3,128,128]{2,1,0:T(8,128)S(1)}, u32[]{:S(2)}, u32[]{:S(2)}) %collective-permute-start.10) | collective-permute-done | bytes 196640 | tf_op jit(solution)/shard_map/ppermute | solution.py:355
  81.6 0.3 collective-permute-done.11
  81.8 2.7 %collective-permute-done.12 = f32[3,128,128]{2,1,0:T(8,128)S(1)} collective-permute-done((f32[3,128,128]{2,1,0:T(8,128)}, f32[3,128,128]{2,1,0:T(8,128)S(1)}, u32[]{:S(2)}, u32[]{:S(2)}) %collective-permute-start.12) | collective-permute-done | bytes 196640 | tf_op jit(solution)/shard_map/ppermute | solution.py:355
  84.5 0.1 pad_maximum_fusion.1.rest_0_
  84.6 1.1 collective-permute-start.13
  85.7 1.1 collective-permute-start.17
  86.8 0.0 collective-permute-done.3
  86.8 1.0 add.404
  87.8 0.7 collective-permute-start.4
  88.5 0.7 pad_add_fusion.4.columns
  90.4 2.5 %collective-permute-start.1 = (f32[12,128,128]{2,1,0:T(8,128)}, f32[12,128,128]{2,1,0:T(8,128)}, u32[]{:S(2)}, u32[]{:S(2)}) collective-permute-start(f32[12,128,128]{2,1,0:T(8,128)} %get-tuple-element.15.t0), channel_id=1, source_target_pairs={{0,2},{1,3},{2,0},{3,1},{4,6},{5,7},{6,4},{7,5},{8,10},{9,11},{10,... | collective-permute-start | bytes 2359304 | tf_op jit(solution)/shard_map/ppermute | solution.py:395
  92.9 0.6 pad_add_fusion.5.places
  93.5 0.0 collective-permute-done.4
  93.6 0.7 collective-permute-start.5
  94.3 0.6 pad_add_fusion.2.columns
  99.4 0.7 pad_add_fusion.3.places
  100.1 0.0 collective-permute-done.5
  100.1 0.7 collective-permute-start.6
  100.8 4.1 %collective-permute-done.13.rest_1_ = f32[4,3,128,128]{3,2,1,0:T(8,128)S(1)} collective-permute-done((f32[4,3,128,128]{3,2,1,0:T(8,128)S(1)}, f32[4,3,128,128]{3,2,1,0:T(8,128)S(1)}, u32[]{:S(2)}, u32[]{:S(2)}) %collective-permute-start.13) | collective-permute-done | bytes 786464 | tf_op jit(solution)/shard_map/ppermute | solution.py:364
  104.9 14.7 %collective-permute-start.14 = (f32[4,3,128,128]{3,2,1,0:T(8,128)S(1)}, f32[4,3,128,128]{3,2,1,0:T(8,128)}, u32[]{:S(2)}, u32[]{:S(2)}) collective-permute-start(f32[4,3,128,128]{3,2,1,0:T(8,128)S(1)} %collective-permute-done.13.rest_1_), channel_id=1, source_target_pairs={{0,8},{8,16},{16,24},{24,28},{28,20},{20,12},{12,4},{4,0},{1,9},{9... | collective-permute-start | bytes 2359304 | tf_op jit(solution)/shard_map/ppermute | solution.py:364
  119.6 0.5 multiply_add_fusion.7.columns
  121.5 1.3 collective-permute-start.8
  122.8 0.7 pad_add_fusion.6.columns
  123.4 0.5 collective-permute-start.2
  123.9 0.6 pad_add_fusion.7.places
  124.5 0.2 convert_reduce_fusion.1
  124.8 18.8 %collective-permute-done.8 = f32[2,2,128,128]{3,2,1,0:T(8,128)S(1)} collective-permute-done((f32[2,2,128,128]{3,2,1,0:T(8,128)S(1)}, f32[2,2,128,128]{3,2,1,0:T(8,128)S(1)}, u32[]{:S(2)}, u32[]{:S(2)}) %collective-permute-start.8) | collective-permute-done | bytes 262176 | tf_op jit(solution)/shard_map/ppermute | solution.py:300
  143.6 0.7 collective-permute-start.7
  144.3 0.1 select_reduce_fusion.1
  144.4 0.8 convert_reduce_fusion.starts
  145.2 2.0 collective-permute-start.19
  147.2 0.1 copy.21
  147.3 0.6 reshape.111.order
  147.9 0.7 add_add_fusion.lead_ref
  148.6 8.0 %row_panels.1 = (bf16[1536,1024]{1,0:T(8,128)(2,1)}, f32[12,128,128]{2,1,0:T(8,128)}, bf16[3,256,256]{2,1,0:T(8,128)(2,1)}, bf16[3,256,256]{2,1,0:T(8,128)(2,1)}) custom-call(s32[2]{0:T(128)} %pad_add_fusion.1.place, f32[12,128,128]{2,1,0:T(8,128)} %get-tuple-element.15.t0, f32[12,128,128]{2,1,0:T(8,128)} %collective-permute-done.t1, ...), custom_call_target="tpu_custom_call" | custom-call | tf_op jit(solution)/shard_map/row_panels/pallas_call | solution.py:146
  156.7 16.8 %trailing.4.rest_2_ = f32[12,1,24,1,128,128]{5,4,3,2,1,0:T(8,128)} custom-call(s32[9]{0:T(128)} %pad_add_fusion.6.columns, s32[12]{0:T(128)} %pad_add_fusion.7.places, s32[64]{0:T(128)} %reshape.111.order, s32[25]{0:T(128)} %convert_reduce_fusion.starts, f32[12,1,24,1,128,128]{5,4,3,2,1,0:T(8,128)} %front_two.7, f32[12,1,24,1,128,128]{5,4,3,2,1,0:T(8,128)} %front_two.7, ...), custom_call_target="tpu_custom_call" | custom-call | flops 5435817984 | bytes 14155776 | tf_op jit(solution)/shard_map/trailing/pallas_call | solution.py:264
  173.5 0.1 collective-permute-start.16
  173.7 2.2 %collective-permute-start.20 = (f32[2,3,128,128]{3,2,1,0:T(8,128)S(1)}, f32[2,3,128,128]{3,2,1,0:T(8,128)S(1)}, u32[]{:S(2)}, u32[]{:S(2)}) collective-permute-start(f32[2,3,128,128]{3,2,1,0:T(8,128)S(1)} %slice.16), channel_id=1, source_target_pairs={{8,0},{16,8},{24,16},{28,24},{20,28},{12,20},{4,12},{0,4},{9,1},{1... | collective-permute-start | bytes 1179656 | tf_op jit(solution)/shard_map/ppermute | solution.py:368
  175.9 12.6 %trailing.5.rest_2_ = f32[12,1,24,1,128,128]{5,4,3,2,1,0:T(8,128)} custom-call(s32[6]{0:T(128)} %pad_add_fusion.4.columns, s32[8]{0:T(128)} %pad_add_fusion.5.places, s32[64]{0:T(128)} %reshape.111.order, s32[25]{0:T(128)} %convert_reduce_fusion.starts, f32[12,1,24,1,128,128]{5,4,3,2,1,0:T(8,128)} %front_two.7, ...), custom_call_target="tpu_custom_call", output_to_operand_aliasing={{}: (13, {})} | custom-call | flops 3623878656 | bytes 9437184 | tf_op jit(solution)/shard_map/trailing/pallas_call | solution.py:264
  188.5 12.6 %trailing.6.rest_1_ = f32[12,1,24,1,128,128]{5,4,3,2,1,0:T(8,128)} custom-call(s32[6]{0:T(128)} %pad_add_fusion.2.columns, s32[8]{0:T(128)} %pad_add_fusion.3.places, s32[64]{0:T(128)} %reshape.111.order, s32[25]{0:T(128)} %convert_reduce_fusion.starts, f32[12,1,24,1,128,128]{5,4,3,2,1,0:T(8,128)} %front_two.7, ...), custom_call_target="tpu_custom_call", output_to_operand_aliasing={{}: (13, {})} | custom-call | flops 3623878656 | bytes 9437184 | tf_op jit(solution)/shard_map/trailing/pallas_call | solution.py:264
  201.1 0.9 pad_maximum_fusion.2.rest_0_
  202.0 9.6 %trailing.7 = f32[12,1,24,1,128,128]{5,4,3,2,1,0:T(8,128)} custom-call(s32[3]{0:T(128)} %multiply_add_fusion.7.columns, s32[4]{0:T(128)} %and_select_fusion.9.places, s32[64]{0:T(128)} %reshape.111.order, s32[25]{0:T(128)} %convert_reduce_fusion.starts, f32[12,1,24,1,128,128]{5,4,3,2,1,0:T(8,128)} %front_two.7, ...), custom_call_target="tpu_custom_call", output_to_operand_aliasing={{}: (12, {})} | custom-call | flops 1811939328 | bytes 4718592 | tf_op jit(solution)/shard_map/trailing/pallas_call | solution.py:264
  (55 shorter events, 0.3 us)
Async XLA Ops:
  0.0 2.2 %copy-start = (f32[16,128,128]{2,1,0:T(8,128)S(1)}, f32[16,128,128]{2,1,0:T(8,128)}, u32[]{:S(2)}) copy-start(f32[16,128,128]{2,1,0:T(8,128)} %param.16) | copy-start | bytes 3145732
  4.8 7.3 %copy-start.9 = (s32[8]{0:T(128)S(1)}, s32[8]{0:T(128)}, u32[]{:S(2)}) copy-start(s32[8]{0:T(128)} %constant.268.clone) | copy-start | bytes 100
  4.8 12.4 %copy-start.7 = (s32[8]{0:T(128)S(1)}, s32[8]{0:T(128)}, u32[]{:S(2)}) copy-start(s32[8]{0:T(128)} %constant.269.clone) | copy-start | bytes 100
  4.8 58.9 %all-to-all-start = ((f32[32,136,128]{2,1,0:T(8,128)}), f32[32,136,128]{2,1,0:T(8,128)S(1)}, u32[]{:S(2)}, u32[]{:S(2)}) async-start(f32[32,136,128]{2,1,0:T(8,128)} %pad_maximum_fusion), calls=%async_computation | async-start | bytes 4456448 | tf_op jit(solution)/shard_map/all_to_all | solution.py:327
  63.7 3.1 %copy-start.2 = (f32[32,136,128]{2,1,0:T(8,128)}, f32[32,136,128]{2,1,0:T(8,128)S(1)}, u32[]{:S(2)}) copy-start(f32[32,136,128]{2,1,0:T(8,128)S(1)} %all-to-all-done.incoming_ref) | copy-start | bytes 6684676
  71.2 7.2 %collective-permute-start.9 = (f32[3,128,128]{2,1,0:T(8,128)}, f32[3,128,128]{2,1,0:T(8,128)S(1)}, u32[]{:S(2)}, u32[]{:S(2)}) collective-permute-start(f32[3,128,128]{2,1,0:T(8,128)} %get-tuple-element.21), channel_id=1, source_target_pairs={{0,0},{1,4},{2,8},{3,12},{4,1},{5,5},{6,9},{7,13},{8,2},{9,6},{10,... | collective-permute-start | bytes 589832 | tf_op jit(solution)/shard_map/ppermute | solution.py:355
  72.8 8.7 %collective-permute-start.10 = (f32[3,128,128]{2,1,0:T(8,128)}, f32[3,128,128]{2,1,0:T(8,128)S(1)}, u32[]{:S(2)}, u32[]{:S(2)}) collective-permute-start(f32[3,128,128]{2,1,0:T(8,128)} %get-tuple-element.22), channel_id=1, source_target_pairs={{0,4},{1,8},{2,12},{3,0},{4,5},{5,9},{6,13},{7,1},{8,6},{9,10},{10... | collective-permute-start | bytes 589832 | tf_op jit(solution)/shard_map/ppermute | solution.py:355
  73.8 8.1 %collective-permute-start.11 = (f32[3,128,128]{2,1,0:T(8,128)}, f32[3,128,128]{2,1,0:T(8,128)S(1)}, u32[]{:S(2)}, u32[]{:S(2)}) collective-permute-start(f32[3,128,128]{2,1,0:T(8,128)} %get-tuple-element.23), channel_id=1, source_target_pairs={{0,8},{1,12},{2,0},{3,4},{4,9},{5,13},{6,1},{7,5},{8,10},{9,14},{1... | collective-permute-start | bytes 589832 | tf_op jit(solution)/shard_map/ppermute | solution.py:355
  76.2 8.4 %collective-permute-start.12 = (f32[3,128,128]{2,1,0:T(8,128)}, f32[3,128,128]{2,1,0:T(8,128)S(1)}, u32[]{:S(2)}, u32[]{:S(2)}) collective-permute-start(f32[3,128,128]{2,1,0:T(8,128)} %get-tuple-element.24), channel_id=1, source_target_pairs={{0,12},{1,0},{2,4},{3,8},{4,13},{5,1},{6,5},{7,9},{8,14},{9,2},{10... | collective-permute-start | bytes 589832 | tf_op jit(solution)/shard_map/ppermute | solution.py:355
  76.5 10.3 %collective-permute-start.3 = (f32[2,2,128,128]{3,2,1,0:T(8,128)}, f32[2,2,128,128]{3,2,1,0:T(8,128)S(1)}, u32[]{:S(2)}, u32[]{:S(2)}) collective-permute-start(f32[2,2,128,128]{3,2,1,0:T(8,128)} %get-tuple-element.16), channel_id=1, source_target_pairs={{8,9},{9,8},{12,13},{13,12}} | collective-permute-start | bytes 786440 | tf_op jit(solution)/shard_map/ppermute | solution.py:291
  84.5 59.8 %copy-start.8 = (s32[32]{0:T(128)S(1)}, s32[32]{0:T(128)}, u32[]{:S(2)}) copy-start(s32[32]{0:T(128)} %get-tuple-element.35.row_of) | copy-start | bytes 388
  84.6 72.1 %copy-start.3 = (f32[4,3,128,128]{3,2,1,0:T(8,128)}, f32[4,3,128,128]{3,2,1,0:T(8,128)S(1)}, u32[]{:S(2)}) copy-start(f32[4,3,128,128]{3,2,1,0:T(8,128)S(1)} %pad_maximum_fusion.1.rest_0_) | copy-start | bytes 2359300
  84.6 20.3 %collective-permute-start.13 = (f32[4,3,128,128]{3,2,1,0:T(8,128)S(1)}, f32[4,3,128,128]{3,2,1,0:T(8,128)S(1)}, u32[]{:S(2)}, u32[]{:S(2)}) collective-permute-start(f32[4,3,128,128]{3,2,1,0:T(8,128)S(1)} %pad_maximum_fusion.1.rest_0_), channel_id=1, source_target_pairs={{0,8},{8,16},{16,24},{24,28},{28,20},{20,12},{12,4},{4,0},{1,9},{9... | collective-permute-start | bytes 2359304 | tf_op jit(solution)/shard_map/ppermute | solution.py:364
  85.7 33.8 %collective-permute-start.17 = (f32[4,3,128,128]{3,2,1,0:T(8,128)S(1)}, f32[4,3,128,128]{3,2,1,0:T(8,128)}, u32[]{:S(2)}, u32[]{:S(2)}) collective-permute-start(f32[4,3,128,128]{3,2,1,0:T(8,128)S(1)} %pad_maximum_fusion.1.rest_0_), channel_id=1, source_target_pairs={{8,0},{16,8},{24,16},{28,24},{20,28},{12,20},{4,12},{0,4},{9,1},{1... | collective-permute-start | bytes 2359304 | tf_op jit(solution)/shard_map/ppermute | solution.py:365
  87.8 5.7 %collective-permute-start.4 = (f32[2,2,128,128]{3,2,1,0:T(8,128)S(1)}, f32[2,2,128,128]{3,2,1,0:T(8,128)S(1)}, u32[]{:S(2)}, u32[]{:S(2)}) collective-permute-start(f32[2,2,128,128]{3,2,1,0:T(8,128)S(1)} %add.404), channel_id=1, source_target_pairs={{8,12},{9,13},{12,8},{13,9}} | collective-permute-start | bytes 786440 | tf_op jit(solution)/shard_map/ppermute | solution.py:294
  90.4 33.0 %collective-permute-start.1 = (f32[12,128,128]{2,1,0:T(8,128)}, f32[12,128,128]{2,1,0:T(8,128)}, u32[]{:S(2)}, u32[]{:S(2)}) collective-permute-start(f32[12,128,128]{2,1,0:T(8,128)} %get-tuple-element.15.t0), channel_id=1, source_target_pairs={{0,2},{1,3},{2,0},{3,1},{4,6},{5,7},{6,4},{7,5},{8,10},{9,11},{10,... | collective-permute-start | bytes 2359304 | tf_op jit(solution)/shard_map/ppermute | solution.py:395
  93.6 6.5 %collective-permute-start.5 = (f32[2,2,128,128]{3,2,1,0:T(8,128)S(1)}, f32[2,2,128,128]{3,2,1,0:T(8,128)S(1)}, u32[]{:S(2)}, u32[]{:S(2)}) collective-permute-start(f32[2,2,128,128]{3,2,1,0:T(8,128)S(1)} %add.405), channel_id=1, source_target_pairs={{8,10},{9,11},{12,14},{13,15}} | collective-permute-start | bytes 786440 | tf_op jit(solution)/shard_map/ppermute | solution.py:297
  100.1 23.3 %collective-permute-start.6 = (f32[2,2,128,128]{3,2,1,0:T(8,128)S(1)}, f32[2,2,128,128]{3,2,1,0:T(8,128)S(1)}, u32[]{:S(2)}, u32[]{:S(2)}) collective-permute-start(f32[2,2,128,128]{3,2,1,0:T(8,128)S(1)} %add.406), channel_id=1, source_target_pairs={{8,16},{12,20},{9,17},{13,21},{10,18},{14,22},{11,19},{15,23}} | collective-permute-start | bytes 786440 | tf_op jit(solution)/shard_map/ppermute | solution.py:302
  104.9 40.3 %copy-start.6 = (f32[4,3,128,128]{3,2,1,0:T(8,128)}, f32[4,3,128,128]{3,2,1,0:T(8,128)S(1)}, u32[]{:S(2)}) copy-start(f32[4,3,128,128]{3,2,1,0:T(8,128)S(1)} %collective-permute-done.13.rest_1_) | copy-start | bytes 2359300
  104.9 40.3 %collective-permute-start.14 = (f32[4,3,128,128]{3,2,1,0:T(8,128)S(1)}, f32[4,3,128,128]{3,2,1,0:T(8,128)}, u32[]{:S(2)}, u32[]{:S(2)}) collective-permute-start(f32[4,3,128,128]{3,2,1,0:T(8,128)S(1)} %collective-permute-done.13.rest_1_), channel_id=1, source_target_pairs={{0,8},{8,16},{16,24},{24,28},{28,20},{20,12},{12,4},{4,0},{1,9},{9... | collective-permute-start | bytes 2359304 | tf_op jit(solution)/shard_map/ppermute | solution.py:364
  119.6 25.6 %collective-permute-start.18 = (f32[4,3,128,128]{3,2,1,0:T(8,128)}, f32[4,3,128,128]{3,2,1,0:T(8,128)}, u32[]{:S(2)}, u32[]{:S(2)}) collective-permute-start(f32[4,3,128,128]{3,2,1,0:T(8,128)} %collective-permute-done.17.rest_2_), channel_id=1, source_target_pairs={{8,0},{16,8},{24,16},{28,24},{20,28},{12,20},{4,12},{0,4},{9,1},{1... | collective-permute-start | bytes 2359304 | tf_op jit(solution)/shard_map/ppermute | solution.py:365
  121.5 22.1 %collective-permute-start.8 = (f32[2,2,128,128]{3,2,1,0:T(8,128)S(1)}, f32[2,2,128,128]{3,2,1,0:T(8,128)S(1)}, u32[]{:S(2)}, u32[]{:S(2)}) collective-permute-start(f32[2,2,128,128]{3,2,1,0:T(8,128)S(1)} %add.406), channel_id=1, source_target_pairs={{8,0},{12,4},{9,1},{13,5},{10,2},{14,6},{11,3},{15,7}} | collective-permute-start | bytes 786440 | tf_op jit(solution)/shard_map/ppermute | solution.py:300
  123.4 25.2 %collective-permute-start = (f32[12,128,128]{2,1,0:T(8,128)}, f32[12,128,128]{2,1,0:T(8,128)}, u32[]{:S(2)}, u32[]{:S(2)}) collective-permute-start(f32[12,128,128]{2,1,0:T(8,128)} %get-tuple-element.15.t0), channel_id=1, source_target_pairs={{0,1},{1,0},{2,3},{3,2},{4,5},{5,4},{6,7},{7,6},{8,9},{9,8},{10,11... | collective-permute-start | bytes 2359304 | tf_op jit(solution)/shard_map/ppermute | solution.py:394
  123.4 25.2 %collective-permute-start.2 = (f32[12,128,128]{2,1,0:T(8,128)}, f32[12,128,128]{2,1,0:T(8,128)}, u32[]{:S(2)}, u32[]{:S(2)}) collective-permute-start(f32[12,128,128]{2,1,0:T(8,128)} %collective-permute-done.1.t2), channel_id=1, source_target_pairs={{0,1},{1,0},{2,3},{3,2},{4,5},{5,4},{6,7},{7,6},{8,9},{9,8},{10,11... | collective-permute-start | bytes 2359304 | tf_op jit(solution)/shard_map/ppermute | solution.py:396
  143.6 4.3 %collective-permute-start.7 = (f32[2,2,128,128]{3,2,1,0:T(8,128)S(1)}, f32[2,2,128,128]{3,2,1,0:T(8,128)S(1)}, u32[]{:S(2)}, u32[]{:S(2)}) collective-permute-start(f32[2,2,128,128]{3,2,1,0:T(8,128)S(1)} %add.407), channel_id=1, source_target_pairs={{16,24},{20,28},{17,25},{21,29},{18,26},{22,30},{19,27},{23,31}} | collective-permute-start | bytes 786440 | tf_op jit(solution)/shard_map/ppermute | solution.py:302
  145.2 28.3 %collective-permute-start.15 = (f32[4,3,128,128]{3,2,1,0:T(8,128)}, f32[4,3,128,128]{3,2,1,0:T(8,128)S(1)}, u32[]{:S(2)}, u32[]{:S(2)}) collective-permute-start(f32[4,3,128,128]{3,2,1,0:T(8,128)} %collective-permute-done.14.rest_0_), channel_id=1, source_target_pairs={{0,8},{8,16},{16,24},{24,28},{28,20},{20,12},{12,4},{4,0},{1,9},{9... | collective-permute-start | bytes 2359304 | tf_op jit(solution)/shard_map/ppermute | solution.py:364
  145.2 28.4 %collective-permute-start.19 = (f32[4,3,128,128]{3,2,1,0:T(8,128)}, f32[4,3,128,128]{3,2,1,0:T(8,128)S(1)}, u32[]{:S(2)}, u32[]{:S(2)}) collective-permute-start(f32[4,3,128,128]{3,2,1,0:T(8,128)} %collective-permute-done.18.rest_1_), channel_id=1, source_target_pairs={{8,0},{16,8},{24,16},{28,24},{20,28},{12,20},{4,12},{0,4},{9,1},{1... | collective-permute-start | bytes 2359304 | tf_op jit(solution)/shard_map/ppermute | solution.py:365
  173.5 15.0 %copy-start.4 = (f32[4,3,128,128]{3,2,1,0:T(8,128)}, f32[4,3,128,128]{3,2,1,0:T(8,128)S(1)}, u32[]{:S(2)}) copy-start(f32[4,3,128,128]{3,2,1,0:T(8,128)S(1)} %collective-permute-done.15.rest_0_) | copy-start | bytes 2359300
  173.5 27.5 %collective-permute-start.16 = (f32[2,3,128,128]{3,2,1,0:T(8,128)S(1)}, f32[2,3,128,128]{3,2,1,0:T(8,128)S(1)}, u32[]{:S(2)}, u32[]{:S(2)}) collective-permute-start(f32[2,3,128,128]{3,2,1,0:T(8,128)S(1)} %slice.15), channel_id=1, source_target_pairs={{0,8},{8,16},{16,24},{24,28},{28,20},{20,12},{12,4},{4,0},{1,9},{9... | collective-permute-start | bytes 1179656 | tf_op jit(solution)/shard_map/ppermute | solution.py:368
  173.6 14.8 %copy-start.5 = (f32[4,3,128,128]{3,2,1,0:T(8,128)}, f32[4,3,128,128]{3,2,1,0:T(8,128)S(1)}, u32[]{:S(2)}) copy-start(f32[4,3,128,128]{3,2,1,0:T(8,128)S(1)} %collective-permute-done.19.rest_1_) | copy-start | bytes 2359300
  173.7 27.4 %collective-permute-start.20 = (f32[2,3,128,128]{3,2,1,0:T(8,128)S(1)}, f32[2,3,128,128]{3,2,1,0:T(8,128)S(1)}, u32[]{:S(2)}, u32[]{:S(2)}) collective-permute-start(f32[2,3,128,128]{3,2,1,0:T(8,128)S(1)} %slice.16), channel_id=1, source_target_pairs={{8,0},{16,8},{24,16},{28,24},{20,28},{12,20},{4,12},{0,4},{9,1},{1... | collective-permute-start | bytes 1179656 | tf_op jit(solution)/shard_map/ppermute | solution.py:368
  202.0 9.6 %copy-start.1 = (f32[16,128,128]{2,1,0:T(8,128)S(1)}, f32[16,128,128]{2,1,0:T(8,128)}, u32[]{:S(2)}) copy-start(f32[16,128,128]{2,1,0:T(8,128)} %param.16) | copy-start | bytes 3145732
where the time goes:
time: 213 us; the launch traced here: 212 us
  Pallas kernels  64 us (30%)
  waiting for transfers between devices  61.7 us (29%)
  starting transfers between devices  41.4 us (19%)
  between operations  26.2 us (12%)
  other arithmetic  15.7 us (7%)
  local copies, waits for them, and re-layouts  2.81 us (1%)
    pallas_call x4, Pallas kernels, trailing(): pl.pallas_call(functools.partial(trailing_kernel, len(pieces)), grid_spec...  51.5 us
    all_to_all x1, waiting for transfers between devices, body(): lax.all_to_all(outgoing, BOTH, split_axis=0, concat_axis=0, tiled=True)  32.6 us
    ppermute x1, waiting for transfers between devices, spread_lead(): below = lax.ppermute(lead, 'row', [(2, 0), (3, 1)])  18.8 us
    ppermute x3, starting transfers between devices, body(): ahead = lax.ppermute(ahead, 'row', up)  15.8 us
    pallas_call x1, Pallas kernels, row_panels(): pl.pallas_call(row_panels_kernel, grid_spec=pltpu.PrefetchScalarGridSpec(...  8.05 us
    all_to_all x1, starting transfers between devices, body(): lax.all_to_all(outgoing, BOTH, split_axis=0, concat_axis=0, tiled=True)  7.3 us
    ppermute x4, waiting for transfers between devices, body(): arrived.append(lax.ppermute(part, BOTH, pairs))  6.11 us
    ppermute x4, starting transfers between devices, body(): arrived.append(lax.ppermute(part, BOTH, pairs))  5.22 us
  transfers between devices with their start and end apart: 22, of which 6 were waited for; matrix products, arithmetic and copies ran while one was open for 5% of the time, Pallas kernels for 24%

commit v1 on v0

v1 whole, which is shorter than its diff:
```python
import functools

import jax
import jax.numpy as jnp
from jax import lax
from jax.experimental import pallas as pl
from jax.experimental.pallas import tpu as pltpu
from jax.sharding import PartitionSpec as P

TILE = 128
PANEL = 256
WIDTH = 2 * PANEL
NOTE = 8
VMEM = 48 * 1024 * 1024
NT = (((1,), (1,)), ((), ()))
NN = (((1,), (0,)), ((), ()))
BOTH = ("row", "col")


def halves(value):
    high = value.astype(jnp.bfloat16)
    low = (value - high.astype(jnp.float32)).astype(jnp.bfloat16)
    return high, low


def product(left, right, dims):
    dot = functools.partial(
        lax.dot_general, dimension_numbers=dims, preferred_element_type=jnp.float32
    )
    return dot(left[0], right[0]) + (dot(left[0], right[1]) + dot(left[1], right[0]))


def whole_spec(array):
    rank = len(array.shape)
    return pl.BlockSpec(array.shape, lambda *_: (0,) * rank)


def columns_kernel(place, slot_in, front_ref, incoming_ref, out_ref, *rest):
    *parts, tile_ref, sem = rest
    cols = place[2]
    out_ref[...] = front_ref[:, 0, 0, 0]

    @pl.loop(0, incoming_ref.shape[0])
    def _(s):
        slot = slot_in[s]

        @pl.when(jnp.logical_and(slot >= 0, lax.rem(slot, cols) == 0))
        def _():
            copy = pltpu.make_async_copy(incoming_ref.at[s, pl.ds(0, TILE)], tile_ref, sem)
            copy.start()
            copy.wait()
            row = lax.div(slot, cols)
            out_ref[row] = out_ref[row] + tile_ref[...]

    count = len(parts)
    for j, part_ref in enumerate(parts):
        group = part_ref.shape[0]
        part_ref[...] = out_ref[pl.ds(lax.rem(place[1] + j, count) * group, group)]


def assemble_columns(front, incoming, place, slot_in, parts):
    rows = front.shape[0]
    shapes = [(rows, TILE, TILE)] + [(rows // parts, TILE, TILE)] * parts
    out_shape = [jax.ShapeDtypeStruct(shape, jnp.float32) for shape in shapes]
    return pl.pallas_call(
        columns_kernel,
        grid_spec=pltpu.PrefetchScalarGridSpec(
            num_scalar_prefetch=2,
            grid=(1,),
            in_specs=[
                pl.BlockSpec((rows, 1, 1, 1, TILE, TILE), lambda i, *_: (0, 0, 0, 0, 0, 0)),
                pl.BlockSpec(memory_space=pl.ANY),
            ],
            out_specs=[whole_spec(a) for a in out_shape],
            scratch_shapes=[pltpu.VMEM((TILE, TILE), jnp.float32), pltpu.SemaphoreType.DMA],
        ),
        out_shape=out_shape,
        compiler_params=pltpu.CompilerParams(vmem_limit_bytes=VMEM),
        name="panel_columns",
    )(place, slot_in, front, incoming)


def row_panels_kernel(
    place, tiles_ref, lead_ref, diag_ref, pair_ref, out_ref, small_high_ref, small_low_ref
):
    step = pl.program_id(0)
    my_row, my_col = place[0], place[1]
    group = tiles_ref.shape[1]
    height = group * TILE

    @pl.when(step == 0)
    def _():
        inverse_one = halves(diag_ref[0])
        lead = jnp.concatenate(
            [jnp.concatenate([lead_ref[i, 0], lead_ref[i, 1]], axis=1) for i in range(2)], axis=0
        )
        lead = halves(product(halves(lead), inverse_one, NN))
        inverse_two = halves(diag_ref[1])
        for index, pair in enumerate((inverse_one, lead, inverse_two)):
            small_high_ref[index] = pair[0]
            small_low_ref[index] = pair[1]

    small = [(small_high_ref[i], small_low_ref[i]) for i in range(3)]
    columns = [tiles_ref[c].reshape(height, TILE) for c in range(4)]
    tile_row = lax.broadcasted_iota(jnp.int32, (height, PANEL), 0) // TILE
    first = jnp.logical_and(step == 0, tile_row == 0)
    above_one = jnp.logical_and(first, my_row < 2)
    above_two = jnp.logical_and(first, my_row < 4)
    one = product(halves(jnp.concatenate(columns[:2], axis=1)), small[0], NN)
    one_pair = halves(jnp.where(above_one, 0.0, one))
    field = jnp.concatenate(columns[2:], axis=1) - product(one_pair, small[1], NT)
    two = jnp.where(above_one, 0.0, product(halves(field), small[2], NN))
    two_pair = halves(jnp.where(above_two, 0.0, two))
    for i in range(2):
        pair_ref[:, i * WIDTH : i * WIDTH + PANEL] = one_pair[i]
        pair_ref[:, i * WIDTH + PANEL : (i + 1) * WIDTH] = two_pair[i]
    pieces = (one[:, :TILE], one[:, TILE:], two[:, :TILE], two[:, TILE:])
    for c in range(4):

        @pl.when(my_col == c)
        def _():
            out_ref[:, 0, 0, 0] = pieces[c].reshape(group, TILE, TILE)


def row_panels(tiles, lead, diag, place, front):
    rows = tiles.shape[1]
    group = rows // 3
    height = group * TILE
    out_shape = [
        jax.ShapeDtypeStruct((rows * TILE, 2 * WIDTH), jnp.bfloat16),
        jax.ShapeDtypeStruct(front.shape, jnp.float32),
        jax.ShapeDtypeStruct((3, PANEL, PANEL), jnp.bfloat16),
        jax.ShapeDtypeStruct((3, PANEL, PANEL), jnp.bfloat16),
    ]
    return pl.pallas_call(
        row_panels_kernel,
        grid_spec=pltpu.PrefetchScalarGridSpec(
            num_scalar_prefetch=1,
            grid=(3,),
            in_specs=[
                pl.BlockSpec((4, group, TILE, TILE), lambda i, *_: (0, i, 0, 0)),
                whole_spec(lead),
                whole_spec(diag),
            ],
            out_specs=[
                pl.BlockSpec((height, 2 * WIDTH), lambda i, *_: (i, 0)),
                pl.BlockSpec((group, 1, 1, 1, TILE, TILE), lambda i, *_: (i, 0, 0, 0, 0, 0)),
                whole_spec(out_shape[2]),
                whole_spec(out_shape[3]),
            ],
        ),
        out_shape=out_shape,
        compiler_params=pltpu.CompilerParams(vmem_limit_bytes=VMEM),
        name="row_panels",
    )(place, tiles, lead, diag)


def trailing_kernel(
    n_pieces, columns, places, order, starts, front_one, front_two, pair_ref, small_high_ref,
    small_low_ref, incoming_ref, *rest,
):
    piece_refs = rest[:n_pieces]
    out_ref, right_ref, buffer, sems, child_ref, child_sems = rest[-6:]
    step, steps = pl.program_id(0), pl.num_programs(0)
    group = piece_refs[0].shape[1]
    count = n_pieces * group
    rows = front_one.shape[0]
    slot = lax.rem(step, 2)

    def columns_of(at_step):
        for j in range(2):
            index = jnp.minimum(2 * at_step, count - 2) + j
            wanted = columns[index] > 0
            if count % 2 and j == 0:
                wanted = jnp.logical_and(wanted, at_step < steps - 1)
            yield j, columns[index], wanted

    def each_copy(at_step, act):
        at_slot = lax.rem(at_step, 2)
        for j, b, wanted in columns_of(at_step):

            @pl.when(wanted)
            def _():
                act(
                    pltpu.make_async_copy(
                        buffer.at[at_slot, j], out_ref.at[:, 0, b, 0], sems.at[at_slot, j]
                    )
                )

    def child_copy(s):
        return pltpu.make_async_copy(
            incoming_ref.at[s, pl.ds(0, TILE)], child_ref.at[s], child_sems.at[s]
        )

    @pl.when(step == 0)
    def _():
        for t in range(count):
            b = columns[t]

            @pl.when(b > 0)
            def _():
                @pl.loop(starts[b], starts[b + 1])
                def _(i):
                    child_copy(order[2 * i]).start()

        small = [(small_high_ref[i], small_low_ref[i]) for i in range(3)]
        for p, piece in enumerate(piece_refs):
            columns_here = [piece[places[4 * p + c]].reshape(group * TILE, TILE) for c in range(4)]
            one = product(halves(jnp.concatenate(columns_here[:2], axis=1)), small[0], NN)
            field = jnp.concatenate(columns_here[2:], axis=1)
            field = field - product(halves(one), small[1], NT)
            two = product(halves(field), small[2], NN)
            span = slice(p * group * TILE, (p + 1) * group * TILE)
            for i, panel in enumerate((one, two)):
                for k, half in enumerate(halves(panel.T)):
                    top = 2 * k * WIDTH + i * PANEL
                    right_ref[top : top + PANEL, span] = half
                    if k == 0:
                        right_ref[top + WIDTH : top + WIDTH + PANEL, span] = half

    @pl.when(step >= 2)
    def _():
        each_copy(step - 2, lambda copy: copy.wait())

    start = jnp.minimum(2 * step, count - 2)
    lanes = pl.ds(pl.multiple_of(start * TILE, TILE), 2 * TILE)
    block = rows // 3
    for m in range(3):
        left = pair_ref[m * block * TILE : (m + 1) * block * TILE]
        left = jnp.concatenate([left, left[:, :WIDTH]], axis=1)
        update = jnp.dot(left, right_ref[:, lanes], preferred_element_type=jnp.float32)
        span = slice(m * block, (m + 1) * block)
        for j, front_ref in enumerate((front_one, front_two)):
            part = update[:, j * TILE : (j + 1) * TILE].reshape(block, TILE, TILE)
            buffer[slot, j, span] = front_ref[span, 0, 0, 0] - part

    for j, b, wanted in columns_of(step):

        @pl.when(wanted)
        def _():
            @pl.loop(starts[b], starts[b + 1])
            def _(i):
                s, a = order[2 * i], order[2 * i + 1]
                child_copy(s).wait()
                buffer[slot, j, a] = buffer[slot, j, a] + child_ref[s]

    each_copy(step, lambda copy: copy.start())

    @pl.when(step == steps - 1)
    def _():
        if count > 2:
            each_copy(step - 1, lambda copy: copy.wait())
        each_copy(step, lambda copy: copy.wait())


def trailing(front, pieces, columns, places, panels, incoming, order, starts):
    rows = front.shape[0]
    pair, out, small_high, small_low = panels
    group = pieces[0].shape[1]
    count = len(pieces) * group
    steps = (count + 1) // 2

    def strip(j):
        def index(i, columns, *_):
            return (0, 0, columns[jnp.minimum(2 * i, count - 2) + j], 0, 0, 0)

        return pl.BlockSpec((rows, 1, 1, 1, TILE, TILE), index)

    anywhere = pl.BlockSpec(memory_space=pl.ANY)
    operands = [front, front, pair, small_high, small_low, incoming, *pieces, out]
    in_specs = [strip(0), strip(1), *[whole_spec(a) for a in operands[2:5]], anywhere]
    in_specs += [*[whole_spec(a) for a in pieces], anywhere]
    height = rows * TILE
    devices = incoming.shape[0]
    return pl.pallas_call(
        functools.partial(trailing_kernel, len(pieces)),
        grid_spec=pltpu.PrefetchScalarGridSpec(
            num_scalar_prefetch=4,
            grid=(steps,),
            in_specs=in_specs,
            out_specs=anywhere,
            scratch_shapes=[
                pltpu.VMEM((3 * WIDTH, count * TILE), jnp.bfloat16),
                pltpu.VMEM((2, 2, rows, TILE, TILE), jnp.float32),
                pltpu.SemaphoreType.DMA((2, 2)),
                pltpu.VMEM((devices, TILE, TILE), jnp.float32),
                pltpu.SemaphoreType.DMA((devices,)),
            ],
        ),
        out_shape=jax.ShapeDtypeStruct(front.shape, jnp.float32),
        input_output_aliases={len(operands) + 3: 0},
        compiler_params=pltpu.CompilerParams(vmem_limit_bytes=VMEM),
        cost_estimate=pl.CostEstimate(
            flops=count * 2 * height * TILE * WIDTH * 3,
            bytes_accessed=count * 2 * height * TILE * 4,
            transcendentals=0,
        ),
        name="trailing",
    )(columns, places, order, starts, *operands)


def body(front, child_tiles, tile_dest, tile_slot, tile_count, diag_inverses):
    n_row = lax.axis_size("row")
    n_col = lax.axis_size("col")
    my_row = lax.axis_index("row").astype(jnp.int32)
    my_col = lax.axis_index("col").astype(jnp.int32)
    rows_here, cols_here = (front.shape[0], front.shape[2])
    slots = child_tiles.shape[0]
    devices = n_row * n_col
    assert n_col == 4 and n_row % 4 == 0 and rows_here % 3 == 0
    place = jnp.stack([my_row, my_col, jnp.int32(cols_here)])

    numbers = jnp.arange(slots, dtype=jnp.int32)
    live = numbers < tile_count[0]
    dest = tile_dest[:, 0]
    hits = (dest[None, :] == jnp.arange(devices, dtype=jnp.int32)[:, None]) & live[None, :]
    picked = jnp.sum(jnp.where(hits, numbers[None, :], 0), axis=1)
    slot_out = jnp.sum(jnp.where(hits, tile_slot[None, :] + 1, 0), axis=1) - 1
    notes = jnp.broadcast_to(
        slot_out.astype(jnp.float32)[:, None, None], (devices, NOTE, TILE)
    )
    taken = jnp.take(child_tiles, picked, axis=0)
    outgoing = jnp.concatenate([taken, notes], axis=1)
    incoming = lax.all_to_all(outgoing, BOTH, split_axis=0, concat_axis=0, tiled=True)
    slot_in = lax.optimization_barrier(incoming[:, TILE, 0].astype(jnp.int32))

    me = my_row * n_col + my_col
    lead = []
    for owner in [r * n_col + c for r in (2, 3) for c in (0, 1)]:
        own = jnp.where(me == owner, front[0, 0, 0, 0], 0.0)
        lead.append(own + jnp.where(slot_out[owner] == 0, taken[owner], 0.0))
    lead = lax.psum(jnp.stack(lead).reshape(2, 2, TILE, TILE), BOTH)

    row_of = jnp.where(slot_in >= 0, slot_in // cols_here, 0)
    col_of = jnp.where(slot_in >= 0, slot_in % cols_here, -1)
    sources = jnp.arange(devices, dtype=jnp.int32)
    key = jnp.where(slot_in >= 0, col_of, cols_here) * devices + sources
    rank = jnp.sum((key[None, :] < key[:, None]).astype(jnp.int32), axis=1)
    at = rank[None, :] == sources[:, None]
    order = jnp.stack(
        [jnp.sum(jnp.where(at, v[None, :], 0), axis=1) for v in (sources, row_of)], axis=1
    ).reshape(-1)
    edges = jnp.arange(cols_here + 1, dtype=jnp.int32) * devices
    starts = jnp.sum((key[None, :] < edges[:, None]).astype(jnp.int32), axis=1)

    ring = rows_here % n_col == 0
    mine, *parts = assemble_columns(front, incoming, place, slot_in, n_col if ring else 1)
    tiles = lax.all_gather(mine, "col", axis=0, tiled=False)

    sets = n_row // n_col
    if ring:
        arrived = []
        for j, part in enumerate(parts):
            pairs = [
                (r * n_col + c, ((r // n_col) * n_col + (c + j) % n_col) * n_col + r % n_col)
                for r in range(n_row)
                for c in range(n_col)
            ]
            arrived.append(lax.ppermute(part, BOTH, pairs))
        piece = jnp.stack(arrived)
        circle = list(range(0, n_row, 2)) + list(range(n_row - 1, 0, -2))
        spot = jnp.asarray([circle.index(r) for r in range(n_row)], jnp.int32)[my_row]
        up = [(circle[i], circle[(i + 1) % n_row]) for i in range(n_row)]
        down = [(b, a) for a, b in up]
        rounds = [[(piece, 0)]]
        ahead = behind = piece
        for step in range(1, n_row // 2):
            ahead = lax.ppermute(ahead, "row", up)
            behind = lax.ppermute(behind, "row", down)
            rounds.append([(ahead, -step), (behind, step)])
        last = jnp.concatenate(
            [lax.ppermute(ahead[:2], "row", up), lax.ppermute(behind[2:], "row", down)]
        )
        rounds.append([(last, n_row // 2)])
        rounds = [rounds[0] + rounds[1]] + rounds[2:]

        def described(shift):
            origin = jnp.asarray(circle, jnp.int32)[(spot + shift + n_row) % n_row]
            part, group = origin % n_col, rows_here // n_col
            row = part * group + jnp.arange(group, dtype=jnp.int32)
            places = (part - jnp.arange(n_col, dtype=jnp.int32) + n_col) % n_col
            return row * sets + origin // n_col, places

    else:
        pairs = [
            (r * n_col + c, ((r // n_col) * n_col + c) * n_col + r % n_col)
            for r in range(n_row)
            for c in range(n_col)
        ]
        moved = lax.all_gather(lax.ppermute(mine, BOTH, pairs), "row", axis=0, tiled=False)
        rounds = [[(moved[h * n_col : (h + 1) * n_col], h)] for h in range(sets)]

        def described(h):
            row = jnp.arange(rows_here, dtype=jnp.int32)
            return row * sets + h, jnp.arange(n_col, dtype=jnp.int32)

    panels = row_panels(tiles, lead, diag_inverses, place, front)
    for entries in rounds:
        described_here = [described(shift) for _, shift in entries]
        columns = jnp.concatenate([d[0] for d in described_here])
        places = jnp.concatenate([d[1] for d in described_here])
        pieces = [p for p, _ in entries]
        out = trailing(front, pieces, columns, places, panels, incoming, order, starts)
        panels = [panels[0], out, *panels[2:]]
    return panels[1]


def solution(mesh):
    return jax.shard_map(
        body,
        mesh=mesh,
        in_specs=(
            P(None, "row", None, "col", None, None),
            P(BOTH, None, None),
            P(BOTH, None),
            P(BOTH),
            P(BOTH),
            P(),
        ),
        out_specs=P(None, "row", None, "col", None, None),
        check_vma=False,
    )
```

time: 213 us -> 248 us (1.16)
  waiting for transfers between devices: 61.7 us -> 96.2 us
  starting transfers between devices: 41.4 us -> 23.8 us
  between operations: 26.2 us -> 43.8 us
  local copies, waits for them, and re-layouts: 2.81 us -> 14.5 us
  Pallas kernels: 64 us -> 56.8 us
  other arithmetic: 15.7 us -> 11.5 us
    ppermute x3, waiting for transfers between devices: 0.01 us -> 30.9 us  [body(): behind = lax.ppermute(behind, 'row', down)]
    ppermute x9 -> x0, waiting for transfers between devices: 18.9 us -> none  [the longest x1 18.8 us: spread_lead(): below = lax.ppermute(lead, 'row', [(2, 0), (3, 1)])]
    all_to_all x1, waiting for transfers between devices: 32.6 us -> 47.9 us  [body(): lax.all_to_all(outgoing, BOTH, split_axis=0, concat_axis=0, tiled=True)]
    ppermute x3, starting transfers between devices: 15.8 us -> 0.82 us  [body(): ahead = lax.ppermute(ahead, 'row', up)]
    ppermute x9 -> x0, starting transfers between devices: 7.67 us -> none  [the longest x1 2.5 us: body(): far = lax.ppermute(mine, 'col', [(c, c ^ 2) for c in range(n_col)])]
    unnamed x20 -> x24, local copies, waits for them, and re-layouts: 0.04 us -> 6.71 us
    ppermute x1, waiting for transfers between devices: 0.01 us -> 6.5 us  [body(): lax.ppermute(behind[2:], 'row', down)]
    ppermute x3, starting transfers between devices: 3.1 us -> 7.55 us  [body(): behind = lax.ppermute(behind, 'row', down)]
  transfers between devices with their start and end apart: 22 -> 15, of which waited for: 6 -> 8; matrix products, arithmetic and copies ran while one was open for 5% -> 5% of each run, Pallas kernels for 24% -> 1%
where the time goes in v1:
time: 248 us; the launch traced here: 247 us
  waiting for transfers between devices  96.2 us (39%)
  Pallas kernels  56.8 us (23%)
  between operations  43.8 us (18%)
  starting transfers between devices  23.8 us (10%)
  local copies, waits for them, and re-layouts  14.5 us (6%)
  other arithmetic  11.5 us (5%)
    all_to_all x1, waiting for transfers between devices, body(): lax.all_to_all(outgoing, BOTH, split_axis=0, concat_axis=0, tiled=True)  47.9 us
    pallas_call x4, Pallas kernels, trailing(): pl.pallas_call(functools.partial(trailing_kernel, len(pieces)), grid_spec...  47.5 us
    ppermute x3, waiting for transfers between devices, body(): behind = lax.ppermute(behind, 'row', down)  30.9 us
    ppermute x4, waiting for transfers between devices, body(): arrived.append(lax.ppermute(part, BOTH, pairs))  8.09 us
    ppermute x3, starting transfers between devices, body(): behind = lax.ppermute(behind, 'row', down)  7.55 us
    all_to_all x1, starting transfers between devices, body(): lax.all_to_all(outgoing, BOTH, split_axis=0, concat_axis=0, tiled=True)  7.3 us
    pallas_call x1, Pallas kernels, row_panels(): pl.pallas_call(row_panels_kernel, grid_spec=pltpu.PrefetchScalarGridSpec(...  6.73 us
    unnamed x24, local copies, waits for them, and re-layouts  6.71 us
  transfers between devices with their start and end apart: 15, of which 8 were waited for; matrix products, arithmetic and copies ran while one was open for 5% of the time, Pallas kernels for 1%

profile of v1, /device:TPU:0, one launch (start us, length us, event | category | flops | bytes accessed | tf_op | source)
XLA Modules:
  0.0 246.7 jit_solution(14020332638619867812)
XLA Ops:
  8.1 0.7 broadcast_add_fusion.1
  8.8 0.7 select_reduce_fusion.3
  9.6 2.0 gather_fusion
  11.6 1.8 broadcast_select_fusion
  13.4 0.1 broadcast_in_dim.86
  13.5 1.8 pad_maximum_fusion
  15.3 0.2 copy-done.9
  15.5 7.3 %all-to-all-start = ((f32[32,136,128]{2,1,0:T(8,128)}), f32[32,136,128]{2,1,0:T(8,128)S(1)}, u32[]{:S(2)}, u32[]{:S(2)}) async-start(f32[32,136,128]{2,1,0:T(8,128)} %pad_maximum_fusion), calls=%async_computation | async-start | bytes 4456448 | tf_op jit(solution)/shard_map/all_to_all | solution.py:324
  22.8 0.0 all-reduce.2.cloned.1.call-start
  22.8 0.6 fusion.17
  26.0 1.0 fusion.3
  27.0 0.7 pad_maximum_fusion.3
  27.7 0.0 all-gather.3.cloned.1.call-start
  27.7 0.1 pad_add_fusion.1.place
  27.8 47.9 %all-to-all-done.incoming_ref = f32[32,136,128]{2,1,0:T(8,128)S(1)} async-done(((f32[32,136,128]{2,1,0:T(8,128)}), f32[32,136,128]{2,1,0:T(8,128)S(1)}, u32[]{:S(2)}, u32[]{:S(2)}) %all-to-all-start) | async-done | bytes 2228256 | tf_op jit(solution)/shard_map/all_to_all | solution.py:324
  75.7 0.7 fusion.4.slot_in
  76.4 2.6 %panel_columns.1 = (f32[12,128,128]{2,1,0:T(8,128)S(1)}, f32[3,128,128]{2,1,0:T(8,128)S(1)}, f32[3,128,128]{2,1,0:T(8,128)S(1)}, f32[3,128,128]{2,1,0:T(8,128)S(1)}, f32[3,128,128]{2,1,0:T(8,128)S(1)}) custom-call(s32[3]{0:T(128)S(1)} %pad_add_fusion.1.place, s32[32]{0:T(128)S(1)} %fusion.4.slot_in, f32[12,1,24,1,128,128]{5,4,3,2,1,0:T(8,128)} %front_two.7, ...), custom_call_target="tpu_custom_call" | custom-call | tf_op jit(solution)/shard_map/panel_columns/pallas_call | solution.py:65
  79.0 0.9 copy-done.3
  79.9 0.7 copy-done.6
  80.5 0.7 copy-done.7
  81.2 0.7 copy-done.8
  81.9 0.0 all-gather.3.cloned.1.call-update
  81.9 1.6 collective-permute-start
  83.5 1.7 collective-permute-start.1
  85.3 2.7 %collective-permute-start.2 = (f32[3,128,128]{2,1,0:T(8,128)}, f32[3,128,128]{2,1,0:T(8,128)S(1)}, u32[]{:S(2)}, u32[]{:S(2)}) collective-permute-start(f32[3,128,128]{2,1,0:T(8,128)} %copy-done.6), channel_id=1, source_target_pairs={{0,8},{1,12},{2,0},{3,4},{4,9},{5,13},{6,1},{7,5},{8,10},{9,14},{1... | collective-permute-start | bytes 589832 | tf_op jit(solution)/shard_map/ppermute | solution.py:359
  88.0 5.1 %collective-permute-done.1 = f32[3,128,128]{2,1,0:T(8,128)S(1)} collective-permute-done((f32[3,128,128]{2,1,0:T(8,128)}, f32[3,128,128]{2,1,0:T(8,128)S(1)}, u32[]{:S(2)}, u32[]{:S(2)}) %collective-permute-start.1) | collective-permute-done | bytes 196640 | tf_op jit(solution)/shard_map/ppermute | solution.py:359
  93.1 0.8 collective-permute-done.2
  93.8 2.2 collective-permute-done.3
  96.1 0.9 pad_maximum_fusion.1.rest_0_
  97.0 2.7 %collective-permute-start.8 = (f32[4,3,128,128]{3,2,1,0:T(8,128)}, f32[4,3,128,128]{3,2,1,0:T(8,128)}, u32[]{:S(2)}, u32[]{:S(2)}) collective-permute-start(f32[4,3,128,128]{3,2,1,0:T(8,128)} %pad_maximum_fusion.1.rest_0_), channel_id=1, source_target_pairs={{8,0},{16,8},{24,16},{28,24},{20,28},{12,20},{4,12},{0,4},{9,1},{1... | collective-permute-start | bytes 2359304 | tf_op jit(solution)/shard_map/ppermute | solution.py:369
  99.7 0.8 collective-permute-start.4
  100.5 0.7 dynamic_slice.27
  106.8 0.7 fusion.16
  121.6 2.4 collective-permute-start.9
  127.3 0.1 pad_add_fusion.4.columns
  127.4 0.1 pad_add_fusion.5.places
  127.4 0.1 pad_add_fusion.2.columns
  127.5 0.1 pad_add_fusion.3.places
  127.6 14.8 %collective-permute-done.9.rest_1_ = f32[4,3,128,128]{3,2,1,0:T(8,128)} collective-permute-done((f32[4,3,128,128]{3,2,1,0:T(8,128)}, f32[4,3,128,128]{3,2,1,0:T(8,128)}, u32[]{:S(2)}, u32[]{:S(2)}) %collective-permute-start.9) | collective-permute-done | bytes 786464 | tf_op jit(solution)/shard_map/ppermute | solution.py:369
  142.4 2.5 %collective-permute-start.10 = (f32[4,3,128,128]{3,2,1,0:T(8,128)}, f32[4,3,128,128]{3,2,1,0:T(8,128)}, u32[]{:S(2)}, u32[]{:S(2)}) collective-permute-start(f32[4,3,128,128]{3,2,1,0:T(8,128)} %collective-permute-done.9.rest_1_), channel_id=1, source_target_pairs={{8,0},{16,8},{24,16},{28,24},{20,28},{12,20},{4,12},{0,4},{9,1},{1... | collective-permute-start | bytes 2359304 | tf_op jit(solution)/shard_map/ppermute | solution.py:369
  145.5 0.1 collective-permute-start.6
  147.4 0.1 pad_add_fusion.6.columns
  147.5 0.1 pad_add_fusion.7.places
  147.6 16.0 %collective-permute-done.10.rest_1_ = f32[4,3,128,128]{3,2,1,0:T(8,128)} collective-permute-done((f32[4,3,128,128]{3,2,1,0:T(8,128)}, f32[4,3,128,128]{3,2,1,0:T(8,128)}, u32[]{:S(2)}, u32[]{:S(2)}) %collective-permute-start.10) | collective-permute-done | bytes 786464 | tf_op jit(solution)/shard_map/ppermute | solution.py:369
  163.7 1.8 slice.59
  165.5 1.6 collective-permute-start.11
  167.1 1.8 slice.58
  168.8 0.4 collective-permute-start.7
  169.3 0.2 convert_reduce_fusion.1
  169.5 0.1 select_reduce_fusion.1
  169.6 0.1 copy.23
  169.7 0.1 reshape.120.order
  169.8 0.2 convert_reduce_fusion.starts
  170.0 6.5 %collective-permute-done.11 = f32[2,3,128,128]{3,2,1,0:T(8,128)} collective-permute-done((f32[2,3,128,128]{3,2,1,0:T(8,128)}, f32[2,3,128,128]{3,2,1,0:T(8,128)}, u32[]{:S(2)}, u32[]{:S(2)}) %collective-permute-start.11) | collective-permute-done | bytes 393248 | tf_op jit(solution)/shard_map/ppermute | solution.py:372
  176.5 2.8 %collective-permute-done.7 = f32[2,3,128,128]{3,2,1,0:T(8,128)} collective-permute-done((f32[2,3,128,128]{3,2,1,0:T(8,128)}, f32[2,3,128,128]{3,2,1,0:T(8,128)}, u32[]{:S(2)}, u32[]{:S(2)}) %collective-permute-start.7) | collective-permute-done | bytes 393248 | tf_op jit(solution)/shard_map/ppermute | solution.py:372
  179.2 2.1 pad_maximum_fusion.2.rest_0_
  181.3 1.0 copy-done.4
  182.4 0.9 copy-done.5
  183.3 6.7 %row_panels.1 = (bf16[1536,1024]{1,0:T(8,128)(2,1)S(1)}, f32[12,1,24,1,128,128]{5,4,3,2,1,0:T(8,128)}, bf16[3,256,256]{2,1,0:T(8,128)(2,1)S(1)}, bf16[3,256,256]{2,1,0:T(8,128)(2,1)S(1)}) custom-call(s32[3]{0:T(128)S(1)} %pad_add_fusion.1.place, f32[4,12,128,128]{3,2,1,0:T(8,128)} %bitcast.45, f32[2,2,128,128]{3,2,1,0:T(8,128)S(1)} %copy-done.5, ...), custom_call_target="tpu_custom_call" | custom-call | tf_op jit(solution)/shard_map/row_panels/pallas_call | solution.py:135
  190.1 1.6 copy-done.1
  191.7 15.5 %trailing.4.rest_2_ = f32[12,1,24,1,128,128]{5,4,3,2,1,0:T(8,128)} custom-call(s32[9]{0:T(128)S(1)} %pad_add_fusion.6.columns, s32[12]{0:T(128)S(1)} %pad_add_fusion.7.places, s32[64]{0:T(128)S(1)} %reshape.120.order, s32[25]{0:T(128)S(1)} %convert_reduce_fusion.starts, f32[12,1,24,1,128,128]{5,4,3,2,1,0:T(8,128)} %front_two.7, ...), custom_call_target="tpu_custom_call", output_to_operand_aliasing={{}: (13, {})} | custom-call | flops 5435817984 | bytes 14155776 | tf_op jit(solution)/shard_map/trailing/pallas_call | solution.py:275
  207.2 11.6 %trailing.5.rest_2_ = f32[12,1,24,1,128,128]{5,4,3,2,1,0:T(8,128)} custom-call(s32[6]{0:T(128)S(1)} %pad_add_fusion.4.columns, s32[8]{0:T(128)S(1)} %pad_add_fusion.5.places, s32[64]{0:T(128)S(1)} %reshape.120.order, s32[25]{0:T(128)S(1)} %convert_reduce_fusion.starts, f32[12,1,24,1,128,128]{5,4,3,2,1,0:T(8,128)} %front_two.7, ...), custom_call_target="tpu_custom_call", output_to_operand_aliasing={{}: (12, {})} | custom-call | flops 3623878656 | bytes 9437184 | tf_op jit(solution)/shard_map/trailing/pallas_call | solution.py:275
  218.8 11.7 %trailing.6.rest_1_ = f32[12,1,24,1,128,128]{5,4,3,2,1,0:T(8,128)} custom-call(s32[6]{0:T(128)S(1)} %pad_add_fusion.2.columns, s32[8]{0:T(128)S(1)} %pad_add_fusion.3.places, s32[64]{0:T(128)S(1)} %reshape.120.order, s32[25]{0:T(128)S(1)} %convert_reduce_fusion.starts, f32[12,1,24,1,128,128]{5,4,3,2,1,0:T(8,128)} %front_two.7, ...), custom_call_target="tpu_custom_call", output_to_operand_aliasing={{}: (12, {})} | custom-call | flops 3623878656 | bytes 9437184 | tf_op jit(solution)/shard_map/trailing/pallas_call | solution.py:275
  230.6 8.7 %trailing.7 = f32[12,1,24,1,128,128]{5,4,3,2,1,0:T(8,128)} custom-call(s32[3]{0:T(128)S(1)} %multiply_add_fusion.7.columns, s32[4]{0:T(128)S(1)} %and_select_fusion.9.places, s32[64]{0:T(128)S(1)} %reshape.120.order, s32[25]{0:T(128)S(1)} %convert_reduce_fusion.starts, f32[12,1,24,1,128,128]{5,4,3,2,1,0:T(8,128)} %front_two.7, ...), custom_call_target="tpu_custom_call", output_to_operand_aliasing={{}: (11, {})} | custom-call | flops 1811939328 | bytes 4718592 | tf_op jit(solution)/shard_map/trailing/pallas_call | solution.py:275
  (44 shorter events, 0.2 us)
Async XLA Ops:
  7.4 2.2 copy-start
  13.4 2.1 copy-start.9
  15.5 60.3 %all-to-all-start = ((f32[32,136,128]{2,1,0:T(8,128)}), f32[32,136,128]{2,1,0:T(8,128)S(1)}, u32[]{:S(2)}, u32[]{:S(2)}) async-start(f32[32,136,128]{2,1,0:T(8,128)} %pad_maximum_fusion), calls=%async_computation | async-start | bytes 4456448 | tf_op jit(solution)/shard_map/all_to_all | solution.py:324
  22.8 158.6 %all-reduce.2.cloned.1.call-start = ((), (), s32[]{:S(2)}) async-start(), calls=%async_computation.1 | async-start | bytes 524288 | tf_op jit(solution)/shard_map/psum | solution.py:332
  27.7 153.6 %all-gather.3.cloned.1.call-start = ((), (), s32[]{:S(2)}) async-start(), calls=%async_computation.2 | async-start | bytes 3932160 | tf_op jit(solution)/shard_map/all_gather | solution.py:348
  79.0 0.9 copy-start.3
  79.9 0.7 copy-start.6
  80.5 0.7 copy-start.7
  81.2 0.7 copy-start.8
  81.9 18.6 %copy-start.11 = (s32[8]{0:T(128)S(1)}, s32[8]{0:T(128)}, u32[]{:S(2)}) copy-start(s32[8]{0:T(128)} %constant.283.clone) | copy-start | bytes 100
  81.9 24.9 %copy-start.10 = (s32[8]{0:T(128)S(1)}, s32[8]{0:T(128)}, u32[]{:S(2)}) copy-start(s32[8]{0:T(128)} %constant.284.clone) | copy-start | bytes 100
  81.9 6.1 %collective-permute-start = (f32[3,128,128]{2,1,0:T(8,128)}, f32[3,128,128]{2,1,0:T(8,128)S(1)}, u32[]{:S(2)}, u32[]{:S(2)}) collective-permute-start(f32[3,128,128]{2,1,0:T(8,128)} %copy-done.8), channel_id=1, source_target_pairs={{0,0},{1,4},{2,8},{3,12},{4,1},{5,5},{6,9},{7,13},{8,2},{9,6},{10,... | collective-permute-start | bytes 589832 | tf_op jit(solution)/shard_map/ppermute | solution.py:359
  83.5 9.6 %collective-permute-start.1 = (f32[3,128,128]{2,1,0:T(8,128)}, f32[3,128,128]{2,1,0:T(8,128)S(1)}, u32[]{:S(2)}, u32[]{:S(2)}) collective-permute-start(f32[3,128,128]{2,1,0:T(8,128)} %copy-done.7), channel_id=1, source_target_pairs={{0,4},{1,8},{2,12},{3,0},{4,5},{5,9},{6,13},{7,1},{8,6},{9,10},{10... | collective-permute-start | bytes 589832 | tf_op jit(solution)/shard_map/ppermute | solution.py:359
  85.3 8.6 %collective-permute-start.2 = (f32[3,128,128]{2,1,0:T(8,128)}, f32[3,128,128]{2,1,0:T(8,128)S(1)}, u32[]{:S(2)}, u32[]{:S(2)}) collective-permute-start(f32[3,128,128]{2,1,0:T(8,128)} %copy-done.6), channel_id=1, source_target_pairs={{0,8},{1,12},{2,0},{3,4},{4,9},{5,13},{6,1},{7,5},{8,10},{9,14},{1... | collective-permute-start | bytes 589832 | tf_op jit(solution)/shard_map/ppermute | solution.py:359
  88.0 8.1 %collective-permute-start.3 = (f32[3,128,128]{2,1,0:T(8,128)S(1)}, f32[3,128,128]{2,1,0:T(8,128)S(1)}, u32[]{:S(2)}, u32[]{:S(2)}) collective-permute-start(f32[3,128,128]{2,1,0:T(8,128)S(1)} %get-tuple-element.21), channel_id=1, source_target_pairs={{0,12},{1,0},{2,4},{3,8},{4,13},{5,1},{6,5},{7,9},{8,14},{9,2},{10... | collective-permute-start | bytes 589832 | tf_op jit(solution)/shard_map/ppermute | solution.py:359
  97.0 24.6 %collective-permute-start.8 = (f32[4,3,128,128]{3,2,1,0:T(8,128)}, f32[4,3,128,128]{3,2,1,0:T(8,128)}, u32[]{:S(2)}, u32[]{:S(2)}) collective-permute-start(f32[4,3,128,128]{3,2,1,0:T(8,128)} %pad_maximum_fusion.1.rest_0_), channel_id=1, source_target_pairs={{8,0},{16,8},{24,16},{28,24},{20,28},{12,20},{4,12},{0,4},{9,1},{1... | collective-permute-start | bytes 2359304 | tf_op jit(solution)/shard_map/ppermute | solution.py:369
  99.7 24.3 %collective-permute-start.4 = (f32[4,3,128,128]{3,2,1,0:T(8,128)}, f32[4,3,128,128]{3,2,1,0:T(8,128)}, u32[]{:S(2)}, u32[]{:S(2)}) collective-permute-start(f32[4,3,128,128]{3,2,1,0:T(8,128)} %pad_maximum_fusion.1.rest_0_), channel_id=1, source_target_pairs={{0,8},{8,16},{16,24},{24,28},{28,20},{20,12},{12,4},{4,0},{1,9},{9... | collective-permute-start | bytes 2359304 | tf_op jit(solution)/shard_map/ppermute | solution.py:368
  121.6 20.8 %collective-permute-start.9 = (f32[4,3,128,128]{3,2,1,0:T(8,128)}, f32[4,3,128,128]{3,2,1,0:T(8,128)}, u32[]{:S(2)}, u32[]{:S(2)}) collective-permute-start(f32[4,3,128,128]{3,2,1,0:T(8,128)} %collective-permute-done.8.rest_2_), channel_id=1, source_target_pairs={{8,0},{16,8},{24,16},{28,24},{20,28},{12,20},{4,12},{0,4},{9,1},{1... | collective-permute-start | bytes 2359304 | tf_op jit(solution)/shard_map/ppermute | solution.py:369
  124.0 21.5 %collective-permute-start.5 = (f32[4,3,128,128]{3,2,1,0:T(8,128)}, f32[4,3,128,128]{3,2,1,0:T(8,128)}, u32[]{:S(2)}, u32[]{:S(2)}) collective-permute-start(f32[4,3,128,128]{3,2,1,0:T(8,128)} %collective-permute-done.4.rest_1_), channel_id=1, source_target_pairs={{0,8},{8,16},{16,24},{24,28},{28,20},{20,12},{12,4},{4,0},{1,9},{9... | collective-permute-start | bytes 2359304 | tf_op jit(solution)/shard_map/ppermute | solution.py:368
  142.4 21.2 %collective-permute-start.10 = (f32[4,3,128,128]{3,2,1,0:T(8,128)}, f32[4,3,128,128]{3,2,1,0:T(8,128)}, u32[]{:S(2)}, u32[]{:S(2)}) collective-permute-start(f32[4,3,128,128]{3,2,1,0:T(8,128)} %collective-permute-done.9.rest_1_), channel_id=1, source_target_pairs={{8,0},{16,8},{24,16},{28,24},{20,28},{12,20},{4,12},{0,4},{9,1},{1... | collective-permute-start | bytes 2359304 | tf_op jit(solution)/shard_map/ppermute | solution.py:369
  145.5 21.6 %collective-permute-start.6 = (f32[4,3,128,128]{3,2,1,0:T(8,128)}, f32[4,3,128,128]{3,2,1,0:T(8,128)}, u32[]{:S(2)}, u32[]{:S(2)}) collective-permute-start(f32[4,3,128,128]{3,2,1,0:T(8,128)} %collective-permute-done.5.rest_0_), channel_id=1, source_target_pairs={{0,8},{8,16},{16,24},{24,28},{28,20},{20,12},{12,4},{4,0},{1,9},{9... | collective-permute-start | bytes 2359304 | tf_op jit(solution)/shard_map/ppermute | solution.py:368
  165.5 11.0 %collective-permute-start.11 = (f32[2,3,128,128]{3,2,1,0:T(8,128)}, f32[2,3,128,128]{3,2,1,0:T(8,128)}, u32[]{:S(2)}, u32[]{:S(2)}) collective-permute-start(f32[2,3,128,128]{3,2,1,0:T(8,128)} %slice.59), channel_id=1, source_target_pairs={{8,0},{16,8},{24,16},{28,24},{20,28},{12,20},{4,12},{0,4},{9,1},{1... | collective-permute-start | bytes 1179656 | tf_op jit(solution)/shard_map/ppermute | solution.py:372
  168.8 10.4 %collective-permute-start.7 = (f32[2,3,128,128]{3,2,1,0:T(8,128)}, f32[2,3,128,128]{3,2,1,0:T(8,128)}, u32[]{:S(2)}, u32[]{:S(2)}) collective-permute-start(f32[2,3,128,128]{3,2,1,0:T(8,128)} %slice.58), channel_id=1, source_target_pairs={{0,8},{8,16},{16,24},{24,28},{28,20},{20,12},{12,4},{4,0},{1,9},{9... | collective-permute-start | bytes 1179656 | tf_op jit(solution)/shard_map/ppermute | solution.py:372
  181.3 1.0 copy-start.4
  182.4 0.9 copy-start.5
  190.1 1.6 copy-start.1
  218.8 11.7 %copy-start.2 = (f32[4,3,128,128]{3,2,1,0:T(8,128)S(1)}, f32[4,3,128,128]{3,2,1,0:T(8,128)}, u32[]{:S(2)}) copy-start(f32[4,3,128,128]{3,2,1,0:T(8,128)} %pad_maximum_fusion.2.rest_0_) | copy-start | bytes 2359300
Sparse Core Ops, SparseCore 0:
  29.1 139.4 all-reduce.1
Sparse Core Ops, SparseCore 1:
  82.0 32.6 all-gather.2

commit v2 on v1

v2 whole, which is shorter than its diff:
```python
import functools

import jax
import jax.numpy as jnp
from jax import lax
from jax.experimental import pallas as pl
from jax.experimental.pallas import tpu as pltpu
from jax.sharding import PartitionSpec as P

TILE = 128
PANEL = 256
WIDTH = 2 * PANEL
NOTE = 8
VMEM = 30 * 1024 * 1024
BOTH = ("row", "col")


def halves(value):
    high = value.astype(jnp.bfloat16)
    low = (value - high.astype(jnp.float32)).astype(jnp.bfloat16)
    return high, low


def deep(value):
    high, low = halves(value)
    return jnp.concatenate([high, low, high], axis=1)


def stacked(value):
    high, low = halves(value)
    return jnp.concatenate([high, high, low], axis=0)


def dot(left, right):
    return jnp.dot(left, right, preferred_element_type=jnp.float32)


def two_panels(columns, small_ref, mask):
    one = mask(0, dot(deep(jnp.concatenate(columns[:2], axis=1)), small_ref[0]))
    field = jnp.concatenate(columns[2:], axis=1) - dot(deep(mask(1, one)), small_ref[1])
    return one, mask(1, dot(deep(field), small_ref[2]))


def whole_spec(array):
    rank = len(array.shape)
    return pl.BlockSpec(array.shape, lambda *_: (0,) * rank)


def columns_kernel(place, slot_in, front_ref, incoming_ref, out_ref, *rest):
    *parts, tile_ref, sem = rest
    cols = place[2]
    out_ref[...] = front_ref[:, 0, 0, 0]

    @pl.loop(0, incoming_ref.shape[0])
    def _(s):
        slot = slot_in[s]

        @pl.when(jnp.logical_and(slot >= 0, lax.rem(slot, cols) == 0))
        def _():
            copy = pltpu.make_async_copy(incoming_ref.at[s, pl.ds(0, TILE)], tile_ref, sem)
            copy.start()
            copy.wait()
            row = lax.div(slot, cols)
            out_ref[row] = out_ref[row] + tile_ref[...]

    count = len(parts)
    for j, part_ref in enumerate(parts):
        group = part_ref.shape[0]
        part_ref[...] = out_ref[pl.ds(lax.rem(place[1] + j, count) * group, group)]


def assemble_columns(front, incoming, place, slot_in, parts):
    rows = front.shape[0]
    shapes = [(rows, TILE, TILE)] + [(rows // parts, TILE, TILE)] * parts
    out_shape = [jax.ShapeDtypeStruct(shape, jnp.float32) for shape in shapes]
    return pl.pallas_call(
        columns_kernel,
        grid_spec=pltpu.PrefetchScalarGridSpec(
            num_scalar_prefetch=2,
            grid=(1,),
            in_specs=[
                pl.BlockSpec((rows, 1, 1, 1, TILE, TILE), lambda i, *_: (0, 0, 0, 0, 0, 0)),
                pl.BlockSpec(memory_space=pl.ANY),
            ],
            out_specs=[whole_spec(a) for a in out_shape],
            scratch_shapes=[pltpu.VMEM((TILE, TILE), jnp.float32), pltpu.SemaphoreType.DMA],
        ),
        out_shape=out_shape,
        compiler_params=pltpu.CompilerParams(vmem_limit_bytes=VMEM),
        name="panel_columns",
    )(place, slot_in, front, incoming)


def row_panels_kernel(
    place, t0, t1, t2, t3, lead_ref, diag_ref, pair_ref, out_ref, small_ref, tiles_ref
):
    step = pl.program_id(0)
    my_row, my_col = place[0], place[1]
    group = t0.shape[0]
    height = group * TILE

    @pl.when(step == 0)
    def _():
        small_ref[0] = stacked(diag_ref[0])
        lead = jnp.concatenate(
            [jnp.concatenate([lead_ref[i, 0], lead_ref[i, 1]], axis=1) for i in range(2)], axis=0
        )
        small_ref[1] = stacked(dot(deep(lead), small_ref[0]).T)
        small_ref[2] = stacked(diag_ref[1])

    for i, tile_ref in enumerate((t0, t1, t2, t3)):
        tiles_ref[jnp.bitwise_xor(my_col, i)] = tile_ref[...]
    columns = [tiles_ref[c].reshape(height, TILE) for c in range(4)]
    tile_row = lax.broadcasted_iota(jnp.int32, (height, PANEL), 0) // TILE
    first = jnp.logical_and(step == 0, tile_row == 0)

    def mask(panels_above, value):
        above = jnp.logical_and(first, my_row < 2 * panels_above)
        return jnp.where(above, 0.0, value) if panels_above else value

    one, two = two_panels(columns, small_ref, mask)
    pair_ref[:, :PANEL], pair_ref[:, WIDTH : WIDTH + PANEL] = halves(mask(1, one))
    pair_ref[:, PANEL:WIDTH], pair_ref[:, WIDTH + PANEL :] = halves(mask(2, two))
    pieces = (one[:, :TILE], one[:, TILE:], two[:, :TILE], two[:, TILE:])
    for c in range(4):

        @pl.when(my_col == c)
        def _():
            out_ref[:, 0, 0, 0] = pieces[c].reshape(group, TILE, TILE)


def row_panels(tiles, lead, diag, place, front):
    rows = front.shape[0]
    group = rows // 3
    height = group * TILE
    out_shape = [
        jax.ShapeDtypeStruct((rows * TILE, 2 * WIDTH), jnp.bfloat16),
        jax.ShapeDtypeStruct(front.shape, jnp.float32),
        jax.ShapeDtypeStruct((3, 3 * PANEL, PANEL), jnp.bfloat16),
    ]
    strip = pl.BlockSpec((group, TILE, TILE), lambda i, *_: (i, 0, 0))
    return pl.pallas_call(
        row_panels_kernel,
        grid_spec=pltpu.PrefetchScalarGridSpec(
            num_scalar_prefetch=1,
            grid=(3,),
            in_specs=[strip] * 4 + [whole_spec(lead), whole_spec(diag)],
            out_specs=[
                pl.BlockSpec((height, 2 * WIDTH), lambda i, *_: (i, 0)),
                pl.BlockSpec((group, 1, 1, 1, TILE, TILE), lambda i, *_: (i, 0, 0, 0, 0, 0)),
                whole_spec(out_shape[2]),
            ],
            scratch_shapes=[pltpu.VMEM((4, group, TILE, TILE), jnp.float32)],
        ),
        out_shape=out_shape,
        compiler_params=pltpu.CompilerParams(vmem_limit_bytes=VMEM),
        name="row_panels",
    )(place, *tiles, lead, diag)


def trailing_kernel(n_pieces, columns, places, order, starts, pair_ref, small_ref, *rest):
    piece_refs = rest[:n_pieces]
    front_ref, incoming_ref, _, out_ref, right_ref, taken, given, child_ref = rest[n_pieces:-3]
    take_sems, give_sems, child_sems = rest[-3:]
    group = piece_refs[0].shape[1]
    count = n_pieces * group
    steps = (count + 1) // 2
    rows = front_ref.shape[0]

    def columns_of(step):
        for j in range(2):
            index = jnp.minimum(2 * step, count - 2) + j
            wanted = columns[index] > 0
            if count % 2 and j == 0:
                wanted = jnp.logical_and(wanted, step < steps - 1)
            yield j, columns[index], wanted

    def each_take(step, act):
        slot = lax.rem(step, 2)
        for j, b, wanted in columns_of(step):

            @pl.when(wanted)
            def _():
                act(
                    pltpu.make_async_copy(
                        front_ref.at[:, 0, b, 0], taken.at[slot, j], take_sems.at[slot, j]
                    )
                )

    def each_give(step, act):
        slot = lax.rem(step, 2)
        for j, b, wanted in columns_of(step):

            @pl.when(wanted)
            def _():
                act(
                    pltpu.make_async_copy(
                        given.at[slot, j], out_ref.at[:, 0, b, 0], give_sems.at[slot, j]
                    )
                )

    def each_child(step, act):
        for j, b, wanted in columns_of(step):

            @pl.when(wanted)
            def _():
                @pl.loop(starts[b], starts[b + 1])
                def _(i):
                    s = order[2 * i]
                    copy = pltpu.make_async_copy(
                        incoming_ref.at[s, pl.ds(0, TILE)], child_ref.at[s], child_sems.at[s]
                    )
                    act(copy, j, s, order[2 * i + 1])

    for step in range(min(steps, 2)):
        each_take(step, lambda copy: copy.start())
    for step in range(steps):
        each_child(step, lambda copy, *_: copy.start())

    tile_columns = [
        jnp.concatenate(
            [
                piece[places[4 * p + c]].reshape(group * TILE, TILE)
                for p, piece in enumerate(piece_refs)
            ],
            axis=0,
        )
        for c in range(4)
    ]
    for i, panel in enumerate(two_panels(tile_columns, small_ref, lambda _, value: value)):
        high, low = halves(panel.T)
        for k, half in enumerate((high, high, low)):
            right_ref[k * WIDTH + i * PANEL : k * WIDTH + (i + 1) * PANEL] = half

    @pl.loop(0, steps)
    def _(step):
        slot = lax.rem(step, 2)
        each_take(step, lambda copy: copy.wait())

        @pl.when(step >= 2)
        def _():
            each_give(step - 2, lambda copy: copy.wait())

        start = jnp.minimum(2 * step, count - 2)
        lanes = pl.ds(pl.multiple_of(start * TILE, TILE), 2 * TILE)
        block = rows // 3
        for m in range(3):
            left = pair_ref[m * block * TILE : (m + 1) * block * TILE]
            update = dot(jnp.concatenate([left, left[:, :WIDTH]], axis=1), right_ref[:, lanes])
            span = slice(m * block, (m + 1) * block)
            for j in range(2):
                part = update[:, j * TILE : (j + 1) * TILE].reshape(block, TILE, TILE)
                given[slot, j, span] = taken[slot, j, span] - part

        def add(copy, j, s, a):
            copy.wait()
            given[slot, j, a] = given[slot, j, a] + child_ref[s]

        each_child(step, add)
        each_give(step, lambda copy: copy.start())

        @pl.when(step + 2 < steps)
        def _():
            each_take(step + 2, lambda copy: copy.start())

    for step in range(max(steps - 2, 0), steps):
        each_give(step, lambda copy: copy.wait())


def trailing(front, pieces, columns, places, panels, incoming, order, starts):
    rows = front.shape[0]
    pair, out, small = panels
    group = pieces[0].shape[1]
    count = len(pieces) * group
    scalars = [columns, places, order, starts]
    held = [pair, small, *pieces]
    distant = [front, incoming, out]
    spec = lambda space, n: [pl.BlockSpec(memory_space=space)] * n
    height = rows * TILE
    devices = incoming.shape[0]
    return pl.pallas_call(
        functools.partial(trailing_kernel, len(pieces)),
        in_specs=spec(pltpu.SMEM, 4) + spec(pltpu.VMEM, len(held)) + spec(pl.ANY, 3),
        out_specs=pl.BlockSpec(memory_space=pl.ANY),
        scratch_shapes=[
            pltpu.VMEM((3 * WIDTH, count * TILE), jnp.bfloat16),
            pltpu.VMEM((2, 2, rows, TILE, TILE), jnp.float32),
            pltpu.VMEM((2, 2, rows, TILE, TILE), jnp.float32),
            pltpu.VMEM((devices, TILE, TILE), jnp.float32),
            pltpu.SemaphoreType.DMA((2, 2)),
            pltpu.SemaphoreType.DMA((2, 2)),
            pltpu.SemaphoreType.DMA((devices,)),
        ],
        out_shape=jax.ShapeDtypeStruct(front.shape, jnp.float32),
        input_output_aliases={len(held) + 6: 0},
        compiler_params=pltpu.CompilerParams(vmem_limit_bytes=VMEM),
        cost_estimate=pl.CostEstimate(
            flops=count * 2 * height * TILE * WIDTH * 3,
            bytes_accessed=count * 2 * height * TILE * 4,
            transcendentals=0,
        ),
        name="trailing",
    )(*scalars, *held, *distant)


def body(front, child_tiles, tile_dest, tile_slot, tile_count, diag_inverses):
    n_row = lax.axis_size("row")
    n_col = lax.axis_size("col")
    my_row = lax.axis_index("row").astype(jnp.int32)
    my_col = lax.axis_index("col").astype(jnp.int32)
    rows_here, cols_here = (front.shape[0], front.shape[2])
    slots = child_tiles.shape[0]
    devices = n_row * n_col
    assert n_col == 4 and n_row % 4 == 0 and rows_here % 3 == 0
    place = jnp.stack([my_row, my_col, jnp.int32(cols_here)])

    numbers = jnp.arange(slots, dtype=jnp.int32)
    live = numbers < tile_count[0]
    dest = tile_dest[:, 0]
    hits = (dest[None, :] == jnp.arange(devices, dtype=jnp.int32)[:, None]) & live[None, :]
    picked = jnp.sum(jnp.where(hits, numbers[None, :], 0), axis=1)
    slot_out = jnp.sum(jnp.where(hits, tile_slot[None, :] + 1, 0), axis=1) - 1
    notes = jnp.broadcast_to(
        slot_out.astype(jnp.float32)[:, None, None], (devices, NOTE, TILE)
    )
    outgoing = jnp.concatenate([jnp.take(child_tiles, picked, axis=0), notes], axis=1)
    incoming = lax.all_to_all(outgoing, BOTH, split_axis=0, concat_axis=0, tiled=True)
    slot_in = lax.optimization_barrier(incoming[:, TILE, 0].astype(jnp.int32))

    row_of = jnp.where(slot_in >= 0, slot_in // cols_here, 0)
    col_of = jnp.where(slot_in >= 0, slot_in % cols_here, -1)
    sources = jnp.arange(devices, dtype=jnp.int32)
    key = jnp.where(slot_in >= 0, col_of, cols_here) * devices + sources
    rank = jnp.sum((key[None, :] < key[:, None]).astype(jnp.int32), axis=1)
    at = rank[None, :] == sources[:, None]
    order = jnp.stack(
        [jnp.sum(jnp.where(at, v[None, :], 0), axis=1) for v in (sources, row_of)], axis=1
    ).reshape(-1)
    edges = jnp.arange(cols_here + 1, dtype=jnp.int32) * devices
    starts = jnp.sum((key[None, :] < edges[:, None]).astype(jnp.int32), axis=1)

    ring = rows_here % n_col == 0
    mine, *parts = assemble_columns(front, incoming, place, slot_in, n_col if ring else 1)

    sets = n_row // n_col
    if ring:
        arrived = []
        for j, part in enumerate(parts):
            pairs = [
                (r * n_col + c, ((r // n_col) * n_col + (c + j) % n_col) * n_col + r % n_col)
                for r in range(n_row)
                for c in range(n_col)
            ]
            arrived.append(lax.ppermute(part, BOTH, pairs))
        piece = jnp.stack(arrived)
        circle = list(range(0, n_row, 2)) + list(range(n_row - 1, 0, -2))
        spot = jnp.asarray([circle.index(r) for r in range(n_row)], jnp.int32)[my_row]
        up = [(circle[i], circle[(i + 1) % n_row]) for i in range(n_row)]
        down = [(b, a) for a, b in up]
        rounds = [[(piece, 0)]]
        ahead = behind = piece
        for step in range(1, n_row // 2):
            ahead = lax.ppermute(ahead, "row", up)
            behind = lax.ppermute(behind, "row", down)
            rounds.append([(ahead, -step), (behind, step)])
        last = jnp.concatenate(
            [lax.ppermute(ahead[:2], "row", up), lax.ppermute(behind[2:], "row", down)]
        )
        rounds.append([(last, n_row // 2)])
        rounds = [rounds[0] + rounds[1]] + rounds[2:]

        def described(shift):
            origin = jnp.asarray(circle, jnp.int32)[(spot + shift + n_row) % n_row]
            part, group = origin % n_col, rows_here // n_col
            row = part * group + jnp.arange(group, dtype=jnp.int32)
            places = (part - jnp.arange(n_col, dtype=jnp.int32) + n_col) % n_col
            return row * sets + origin // n_col, places

    else:
        pairs = [
            (r * n_col + c, ((r // n_col) * n_col + c) * n_col + r % n_col)
            for r in range(n_row)
            for c in range(n_col)
        ]
        moved = lax.all_gather(lax.ppermute(mine, BOTH, pairs), "row", axis=0, tiled=False)
        rounds = [[(moved[h * n_col : (h + 1) * n_col], h)] for h in range(sets)]

        def described(h):
            row = jnp.arange(rows_here, dtype=jnp.int32)
            return row * sets + h, jnp.arange(n_col, dtype=jnp.int32)

    owners = [r * n_col + c for r in (2, 3) for c in (0, 1)]
    slices = lax.all_to_all(
        mine[0].reshape(devices, TILE // devices, TILE), BOTH, split_axis=0, concat_axis=0, tiled=True
    )
    own = jnp.stack([slices[owner] for owner in owners])
    own = jnp.broadcast_to(own[None], (devices,) + own.shape)
    lead = lax.all_to_all(own, BOTH, split_axis=0, concat_axis=0, tiled=True)
    lead = lead.transpose(1, 0, 2, 3).reshape(2, 2, TILE, TILE)

    near = lax.ppermute(mine, "col", [(c, c ^ 1) for c in range(n_col)])
    far = lax.ppermute(mine, "col", [(c, c ^ 2) for c in range(n_col)])
    other = lax.ppermute(far, "col", [(c, c ^ 1) for c in range(n_col)])
    panels = row_panels([mine, near, far, other], lead, diag_inverses, place, front)

    for entries in rounds:
        described_here = [described(shift) for _, shift in entries]
        columns = jnp.concatenate([d[0] for d in described_here])
        places = jnp.concatenate([d[1] for d in described_here])
        pieces = [p for p, _ in entries]
        out = trailing(front, pieces, columns, places, panels, incoming, order, starts)
        panels = [panels[0], out, panels[2]]
    return panels[1]


def solution(mesh):
    return jax.shard_map(
        body,
        mesh=mesh,
        in_specs=(
            P(None, "row", None, "col", None, None),
            P(BOTH, None, None),
            P(BOTH, None),
            P(BOTH),
            P(BOTH),
            P(),
        ),
        out_specs=P(None, "row", None, "col", None, None),
        check_vma=False,
    )
```

time: 248 us -> 196 us (0.79)
  waiting for transfers between devices: 96.2 us -> 62.7 us
  between operations: 43.8 us -> 27.4 us
  Pallas kernels: 56.8 us -> 48.8 us
  starting transfers between devices: 23.8 us -> 30.8 us
  other arithmetic: 11.5 us -> 7.55 us
  local copies, waits for them, and re-layouts: 14.5 us -> 18.3 us
    all_to_all x1, waiting for transfers between devices: 47.9 us -> 25.9 us  [body(): lax.all_to_all(outgoing, BOTH, split_axis=0, concat_axis=0, tiled=True)]
    ppermute x3, waiting for transfers between devices: 30.9 us -> 23.7 us  [body(): behind = lax.ppermute(behind, 'row', down)]
    pallas_call x4, Pallas kernels: 47.5 us -> 40.8 us  [trailing(): pl.pallas_call(functools.partial(trailing_kernel, len(pieces)), in_specs=...]
    all_to_all x0 -> x2, starting transfers between devices: none -> 6.5 us  [the longest x1 3.7 us: body(): lead = lax.all_to_all(own, BOTH, split_axis=0, concat_axis=0, tiled=True)]
    ppermute x1, waiting for transfers between devices: 6.5 us -> 0.01 us  [body(): lax.ppermute(behind[2:], 'row', down)]
    all_to_all x0 -> x2, waiting for transfers between devices: none -> 5.19 us  [the longest x1 3.93 us: body(): lead = lax.all_to_all(own, BOTH, split_axis=0, concat_axis=0, tiled=True)]
    ppermute x3, starting transfers between devices: 7.55 us -> 3.75 us  [body(): behind = lax.ppermute(behind, 'row', down)]
    ppermute x1, waiting for transfers between devices: 2.77 us -> 0.01 us  [body(): lax.ppermute(ahead[:2], 'row', up)]
  transfers between devices with their start and end apart: 15 -> 18, of which waited for: 8 -> 9; matrix products, arithmetic and copies ran while one was open for 5% -> 4% of each run, Pallas kernels for 1% -> 21%
where the time goes in v2:
time: 196 us
  waiting for transfers between devices  62.7 us (32%)
  Pallas kernels  48.8 us (25%)
  starting transfers between devices  30.8 us (16%)
  between operations  27.4 us (14%)
  local copies, waits for them, and re-layouts  18.3 us (9%)
  other arithmetic  7.55 us (4%)
    pallas_call x4, Pallas kernels, trailing(): pl.pallas_call(functools.partial(trailing_kernel, len(pieces)), in_specs=...  40.8 us
    all_to_all x1, waiting for transfers between devices, body(): lax.all_to_all(outgoing, BOTH, split_axis=0, concat_axis=0, tiled=True)  25.9 us
    ppermute x3, waiting for transfers between devices, body(): behind = lax.ppermute(behind, 'row', down)  23.7 us
    unnamed x14, local copies, waits for them, and re-layouts  9.42 us
    ppermute x4, waiting for transfers between devices, body(): arrived.append(lax.ppermute(part, BOTH, pairs))  7.66 us
    all_to_all x1, starting transfers between devices, body(): lax.all_to_all(outgoing, BOTH, split_axis=0, concat_axis=0, tiled=True)  7.3 us
    pallas_call x1, Pallas kernels, row_panels(): pl.pallas_call(row_panels_kernel, grid_spec=pltpu.PrefetchScalarGridSpec(...  6.6 us
    ppermute x4, starting transfers between devices, body(): arrived.append(lax.ppermute(part, BOTH, pairs))  6.23 us
  transfers between devices with their start and end apart: 18, of which 9 were waited for; matrix products, arithmetic and copies ran while one was open for 4% of the time, Pallas kernels for 21%

profile of v2, /device:TPU:0, one launch (start us, length us, event | category | flops | bytes accessed | tf_op | source)
XLA Modules:
  0.0 195.6 jit_solution(9859729480799174085)
XLA Ops:
  0.8 0.7 broadcast_add_fusion
  1.4 0.7 select_reduce_fusion.3
  2.2 2.0 %gather_fusion = f32[32,128,128]{2,1,0:T(8,128)} fusion(f32[16,128,128]{2,1,0:T(8,128)S(1)} %copy-done, s32[1024]{0:T(1024)S(1)} %pad_clamp_fusion), kind=kCustom, calls=%fused_computation | custom fusion | bytes 4194432 | tf_op jit(solution)/shard_map/jit(_take)/gather | solution.py:326
  4.2 1.8 broadcast_select_fusion
  6.0 0.1 broadcast_in_dim.79
  6.1 1.5 pad_maximum_fusion
  7.7 7.3 %all-to-all-start = ((f32[32,136,128]{2,1,0:T(8,128)}), f32[32,136,128]{2,1,0:T(8,128)S(1)}, u32[]{:S(2)}, u32[]{:S(2)}) async-start(f32[32,136,128]{2,1,0:T(8,128)} %pad_maximum_fusion), calls=%async_computation | async-start | bytes 4456448 | tf_op jit(solution)/shard_map/all_to_all | solution.py:327
  15.0 0.6 dynamic_slice.27
  20.7 0.7 fusion.12
  40.5 0.1 pad_add_fusion.4.columns
  40.6 0.1 pad_add_fusion.1.place
  40.6 25.9 %all-to-all-done.incoming_ref.rest_4_.rest_3_.rest_2_ = f32[32,136,128]{2,1,0:T(8,128)S(1)} async-done(((f32[32,136,128]{2,1,0:T(8,128)}), f32[32,136,128]{2,1,0:T(8,128)S(1)}, u32[]{:S(2)}, u32[]{:S(2)}) %all-to-all-start) | async-done | bytes 2228256 | tf_op jit(solution)/shard_map/all_to_all | solution.py:327
  66.6 0.7 fusion.slot_in
  67.2 6.4 %copy-done.1 = f32[12,1,24,1,128,128]{5,4,3,2,1,0:T(8,128)S(1)} copy-done((f32[12,1,24,1,128,128]{5,4,3,2,1,0:T(8,128)S(1)}, f32[12,1,24,1,128,128]{5,4,3,2,1,0:T(8,128)}, u32[]{:S(2)}) %copy-start.1) | copy-done | bytes 18874392
  73.6 1.5 panel_columns.1
  75.1 0.0 copy-start.2
  75.1 0.9 copy-done.2
  76.0 0.7 collective-permute-start.3
  76.6 2.6 %collective-permute-start.4 = (f32[3,128,128]{2,1,0:T(8,128)S(1)}, f32[3,128,128]{2,1,0:T(8,128)S(1)}, u32[]{:S(2)}, u32[]{:S(2)}) collective-permute-start(f32[3,128,128]{2,1,0:T(8,128)S(1)} %get-tuple-element.17), channel_id=1, source_target_pairs={{0,4},{1,8},{2,12},{3,0},{4,5},{5,9},{6,13},{7,1},{8,6},{9,10},{10... | collective-permute-start | bytes 589832 | tf_op jit(solution)/shard_map/ppermute | solution.py:354
  79.2 2.5 %collective-permute-start.5 = (f32[3,128,128]{2,1,0:T(8,128)S(1)}, f32[3,128,128]{2,1,0:T(8,128)S(1)}, u32[]{:S(2)}, u32[]{:S(2)}) collective-permute-start(f32[3,128,128]{2,1,0:T(8,128)S(1)} %get-tuple-element.18), channel_id=1, source_target_pairs={{0,8},{1,12},{2,0},{3,4},{4,9},{5,13},{6,1},{7,5},{8,10},{9,14},{1... | collective-permute-start | bytes 589832 | tf_op jit(solution)/shard_map/ppermute | solution.py:354
  81.7 0.5 collective-permute-start.6
  82.2 0.1 pad_add_fusion.5.places
  82.3 3.9 %collective-permute-done.4 = f32[3,128,128]{2,1,0:T(8,128)S(1)} collective-permute-done((f32[3,128,128]{2,1,0:T(8,128)S(1)}, f32[3,128,128]{2,1,0:T(8,128)S(1)}, u32[]{:S(2)}, u32[]{:S(2)}) %collective-permute-start.4) | collective-permute-done | bytes 196640 | tf_op jit(solution)/shard_map/ppermute | solution.py:354
  86.2 0.8 collective-permute-done.5
  87.0 2.9 %collective-permute-done.6 = f32[3,128,128]{2,1,0:T(8,128)S(1)} collective-permute-done((f32[3,128,128]{2,1,0:T(8,128)S(1)}, f32[3,128,128]{2,1,0:T(8,128)S(1)}, u32[]{:S(2)}, u32[]{:S(2)}) %collective-permute-start.6) | collective-permute-done | bytes 196640 | tf_op jit(solution)/shard_map/ppermute | solution.py:354
  89.9 0.9 pad_maximum_fusion.1.rest_0_
  90.9 2.6 %collective-permute-start.11 = (f32[4,3,128,128]{3,2,1,0:T(8,128)}, f32[4,3,128,128]{3,2,1,0:T(8,128)}, u32[]{:S(2)}, u32[]{:S(2)}) collective-permute-start(f32[4,3,128,128]{3,2,1,0:T(8,128)} %pad_maximum_fusion.1.rest_0_), channel_id=1, source_target_pairs={{8,0},{16,8},{24,16},{28,24},{20,28},{12,20},{4,12},{0,4},{9,1},{1... | collective-permute-start | bytes 2359304 | tf_op jit(solution)/shard_map/ppermute | solution.py:364
  94.8 0.1 pad_add_fusion.2.columns
  94.9 0.1 pad_add_fusion.3.places
  95.0 1.8 collective-permute-start.1
  97.6 1.5 slice.23
  99.1 2.8 %all-to-all-start.1 = ((f32[32,4,128]{2,1,0:T(4,128)}), f32[32,4,128]{2,1,0:T(4,128)S(1)}, u32[]{:S(2)}, u32[]{:S(2)}) async-start(f32[32,4,128]{2,1,0:T(4,128)} %bitcast.10), calls=%async_computation.1 | async-start | bytes 131072 | tf_op jit(solution)/shard_map/all_to_all | solution.py:393
  101.9 0.1 pad_add_fusion.6.columns
  102.0 9.8 %collective-permute-done.11.rest_2_ = f32[4,3,128,128]{3,2,1,0:T(8,128)} collective-permute-done((f32[4,3,128,128]{3,2,1,0:T(8,128)}, f32[4,3,128,128]{3,2,1,0:T(8,128)}, u32[]{:S(2)}, u32[]{:S(2)}) %collective-permute-start.11) | collective-permute-done | bytes 786464 | tf_op jit(solution)/shard_map/ppermute | solution.py:364
  111.8 1.1 collective-permute-start.12
  112.9 0.1 collective-permute-done.7.rest_1_
  113.0 1.0 collective-permute-start.8
  114.0 0.1 pad_add_fusion.7.places
  114.1 0.0 collective-permute-start
  114.1 1.3 all-to-all-done.1
  115.3 0.1 collective-permute-start.2
  115.5 0.8 broadcast_in_dim.83
  116.2 3.7 %all-to-all-start.2 = ((f32[32,4,4,128]{3,2,1,0:T(4,128)}), f32[32,4,4,128]{3,2,1,0:T(4,128)}, u32[]{:S(2)}, u32[]{:S(2)}) async-start(f32[32,4,4,128]{3,2,1,0:T(4,128)} %broadcast_in_dim.83), calls=%async_computation.2 | async-start | bytes 524288 | tf_op jit(solution)/shard_map/all_to_all | solution.py:398
  120.0 0.2 convert_reduce_fusion.1
  120.1 13.9 %collective-permute-done.12.rest_1_ = f32[4,3,128,128]{3,2,1,0:T(8,128)} collective-permute-done((f32[4,3,128,128]{3,2,1,0:T(8,128)}, f32[4,3,128,128]{3,2,1,0:T(8,128)}, u32[]{:S(2)}, u32[]{:S(2)}) %collective-permute-start.12) | collective-permute-done | bytes 786464 | tf_op jit(solution)/shard_map/ppermute | solution.py:364
  134.1 2.0 %collective-permute-start.9 = (f32[4,3,128,128]{3,2,1,0:T(8,128)}, f32[4,3,128,128]{3,2,1,0:T(8,128)}, u32[]{:S(2)}, u32[]{:S(2)}) collective-permute-start(f32[4,3,128,128]{3,2,1,0:T(8,128)} %collective-permute-done.8.rest_0_), channel_id=1, source_target_pairs={{0,8},{8,16},{16,24},{24,28},{28,20},{20,12},{12,4},{4,0},{1,9},{9... | collective-permute-start | bytes 2359304 | tf_op jit(solution)/shard_map/ppermute | solution.py:363
  136.1 0.1 select_reduce_fusion.1
  136.2 0.1 copy.24
  136.3 0.1 reshape.61.order
  136.4 0.2 convert_reduce_fusion.starts
  136.6 3.9 %all-to-all-done.2 = f32[32,4,4,128]{3,2,1,0:T(4,128)} async-done(((f32[32,4,4,128]{3,2,1,0:T(4,128)}), f32[32,4,4,128]{3,2,1,0:T(4,128)}, u32[]{:S(2)}, u32[]{:S(2)}) %all-to-all-start.2) | async-done | bytes 262176 | tf_op jit(solution)/shard_map/all_to_all | solution.py:398
  140.5 1.0 copy.25
  141.6 1.1 copy-done.3
  142.7 1.0 copy-done.4
  143.7 6.6 %row_panels.1 = (bf16[1536,1024]{1,0:T(8,128)(2,1)S(1)}, f32[12,1,24,1,128,128]{5,4,3,2,1,0:T(8,128)}, bf16[3,768,256]{2,1,0:T(8,128)(2,1)S(1)}) custom-call(s32[3]{0:T(128)S(1)} %pad_add_fusion.1.place, f32[12,128,128]{2,1,0:T(8,128)S(1)} %copy-done.3, f32[12,128,128]{2,1,0:T(8,128)} %collective-permute-done.t1, f32[12,128,128]{2,1,0:T(8,128)} %collective-permute-done.1.t2, ...), custom_call_target="tpu_custom_call" | custom-call | tf_op jit(solution)/shard_map/row_panels/pallas_call | solution.py:142
  150.3 13.5 %trailing.4.rest_4_ = f32[12,1,24,1,128,128]{5,4,3,2,1,0:T(8,128)} custom-call(s32[9]{0:T(128)S(1)} %pad_add_fusion.6.columns, s32[12]{0:T(128)S(1)} %pad_add_fusion.7.places, s32[64]{0:T(128)S(1)} %reshape.61.order, s32[25]{0:T(128)S(1)} %convert_reduce_fusion.starts, ...), custom_call_target="tpu_custom_call", output_to_operand_aliasing={{}: (11, {})} | custom-call | flops 5435817984 | bytes 14155776 | tf_op jit(solution)/shard_map/trailing/pallas_call | solution.py:281
  163.9 1.0 slice.33
  164.9 1.2 collective-permute-start.10
  166.2 1.0 slice.34
  167.2 0.9 collective-permute-start.14
  168.1 10.2 %trailing.5.rest_4_ = f32[12,1,24,1,128,128]{5,4,3,2,1,0:T(8,128)} custom-call(s32[6]{0:T(128)S(1)} %pad_add_fusion.4.columns, s32[8]{0:T(128)S(1)} %pad_add_fusion.5.places, s32[64]{0:T(128)S(1)} %reshape.61.order, s32[25]{0:T(128)S(1)} %convert_reduce_fusion.starts, ...), custom_call_target="tpu_custom_call", output_to_operand_aliasing={{}: (10, {})} | custom-call | flops 3623878656 | bytes 9437184 | tf_op jit(solution)/shard_map/trailing/pallas_call | solution.py:281
  178.2 10.5 %trailing.6.rest_3_ = f32[12,1,24,1,128,128]{5,4,3,2,1,0:T(8,128)} custom-call(s32[6]{0:T(128)S(1)} %pad_add_fusion.2.columns, s32[8]{0:T(128)S(1)} %pad_add_fusion.3.places, s32[64]{0:T(128)S(1)} %reshape.61.order, s32[25]{0:T(128)S(1)} %convert_reduce_fusion.starts, ...), custom_call_target="tpu_custom_call", output_to_operand_aliasing={{}: (10, {})} | custom-call | flops 3623878656 | bytes 9437184 | tf_op jit(solution)/shard_map/trailing/pallas_call | solution.py:281
  188.8 0.1 pad_maximum_fusion.2.rest_0_
  188.9 6.5 %trailing.7 = f32[12,1,24,1,128,128]{5,4,3,2,1,0:T(8,128)} custom-call(s32[3]{0:T(128)S(1)} %multiply_add_fusion.7.columns, s32[4]{0:T(128)S(1)} %and_select_fusion.9.places, s32[64]{0:T(128)S(1)} %reshape.61.order, s32[25]{0:T(128)S(1)} %convert_reduce_fusion.starts, ...), custom_call_target="tpu_custom_call", output_to_operand_aliasing={{}: (9, {})} | custom-call | flops 1811939328 | bytes 4718592 | tf_op jit(solution)/shard_map/trailing/pallas_call | solution.py:281
  (40 shorter events, 0.2 us)
Async XLA Ops:
  0.0 2.2 %copy-start = (f32[16,128,128]{2,1,0:T(8,128)S(1)}, f32[16,128,128]{2,1,0:T(8,128)}, u32[]{:S(2)}) copy-start(f32[16,128,128]{2,1,0:T(8,128)} %param.16) | copy-start | bytes 3145732
  7.7 7.3 %copy-start.6 = (s32[8]{0:T(128)S(1)}, s32[8]{0:T(128)}, u32[]{:S(2)}) copy-start(s32[8]{0:T(128)} %constant.270.clone) | copy-start | bytes 100
  7.7 13.1 %copy-start.5 = (s32[8]{0:T(128)S(1)}, s32[8]{0:T(128)}, u32[]{:S(2)}) copy-start(s32[8]{0:T(128)} %constant.271.clone) | copy-start | bytes 100
  7.7 58.9 %all-to-all-start = ((f32[32,136,128]{2,1,0:T(8,128)}), f32[32,136,128]{2,1,0:T(8,128)S(1)}, u32[]{:S(2)}, u32[]{:S(2)}) async-start(f32[32,136,128]{2,1,0:T(8,128)} %pad_maximum_fusion), calls=%async_computation | async-start | bytes 4456448 | tf_op jit(solution)/shard_map/all_to_all | solution.py:327
  67.2 6.4 %copy-start.1 = (f32[12,1,24,1,128,128]{5,4,3,2,1,0:T(8,128)S(1)}, f32[12,1,24,1,128,128]{5,4,3,2,1,0:T(8,128)}, u32[]{:S(2)}) copy-start(f32[12,1,24,1,128,128]{5,4,3,2,1,0:T(8,128)} %rest_1_.1) | copy-start | bytes 56623108
  75.1 0.9 copy-start.2
  76.0 6.3 %collective-permute-start.3 = (f32[3,128,128]{2,1,0:T(8,128)S(1)}, f32[3,128,128]{2,1,0:T(8,128)S(1)}, u32[]{:S(2)}, u32[]{:S(2)}) collective-permute-start(f32[3,128,128]{2,1,0:T(8,128)S(1)} %get-tuple-element.16), channel_id=1, source_target_pairs={{0,0},{1,4},{2,8},{3,12},{4,1},{5,5},{6,9},{7,13},{8,2},{9,6},{10,... | collective-permute-start | bytes 589832 | tf_op jit(solution)/shard_map/ppermute | solution.py:354
  76.6 9.6 %collective-permute-start.4 = (f32[3,128,128]{2,1,0:T(8,128)S(1)}, f32[3,128,128]{2,1,0:T(8,128)S(1)}, u32[]{:S(2)}, u32[]{:S(2)}) collective-permute-start(f32[3,128,128]{2,1,0:T(8,128)S(1)} %get-tuple-element.17), channel_id=1, source_target_pairs={{0,4},{1,8},{2,12},{3,0},{4,5},{5,9},{6,13},{7,1},{8,6},{9,10},{10... | collective-permute-start | bytes 589832 | tf_op jit(solution)/shard_map/ppermute | solution.py:354
  79.2 7.8 %collective-permute-start.5 = (f32[3,128,128]{2,1,0:T(8,128)S(1)}, f32[3,128,128]{2,1,0:T(8,128)S(1)}, u32[]{:S(2)}, u32[]{:S(2)}) collective-permute-start(f32[3,128,128]{2,1,0:T(8,128)S(1)} %get-tuple-element.18), channel_id=1, source_target_pairs={{0,8},{1,12},{2,0},{3,4},{4,9},{5,13},{6,1},{7,5},{8,10},{9,14},{1... | collective-permute-start | bytes 589832 | tf_op jit(solution)/shard_map/ppermute | solution.py:354
  81.7 8.2 %collective-permute-start.6 = (f32[3,128,128]{2,1,0:T(8,128)S(1)}, f32[3,128,128]{2,1,0:T(8,128)S(1)}, u32[]{:S(2)}, u32[]{:S(2)}) collective-permute-start(f32[3,128,128]{2,1,0:T(8,128)S(1)} %get-tuple-element.19), channel_id=1, source_target_pairs={{0,12},{1,0},{2,4},{3,8},{4,13},{5,1},{6,5},{7,9},{8,14},{9,2},{10... | collective-permute-start | bytes 589832 | tf_op jit(solution)/shard_map/ppermute | solution.py:354
  90.9 20.9 %collective-permute-start.11 = (f32[4,3,128,128]{3,2,1,0:T(8,128)}, f32[4,3,128,128]{3,2,1,0:T(8,128)}, u32[]{:S(2)}, u32[]{:S(2)}) collective-permute-start(f32[4,3,128,128]{3,2,1,0:T(8,128)} %pad_maximum_fusion.1.rest_0_), channel_id=1, source_target_pairs={{8,0},{16,8},{24,16},{28,24},{20,28},{12,20},{4,12},{0,4},{9,1},{1... | collective-permute-start | bytes 2359304 | tf_op jit(solution)/shard_map/ppermute | solution.py:364
  93.5 19.6 %collective-permute-start.7 = (f32[4,3,128,128]{3,2,1,0:T(8,128)}, f32[4,3,128,128]{3,2,1,0:T(8,128)}, u32[]{:S(2)}, u32[]{:S(2)}) collective-permute-start(f32[4,3,128,128]{3,2,1,0:T(8,128)} %pad_maximum_fusion.1.rest_0_), channel_id=1, source_target_pairs={{0,8},{8,16},{16,24},{24,28},{28,20},{20,12},{12,4},{4,0},{1,9},{9... | collective-permute-start | bytes 2359304 | tf_op jit(solution)/shard_map/ppermute | solution.py:363
  95.0 20.4 %collective-permute-start.1 = (f32[12,128,128]{2,1,0:T(8,128)}, f32[12,128,128]{2,1,0:T(8,128)}, u32[]{:S(2)}, u32[]{:S(2)}) collective-permute-start(f32[12,128,128]{2,1,0:T(8,128)} %copy-done.2), channel_id=1, source_target_pairs={{0,2},{1,3},{2,0},{3,1},{4,6},{5,7},{6,4},{7,5},{8,10},{9,11},{10,... | collective-permute-start | bytes 2359304 | tf_op jit(solution)/shard_map/ppermute | solution.py:402
  99.1 16.2 %all-to-all-start.1 = ((f32[32,4,128]{2,1,0:T(4,128)}), f32[32,4,128]{2,1,0:T(4,128)S(1)}, u32[]{:S(2)}, u32[]{:S(2)}) async-start(f32[32,4,128]{2,1,0:T(4,128)} %bitcast.10), calls=%async_computation.1 | async-start | bytes 131072 | tf_op jit(solution)/shard_map/all_to_all | solution.py:393
  111.8 22.3 %collective-permute-start.12 = (f32[4,3,128,128]{3,2,1,0:T(8,128)}, f32[4,3,128,128]{3,2,1,0:T(8,128)}, u32[]{:S(2)}, u32[]{:S(2)}) collective-permute-start(f32[4,3,128,128]{3,2,1,0:T(8,128)} %collective-permute-done.11.rest_2_), channel_id=1, source_target_pairs={{8,0},{16,8},{24,16},{28,24},{20,28},{12,20},{4,12},{0,4},{9,1},{1... | collective-permute-start | bytes 2359304 | tf_op jit(solution)/shard_map/ppermute | solution.py:364
  113.0 21.0 %collective-permute-start.8 = (f32[4,3,128,128]{3,2,1,0:T(8,128)}, f32[4,3,128,128]{3,2,1,0:T(8,128)}, u32[]{:S(2)}, u32[]{:S(2)}) collective-permute-start(f32[4,3,128,128]{3,2,1,0:T(8,128)} %collective-permute-done.7.rest_1_), channel_id=1, source_target_pairs={{0,8},{8,16},{16,24},{24,28},{28,20},{20,12},{12,4},{4,0},{1,9},{9... | collective-permute-start | bytes 2359304 | tf_op jit(solution)/shard_map/ppermute | solution.py:363
  114.1 27.5 %collective-permute-start = (f32[12,128,128]{2,1,0:T(8,128)}, f32[12,128,128]{2,1,0:T(8,128)}, u32[]{:S(2)}, u32[]{:S(2)}) collective-permute-start(f32[12,128,128]{2,1,0:T(8,128)} %copy-done.2), channel_id=1, source_target_pairs={{0,1},{1,0},{2,3},{3,2},{4,5},{5,4},{6,7},{7,6},{8,9},{9,8},{10,11... | collective-permute-start | bytes 2359304 | tf_op jit(solution)/shard_map/ppermute | solution.py:401
  115.3 26.2 %collective-permute-start.2 = (f32[12,128,128]{2,1,0:T(8,128)}, f32[12,128,128]{2,1,0:T(8,128)}, u32[]{:S(2)}, u32[]{:S(2)}) collective-permute-start(f32[12,128,128]{2,1,0:T(8,128)} %collective-permute-done.1.t2), channel_id=1, source_target_pairs={{0,1},{1,0},{2,3},{3,2},{4,5},{5,4},{6,7},{7,6},{8,9},{9,8},{10,11... | collective-permute-start | bytes 2359304 | tf_op jit(solution)/shard_map/ppermute | solution.py:403
  116.2 24.3 %all-to-all-start.2 = ((f32[32,4,4,128]{3,2,1,0:T(4,128)}), f32[32,4,4,128]{3,2,1,0:T(4,128)}, u32[]{:S(2)}, u32[]{:S(2)}) async-start(f32[32,4,4,128]{3,2,1,0:T(4,128)} %broadcast_in_dim.83), calls=%async_computation.2 | async-start | bytes 524288 | tf_op jit(solution)/shard_map/all_to_all | solution.py:398
  134.1 32.1 %collective-permute-start.13 = (f32[4,3,128,128]{3,2,1,0:T(8,128)}, f32[4,3,128,128]{3,2,1,0:T(8,128)}, u32[]{:S(2)}, u32[]{:S(2)}) collective-permute-start(f32[4,3,128,128]{3,2,1,0:T(8,128)} %collective-permute-done.12.rest_1_), channel_id=1, source_target_pairs={{8,0},{16,8},{24,16},{28,24},{20,28},{12,20},{4,12},{0,4},{9,1},{1... | collective-permute-start | bytes 2359304 | tf_op jit(solution)/shard_map/ppermute | solution.py:364
  134.1 29.8 %collective-permute-start.9 = (f32[4,3,128,128]{3,2,1,0:T(8,128)}, f32[4,3,128,128]{3,2,1,0:T(8,128)}, u32[]{:S(2)}, u32[]{:S(2)}) collective-permute-start(f32[4,3,128,128]{3,2,1,0:T(8,128)} %collective-permute-done.8.rest_0_), channel_id=1, source_target_pairs={{0,8},{8,16},{16,24},{24,28},{28,20},{20,12},{12,4},{4,0},{1,9},{9... | collective-permute-start | bytes 2359304 | tf_op jit(solution)/shard_map/ppermute | solution.py:363
  141.6 1.1 copy-start.3
  142.7 1.0 copy-start.4
  164.9 23.9 %collective-permute-start.10 = (f32[2,3,128,128]{3,2,1,0:T(8,128)S(1)}, f32[2,3,128,128]{3,2,1,0:T(8,128)S(1)}, u32[]{:S(2)}, u32[]{:S(2)}) collective-permute-start(f32[2,3,128,128]{3,2,1,0:T(8,128)S(1)} %slice.33), channel_id=1, source_target_pairs={{0,8},{8,16},{16,24},{24,28},{28,20},{20,12},{12,4},{4,0},{1,9},{9... | collective-permute-start | bytes 1179656 | tf_op jit(solution)/shard_map/ppermute | solution.py:367
  167.2 21.6 %collective-permute-start.14 = (f32[2,3,128,128]{3,2,1,0:T(8,128)S(1)}, f32[2,3,128,128]{3,2,1,0:T(8,128)S(1)}, u32[]{:S(2)}, u32[]{:S(2)}) collective-permute-start(f32[2,3,128,128]{3,2,1,0:T(8,128)S(1)} %slice.34), channel_id=1, source_target_pairs={{8,0},{16,8},{24,16},{28,24},{20,28},{12,20},{4,12},{0,4},{9,1},{1... | collective-permute-start | bytes 1179656 | tf_op jit(solution)/shard_map/ppermute | solution.py:367

commit v3 on v2

--- a/solution.py
+++ b/solution.py
@@ -44,6 +44,48 @@
 def whole_spec(array):
     rank = len(array.shape)
     return pl.BlockSpec(array.shape, lambda *_: (0,) * rank)
+
+
+def pack_kernel(dest, slot, count, child_ref, out_ref, notes_ref, sems, notes_sem):
+    slots = child_ref.shape[0]
+
+    def copy(k):
+        return pltpu.make_async_copy(
+            child_ref.at[k], out_ref.at[dest[k], pl.ds(0, TILE)], sems.at[k]
+        )
+
+    notes_ref[...] = jnp.full_like(notes_ref, -1.0)
+    live = jnp.minimum(count[0], slots)
+
+    @pl.loop(0, live)
+    def _(k):
+        copy(k).start()
+        notes_ref[dest[k]] = jnp.full(notes_ref.shape[1:], slot[k].astype(jnp.float32))
+
+    notes = pltpu.make_async_copy(notes_ref, out_ref.at[:, pl.ds(TILE, NOTE)], notes_sem)
+    notes.start()
+    notes.wait()
+
+    @pl.loop(0, live)
+    def _(k):
+        copy(k).wait()
+
+
+def pack(child_tiles, dest, slot, count, devices):
+    slots = child_tiles.shape[0]
+    hbm = pl.BlockSpec(memory_space=pltpu.HBM)
+    return pl.pallas_call(
+        pack_kernel,
+        in_specs=[pl.BlockSpec(memory_space=pltpu.SMEM)] * 3 + [hbm],
+        out_specs=hbm,
+        scratch_shapes=[
+            pltpu.VMEM((devices, NOTE, TILE), jnp.float32),
+            pltpu.SemaphoreType.DMA((slots,)),
+            pltpu.SemaphoreType.DMA,
+        ],
+        out_shape=jax.ShapeDtypeStruct((devices, TILE + NOTE, TILE), jnp.float32),
+        name="pack",
+    )(dest, slot, count, child_tiles)
 
 
 def columns_kernel(place, slot_in, front_ref, incoming_ref, out_ref, *rest):
@@ -80,7 +122,7 @@
             grid=(1,),
             in_specs=[
                 pl.BlockSpec((rows, 1, 1, 1, TILE, TILE), lambda i, *_: (0, 0, 0, 0, 0, 0)),
-                pl.BlockSpec(memory_space=pl.ANY),
+                pl.BlockSpec(memory_space=pltpu.HBM),
             ],
             out_specs=[whole_spec(a) for a in out_shape],
             scratch_shapes=[pltpu.VMEM((TILE, TILE), jnp.float32), pltpu.SemaphoreType.DMA],
@@ -280,8 +322,8 @@
     devices = incoming.shape[0]
     return pl.pallas_call(
         functools.partial(trailing_kernel, len(pieces)),
-        in_specs=spec(pltpu.SMEM, 4) + spec(pltpu.VMEM, len(held)) + spec(pl.ANY, 3),
-        out_specs=pl.BlockSpec(memory_space=pl.ANY),
+        in_specs=spec(pltpu.SMEM, 4) + spec(pltpu.VMEM, len(held)) + spec(pltpu.HBM, 3),
+        out_specs=pl.BlockSpec(memory_space=pltpu.HBM),
         scratch_shapes=[
             pltpu.VMEM((3 * WIDTH, count * TILE), jnp.bfloat16),
             pltpu.VMEM((2, 2, rows, TILE, TILE), jnp.float32),
@@ -295,7 +337,7 @@
         input_output_aliases={len(held) + 6: 0},
         compiler_params=pltpu.CompilerParams(vmem_limit_bytes=VMEM),
         cost_estimate=pl.CostEstimate(
-            flops=count * 2 * height * TILE * WIDTH * 3,
+            flops=8 * count * 2 * height * TILE * WIDTH,
             bytes_accessed=count * 2 * height * TILE * 4,
             transcendentals=0,
         ),
@@ -309,21 +351,11 @@
     my_row = lax.axis_index("row").astype(jnp.int32)
     my_col = lax.axis_index("col").astype(jnp.int32)
     rows_here, cols_here = (front.shape[0], front.shape[2])
-    slots = child_tiles.shape[0]
     devices = n_row * n_col
     assert n_col == 4 and n_row % 4 == 0 and rows_here % 3 == 0
     place = jnp.stack([my_row, my_col, jnp.int32(cols_here)])
 
-    numbers = jnp.arange(slots, dtype=jnp.int32)
-    live = numbers < tile_count[0]
-    dest = tile_dest[:, 0]
-    hits = (dest[None, :] == jnp.arange(devices, dtype=jnp.int32)[:, None]) & live[None, :]
-    picked = jnp.sum(jnp.where(hits, numbers[None, :], 0), axis=1)
-    slot_out = jnp.sum(jnp.where(hits, tile_slot[None, :] + 1, 0), axis=1) - 1
-    notes = jnp.broadcast_to(
-        slot_out.astype(jnp.float32)[:, None, None], (devices, NOTE, TILE)
-    )
-    outgoing = jnp.concatenate([jnp.take(child_tiles, picked, axis=0), notes], axis=1)
+    outgoing = pack(child_tiles, tile_dest[:, 0], tile_slot, tile_count, devices)
     incoming = lax.all_to_all(outgoing, BOTH, split_axis=0, concat_axis=0, tiled=True)
     slot_in = lax.optimization_barrier(incoming[:, TILE, 0].astype(jnp.int32))
 
@@ -342,6 +374,21 @@
     ring = rows_here % n_col == 0
     mine, *parts = assemble_columns(front, incoming, place, slot_in, n_col if ring else 1)
 
+    owners = [r * n_col + c for r in (2, 3) for c in (0, 1)]
+    slices = lax.all_to_all(
+        mine[0].reshape(devices, TILE // devices, TILE), BOTH, split_axis=0, concat_axis=0, tiled=True
+    )
+    own = jnp.stack([slices[owner] for owner in owners])
+
+    def hand_on(own):
+        lead = lax.all_to_all(own, BOTH, split_axis=0, concat_axis=0, tiled=True)
+        return lead.transpose(1, 0, 2, 3).reshape(2, 2, TILE, TILE)
+
+    own = jnp.broadcast_to(own[None], (devices,) + own.shape)
+    near = lax.ppermute(mine, "col", [(c, c ^ 1) for c in range(n_col)])
+    far = lax.ppermute(mine, "col", [(c, c ^ 2) for c in range(n_col)])
+    other = lax.ppermute(far, "col", [(c, c ^ 1) for c in range(n_col)])
+    others = [near, far, other]
     sets = n_row // n_col
     if ring:
         arrived = []
@@ -352,6 +399,7 @@
                 for c in range(n_col)
             ]
             arrived.append(lax.ppermute(part, BOTH, pairs))
+        arrived, own = lax.optimization_barrier((arrived, own))
         piece = jnp.stack(arrived)
         circle = list(range(0, n_row, 2)) + list(range(n_row - 1, 0, -2))
         spot = jnp.asarray([circle.index(r) for r in range(n_row)], jnp.int32)[my_row]
@@ -362,6 +410,10 @@
         for step in range(1, n_row // 2):
             ahead = lax.ppermute(ahead, "row", up)
             behind = lax.ppermute(behind, "row", down)
+            if step == 1:
+                ahead, behind, lead, others = lax.optimization_barrier(
+                    (ahead, behind, hand_on(own), others)
+                )
             rounds.append([(ahead, -step), (behind, step)])
         last = jnp.concatenate(
             [lax.ppermute(ahead[:2], "row", up), lax.ppermute(behind[2:], "row", down)]
@@ -384,24 +436,13 @@
         ]
         moved = lax.all_gather(lax.ppermute(mine, BOTH, pairs), "row", axis=0, tiled=False)
         rounds = [[(moved[h * n_col : (h + 1) * n_col], h)] for h in range(sets)]
+        lead = hand_on(own)
 
         def described(h):
             row = jnp.arange(rows_here, dtype=jnp.int32)
             return row * sets + h, jnp.arange(n_col, dtype=jnp.int32)
 
-    owners = [r * n_col + c for r in (2, 3) for c in (0, 1)]
-    slices = lax.all_to_all(
-        mine[0].reshape(devices, TILE // devices, TILE), BOTH, split_axis=0, concat_axis=0, tiled=True
-    )
-    own = jnp.stack([slices[owner] for owner in owners])
-    own = jnp.broadcast_to(own[None], (devices,) + own.shape)
-    lead = lax.all_to_all(own, BOTH, split_axis=0, concat_axis=0, tiled=True)
-    lead = lead.transpose(1, 0, 2, 3).reshape(2, 2, TILE, TILE)
-
-    near = lax.ppermute(mine, "col", [(c, c ^ 1) for c in range(n_col)])
-    far = lax.ppermute(mine, "col", [(c, c ^ 2) for c in range(n_col)])
-    other = lax.ppermute(far, "col", [(c, c ^ 1) for c in range(n_col)])
-    panels = row_panels([mine, near, far, other], lead, diag_inverses, place, front)
+    panels = row_panels([mine, *others], lead, diag_inverses, place, front)
 
     for entries in rounds:
         described_here = [described(shift) for _, shift in entries]

time: 196 us -> 222 us (1.13)
  Pallas kernels: 48.8 us -> 78.2 us
  waiting for transfers between devices: 62.7 us -> 54.5 us
  other arithmetic: 7.55 us -> 11.7 us
  starting transfers between devices: 30.8 us -> 34 us
  local copies, waits for them, and re-layouts: 18.3 us -> 15.8 us
    pallas_call x0 -> x1, Pallas kernels: none -> 31.7 us  [pack(): pl.pallas_call(pack_kernel, in_specs=[pl.BlockSpec(memory_space=pltpu.SME...]
    ppermute x3, waiting for transfers between devices: 23.7 us -> 0.01 us  [body(): behind = lax.ppermute(behind, 'row', down)]
    all_to_all x1, waiting for transfers between devices: 3.93 us -> 15.8 us  [hand_on(): lead = lax.all_to_all(own, BOTH, split_axis=0, concat_axis=0, tiled=True)]
    all_to_all x1, waiting for transfers between devices: 1.26 us -> 11.2 us  [body(): lax.all_to_all(mine[0].reshape(devices, TILE // devices, TILE), BOTH, spl...]
    all_to_all x1, waiting for transfers between devices: 25.9 us -> 18 us  [body(): lax.all_to_all(outgoing, BOTH, split_axis=0, concat_axis=0, tiled=True)]
    ppermute x3, waiting for transfers between devices: 0.14 us -> 7.62 us  [body(): ahead = lax.ppermute(ahead, 'row', up)]
    ppermute x4, waiting for transfers between devices: 7.66 us -> 0.23 us  [body(): arrived.append(lax.ppermute(part, BOTH, pairs))]
    pallas_call x4, Pallas kernels: 40.8 us -> 37.6 us  [trailing(): pl.pallas_call(functools.partial(trailing_kernel, len(pieces)), in_specs=...]
  transfers between devices with their start and end apart: 18 -> 18, of which waited for: 9 -> 6; matrix products, arithmetic and copies ran while one was open for 4% -> 9% of each run, Pallas kernels for 21% -> 17%
where the time goes in v3:
time: 222 us; the launch traced here: 221 us
  Pallas kernels  78.2 us (35%)
  waiting for transfers between devices  54.5 us (25%)
  starting transfers between devices  34 us (15%)
  between operations  26.5 us (12%)
  local copies, waits for them, and re-layouts  15.8 us (7%)
  other arithmetic  11.7 us (5%)
    pallas_call x4, Pallas kernels, trailing(): pl.pallas_call(functools.partial(trailing_kernel, len(pieces)), in_specs=...  37.6 us
    pallas_call x1, Pallas kernels, pack(): pl.pallas_call(pack_kernel, in_specs=[pl.BlockSpec(memory_space=pltpu.SME...  31.7 us
    all_to_all x1, waiting for transfers between devices, body(): lax.all_to_all(outgoing, BOTH, split_axis=0, concat_axis=0, tiled=True)  18 us
    all_to_all x1, waiting for transfers between devices, hand_on(): lead = lax.all_to_all(own, BOTH, split_axis=0, concat_axis=0, tiled=True)  15.8 us
    all_to_all x1, waiting for transfers between devices, body(): lax.all_to_all(mine[0].reshape(devices, TILE // devices, TILE), BOTH, spl...  11.2 us
    ppermute x4, starting transfers between devices, body(): arrived.append(lax.ppermute(part, BOTH, pairs))  7.77 us
    ppermute x3, waiting for transfers between devices, body(): ahead = lax.ppermute(ahead, 'row', up)  7.62 us
    all_to_all x1, starting transfers between devices, body(): lax.all_to_all(outgoing, BOTH, split_axis=0, concat_axis=0, tiled=True)  7.41 us
  transfers between devices with their start and end apart: 18, of which 6 were waited for; matrix products, arithmetic and copies ran while one was open for 9% of the time, Pallas kernels for 17%

profile of v3, /device:TPU:0, one launch (start us, length us, event | category | flops | bytes accessed | tf_op | source)
XLA Modules:
  0.0 220.6 jit_solution(12969710886142791413)
XLA Ops:
  0.7 31.7 %pack.1 = f32[32,136,128]{2,1,0:T(8,128)} custom-call(s32[16]{0:T(128)} %bitcast.32, s32[16]{0:T(128)} %slot.1, s32[1]{0:T(128)S(6)} %copy.30.count, f32[16,128,128]{2,1,0:T(8,128)} %child_ref.1), custom_call_target="tpu_custom_call" | custom-call | tf_op jit(solution)/shard_map/pack/pallas_call | solution.py:77
  32.4 7.4 %all-to-all-start = ((f32[32,136,128]{2,1,0:T(8,128)}), f32[32,136,128]{2,1,0:T(8,128)S(1)}, u32[]{:S(2)}, u32[]{:S(2)}) async-start(f32[32,136,128]{2,1,0:T(8,128)} %pack.1), calls=%async_computation | async-start | bytes 4456448 | tf_op jit(solution)/shard_map/all_to_all | solution.py:359
  39.9 1.3 dynamic_slice.27
  46.3 1.7 fusion.10
  68.1 0.6 and_select_fusion.2
  68.7 0.6 iota_multiply_fusion
  69.3 0.5 and_select_fusion.9.places
  69.9 0.6 multiply_add_fusion.2
  70.4 0.7 pad_add_fusion.4.columns
  71.1 0.6 pad_add_fusion.5.places
  71.7 0.6 pad_add_fusion.2.columns
  72.3 0.6 pad_add_fusion.3.places
  72.9 0.1 pad_add_fusion.1.place
  72.9 0.5 multiply_add_fusion
  73.5 18.0 %all-to-all-done.incoming_ref.rest_4_.rest_3_.rest_2_ = f32[32,136,128]{2,1,0:T(8,128)S(1)} async-done(((f32[32,136,128]{2,1,0:T(8,128)}), f32[32,136,128]{2,1,0:T(8,128)S(1)}, u32[]{:S(2)}, u32[]{:S(2)}) %all-to-all-start) | async-done | bytes 2228256 | tf_op jit(solution)/shard_map/all_to_all | solution.py:359
  91.5 0.7 fusion.slot_in
  92.1 6.4 %copy-done = f32[12,1,24,1,128,128]{5,4,3,2,1,0:T(8,128)S(1)} copy-done((f32[12,1,24,1,128,128]{5,4,3,2,1,0:T(8,128)S(1)}, f32[12,1,24,1,128,128]{5,4,3,2,1,0:T(8,128)}, u32[]{:S(2)}) %copy-start) | copy-done | bytes 18874392
  98.5 2.2 panel_columns.1
  100.7 1.5 collective-permute-start.7
  102.2 0.6 multiply_add_fusion.7.columns
  102.8 1.5 slice.23
  104.2 3.7 %all-to-all-start.1 = ((f32[32,4,128]{2,1,0:T(4,128)}), f32[32,4,128]{2,1,0:T(4,128)}, u32[]{:S(2)}, u32[]{:S(2)}) async-start(f32[32,4,128]{2,1,0:T(4,128)} %bitcast.29), calls=%async_computation.1 | async-start | bytes 131072 | tf_op jit(solution)/shard_map/all_to_all | solution.py:378
  108.0 0.7 pad_add_fusion.6.columns
  108.7 0.6 and_select_fusion
  109.3 1.3 collective-permute-start
  110.6 2.4 %collective-permute-start.1 = (f32[3,128,128]{2,1,0:T(8,128)S(1)}, f32[3,128,128]{2,1,0:T(8,128)}, u32[]{:S(2)}, u32[]{:S(2)}) collective-permute-start(f32[3,128,128]{2,1,0:T(8,128)S(1)} %get-tuple-element.26), channel_id=1, source_target_pairs={{0,4},{1,8},{2,12},{3,0},{4,5},{5,9},{6,13},{7,1},{8,6},{9,10},{10... | collective-permute-start | bytes 589832 | tf_op jit(solution)/shard_map/ppermute | solution.py:401
  113.1 3.5 %collective-permute-start.2 = (f32[3,128,128]{2,1,0:T(8,128)S(1)}, f32[3,128,128]{2,1,0:T(8,128)}, u32[]{:S(2)}, u32[]{:S(2)}) collective-permute-start(f32[3,128,128]{2,1,0:T(8,128)S(1)} %get-tuple-element.27), channel_id=1, source_target_pairs={{0,8},{1,12},{2,0},{3,4},{4,9},{5,13},{6,1},{7,5},{8,10},{9,14},{1... | collective-permute-start | bytes 589832 | tf_op jit(solution)/shard_map/ppermute | solution.py:401
  116.5 0.5 collective-permute-start.3
  117.1 11.2 %all-to-all-done.1 = f32[32,4,128]{2,1,0:T(4,128)} async-done(((f32[32,4,128]{2,1,0:T(4,128)}), f32[32,4,128]{2,1,0:T(4,128)}, u32[]{:S(2)}, u32[]{:S(2)}) %all-to-all-start.1) | async-done | bytes 65568 | tf_op jit(solution)/shard_map/all_to_all | solution.py:378
  128.3 0.7 fusion.9
  129.0 0.0 collective-permute-done
  129.0 0.1 collective-permute-start.6
  129.1 0.2 collective-permute-done.2
  129.3 0.7 broadcast_in_dim.42
  130.0 1.3 pad_maximum_fusion.rest_0_
  131.3 1.6 collective-permute-start.4
  132.9 0.5 collective-permute-start.5
  133.4 1.3 pad_add_fusion.7.places
  134.7 4.8 %all-to-all-start.2 = ((f32[32,4,4,128]{3,2,1,0:T(4,128)}), f32[32,4,4,128]{3,2,1,0:T(4,128)}, u32[]{:S(2)}, u32[]{:S(2)}) async-start(f32[32,4,4,128]{3,2,1,0:T(4,128)} %broadcast_in_dim.42), calls=%async_computation.2 | async-start | bytes 524288 | tf_op jit(solution)/shard_map/all_to_all | solution.py:384
  139.4 0.2 convert_reduce_fusion.1
  139.6 0.4 copy-done.9
  140.0 0.1 select_reduce_fusion.1
  140.1 0.7 copy.24
  140.8 0.8 reshape.32.order
  141.6 0.9 convert_reduce_fusion.starts
  142.5 15.8 %all-to-all-done.2 = f32[32,4,4,128]{3,2,1,0:T(4,128)} async-done(((f32[32,4,4,128]{3,2,1,0:T(4,128)}), f32[32,4,4,128]{3,2,1,0:T(4,128)}, u32[]{:S(2)}, u32[]{:S(2)}) %all-to-all-start.2) | async-done | bytes 262176 | tf_op jit(solution)/shard_map/all_to_all | solution.py:384
  158.3 1.0 copy.25
  159.3 0.0 collective-permute-done.4.rest_1_
  159.3 1.9 collective-permute-start.12
  161.3 0.1 collective-permute-start.9
  161.4 6.7 %row_panels.1 = (bf16[1536,1024]{1,0:T(8,128)(2,1)S(1)}, f32[12,1,24,1,128,128]{5,4,3,2,1,0:T(8,128)}, bf16[3,768,256]{2,1,0:T(8,128)(2,1)S(1)}) custom-call(s32[3]{0:T(128)S(1)} %pad_add_fusion.1.place, f32[12,128,128]{2,1,0:T(8,128)} %get-tuple-element.24.t0, f32[12,128,128]{2,1,0:T(8,128)} %collective-permute-done.6.t1, ...), custom_call_target="tpu_custom_call" | custom-call | tf_op jit(solution)/shard_map/row_panels/pallas_call | solution.py:184
  168.1 0.6 copy-done.2
  168.7 13.5 %trailing.4.rest_4_ = f32[12,1,24,1,128,128]{5,4,3,2,1,0:T(8,128)} custom-call(s32[9]{0:T(128)S(1)} %pad_add_fusion.6.columns, s32[12]{0:T(128)S(1)} %copy-done.2, s32[64]{0:T(128)S(1)} %reshape.32.order, s32[25]{0:T(128)S(1)} %convert_reduce_fusion.starts, bf16[1536,1024]{1,0:T(8,128)(2,1)S(1)} %get-tuple-element.38.pair_ref, ...), custom_call_target="tpu_custom_call", output_to_operand_aliasing={{}: (11, {})} | custom-call | flops 14495514624 | bytes 14155776 | tf_op jit(solution)/shard_map/trailing/pallas_call | solution.py:323
  182.2 0.0 collective-permute-done.9.rest_0_
  182.2 0.9 collective-permute-start.10
  183.1 1.2 collective-permute-start.13
  184.3 8.9 %trailing.5.rest_4_ = f32[12,1,24,1,128,128]{5,4,3,2,1,0:T(8,128)} custom-call(s32[6]{0:T(128)S(1)} %copy-done.5, s32[8]{0:T(128)S(1)} %copy-done.7, s32[64]{0:T(128)S(1)} %reshape.32.order, s32[25]{0:T(128)S(1)} %convert_reduce_fusion.starts, bf16[1536,1024]{1,0:T(8,128)(2,1)S(1)} %get-tuple-element.38.pair_ref, ...), custom_call_target="tpu_custom_call", output_to_operand_aliasing={{}: (10, {})} | custom-call | flops 9663676416 | bytes 9437184 | tf_op jit(solution)/shard_map/trailing/pallas_call | solution.py:323
  193.3 7.6 %collective-permute-done.10.rest_0_ = f32[4,3,128,128]{3,2,1,0:T(8,128)S(1)} collective-permute-done((f32[4,3,128,128]{3,2,1,0:T(8,128)S(1)}, f32[4,3,128,128]{3,2,1,0:T(8,128)S(1)}, u32[]{:S(2)}, u32[]{:S(2)}) %collective-permute-start.10) | collective-permute-done | bytes 786464 | tf_op jit(solution)/shard_map/ppermute | solution.py:411
  200.9 2.5 %collective-permute-start.11 = (f32[2,3,128,128]{3,2,1,0:T(8,128)S(1)}, f32[2,3,128,128]{3,2,1,0:T(8,128)S(1)}, u32[]{:S(2)}, u32[]{:S(2)}) collective-permute-start(f32[2,3,128,128]{3,2,1,0:T(8,128)S(1)} %slice.31), channel_id=1, source_target_pairs={{0,8},{8,16},{16,24},{24,28},{28,20},{20,12},{12,4},{4,0},{1,9},{9... | collective-permute-start | bytes 1179656 | tf_op jit(solution)/shard_map/ppermute | solution.py:419
  203.5 0.1 collective-permute-start.14
  203.6 9.0 %trailing.6.rest_3_ = f32[12,1,24,1,128,128]{5,4,3,2,1,0:T(8,128)} custom-call(s32[6]{0:T(128)S(1)} %copy-done.4, s32[8]{0:T(128)S(1)} %copy-done.6, s32[64]{0:T(128)S(1)} %reshape.32.order, s32[25]{0:T(128)S(1)} %convert_reduce_fusion.starts, bf16[1536,1024]{1,0:T(8,128)(2,1)S(1)} %get-tuple-element.38.pair_ref, ...), custom_call_target="tpu_custom_call", output_to_operand_aliasing={{}: (10, {})} | custom-call | flops 9663676416 | bytes 9437184 | tf_op jit(solution)/shard_map/trailing/pallas_call | solution.py:323
  212.6 1.6 collective-permute-done.14
  214.2 0.1 pad_maximum_fusion.1.rest_0_
  214.3 6.1 %trailing.7 = f32[12,1,24,1,128,128]{5,4,3,2,1,0:T(8,128)} custom-call(s32[3]{0:T(128)S(1)} %copy-done.8, s32[4]{0:T(128)S(1)} %copy-done.3, s32[64]{0:T(128)S(1)} %reshape.32.order, s32[25]{0:T(128)S(1)} %convert_reduce_fusion.starts, bf16[1536,1024]{1,0:T(8,128)(2,1)S(1)} %get-tuple-element.38.pair_ref, ...), custom_call_target="tpu_custom_call", output_to_operand_aliasing={{}: (9, {})} | custom-call | flops 4831838208 | bytes 4718592 | tf_op jit(solution)/shard_map/trailing/pallas_call | solution.py:323
  (36 shorter events, 0.2 us)
Async XLA Ops:
  0.0 161.4 %copy-start.1 = (f32[2,256,256]{2,1,0:T(8,128)S(1)}, f32[2,256,256]{2,1,0:T(8,128)}, u32[]{:S(2)}) copy-start(f32[2,256,256]{2,1,0:T(8,128)} %diag_ref.1) | copy-start | bytes 1572868
  32.4 59.0 %all-to-all-start = ((f32[32,136,128]{2,1,0:T(8,128)}), f32[32,136,128]{2,1,0:T(8,128)S(1)}, u32[]{:S(2)}, u32[]{:S(2)}) async-start(f32[32,136,128]{2,1,0:T(8,128)} %pack.1), calls=%async_computation | async-start | bytes 4456448 | tf_op jit(solution)/shard_map/all_to_all | solution.py:359
  92.1 6.4 %copy-start = (f32[12,1,24,1,128,128]{5,4,3,2,1,0:T(8,128)S(1)}, f32[12,1,24,1,128,128]{5,4,3,2,1,0:T(8,128)}, u32[]{:S(2)}) copy-start(f32[12,1,24,1,128,128]{5,4,3,2,1,0:T(8,128)} %rest_1_.1) | copy-start | bytes 56623108
  100.7 32.7 %collective-permute-start.7 = (f32[12,128,128]{2,1,0:T(8,128)}, f32[12,128,128]{2,1,0:T(8,128)}, u32[]{:S(2)}, u32[]{:S(2)}) collective-permute-start(f32[12,128,128]{2,1,0:T(8,128)} %get-tuple-element.24.t0), channel_id=1, source_target_pairs={{0,2},{1,3},{2,0},{3,1},{4,6},{5,7},{6,4},{7,5},{8,10},{9,11},{10,... | collective-permute-start | bytes 2359304 | tf_op jit(solution)/shard_map/ppermute | solution.py:389
  104.2 24.1 %all-to-all-start.1 = ((f32[32,4,128]{2,1,0:T(4,128)}), f32[32,4,128]{2,1,0:T(4,128)}, u32[]{:S(2)}, u32[]{:S(2)}) async-start(f32[32,4,128]{2,1,0:T(4,128)} %bitcast.29), calls=%async_computation.1 | async-start | bytes 131072 | tf_op jit(solution)/shard_map/all_to_all | solution.py:378
  109.3 19.7 %collective-permute-start = (f32[3,128,128]{2,1,0:T(8,128)S(1)}, f32[3,128,128]{2,1,0:T(8,128)}, u32[]{:S(2)}, u32[]{:S(2)}) collective-permute-start(f32[3,128,128]{2,1,0:T(8,128)S(1)} %get-tuple-element.25), channel_id=1, source_target_pairs={{0,0},{1,4},{2,8},{3,12},{4,1},{5,5},{6,9},{7,13},{8,2},{9,6},{10,... | collective-permute-start | bytes 589832 | tf_op jit(solution)/shard_map/ppermute | solution.py:401
  110.6 18.5 %collective-permute-start.1 = (f32[3,128,128]{2,1,0:T(8,128)S(1)}, f32[3,128,128]{2,1,0:T(8,128)}, u32[]{:S(2)}, u32[]{:S(2)}) collective-permute-start(f32[3,128,128]{2,1,0:T(8,128)S(1)} %get-tuple-element.26), channel_id=1, source_target_pairs={{0,4},{1,8},{2,12},{3,0},{4,5},{5,9},{6,13},{7,1},{8,6},{9,10},{10... | collective-permute-start | bytes 589832 | tf_op jit(solution)/shard_map/ppermute | solution.py:401
  113.1 16.2 %collective-permute-start.2 = (f32[3,128,128]{2,1,0:T(8,128)S(1)}, f32[3,128,128]{2,1,0:T(8,128)}, u32[]{:S(2)}, u32[]{:S(2)}) collective-permute-start(f32[3,128,128]{2,1,0:T(8,128)S(1)} %get-tuple-element.27), channel_id=1, source_target_pairs={{0,8},{1,12},{2,0},{3,4},{4,9},{5,13},{6,1},{7,5},{8,10},{9,14},{1... | collective-permute-start | bytes 589832 | tf_op jit(solution)/shard_map/ppermute | solution.py:401
  116.5 12.8 %collective-permute-start.3 = (f32[3,128,128]{2,1,0:T(8,128)S(1)}, f32[3,128,128]{2,1,0:T(8,128)}, u32[]{:S(2)}, u32[]{:S(2)}) collective-permute-start(f32[3,128,128]{2,1,0:T(8,128)S(1)} %get-tuple-element.28), channel_id=1, source_target_pairs={{0,12},{1,0},{2,4},{3,8},{4,13},{5,1},{6,5},{7,9},{8,14},{9,2},{10... | collective-permute-start | bytes 589832 | tf_op jit(solution)/shard_map/ppermute | solution.py:401
  129.0 30.3 %collective-permute-start.6 = (f32[12,128,128]{2,1,0:T(8,128)}, f32[12,128,128]{2,1,0:T(8,128)}, u32[]{:S(2)}, u32[]{:S(2)}) collective-permute-start(f32[12,128,128]{2,1,0:T(8,128)} %get-tuple-element.24.t0), channel_id=1, source_target_pairs={{0,1},{1,0},{2,3},{3,2},{4,5},{5,4},{6,7},{7,6},{8,9},{9,8},{10,11... | collective-permute-start | bytes 2359304 | tf_op jit(solution)/shard_map/ppermute | solution.py:388
  131.3 28.0 %collective-permute-start.4 = (f32[4,3,128,128]{3,2,1,0:T(8,128)S(1)}, f32[4,3,128,128]{3,2,1,0:T(8,128)}, u32[]{:S(2)}, u32[]{:S(2)}) collective-permute-start(f32[4,3,128,128]{3,2,1,0:T(8,128)S(1)} %pad_maximum_fusion.rest_0_), channel_id=1, source_target_pairs={{0,8},{8,16},{16,24},{24,28},{28,20},{20,12},{12,4},{4,0},{1,9},{9... | collective-permute-start | bytes 2359304 | tf_op jit(solution)/shard_map/ppermute | solution.py:411
  132.9 26.4 %collective-permute-start.5 = (f32[4,3,128,128]{3,2,1,0:T(8,128)S(1)}, f32[4,3,128,128]{3,2,1,0:T(8,128)}, u32[]{:S(2)}, u32[]{:S(2)}) collective-permute-start(f32[4,3,128,128]{3,2,1,0:T(8,128)S(1)} %pad_maximum_fusion.rest_0_), channel_id=1, source_target_pairs={{8,0},{16,8},{24,16},{28,24},{20,28},{12,20},{4,12},{0,4},{9,1},{1... | collective-permute-start | bytes 2359304 | tf_op jit(solution)/shard_map/ppermute | solution.py:412
  133.4 25.9 %collective-permute-start.8 = (f32[12,128,128]{2,1,0:T(8,128)}, f32[12,128,128]{2,1,0:T(8,128)}, u32[]{:S(2)}, u32[]{:S(2)}) collective-permute-start(f32[12,128,128]{2,1,0:T(8,128)} %collective-permute-done.7.t2), channel_id=1, source_target_pairs={{0,1},{1,0},{2,3},{3,2},{4,5},{5,4},{6,7},{7,6},{8,9},{9,8},{10,11... | collective-permute-start | bytes 2359304 | tf_op jit(solution)/shard_map/ppermute | solution.py:390
  134.7 23.6 %all-to-all-start.2 = ((f32[32,4,4,128]{3,2,1,0:T(4,128)}), f32[32,4,4,128]{3,2,1,0:T(4,128)}, u32[]{:S(2)}, u32[]{:S(2)}) async-start(f32[32,4,4,128]{3,2,1,0:T(4,128)} %broadcast_in_dim.42), calls=%async_computation.2 | async-start | bytes 524288 | tf_op jit(solution)/shard_map/all_to_all | solution.py:384
  139.4 0.6 copy-start.9
  159.3 23.8 %collective-permute-start.12 = (f32[4,3,128,128]{3,2,1,0:T(8,128)}, f32[4,3,128,128]{3,2,1,0:T(8,128)S(1)}, u32[]{:S(2)}, u32[]{:S(2)}) collective-permute-start(f32[4,3,128,128]{3,2,1,0:T(8,128)} %collective-permute-done.5.rest_2_), channel_id=1, source_target_pairs={{8,0},{16,8},{24,16},{28,24},{20,28},{12,20},{4,12},{0,4},{9,1},{1... | collective-permute-start | bytes 2359304 | tf_op jit(solution)/shard_map/ppermute | solution.py:412
  161.3 21.0 %collective-permute-start.9 = (f32[4,3,128,128]{3,2,1,0:T(8,128)}, f32[4,3,128,128]{3,2,1,0:T(8,128)S(1)}, u32[]{:S(2)}, u32[]{:S(2)}) collective-permute-start(f32[4,3,128,128]{3,2,1,0:T(8,128)} %collective-permute-done.4.rest_1_), channel_id=1, source_target_pairs={{0,8},{8,16},{16,24},{24,28},{28,20},{20,12},{12,4},{4,0},{1,9},{9... | collective-permute-start | bytes 2359304 | tf_op jit(solution)/shard_map/ppermute | solution.py:411
  168.1 0.6 copy-start.2
  168.7 15.6 %copy-start.5 = (s32[6]{0:T(128)S(1)}, s32[6]{0:T(128)}, u32[]{:S(2)}) copy-start(s32[6]{0:T(128)} %pad_add_fusion.4.columns) | copy-start | bytes 76
  168.7 15.6 %copy-start.7 = (s32[8]{0:T(128)S(1)}, s32[8]{0:T(128)}, u32[]{:S(2)}) copy-start(s32[8]{0:T(128)} %pad_add_fusion.5.places) | copy-start | bytes 100
  182.2 21.4 %copy-start.4 = (s32[6]{0:T(128)S(1)}, s32[6]{0:T(128)}, u32[]{:S(2)}) copy-start(s32[6]{0:T(128)} %pad_add_fusion.2.columns) | copy-start | bytes 76
  182.2 21.4 %copy-start.6 = (s32[8]{0:T(128)S(1)}, s32[8]{0:T(128)}, u32[]{:S(2)}) copy-start(s32[8]{0:T(128)} %pad_add_fusion.3.places) | copy-start | bytes 100
  182.2 18.6 %collective-permute-start.10 = (f32[4,3,128,128]{3,2,1,0:T(8,128)S(1)}, f32[4,3,128,128]{3,2,1,0:T(8,128)S(1)}, u32[]{:S(2)}, u32[]{:S(2)}) collective-permute-start(f32[4,3,128,128]{3,2,1,0:T(8,128)S(1)} %collective-permute-done.9.rest_0_), channel_id=1, source_target_pairs={{0,8},{8,16},{16,24},{24,28},{28,20},{20,12},{12,4},{4,0},{1,9},{9... | collective-permute-start | bytes 2359304 | tf_op jit(solution)/shard_map/ppermute | solution.py:411
  183.1 20.3 %collective-permute-start.13 = (f32[4,3,128,128]{3,2,1,0:T(8,128)S(1)}, f32[4,3,128,128]{3,2,1,0:T(8,128)S(1)}, u32[]{:S(2)}, u32[]{:S(2)}) collective-permute-start(f32[4,3,128,128]{3,2,1,0:T(8,128)S(1)} %collective-permute-done.12.rest_1_), channel_id=1, source_target_pairs={{8,0},{16,8},{24,16},{28,24},{20,28},{12,20},{4,12},{0,4},{9,1},{1... | collective-permute-start | bytes 2359304 | tf_op jit(solution)/shard_map/ppermute | solution.py:412
  200.9 11.7 %collective-permute-start.11 = (f32[2,3,128,128]{3,2,1,0:T(8,128)S(1)}, f32[2,3,128,128]{3,2,1,0:T(8,128)S(1)}, u32[]{:S(2)}, u32[]{:S(2)}) collective-permute-start(f32[2,3,128,128]{3,2,1,0:T(8,128)S(1)} %slice.31), channel_id=1, source_target_pairs={{0,8},{8,16},{16,24},{24,28},{28,20},{20,12},{12,4},{4,0},{1,9},{9... | collective-permute-start | bytes 1179656 | tf_op jit(solution)/shard_map/ppermute | solution.py:419
  203.5 10.8 %copy-start.3 = (s32[4]{0:T(128)S(1)}, s32[4]{0:T(128)}, u32[]{:S(2)}) copy-start(s32[4]{0:T(128)} %and_select_fusion.9.places) | copy-start | bytes 52
  203.5 10.8 %copy-start.8 = (s32[3]{0:T(128)S(1)}, s32[3]{0:T(128)}, u32[]{:S(2)}) copy-start(s32[3]{0:T(128)} %multiply_add_fusion.7.columns) | copy-start | bytes 40
  203.5 10.7 %collective-permute-start.14 = (f32[2,3,128,128]{3,2,1,0:T(8,128)S(1)}, f32[2,3,128,128]{3,2,1,0:T(8,128)S(1)}, u32[]{:S(2)}, u32[]{:S(2)}) collective-permute-start(f32[2,3,128,128]{3,2,1,0:T(8,128)S(1)} %slice.32), channel_id=1, source_target_pairs={{8,0},{16,8},{24,16},{28,24},{20,28},{12,20},{4,12},{0,4},{9,1},{1... | collective-permute-start | bytes 1179656 | tf_op jit(solution)/shard_map/ppermute | solution.py:419

commit v4 on v3

--- a/solution.py
+++ b/solution.py
@@ -41,6 +41,12 @@
     return one, mask(1, dot(deep(field), small_ref[2]))
 
 
+def two_panels_across(columns, small_ref):
+    one = dot(small_ref[0], stacked(jnp.concatenate(columns[:2], axis=0)))
+    field = jnp.concatenate(columns[2:], axis=0) - dot(small_ref[1], stacked(one))
+    return one, dot(small_ref[2], stacked(field))
+
+
 def whole_spec(array):
     rank = len(array.shape)
     return pl.BlockSpec(array.shape, lambda *_: (0,) * rank)
@@ -76,7 +82,8 @@
     hbm = pl.BlockSpec(memory_space=pltpu.HBM)
     return pl.pallas_call(
         pack_kernel,
-        in_specs=[pl.BlockSpec(memory_space=pltpu.SMEM)] * 3 + [hbm],
+        in_specs=[pl.BlockSpec(memory_space=pltpu.SMEM)] * 3
+        + [pl.BlockSpec(memory_space=pltpu.VMEM)],
         out_specs=hbm,
         scratch_shapes=[
             pltpu.VMEM((devices, NOTE, TILE), jnp.float32),
@@ -91,7 +98,9 @@
 def columns_kernel(place, slot_in, front_ref, incoming_ref, out_ref, *rest):
     *parts, tile_ref, sem = rest
     cols = place[2]
-    out_ref[...] = front_ref[:, 0, 0, 0]
+    strip = pltpu.make_async_copy(front_ref.at[:, 0, 0, 0], out_ref, sem)
+    strip.start()
+    strip.wait()
 
     @pl.loop(0, incoming_ref.shape[0])
     def _(s):
@@ -108,7 +117,8 @@
     count = len(parts)
     for j, part_ref in enumerate(parts):
         group = part_ref.shape[0]
-        part_ref[...] = out_ref[pl.ds(lax.rem(place[1] + j, count) * group, group)]
+        for t in range(group):
+            part_ref[t] = out_ref[lax.rem(place[1] + j, count) * group + t].T
 
 
 def assemble_columns(front, incoming, place, slot_in, parts):
@@ -121,7 +131,7 @@
             num_scalar_prefetch=2,
             grid=(1,),
             in_specs=[
-                pl.BlockSpec((rows, 1, 1, 1, TILE, TILE), lambda i, *_: (0, 0, 0, 0, 0, 0)),
+                pl.BlockSpec(memory_space=pltpu.HBM),
                 pl.BlockSpec(memory_space=pltpu.HBM),
             ],
             out_specs=[whole_spec(a) for a in out_shape],
@@ -134,7 +144,7 @@
 
 
 def row_panels_kernel(
-    place, t0, t1, t2, t3, lead_ref, diag_ref, pair_ref, out_ref, small_ref, tiles_ref
+    place, t0, t1, t2, t3, lead_ref, diag_ref, pair_ref, out_ref, across_ref, small_ref, tiles_ref
 ):
     step = pl.program_id(0)
     my_row, my_col = place[0], place[1]
@@ -147,8 +157,12 @@
         lead = jnp.concatenate(
             [jnp.concatenate([lead_ref[i, 0], lead_ref[i, 1]], axis=1) for i in range(2)], axis=0
         )
-        small_ref[1] = stacked(dot(deep(lead), small_ref[0]).T)
+        lead = dot(deep(lead), small_ref[0])
+        small_ref[1] = stacked(lead.T)
         small_ref[2] = stacked(diag_ref[1])
+        across_ref[0] = deep(diag_ref[0].T)
+        across_ref[1] = deep(lead)
+        across_ref[2] = deep(diag_ref[1].T)
 
     for i, tile_ref in enumerate((t0, t1, t2, t3)):
         tiles_ref[jnp.bitwise_xor(my_col, i)] = tile_ref[...]
@@ -171,14 +185,14 @@
             out_ref[:, 0, 0, 0] = pieces[c].reshape(group, TILE, TILE)
 
 
-def row_panels(tiles, lead, diag, place, front):
+def row_panels(mine, others, lead, diag, place, front):
     rows = front.shape[0]
     group = rows // 3
     height = group * TILE
     out_shape = [
         jax.ShapeDtypeStruct((rows * TILE, 2 * WIDTH), jnp.bfloat16),
         jax.ShapeDtypeStruct(front.shape, jnp.float32),
-        jax.ShapeDtypeStruct((3, 3 * PANEL, PANEL), jnp.bfloat16),
+        jax.ShapeDtypeStruct((3, PANEL, 3 * PANEL), jnp.bfloat16),
     ]
     strip = pl.BlockSpec((group, TILE, TILE), lambda i, *_: (i, 0, 0))
     return pl.pallas_call(
@@ -192,12 +206,15 @@
                 pl.BlockSpec((group, 1, 1, 1, TILE, TILE), lambda i, *_: (i, 0, 0, 0, 0, 0)),
                 whole_spec(out_shape[2]),
             ],
-            scratch_shapes=[pltpu.VMEM((4, group, TILE, TILE), jnp.float32)],
+            scratch_shapes=[
+                pltpu.VMEM((3, 3 * PANEL, PANEL), jnp.bfloat16),
+                pltpu.VMEM((4, group, TILE, TILE), jnp.float32),
+            ],
         ),
         out_shape=out_shape,
         compiler_params=pltpu.CompilerParams(vmem_limit_bytes=VMEM),
         name="row_panels",
-    )(place, *tiles, lead, diag)
+    )(place, mine, *others, lead, diag)
 
 
 def trailing_kernel(n_pieces, columns, places, order, starts, pair_ref, small_ref, *rest):
@@ -262,15 +279,16 @@
     tile_columns = [
         jnp.concatenate(
             [
-                piece[places[4 * p + c]].reshape(group * TILE, TILE)
+                piece[places[4 * p + c], t]
                 for p, piece in enumerate(piece_refs)
+                for t in range(group)
             ],
-            axis=0,
+            axis=1,
         )
         for c in range(4)
     ]
-    for i, panel in enumerate(two_panels(tile_columns, small_ref, lambda _, value: value)):
-        high, low = halves(panel.T)
+    for i, panel in enumerate(two_panels_across(tile_columns, small_ref)):
+        high, low = halves(panel)
         for k, half in enumerate((high, high, low)):
             right_ref[k * WIDTH + i * PANEL : k * WIDTH + (i + 1) * PANEL] = half
 
@@ -375,9 +393,8 @@
     mine, *parts = assemble_columns(front, incoming, place, slot_in, n_col if ring else 1)
 
     owners = [r * n_col + c for r in (2, 3) for c in (0, 1)]
-    slices = lax.all_to_all(
-        mine[0].reshape(devices, TILE // devices, TILE), BOTH, split_axis=0, concat_axis=0, tiled=True
-    )
+    slices = mine[0].reshape(devices, TILE // devices, TILE)
+    slices = lax.all_to_all(slices, BOTH, split_axis=0, concat_axis=0, tiled=True)
     own = jnp.stack([slices[owner] for owner in owners])
 
     def hand_on(own):
@@ -385,10 +402,12 @@
         return lead.transpose(1, 0, 2, 3).reshape(2, 2, TILE, TILE)
 
     own = jnp.broadcast_to(own[None], (devices,) + own.shape)
-    near = lax.ppermute(mine, "col", [(c, c ^ 1) for c in range(n_col)])
-    far = lax.ppermute(mine, "col", [(c, c ^ 2) for c in range(n_col)])
-    other = lax.ppermute(far, "col", [(c, c ^ 1) for c in range(n_col)])
-    others = [near, far, other]
+
+    def exchange(mine):
+        near = lax.ppermute(mine, "col", [(c, c ^ 1) for c in range(n_col)])
+        far = lax.ppermute(mine, "col", [(c, c ^ 2) for c in range(n_col)])
+        return [near, far, lax.ppermute(far, "col", [(c, c ^ 1) for c in range(n_col)])]
+
     sets = n_row // n_col
     if ring:
         arrived = []
@@ -399,21 +418,20 @@
                 for c in range(n_col)
             ]
             arrived.append(lax.ppermute(part, BOTH, pairs))
-        arrived, own = lax.optimization_barrier((arrived, own))
+        arrived, own, mine = lax.optimization_barrier((arrived, own, mine))
         piece = jnp.stack(arrived)
         circle = list(range(0, n_row, 2)) + list(range(n_row - 1, 0, -2))
         spot = jnp.asarray([circle.index(r) for r in range(n_row)], jnp.int32)[my_row]
         up = [(circle[i], circle[(i + 1) % n_row]) for i in range(n_row)]
         down = [(b, a) for a, b in up]
         rounds = [[(piece, 0)]]
+        panels = row_panels(mine, exchange(mine), hand_on(own), diag_inverses, place, front)
         ahead = behind = piece
         for step in range(1, n_row // 2):
             ahead = lax.ppermute(ahead, "row", up)
             behind = lax.ppermute(behind, "row", down)
-            if step == 1:
-                ahead, behind, lead, others = lax.optimization_barrier(
-                    (ahead, behind, hand_on(own), others)
-                )
+            if step == 2:
+                ahead, behind, panels = lax.optimization_barrier((ahead, behind, panels))
             rounds.append([(ahead, -step), (behind, step)])
         last = jnp.concatenate(
             [lax.ppermute(ahead[:2], "row", up), lax.ppermute(behind[2:], "row", down)]
@@ -434,15 +452,13 @@
             for r in range(n_row)
             for c in range(n_col)
         ]
-        moved = lax.all_gather(lax.ppermute(mine, BOTH, pairs), "row", axis=0, tiled=False)
+        moved = lax.all_gather(lax.ppermute(parts[0], BOTH, pairs), "row", axis=0, tiled=False)
         rounds = [[(moved[h * n_col : (h + 1) * n_col], h)] for h in range(sets)]
-        lead = hand_on(own)
+        panels = row_panels(mine, exchange(mine), hand_on(own), diag_inverses, place, front)
 
         def described(h):
             row = jnp.arange(rows_here, dtype=jnp.int32)
             return row * sets + h, jnp.arange(n_col, dtype=jnp.int32)
-
-    panels = row_panels([mine, *others], lead, diag_inverses, place, front)
 
     for entries in rounds:
         described_here = [described(shift) for _, shift in entries]

time: 222 us -> 205 us (0.923)
  Pallas kernels: 78.2 us -> 48.3 us
  waiting for transfers between devices: 54.5 us -> 65.4 us
    pallas_call x1, Pallas kernels: 31.7 us -> 2.44 us  [pack(): pl.pallas_call(pack_kernel, in_specs=[pl.BlockSpec(memory_space=pltpu.SME...]
    all_to_all x1, waiting for transfers between devices: 18 us -> 30.4 us  [body(): lax.all_to_all(outgoing, BOTH, split_axis=0, concat_axis=0, tiled=True)]
    all_to_all x1, waiting for transfers between devices: 11.2 us -> 0.01 us  [body(): lax.all_to_all(slices, BOTH, split_axis=0, concat_axis=0, tiled=True)]
    ppermute x3, waiting for transfers between devices: 0.01 us -> 10.1 us  [the longest x1 10.1 us: exchange(): far = lax.ppermute(mine, 'col', [(c, c ^ 2) for c in range(n_col)])]
    ppermute x3, waiting for transfers between devices: 7.62 us -> 1.97 us  [body(): ahead = lax.ppermute(ahead, 'row', up)]
    ppermute x4, waiting for transfers between devices: 0.23 us -> 5.58 us  [body(): arrived.append(lax.ppermute(part, BOTH, pairs))]
  transfers between devices with their start and end apart: 18 -> 18, of which waited for: 6 -> 9; matrix products, arithmetic and copies ran while one was open for 9% -> 8% of each run, Pallas kernels for 17% -> 18%
where the time goes in v4:
time: 205 us; the launch traced here: 203 us
  waiting for transfers between devices  65.4 us (32%)
  Pallas kernels  48.3 us (24%)
  starting transfers between devices  34.5 us (17%)
  between operations  27.5 us (13%)
  local copies, waits for them, and re-layouts  15.9 us (8%)
  other arithmetic  11.6 us (6%)
    pallas_call x4, Pallas kernels, trailing(): pl.pallas_call(functools.partial(trailing_kernel, len(pieces)), in_specs=...  36.7 us
    all_to_all x1, waiting for transfers between devices, body(): lax.all_to_all(outgoing, BOTH, split_axis=0, concat_axis=0, tiled=True)  30.4 us
    all_to_all x1, waiting for transfers between devices, hand_on(): lead = lax.all_to_all(own, BOTH, split_axis=0, concat_axis=0, tiled=True)  16.4 us
    ppermute x1, waiting for transfers between devices, exchange(): far = lax.ppermute(mine, 'col', [(c, c ^ 2) for c in range(n_col)])  10.1 us
    ppermute x4, starting transfers between devices, body(): arrived.append(lax.ppermute(part, BOTH, pairs))  7.77 us
    unnamed x20, local copies, waits for them, and re-layouts  7.43 us
    all_to_all x1, starting transfers between devices, body(): lax.all_to_all(outgoing, BOTH, split_axis=0, concat_axis=0, tiled=True)  7.22 us
    pallas_call x1, Pallas kernels, row_panels(): pl.pallas_call(row_panels_kernel, grid_spec=pltpu.PrefetchScalarGridSpec(...  6.75 us
  transfers between devices with their start and end apart: 18, of which 9 were waited for; matrix products, arithmetic and copies ran while one was open for 8% of the time, Pallas kernels for 18%

profile of v4, /device:TPU:0, one launch (start us, length us, event | category | flops | bytes accessed | tf_op | source)
XLA Modules:
  0.0 203.1 jit_solution(6740929464854777939)
XLA Ops:
  0.7 2.4 %pack.1 = f32[32,136,128]{2,1,0:T(8,128)} custom-call(s32[16]{0:T(128)} %bitcast.32, s32[16]{0:T(128)} %slot.1, s32[1]{0:T(128)S(6)} %copy.30.count, f32[16,128,128]{2,1,0:T(8,128)} %child_ref.1), custom_call_target="tpu_custom_call" | custom-call | tf_op jit(solution)/shard_map/pack/pallas_call | solution.py:83
  3.2 7.2 %all-to-all-start = ((f32[32,136,128]{2,1,0:T(8,128)}), f32[32,136,128]{2,1,0:T(8,128)S(1)}, u32[]{:S(2)}, u32[]{:S(2)}) async-start(f32[32,136,128]{2,1,0:T(8,128)} %pack.1), calls=%async_computation | async-start | bytes 4456448 | tf_op jit(solution)/shard_map/all_to_all | solution.py:377
  10.4 1.3 dynamic_slice.27
  17.4 1.7 fusion.10
  28.7 0.5 iota_multiply_fusion
  29.3 0.6 and_select_fusion.9.places
  29.8 0.5 multiply_add_fusion.2
  30.4 0.7 pad_add_fusion.4.columns
  31.0 0.1 pad_add_fusion.1.place
  31.1 0.5 and_select_fusion.3
  31.6 30.4 %all-to-all-done.incoming_ref.rest_4_.rest_3_.rest_2_ = f32[32,136,128]{2,1,0:T(8,128)S(1)} async-done(((f32[32,136,128]{2,1,0:T(8,128)}), f32[32,136,128]{2,1,0:T(8,128)S(1)}, u32[]{:S(2)}, u32[]{:S(2)}) %all-to-all-start) | async-done | bytes 2228256 | tf_op jit(solution)/shard_map/all_to_all | solution.py:377
  62.0 0.7 fusion.slot_in
  62.7 6.4 %copy-done = f32[12,1,24,1,128,128]{5,4,3,2,1,0:T(8,128)S(1)} copy-done((f32[12,1,24,1,128,128]{5,4,3,2,1,0:T(8,128)S(1)}, f32[12,1,24,1,128,128]{5,4,3,2,1,0:T(8,128)}, u32[]{:S(2)}) %copy-start) | copy-done | bytes 18874392
  69.0 2.4 %panel_columns.1 = (f32[12,128,128]{2,1,0:T(8,128)}, f32[3,128,128]{2,1,0:T(8,128)S(1)}, f32[3,128,128]{2,1,0:T(8,128)S(1)}, f32[3,128,128]{2,1,0:T(8,128)S(1)}, f32[3,128,128]{2,1,0:T(8,128)S(1)}) custom-call(s32[3]{0:T(128)S(1)} %pad_add_fusion.1.place, s32[32]{0:T(128)S(1)} %fusion.slot_in, f32[12,1,24,1,128,128]{5,4,3,2,1,0:T(8,128)S(1)} %copy-done, ...), custom_call_target="tpu_custom_call" | custom-call | tf_op jit(solution)/shard_map/panel_columns/pallas_call | solution.py:128
  71.5 1.5 slice.23
  72.9 4.1 %all-to-all-start.1 = ((f32[32,4,128]{2,1,0:T(4,128)}), f32[32,4,128]{2,1,0:T(4,128)}, u32[]{:S(2)}, u32[]{:S(2)}) async-start(f32[32,4,128]{2,1,0:T(4,128)} %bitcast.29), calls=%async_computation.1 | async-start | bytes 131072 | tf_op jit(solution)/shard_map/all_to_all | solution.py:397
  77.1 1.2 pad_add_fusion.5.places
  87.3 0.5 multiply_add_fusion.5
  87.8 1.3 collective-permute-start
  89.2 2.5 %collective-permute-start.1 = (f32[3,128,128]{2,1,0:T(8,128)S(1)}, f32[3,128,128]{2,1,0:T(8,128)}, u32[]{:S(2)}, u32[]{:S(2)}) collective-permute-start(f32[3,128,128]{2,1,0:T(8,128)S(1)} %get-tuple-element.25), channel_id=1, source_target_pairs={{0,4},{1,8},{2,12},{3,0},{4,5},{5,9},{6,13},{7,1},{8,6},{9,10},{10... | collective-permute-start | bytes 589832 | tf_op jit(solution)/shard_map/ppermute | solution.py:420
  91.6 3.5 %collective-permute-start.2 = (f32[3,128,128]{2,1,0:T(8,128)S(1)}, f32[3,128,128]{2,1,0:T(8,128)}, u32[]{:S(2)}, u32[]{:S(2)}) collective-permute-start(f32[3,128,128]{2,1,0:T(8,128)S(1)} %get-tuple-element.26), channel_id=1, source_target_pairs={{0,8},{1,12},{2,0},{3,4},{4,9},{5,13},{6,1},{7,5},{8,10},{9,14},{1... | collective-permute-start | bytes 589832 | tf_op jit(solution)/shard_map/ppermute | solution.py:420
  95.1 0.5 collective-permute-start.3
  95.6 0.7 fusion.9
  96.3 4.3 %collective-permute-done.1 = f32[3,128,128]{2,1,0:T(8,128)} collective-permute-done((f32[3,128,128]{2,1,0:T(8,128)S(1)}, f32[3,128,128]{2,1,0:T(8,128)}, u32[]{:S(2)}, u32[]{:S(2)}) %collective-permute-start.1) | collective-permute-done | bytes 196640 | tf_op jit(solution)/shard_map/ppermute | solution.py:420
  100.6 0.6 collective-permute-done.2
  101.2 0.7 collective-permute-done.3
  101.9 0.7 broadcast_in_dim.42
  102.6 2.7 %collective-permute-start.9 = (f32[12,128,128]{2,1,0:T(8,128)}, f32[12,128,128]{2,1,0:T(8,128)}, u32[]{:S(2)}, u32[]{:S(2)}) collective-permute-start(f32[12,128,128]{2,1,0:T(8,128)} %get-tuple-element.33.t0), channel_id=1, source_target_pairs={{0,2},{1,3},{2,0},{3,1},{4,6},{5,7},{6,4},{7,5},{8,10},{9,11},{10,... | collective-permute-start | bytes 2359304 | tf_op jit(solution)/shard_map/ppermute | solution.py:408
  105.4 1.3 pad_maximum_fusion.rest_0_
  106.6 0.1 collective-permute-start.4
  106.7 2.0 collective-permute-start.6
  110.7 1.3 pad_add_fusion.2.columns
  111.9 0.7 pad_add_fusion.3.places
  112.6 0.5 multiply_add_fusion.7.columns
  113.1 0.7 pad_add_fusion.6.columns
  113.8 0.1 collective-permute-start.8
  113.9 10.1 %collective-permute-done.9.t2 = f32[12,128,128]{2,1,0:T(8,128)} collective-permute-done((f32[12,128,128]{2,1,0:T(8,128)}, f32[12,128,128]{2,1,0:T(8,128)}, u32[]{:S(2)}, u32[]{:S(2)}) %collective-permute-start.9) | collective-permute-done | bytes 786464 | tf_op jit(solution)/shard_map/ppermute | solution.py:408
  124.0 0.1 collective-permute-start.10
  124.1 2.0 collective-permute-done.4.rest_1_
  126.0 0.7 collective-permute-start.5
  126.8 0.7 collective-permute-done.6.rest_2_
  127.4 0.6 collective-permute-start.7
  128.1 0.7 pad_add_fusion.7.places
  128.7 5.0 %all-to-all-start.2 = ((f32[32,4,4,128]{3,2,1,0:T(4,128)}), f32[32,4,4,128]{3,2,1,0:T(4,128)}, u32[]{:S(2)}, u32[]{:S(2)}) async-start(f32[32,4,4,128]{3,2,1,0:T(4,128)} %broadcast_in_dim.42), calls=%async_computation.2 | async-start | bytes 524288 | tf_op jit(solution)/shard_map/all_to_all | solution.py:401
  133.7 0.2 convert_reduce_fusion.1
  133.9 0.4 copy-done.9
  134.3 0.1 select_reduce_fusion.1
  134.4 0.7 copy.24
  135.1 0.8 reshape.32.order
  135.9 0.8 convert_reduce_fusion.starts
  136.7 16.4 %all-to-all-done.2 = f32[32,4,4,128]{3,2,1,0:T(4,128)} async-done(((f32[32,4,4,128]{3,2,1,0:T(4,128)}), f32[32,4,4,128]{3,2,1,0:T(4,128)}, u32[]{:S(2)}, u32[]{:S(2)}) %all-to-all-start.2) | async-done | bytes 262176 | tf_op jit(solution)/shard_map/all_to_all | solution.py:401
  153.1 1.0 copy.25
  154.2 6.8 %row_panels.1 = (bf16[1536,1024]{1,0:T(8,128)(2,1)S(1)}, f32[12,1,24,1,128,128]{5,4,3,2,1,0:T(8,128)}, bf16[3,256,768]{2,1,0:T(8,128)(2,1)S(1)}) custom-call(s32[3]{0:T(128)S(1)} %pad_add_fusion.1.place, f32[12,128,128]{2,1,0:T(8,128)} %get-tuple-element.33.t0, f32[12,128,128]{2,1,0:T(8,128)} %collective-permute-done.8.t1, ...), custom_call_target="tpu_custom_call" | custom-call | tf_op jit(solution)/shard_map/row_panels/pallas_call | solution.py:198
  160.9 0.4 collective-permute-start.11
  161.3 1.7 collective-permute-start.13
  163.0 0.7 copy-done.2
  163.7 12.6 %trailing.4.rest_4_ = f32[12,1,24,1,128,128]{5,4,3,2,1,0:T(8,128)} custom-call(s32[9]{0:T(128)S(1)} %pad_add_fusion.6.columns, s32[12]{0:T(128)S(1)} %copy-done.2, s32[64]{0:T(128)S(1)} %reshape.32.order, s32[25]{0:T(128)S(1)} %convert_reduce_fusion.starts, bf16[1536,1024]{1,0:T(8,128)(2,1)S(1)} %get-tuple-element.38.pair_ref, ...), custom_call_target="tpu_custom_call", output_to_operand_aliasing={{}: (11, {})} | custom-call | flops 14495514624 | bytes 14155776 | tf_op jit(solution)/shard_map/trailing/pallas_call | solution.py:341
  176.3 9.3 %trailing.5.rest_4_ = f32[12,1,24,1,128,128]{5,4,3,2,1,0:T(8,128)} custom-call(s32[6]{0:T(128)S(1)} %copy-done.4, s32[8]{0:T(128)S(1)} %copy-done.5, s32[64]{0:T(128)S(1)} %reshape.32.order, s32[25]{0:T(128)S(1)} %convert_reduce_fusion.starts, bf16[1536,1024]{1,0:T(8,128)(2,1)S(1)} %get-tuple-element.38.pair_ref, ...), custom_call_target="tpu_custom_call", output_to_operand_aliasing={{}: (10, {})} | custom-call | flops 9663676416 | bytes 9437184 | tf_op jit(solution)/shard_map/trailing/pallas_call | solution.py:341
  185.7 0.5 collective-permute-start.12
  186.2 1.7 collective-permute-start.14
  187.9 8.7 %trailing.6.rest_3_ = f32[12,1,24,1,128,128]{5,4,3,2,1,0:T(8,128)} custom-call(s32[6]{0:T(128)S(1)} %copy-done.7, s32[8]{0:T(128)S(1)} %copy-done.8, s32[64]{0:T(128)S(1)} %reshape.32.order, s32[25]{0:T(128)S(1)} %convert_reduce_fusion.starts, bf16[1536,1024]{1,0:T(8,128)(2,1)S(1)} %get-tuple-element.38.pair_ref, ...), custom_call_target="tpu_custom_call", output_to_operand_aliasing={{}: (10, {})} | custom-call | flops 9663676416 | bytes 9437184 | tf_op jit(solution)/shard_map/trailing/pallas_call | solution.py:341
  196.6 0.2 collective-permute-done.14
  196.8 0.1 pad_maximum_fusion.1.rest_0_
  196.9 6.1 %trailing.7 = f32[12,1,24,1,128,128]{5,4,3,2,1,0:T(8,128)} custom-call(s32[3]{0:T(128)S(1)} %copy-done.6, s32[4]{0:T(128)S(1)} %copy-done.3, s32[64]{0:T(128)S(1)} %reshape.32.order, s32[25]{0:T(128)S(1)} %convert_reduce_fusion.starts, bf16[1536,1024]{1,0:T(8,128)(2,1)S(1)} %get-tuple-element.38.pair_ref, ...), custom_call_target="tpu_custom_call", output_to_operand_aliasing={{}: (9, {})} | custom-call | flops 4831838208 | bytes 4718592 | tf_op jit(solution)/shard_map/trailing/pallas_call | solution.py:341
  (36 shorter events, 0.2 us)
Async XLA Ops:
  0.0 154.2 %copy-start.1 = (f32[2,256,256]{2,1,0:T(8,128)S(1)}, f32[2,256,256]{2,1,0:T(8,128)}, u32[]{:S(2)}) copy-start(f32[2,256,256]{2,1,0:T(8,128)} %diag_ref.1) | copy-start | bytes 1572868
  3.2 58.8 %all-to-all-start = ((f32[32,136,128]{2,1,0:T(8,128)}), f32[32,136,128]{2,1,0:T(8,128)S(1)}, u32[]{:S(2)}, u32[]{:S(2)}) async-start(f32[32,136,128]{2,1,0:T(8,128)} %pack.1), calls=%async_computation | async-start | bytes 4456448 | tf_op jit(solution)/shard_map/all_to_all | solution.py:377
  62.7 6.4 %copy-start = (f32[12,1,24,1,128,128]{5,4,3,2,1,0:T(8,128)S(1)}, f32[12,1,24,1,128,128]{5,4,3,2,1,0:T(8,128)}, u32[]{:S(2)}) copy-start(f32[12,1,24,1,128,128]{5,4,3,2,1,0:T(8,128)} %rest_1_.1) | copy-start | bytes 56623108
  72.9 22.7 %all-to-all-start.1 = ((f32[32,4,128]{2,1,0:T(4,128)}), f32[32,4,128]{2,1,0:T(4,128)}, u32[]{:S(2)}, u32[]{:S(2)}) async-start(f32[32,4,128]{2,1,0:T(4,128)} %bitcast.29), calls=%async_computation.1 | async-start | bytes 131072 | tf_op jit(solution)/shard_map/all_to_all | solution.py:397
  87.8 8.5 %collective-permute-start = (f32[3,128,128]{2,1,0:T(8,128)S(1)}, f32[3,128,128]{2,1,0:T(8,128)}, u32[]{:S(2)}, u32[]{:S(2)}) collective-permute-start(f32[3,128,128]{2,1,0:T(8,128)S(1)} %get-tuple-element.24), channel_id=1, source_target_pairs={{0,0},{1,4},{2,8},{3,12},{4,1},{5,5},{6,9},{7,13},{8,2},{9,6},{10,... | collective-permute-start | bytes 589832 | tf_op jit(solution)/shard_map/ppermute | solution.py:420
  89.2 11.4 %collective-permute-start.1 = (f32[3,128,128]{2,1,0:T(8,128)S(1)}, f32[3,128,128]{2,1,0:T(8,128)}, u32[]{:S(2)}, u32[]{:S(2)}) collective-permute-start(f32[3,128,128]{2,1,0:T(8,128)S(1)} %get-tuple-element.25), channel_id=1, source_target_pairs={{0,4},{1,8},{2,12},{3,0},{4,5},{5,9},{6,13},{7,1},{8,6},{9,10},{10... | collective-permute-start | bytes 589832 | tf_op jit(solution)/shard_map/ppermute | solution.py:420
  91.6 9.6 %collective-permute-start.2 = (f32[3,128,128]{2,1,0:T(8,128)S(1)}, f32[3,128,128]{2,1,0:T(8,128)}, u32[]{:S(2)}, u32[]{:S(2)}) collective-permute-start(f32[3,128,128]{2,1,0:T(8,128)S(1)} %get-tuple-element.26), channel_id=1, source_target_pairs={{0,8},{1,12},{2,0},{3,4},{4,9},{5,13},{6,1},{7,5},{8,10},{9,14},{1... | collective-permute-start | bytes 589832 | tf_op jit(solution)/shard_map/ppermute | solution.py:420
  95.1 6.8 %collective-permute-start.3 = (f32[3,128,128]{2,1,0:T(8,128)S(1)}, f32[3,128,128]{2,1,0:T(8,128)}, u32[]{:S(2)}, u32[]{:S(2)}) collective-permute-start(f32[3,128,128]{2,1,0:T(8,128)S(1)} %get-tuple-element.27), channel_id=1, source_target_pairs={{0,12},{1,0},{2,4},{3,8},{4,13},{5,1},{6,5},{7,9},{8,14},{9,2},{10... | collective-permute-start | bytes 589832 | tf_op jit(solution)/shard_map/ppermute | solution.py:420
  102.6 21.4 %collective-permute-start.9 = (f32[12,128,128]{2,1,0:T(8,128)}, f32[12,128,128]{2,1,0:T(8,128)}, u32[]{:S(2)}, u32[]{:S(2)}) collective-permute-start(f32[12,128,128]{2,1,0:T(8,128)} %get-tuple-element.33.t0), channel_id=1, source_target_pairs={{0,2},{1,3},{2,0},{3,1},{4,6},{5,7},{6,4},{7,5},{8,10},{9,11},{10,... | collective-permute-start | bytes 2359304 | tf_op jit(solution)/shard_map/ppermute | solution.py:408
  106.6 19.4 %collective-permute-start.4 = (f32[4,3,128,128]{3,2,1,0:T(8,128)S(1)}, f32[4,3,128,128]{3,2,1,0:T(8,128)}, u32[]{:S(2)}, u32[]{:S(2)}) collective-permute-start(f32[4,3,128,128]{3,2,1,0:T(8,128)S(1)} %pad_maximum_fusion.rest_0_), channel_id=1, source_target_pairs={{0,8},{8,16},{16,24},{24,28},{28,20},{20,12},{12,4},{4,0},{1,9},{9... | collective-permute-start | bytes 2359304 | tf_op jit(solution)/shard_map/ppermute | solution.py:431
  106.7 20.7 %collective-permute-start.6 = (f32[4,3,128,128]{3,2,1,0:T(8,128)S(1)}, f32[4,3,128,128]{3,2,1,0:T(8,128)}, u32[]{:S(2)}, u32[]{:S(2)}) collective-permute-start(f32[4,3,128,128]{3,2,1,0:T(8,128)S(1)} %pad_maximum_fusion.rest_0_), channel_id=1, source_target_pairs={{8,0},{16,8},{24,16},{28,24},{20,28},{12,20},{4,12},{0,4},{9,1},{1... | collective-permute-start | bytes 2359304 | tf_op jit(solution)/shard_map/ppermute | solution.py:432
  113.8 40.3 %collective-permute-start.8 = (f32[12,128,128]{2,1,0:T(8,128)}, f32[12,128,128]{2,1,0:T(8,128)}, u32[]{:S(2)}, u32[]{:S(2)}) collective-permute-start(f32[12,128,128]{2,1,0:T(8,128)} %get-tuple-element.33.t0), channel_id=1, source_target_pairs={{0,1},{1,0},{2,3},{3,2},{4,5},{5,4},{6,7},{7,6},{8,9},{9,8},{10,11... | collective-permute-start | bytes 2359304 | tf_op jit(solution)/shard_map/ppermute | solution.py:407
  124.0 30.1 %collective-permute-start.10 = (f32[12,128,128]{2,1,0:T(8,128)}, f32[12,128,128]{2,1,0:T(8,128)}, u32[]{:S(2)}, u32[]{:S(2)}) collective-permute-start(f32[12,128,128]{2,1,0:T(8,128)} %collective-permute-done.9.t2), channel_id=1, source_target_pairs={{0,1},{1,0},{2,3},{3,2},{4,5},{5,4},{6,7},{7,6},{8,9},{9,8},{10,11... | collective-permute-start | bytes 2359304 | tf_op jit(solution)/shard_map/ppermute | solution.py:409
  126.0 34.9 %collective-permute-start.5 = (f32[4,3,128,128]{3,2,1,0:T(8,128)}, f32[4,3,128,128]{3,2,1,0:T(8,128)}, u32[]{:S(2)}, u32[]{:S(2)}) collective-permute-start(f32[4,3,128,128]{3,2,1,0:T(8,128)} %collective-permute-done.4.rest_1_), channel_id=1, source_target_pairs={{0,8},{8,16},{16,24},{24,28},{28,20},{20,12},{12,4},{4,0},{1,9},{9... | collective-permute-start | bytes 2359304 | tf_op jit(solution)/shard_map/ppermute | solution.py:431
  127.4 33.5 %collective-permute-start.7 = (f32[4,3,128,128]{3,2,1,0:T(8,128)}, f32[4,3,128,128]{3,2,1,0:T(8,128)}, u32[]{:S(2)}, u32[]{:S(2)}) collective-permute-start(f32[4,3,128,128]{3,2,1,0:T(8,128)} %collective-permute-done.6.rest_2_), channel_id=1, source_target_pairs={{8,0},{16,8},{24,16},{28,24},{20,28},{12,20},{4,12},{0,4},{9,1},{1... | collective-permute-start | bytes 2359304 | tf_op jit(solution)/shard_map/ppermute | solution.py:432
  128.7 24.4 %all-to-all-start.2 = ((f32[32,4,4,128]{3,2,1,0:T(4,128)}), f32[32,4,4,128]{3,2,1,0:T(4,128)}, u32[]{:S(2)}, u32[]{:S(2)}) async-start(f32[32,4,4,128]{3,2,1,0:T(4,128)} %broadcast_in_dim.42), calls=%async_computation.2 | async-start | bytes 524288 | tf_op jit(solution)/shard_map/all_to_all | solution.py:401
  133.7 0.5 copy-start.9
  160.9 15.4 %copy-start.4 = (s32[6]{0:T(128)S(1)}, s32[6]{0:T(128)}, u32[]{:S(2)}) copy-start(s32[6]{0:T(128)} %pad_add_fusion.4.columns) | copy-start | bytes 76
  160.9 15.4 %copy-start.5 = (s32[8]{0:T(128)S(1)}, s32[8]{0:T(128)}, u32[]{:S(2)}) copy-start(s32[8]{0:T(128)} %pad_add_fusion.5.places) | copy-start | bytes 100
  160.9 24.7 %collective-permute-start.11 = (f32[4,3,128,128]{3,2,1,0:T(8,128)}, f32[4,3,128,128]{3,2,1,0:T(8,128)S(1)}, u32[]{:S(2)}, u32[]{:S(2)}) collective-permute-start(f32[4,3,128,128]{3,2,1,0:T(8,128)} %collective-permute-done.5.rest_0_), channel_id=1, source_target_pairs={{0,8},{8,16},{16,24},{24,28},{28,20},{20,12},{12,4},{4,0},{1,9},{9... | collective-permute-start | bytes 2359304 | tf_op jit(solution)/shard_map/ppermute | solution.py:431
  161.3 24.8 %collective-permute-start.13 = (f32[4,3,128,128]{3,2,1,0:T(8,128)}, f32[4,3,128,128]{3,2,1,0:T(8,128)S(1)}, u32[]{:S(2)}, u32[]{:S(2)}) collective-permute-start(f32[4,3,128,128]{3,2,1,0:T(8,128)} %collective-permute-done.7.rest_1_), channel_id=1, source_target_pairs={{8,0},{16,8},{24,16},{28,24},{20,28},{12,20},{4,12},{0,4},{9,1},{1... | collective-permute-start | bytes 2359304 | tf_op jit(solution)/shard_map/ppermute | solution.py:432
  163.0 0.7 copy-start.2
  176.3 11.6 %copy-start.7 = (s32[6]{0:T(128)S(1)}, s32[6]{0:T(128)}, u32[]{:S(2)}) copy-start(s32[6]{0:T(128)} %pad_add_fusion.2.columns) | copy-start | bytes 76
  176.3 11.6 %copy-start.8 = (s32[8]{0:T(128)S(1)}, s32[8]{0:T(128)}, u32[]{:S(2)}) copy-start(s32[8]{0:T(128)} %pad_add_fusion.3.places) | copy-start | bytes 100
  185.7 10.9 %collective-permute-start.12 = (f32[2,3,128,128]{3,2,1,0:T(8,128)S(1)}, f32[2,3,128,128]{3,2,1,0:T(8,128)S(1)}, u32[]{:S(2)}, u32[]{:S(2)}) collective-permute-start(f32[2,3,128,128]{3,2,1,0:T(8,128)S(1)} %slice.31), channel_id=1, source_target_pairs={{0,8},{8,16},{16,24},{24,28},{28,20},{20,12},{12,4},{4,0},{1,9},{9... | collective-permute-start | bytes 1179656 | tf_op jit(solution)/shard_map/ppermute | solution.py:437
  186.2 10.7 %copy-start.3 = (s32[4]{0:T(128)S(1)}, s32[4]{0:T(128)}, u32[]{:S(2)}) copy-start(s32[4]{0:T(128)} %and_select_fusion.9.places) | copy-start | bytes 52
  186.2 10.7 %copy-start.6 = (s32[3]{0:T(128)S(1)}, s32[3]{0:T(128)}, u32[]{:S(2)}) copy-start(s32[3]{0:T(128)} %multiply_add_fusion.7.columns) | copy-start | bytes 40
  186.2 10.6 %collective-permute-start.14 = (f32[2,3,128,128]{3,2,1,0:T(8,128)S(1)}, f32[2,3,128,128]{3,2,1,0:T(8,128)S(1)}, u32[]{:S(2)}, u32[]{:S(2)}) collective-permute-start(f32[2,3,128,128]{3,2,1,0:T(8,128)S(1)} %slice.32), channel_id=1, source_target_pairs={{8,0},{16,8},{24,16},{28,24},{20,28},{12,20},{4,12},{0,4},{9,1},{1... | collective-permute-start | bytes 1179656 | tf_op jit(solution)/shard_map/ppermute | solution.py:437

commit v5 on v4

--- a/solution.py
+++ b/solution.py
@@ -2,6 +2,7 @@
 
 import jax
 import jax.numpy as jnp
+import numpy as np
 from jax import lax
 from jax.experimental import pallas as pl
 from jax.experimental.pallas import tpu as pltpu
@@ -11,7 +12,7 @@
 PANEL = 256
 WIDTH = 2 * PANEL
 NOTE = 8
-VMEM = 30 * 1024 * 1024
+VMEM = 46 * 1024 * 1024
 BOTH = ("row", "col")
 
 
@@ -52,8 +53,18 @@
     return pl.BlockSpec(array.shape, lambda *_: (0,) * rank)
 
 
-def pack_kernel(dest, slot, count, child_ref, out_ref, notes_ref, sems, notes_sem):
+def lead_slices(devices):
+    height = max(8, 4 * TILE // devices)
+    return 4 * TILE // height, height
+
+
+def pack_kernel(
+    owners, place, dest, slot, count, child_ref, front_ref, out_ref, notes_ref, lead_ref,
+    tile_ref, sems, notes_sem, lead_sem,
+):
     slots = child_ref.shape[0]
+    n_slices, height, _ = lead_ref.shape
+    each = n_slices // 4
 
     def copy(k):
         return pltpu.make_async_copy(
@@ -61,6 +72,7 @@
         )
 
     notes_ref[...] = jnp.full_like(notes_ref, -1.0)
+    lead_ref[...] = jnp.zeros_like(lead_ref)
     live = jnp.minimum(count[0], slots)
 
     @pl.loop(0, live)
@@ -70,36 +82,68 @@
 
     notes = pltpu.make_async_copy(notes_ref, out_ref.at[:, pl.ds(TILE, NOTE)], notes_sem)
     notes.start()
+
+    for i, owner in enumerate(owners):
+        span = pl.ds(i * each, each)
+
+        @pl.when(place[3] == owner)
+        def _():
+            own = pltpu.make_async_copy(front_ref.at[0, 0, 0, 0], tile_ref, lead_sem)
+            own.start()
+            own.wait()
+            lead_ref[span] = tile_ref[...].reshape(each, height, TILE)
+
+        @pl.loop(0, live)
+        def _(k):
+            @pl.when(jnp.logical_and(slot[k] == 0, dest[k] == owner))
+            def _():
+                lead_ref[span] = lead_ref[span] + child_ref[k].reshape(each, height, TILE)
+
+    lead = pltpu.make_async_copy(
+        lead_ref, out_ref.at[pl.ds(0, n_slices), pl.ds(TILE + NOTE, height)], lead_sem
+    )
+    lead.start()
     notes.wait()
+    lead.wait()
 
     @pl.loop(0, live)
     def _(k):
         copy(k).wait()
 
 
-def pack(child_tiles, dest, slot, count, devices):
+def pack(child_tiles, front, place, dest, slot, count, devices, owners):
     slots = child_tiles.shape[0]
+    n_slices, height = lead_slices(devices)
     hbm = pl.BlockSpec(memory_space=pltpu.HBM)
     return pl.pallas_call(
-        pack_kernel,
-        in_specs=[pl.BlockSpec(memory_space=pltpu.SMEM)] * 3
-        + [pl.BlockSpec(memory_space=pltpu.VMEM)],
+        functools.partial(pack_kernel, owners),
+        in_specs=[pl.BlockSpec(memory_space=pltpu.SMEM)] * 4
+        + [pl.BlockSpec(memory_space=pltpu.VMEM), hbm],
         out_specs=hbm,
         scratch_shapes=[
             pltpu.VMEM((devices, NOTE, TILE), jnp.float32),
+            pltpu.VMEM((n_slices, height, TILE), jnp.float32),
+            pltpu.VMEM((TILE, TILE), jnp.float32),
             pltpu.SemaphoreType.DMA((slots,)),
             pltpu.SemaphoreType.DMA,
+            pltpu.SemaphoreType.DMA,
         ],
-        out_shape=jax.ShapeDtypeStruct((devices, TILE + NOTE, TILE), jnp.float32),
+        out_shape=jax.ShapeDtypeStruct((devices, TILE + NOTE + height, TILE), jnp.float32),
+        compiler_params=pltpu.CompilerParams(vmem_limit_bytes=VMEM),
         name="pack",
-    )(dest, slot, count, child_tiles)
-
-
-def columns_kernel(place, slot_in, front_ref, incoming_ref, out_ref, *rest):
-    *parts, tile_ref, sem = rest
+    )(place, dest, slot, count, child_tiles, front)
+
+
+def columns_kernel(place, slot_in, front_ref, incoming_ref, out_ref, own_ref, *rest):
+    *parts, tile_ref, slices_ref, sem, slices_sem = rest
     cols = place[2]
+    height = own_ref.shape[1]
     strip = pltpu.make_async_copy(front_ref.at[:, 0, 0, 0], out_ref, sem)
     strip.start()
+    slices = pltpu.make_async_copy(
+        incoming_ref.at[:, pl.ds(TILE + NOTE, height)], slices_ref, slices_sem
+    )
+    slices.start()
     strip.wait()
 
     @pl.loop(0, incoming_ref.shape[0])
@@ -120,22 +164,29 @@
         for t in range(group):
             part_ref[t] = out_ref[lax.rem(place[1] + j, count) * group + t].T
 
+    slices.wait()
+    own_ref[...] = jnp.broadcast_to(jnp.sum(slices_ref[...], axis=0)[None], own_ref.shape)
+
 
 def assemble_columns(front, incoming, place, slot_in, parts):
-    rows = front.shape[0]
-    shapes = [(rows, TILE, TILE)] + [(rows // parts, TILE, TILE)] * parts
+    rows, devices = front.shape[0], incoming.shape[0]
+    _, height = lead_slices(devices)
+    shapes = [(rows, TILE, TILE), (devices, height, TILE)]
+    shapes += [(rows // parts, TILE, TILE)] * parts
     out_shape = [jax.ShapeDtypeStruct(shape, jnp.float32) for shape in shapes]
     return pl.pallas_call(
         columns_kernel,
         grid_spec=pltpu.PrefetchScalarGridSpec(
             num_scalar_prefetch=2,
             grid=(1,),
-            in_specs=[
-                pl.BlockSpec(memory_space=pltpu.HBM),
-                pl.BlockSpec(memory_space=pltpu.HBM),
+            in_specs=[pl.BlockSpec(memory_space=pltpu.HBM)] * 2,
+            out_specs=[whole_spec(a) for a in out_shape],
+            scratch_shapes=[
+                pltpu.VMEM((TILE, TILE), jnp.float32),
+                pltpu.VMEM((devices, height, TILE), jnp.float32),
+                pltpu.SemaphoreType.DMA,
+                pltpu.SemaphoreType.DMA,
             ],
-            out_specs=[whole_spec(a) for a in out_shape],
-            scratch_shapes=[pltpu.VMEM((TILE, TILE), jnp.float32), pltpu.SemaphoreType.DMA],
         ),
         out_shape=out_shape,
         compiler_params=pltpu.CompilerParams(vmem_limit_bytes=VMEM),
@@ -144,9 +195,11 @@
 
 
 def row_panels_kernel(
-    place, t0, t1, t2, t3, lead_ref, diag_ref, pair_ref, out_ref, across_ref, small_ref, tiles_ref
+    place, slot_in, t0, t1, t2, t3, lead_ref, diag_ref, pair_ref, out_ref, across_ref, order,
+    starts, small_ref, tiles_ref, cursor,
 ):
     step = pl.program_id(0)
+    cols = starts.shape[0] - 1
     my_row, my_col = place[0], place[1]
     group = t0.shape[0]
     height = group * TILE
@@ -164,6 +217,33 @@
         across_ref[1] = deep(lead)
         across_ref[2] = deep(diag_ref[1].T)
 
+        @pl.loop(0, cols + 1)
+        def _(b):
+            starts[b] = 0
+
+        @pl.loop(0, slot_in.shape[0])
+        def _(s):
+            @pl.when(slot_in[s] >= 0)
+            def _():
+                b = lax.rem(slot_in[s], cols)
+                starts[b + 1] = starts[b + 1] + 1
+
+        @pl.loop(0, cols)
+        def _(b):
+            cursor[b] = starts[b]
+            starts[b + 1] = starts[b + 1] + starts[b]
+
+        @pl.loop(0, slot_in.shape[0])
+        def _(s):
+            @pl.when(slot_in[s] >= 0)
+            def _():
+                b = lax.rem(slot_in[s], cols)
+                i = cursor[b]
+                order[2 * i] = s
+                order[2 * i + 1] = lax.div(slot_in[s], cols)
+                cursor[b] = i + 1
+
+
     for i, tile_ref in enumerate((t0, t1, t2, t3)):
         tiles_ref[jnp.bitwise_xor(my_col, i)] = tile_ref[...]
     columns = [tiles_ref[c].reshape(height, TILE) for c in range(4)]
@@ -175,8 +255,10 @@
         return jnp.where(above, 0.0, value) if panels_above else value
 
     one, two = two_panels(columns, small_ref, mask)
-    pair_ref[:, :PANEL], pair_ref[:, WIDTH : WIDTH + PANEL] = halves(mask(1, one))
-    pair_ref[:, PANEL:WIDTH], pair_ref[:, WIDTH + PANEL :] = halves(mask(2, two))
+    for i, panel in enumerate((mask(1, one), mask(2, two))):
+        high, low = halves(panel)
+        for k, half in enumerate((high, low, high)):
+            pair_ref[:, k * WIDTH + i * PANEL : k * WIDTH + (i + 1) * PANEL] = half
     pieces = (one[:, :TILE], one[:, TILE:], two[:, :TILE], two[:, TILE:])
     for c in range(4):
 
@@ -185,54 +267,65 @@
             out_ref[:, 0, 0, 0] = pieces[c].reshape(group, TILE, TILE)
 
 
-def row_panels(mine, others, lead, diag, place, front):
+def row_panels(mine, others, lead, diag, place, slot_in, front):
     rows = front.shape[0]
+    cols = front.shape[2]
     group = rows // 3
     height = group * TILE
     out_shape = [
-        jax.ShapeDtypeStruct((rows * TILE, 2 * WIDTH), jnp.bfloat16),
+        jax.ShapeDtypeStruct((rows * TILE, 3 * WIDTH), jnp.bfloat16),
         jax.ShapeDtypeStruct(front.shape, jnp.float32),
         jax.ShapeDtypeStruct((3, PANEL, 3 * PANEL), jnp.bfloat16),
+        jax.ShapeDtypeStruct((2 * slot_in.shape[0],), jnp.int32),
+        jax.ShapeDtypeStruct((cols + 1,), jnp.int32),
     ]
     strip = pl.BlockSpec((group, TILE, TILE), lambda i, *_: (i, 0, 0))
     return pl.pallas_call(
         row_panels_kernel,
         grid_spec=pltpu.PrefetchScalarGridSpec(
-            num_scalar_prefetch=1,
+            num_scalar_prefetch=2,
             grid=(3,),
             in_specs=[strip] * 4 + [whole_spec(lead), whole_spec(diag)],
             out_specs=[
-                pl.BlockSpec((height, 2 * WIDTH), lambda i, *_: (i, 0)),
+                pl.BlockSpec((height, 3 * WIDTH), lambda i, *_: (i, 0)),
                 pl.BlockSpec((group, 1, 1, 1, TILE, TILE), lambda i, *_: (i, 0, 0, 0, 0, 0)),
                 whole_spec(out_shape[2]),
+                pl.BlockSpec(memory_space=pltpu.SMEM),
+                pl.BlockSpec(memory_space=pltpu.SMEM),
             ],
             scratch_shapes=[
                 pltpu.VMEM((3, 3 * PANEL, PANEL), jnp.bfloat16),
                 pltpu.VMEM((4, group, TILE, TILE), jnp.float32),
+                pltpu.SMEM((cols,), jnp.int32),
             ],
         ),
         out_shape=out_shape,
         compiler_params=pltpu.CompilerParams(vmem_limit_bytes=VMEM),
         name="row_panels",
-    )(place, mine, *others, lead, diag)
-
-
-def trailing_kernel(n_pieces, columns, places, order, starts, pair_ref, small_ref, *rest):
+    )(place, slot_in, mine, *others, lead, diag)
+
+
+def trailing_kernel(
+    first, n_pieces, place, columns_table, places_table, order, starts, pair_ref, small_ref, *rest
+):
     piece_refs = rest[:n_pieces]
     front_ref, incoming_ref, _, out_ref, right_ref, taken, given, child_ref = rest[n_pieces:-3]
     take_sems, give_sems, child_sems = rest[-3:]
     group = piece_refs[0].shape[1]
     count = n_pieces * group
     steps = (count + 1) // 2
-    rows = front_ref.shape[0]
+    rows, cols = front_ref.shape[0], front_ref.shape[2]
+    columns_base = place[0] * cols + first * group
+    places_base = (place[0] * (cols // group) + first) * 4
 
     def columns_of(step):
         for j in range(2):
             index = jnp.minimum(2 * step, count - 2) + j
-            wanted = columns[index] > 0
+            b = columns_table[columns_base + index]
+            wanted = b > 0
             if count % 2 and j == 0:
                 wanted = jnp.logical_and(wanted, step < steps - 1)
-            yield j, columns[index], wanted
+            yield j, b, wanted
 
     def each_take(step, act):
         slot = lax.rem(step, 2)
@@ -279,7 +372,7 @@
     tile_columns = [
         jnp.concatenate(
             [
-                piece[places[4 * p + c], t]
+                piece[places_table[places_base + 4 * p + c], t]
                 for p, piece in enumerate(piece_refs)
                 for t in range(group)
             ],
@@ -303,14 +396,10 @@
 
         start = jnp.minimum(2 * step, count - 2)
         lanes = pl.ds(pl.multiple_of(start * TILE, TILE), 2 * TILE)
-        block = rows // 3
-        for m in range(3):
-            left = pair_ref[m * block * TILE : (m + 1) * block * TILE]
-            update = dot(jnp.concatenate([left, left[:, :WIDTH]], axis=1), right_ref[:, lanes])
-            span = slice(m * block, (m + 1) * block)
-            for j in range(2):
-                part = update[:, j * TILE : (j + 1) * TILE].reshape(block, TILE, TILE)
-                given[slot, j, span] = taken[slot, j, span] - part
+        update = dot(pair_ref[...], right_ref[:, lanes])
+        for j in range(2):
+            part = update[:, j * TILE : (j + 1) * TILE].reshape(rows, TILE, TILE)
+            given[slot, j] = taken[slot, j] - part
 
         def add(copy, j, s, a):
             copy.wait()
@@ -327,20 +416,20 @@
         each_give(step, lambda copy: copy.wait())
 
 
-def trailing(front, pieces, columns, places, panels, incoming, order, starts):
+def trailing(front, pieces, first, place, tables, panels, incoming):
     rows = front.shape[0]
-    pair, out, small = panels
+    pair, out, small, order, starts = panels
     group = pieces[0].shape[1]
     count = len(pieces) * group
-    scalars = [columns, places, order, starts]
+    scalars = [place, *tables, order, starts]
     held = [pair, small, *pieces]
     distant = [front, incoming, out]
     spec = lambda space, n: [pl.BlockSpec(memory_space=space)] * n
     height = rows * TILE
     devices = incoming.shape[0]
     return pl.pallas_call(
-        functools.partial(trailing_kernel, len(pieces)),
-        in_specs=spec(pltpu.SMEM, 4) + spec(pltpu.VMEM, len(held)) + spec(pltpu.HBM, 3),
+        functools.partial(trailing_kernel, first, len(pieces)),
+        in_specs=spec(pltpu.SMEM, 5) + spec(pltpu.VMEM, len(held)) + spec(pltpu.HBM, 3),
         out_specs=pl.BlockSpec(memory_space=pltpu.HBM),
         scratch_shapes=[
             pltpu.VMEM((3 * WIDTH, count * TILE), jnp.bfloat16),
@@ -352,7 +441,7 @@
             pltpu.SemaphoreType.DMA((devices,)),
         ],
         out_shape=jax.ShapeDtypeStruct(front.shape, jnp.float32),
-        input_output_aliases={len(held) + 6: 0},
+        input_output_aliases={len(held) + 7: 0},
         compiler_params=pltpu.CompilerParams(vmem_limit_bytes=VMEM),
         cost_estimate=pl.CostEstimate(
             flops=8 * count * 2 * height * TILE * WIDTH,
@@ -371,42 +460,30 @@
     rows_here, cols_here = (front.shape[0], front.shape[2])
     devices = n_row * n_col
     assert n_col == 4 and n_row % 4 == 0 and rows_here % 3 == 0
-    place = jnp.stack([my_row, my_col, jnp.int32(cols_here)])
-
-    outgoing = pack(child_tiles, tile_dest[:, 0], tile_slot, tile_count, devices)
+    owners = [r * n_col + c for r in (2, 3) for c in (0, 1)]
+    place = jnp.stack([my_row, my_col, jnp.int32(cols_here), my_row * n_col + my_col])
+
+    outgoing = pack(
+        child_tiles, front, place, tile_dest[:, 0], tile_slot, tile_count, devices, owners
+    )
     incoming = lax.all_to_all(outgoing, BOTH, split_axis=0, concat_axis=0, tiled=True)
     slot_in = lax.optimization_barrier(incoming[:, TILE, 0].astype(jnp.int32))
 
-    row_of = jnp.where(slot_in >= 0, slot_in // cols_here, 0)
-    col_of = jnp.where(slot_in >= 0, slot_in % cols_here, -1)
-    sources = jnp.arange(devices, dtype=jnp.int32)
-    key = jnp.where(slot_in >= 0, col_of, cols_here) * devices + sources
-    rank = jnp.sum((key[None, :] < key[:, None]).astype(jnp.int32), axis=1)
-    at = rank[None, :] == sources[:, None]
-    order = jnp.stack(
-        [jnp.sum(jnp.where(at, v[None, :], 0), axis=1) for v in (sources, row_of)], axis=1
-    ).reshape(-1)
-    edges = jnp.arange(cols_here + 1, dtype=jnp.int32) * devices
-    starts = jnp.sum((key[None, :] < edges[:, None]).astype(jnp.int32), axis=1)
-
     ring = rows_here % n_col == 0
-    mine, *parts = assemble_columns(front, incoming, place, slot_in, n_col if ring else 1)
-
-    owners = [r * n_col + c for r in (2, 3) for c in (0, 1)]
-    slices = mine[0].reshape(devices, TILE // devices, TILE)
-    slices = lax.all_to_all(slices, BOTH, split_axis=0, concat_axis=0, tiled=True)
-    own = jnp.stack([slices[owner] for owner in owners])
+    mine, own, *parts = assemble_columns(front, incoming, place, slot_in, n_col if ring else 1)
 
     def hand_on(own):
         lead = lax.all_to_all(own, BOTH, split_axis=0, concat_axis=0, tiled=True)
-        return lead.transpose(1, 0, 2, 3).reshape(2, 2, TILE, TILE)
-
-    own = jnp.broadcast_to(own[None], (devices,) + own.shape)
+        return lead[: lead_slices(devices)[0]].reshape(2, 2, TILE, TILE)
 
     def exchange(mine):
         near = lax.ppermute(mine, "col", [(c, c ^ 1) for c in range(n_col)])
         far = lax.ppermute(mine, "col", [(c, c ^ 2) for c in range(n_col)])
         return [near, far, lax.ppermute(far, "col", [(c, c ^ 1) for c in range(n_col)])]
+
+    def own_panels(mine, own):
+        tiles = exchange(mine)
+        return row_panels(mine, tiles, hand_on(own), diag_inverses, place, slot_in, front)
 
     sets = n_row // n_col
     if ring:
@@ -421,11 +498,10 @@
         arrived, own, mine = lax.optimization_barrier((arrived, own, mine))
         piece = jnp.stack(arrived)
         circle = list(range(0, n_row, 2)) + list(range(n_row - 1, 0, -2))
-        spot = jnp.asarray([circle.index(r) for r in range(n_row)], jnp.int32)[my_row]
         up = [(circle[i], circle[(i + 1) % n_row]) for i in range(n_row)]
         down = [(b, a) for a, b in up]
         rounds = [[(piece, 0)]]
-        panels = row_panels(mine, exchange(mine), hand_on(own), diag_inverses, place, front)
+        panels = own_panels(mine, own)
         ahead = behind = piece
         for step in range(1, n_row // 2):
             ahead = lax.ppermute(ahead, "row", up)
@@ -439,12 +515,11 @@
         rounds.append([(last, n_row // 2)])
         rounds = [rounds[0] + rounds[1]] + rounds[2:]
 
-        def described(shift):
-            origin = jnp.asarray(circle, jnp.int32)[(spot + shift + n_row) % n_row]
+        def described(row, shift):
+            origin = circle[(circle.index(row) + shift) % n_row]
             part, group = origin % n_col, rows_here // n_col
-            row = part * group + jnp.arange(group, dtype=jnp.int32)
-            places = (part - jnp.arange(n_col, dtype=jnp.int32) + n_col) % n_col
-            return row * sets + origin // n_col, places
+            columns = [(part * group + t) * sets + origin // n_col for t in range(group)]
+            return columns, [(part - c) % n_col for c in range(n_col)]
 
     else:
         pairs = [
@@ -454,19 +529,25 @@
         ]
         moved = lax.all_gather(lax.ppermute(parts[0], BOTH, pairs), "row", axis=0, tiled=False)
         rounds = [[(moved[h * n_col : (h + 1) * n_col], h)] for h in range(sets)]
-        panels = row_panels(mine, exchange(mine), hand_on(own), diag_inverses, place, front)
-
-        def described(h):
-            row = jnp.arange(rows_here, dtype=jnp.int32)
-            return row * sets + h, jnp.arange(n_col, dtype=jnp.int32)
-
+        panels = own_panels(mine, own)
+
+        def described(row, h):
+            return [a * sets + h for a in range(rows_here)], list(range(n_col))
+
+    shifts = [shift for entries in rounds for _, shift in entries]
+    tables = [
+        jnp.asarray(
+            np.concatenate([described(row, shift)[k] for row in range(n_row) for shift in shifts]),
+            jnp.int32,
+        )
+        for k in range(2)
+    ]
+    first = 0
     for entries in rounds:
-        described_here = [described(shift) for _, shift in entries]
-        columns = jnp.concatenate([d[0] for d in described_here])
-        places = jnp.concatenate([d[1] for d in described_here])
-        pieces = [p for p, _ in entries]
-        out = trailing(front, pieces, columns, places, panels, incoming, order, starts)
-        panels = [panels[0], out, panels[2]]
+        pieces = [piece for piece, _ in entries]
+        out = trailing(front, pieces, first, place, tables, panels, incoming)
+        panels = [panels[0], out, *panels[2:]]
+        first += len(pieces)
     return panels[1]
 
 

time: 205 us -> 192 us (0.937)
  blocking collectives: 0 us -> 90 us
  waiting for transfers between devices: 65.4 us -> 22.3 us
  between operations: 27.5 us -> 0.96 us
  starting transfers between devices: 34.5 us -> 19.1 us
  local copies, waits for them, and re-layouts: 15.9 us -> 2.61 us
  other arithmetic: 11.6 us -> 0.85 us
  Pallas kernels: 48.3 us -> 55.7 us
    all_to_all x0 -> x2, blocking collectives: none -> 90 us  [the longest x1 65.4 us: body(): lax.all_to_all(outgoing, BOTH, split_axis=0, concat_axis=0, tiled=True)]
    all_to_all x3 -> x0, waiting for transfers between devices: 46.8 us -> none  [the longest x1 30.4 us: body(): lax.all_to_all(outgoing, BOTH, split_axis=0, concat_axis=0, tiled=True)]
    all_to_all x3 -> x0, starting transfers between devices: 16.3 us -> none  [the longest x1 7.22 us: body(): lax.all_to_all(outgoing, BOTH, split_axis=0, concat_axis=0, tiled=True)]
    pallas_call x5, Pallas kernels: 39.1 us -> 45.6 us  [the longest x4 42.5 us: trailing(): pl.pallas_call(functools.partial(trailing_kernel, first, len(pieces)), in...]
    ppermute x1, waiting for transfers between devices: 10.1 us -> 16 us  [exchange(): far = lax.ppermute(mine, 'col', [(c, c ^ 2) for c in range(n_col)])]
    concatenate x6 -> x0, other arithmetic: 5.16 us -> none  [the longest x3 2.61 us: body(): columns = jnp.concatenate([d[0] for d in described_here])]
    unnamed x20 -> x12, local copies, waits for them, and re-layouts: 7.43 us -> 2.56 us
    dynamic_slice x2 -> x0, local copies, waits for them, and re-layouts: 2.98 us -> none  [the longest x1 1.66 us: described(): origin = jnp.asarray(circle, jnp.int32)[(spot + shift + n_row) % n_row]]
  transfers between devices with their start and end apart: 18 -> 15, of which waited for: 9 -> 5; matrix products, arithmetic and copies ran while one was open for 8% -> 0% of each run, Pallas kernels for 18% -> 22%
where the time goes in v5:
time: 192 us; the launch traced here: 191 us
  blocking collectives  90 us (47%)
  Pallas kernels  55.7 us (29%)
  waiting for transfers between devices  22.3 us (12%)
  starting transfers between devices  19.1 us (10%)
  local copies, waits for them, and re-layouts  2.61 us (1%)
    all_to_all x1, blocking collectives, body(): lax.all_to_all(outgoing, BOTH, split_axis=0, concat_axis=0, tiled=True)  65.4 us
    pallas_call x4, Pallas kernels, trailing(): pl.pallas_call(functools.partial(trailing_kernel, first, len(pieces)), in...  42.5 us
    all_to_all x1, blocking collectives, hand_on(): lead = lax.all_to_all(own, BOTH, split_axis=0, concat_axis=0, tiled=True)  24.6 us
    ppermute x1, waiting for transfers between devices, exchange(): far = lax.ppermute(mine, 'col', [(c, c ^ 2) for c in range(n_col)])  16 us
    pallas_call x1, Pallas kernels, row_panels(): pl.pallas_call(row_panels_kernel, grid_spec=pltpu.PrefetchScalarGridSpec(...  8.03 us
    ppermute x4, starting transfers between devices, body(): arrived.append(lax.ppermute(part, BOTH, pairs))  7.38 us
    ppermute x4, waiting for transfers between devices, body(): arrived.append(lax.ppermute(part, BOTH, pairs))  5.79 us
    ppermute x3, starting transfers between devices, body(): behind = lax.ppermute(behind, 'row', down)  5.12 us
  transfers between devices with their start and end apart: 15, of which 5 were waited for; matrix products, arithmetic and copies ran while one was open for 0% of the time, Pallas kernels for 22%

profile of v5, /device:TPU:0, one launch (start us, length us, event | category | flops | bytes accessed | tf_op | source)
XLA Modules:
  0.0 191.5 jit_solution(9658729932531304539)
XLA Ops:
  0.7 0.1 pad_add_fusion.place
  0.7 0.0 copy-start
  0.7 1.2 copy-done
  2.0 0.0 copy-start.4
  2.0 0.7 copy-done.4
  2.6 0.0 copy-start.5
  2.6 0.7 copy-done.5
  3.3 3.2 %pack.1 = f32[32,152,128]{2,1,0:T(8,128)S(1)} custom-call(s32[4]{0:T(128)S(1)} %pad_add_fusion.place, s32[16]{0:T(128)S(1)} %bitcast.10, s32[16]{0:T(128)S(1)} %copy-done.5, s32[1]{0:T(128)S(6)} %copy.17.count, f32[16,128,128]{2,1,0:T(8,128)S(1)} %copy-done, f32[12,1,24,1,128,128]{5,4,3,2,1,0:T(8,128)} %rest_1_.1), custom_call_target="tpu_custom_call" | custom-call | tf_op jit(solution)/shard_map/pack/pallas_call | solution.py:118
  6.5 0.0 copy-start.1
  6.5 0.0 copy-start.2
  6.5 0.0 copy-start.3
  6.5 65.4 %all_to_all.10.incoming_ref.rest_4_.rest_3_.rest_2_ = f32[32,152,128]{2,1,0:T(8,128)S(1)} all-to-all(f32[32,152,128]{2,1,0:T(8,128)S(1)} %pack.1), channel_id=1, replica_groups=mesh['row'=8,'col'=4] {'row','col'}, dimensions={0} | all-to-all | bytes 4980736 | tf_op jit(solution)/shard_map/all_to_all | solution.py:469
  71.9 0.7 fusion.slot_in
  72.5 2.0 %panel_columns.1 = (f32[12,128,128]{2,1,0:T(8,128)S(1)}, f32[32,16,128]{2,1,0:T(8,128)S(1)}, f32[3,128,128]{2,1,0:T(8,128)S(1)}, f32[3,128,128]{2,1,0:T(8,128)S(...) custom-call(s32[4]{0:T(128)S(1)} %pad_add_fusion.place, s32[32]{0:T(128)S(1)} %fusion.slot_in, ...), custom_call_target="tpu_custom_call" | custom-call | tf_op jit(solution)/shard_map/panel_columns/pallas_call | solution.py:177
  74.6 0.7 collective-permute-start
  75.2 2.4 %collective-permute-start.1 = (f32[3,128,128]{2,1,0:T(8,128)S(1)}, f32[3,128,128]{2,1,0:T(8,128)S(1)}, u32[]{:S(2)}, u32[]{:S(2)}) collective-permute-start(f32[3,128,128]{2,1,0:T(8,128)S(1)} %get-tuple-element.30), channel_id=1, source_target_pairs={{0,4},{1,8},{2,12},{3,0},{4,5},{5,9},{6,13},{7,1},{8,6},{9,10},{10... | collective-permute-start | bytes 589832 | tf_op jit(solution)/shard_map/ppermute | solution.py:497
  77.6 3.3 %collective-permute-start.2 = (f32[3,128,128]{2,1,0:T(8,128)S(1)}, f32[3,128,128]{2,1,0:T(8,128)S(1)}, u32[]{:S(2)}, u32[]{:S(2)}) collective-permute-start(f32[3,128,128]{2,1,0:T(8,128)S(1)} %get-tuple-element.31), channel_id=1, source_target_pairs={{0,8},{1,12},{2,0},{3,4},{4,9},{5,13},{6,1},{7,5},{8,10},{9,14},{1... | collective-permute-start | bytes 589832 | tf_op jit(solution)/shard_map/ppermute | solution.py:497
  80.9 1.1 collective-permute-start.3
  82.0 0.0 collective-permute-done
  82.0 4.9 %collective-permute-done.1 = f32[3,128,128]{2,1,0:T(8,128)S(1)} collective-permute-done((f32[3,128,128]{2,1,0:T(8,128)S(1)}, f32[3,128,128]{2,1,0:T(8,128)S(1)}, u32[]{:S(2)}, u32[]{:S(2)}) %collective-permute-start.1) | collective-permute-done | bytes 196640 | tf_op jit(solution)/shard_map/ppermute | solution.py:497
  86.9 0.6 collective-permute-done.2
  87.4 0.3 collective-permute-done.3
  87.7 3.0 %collective-permute-start.9 = (f32[12,128,128]{2,1,0:T(8,128)S(1)}, f32[12,128,128]{2,1,0:T(8,128)S(1)}, u32[]{:S(2)}, u32[]{:S(2)}) collective-permute-start(f32[12,128,128]{2,1,0:T(8,128)S(1)} %get-tuple-element.39.t0), channel_id=1, source_target_pairs={{0,2},{1,3},{2,0},{3,1},{4,6},{5,7},{6,4},{7,5},{8,10},{9,11},{10,... | collective-permute-start | bytes 2359304 | tf_op jit(solution)/shard_map/ppermute | solution.py:481
  90.8 0.1 pad_maximum_fusion.rest_0_
  90.8 1.5 collective-permute-start.6
  92.3 0.6 collective-permute-start.4
  92.9 0.0 collective-permute-start.8
  92.9 16.0 %collective-permute-done.9.t2 = f32[12,128,128]{2,1,0:T(8,128)S(1)} collective-permute-done((f32[12,128,128]{2,1,0:T(8,128)S(1)}, f32[12,128,128]{2,1,0:T(8,128)S(1)}, u32[]{:S(2)}, u32[]{:S(2)}) %collective-permute-start.9) | collective-permute-done | bytes 786464 | tf_op jit(solution)/shard_map/ppermute | solution.py:481
  108.9 0.0 collective-permute-start.10
  108.9 0.5 collective-permute-done.6.rest_2_
  109.4 2.4 %collective-permute-start.7 = (f32[4,3,128,128]{3,2,1,0:T(8,128)S(1)}, f32[4,3,128,128]{3,2,1,0:T(8,128)S(1)}, u32[]{:S(2)}, u32[]{:S(2)}) collective-permute-start(f32[4,3,128,128]{3,2,1,0:T(8,128)S(1)} %collective-permute-done.6.rest_2_), channel_id=1, source_target_pairs={{8,0},{16,8},{24,16},{28,24},{20,28},{12,20},{4,12},{0,4},{9,1},{1... | collective-permute-start | bytes 2359304 | tf_op jit(solution)/shard_map/ppermute | solution.py:508
  111.8 0.0 collective-permute-done.4.rest_1_
  111.8 0.0 collective-permute-start.5
  111.8 24.6 %all_to_all.11 = f32[32,16,128]{2,1,0:T(8,128)S(1)} all-to-all(f32[32,16,128]{2,1,0:T(8,128)S(1)} %get-tuple-element.40), channel_id=1, replica_groups=mesh['row'=8,'col'=4] {'row','col'}, dimensions={0} | all-to-all | bytes 524288 | tf_op jit(solution)/shard_map/all_to_all | solution.py:476
  136.4 0.0 collective-permute-done.8.t1
  136.4 0.0 collective-permute-done.10.t3
  136.4 0.0 copy-done.1
  136.4 8.0 %row_panels.1 = (bf16[1536,1536]{1,0:T(8,128)(2,1)}, f32[12,1,24,1,128,128]{5,4,3,2,1,0:T(8,128)}, bf16[3,256,768]{2,1,0:T(8,128)(2,1)S(1)}, s32[64]{0:T(128)S(1)}, s32[25]{0:T(128)S(1)}) custom-call(s32[4]{0:T(128)S(1)} %pad_add_fusion.place, s32[32]{0:T(128)S(1)} %fusion.slot_in, f32[12,128,128]{2,1,0:T(8,128)S(1)} %get-tuple-element.39.t0, ...), custom_call_target="tpu_custom_call" | custom-call | tf_op jit(solution)/shard_map/row_panels/pallas_call | solution.py:283
  144.4 0.0 collective-permute-done.7.rest_1_
  144.4 0.0 collective-permute-done.5.rest_0_
  144.4 0.8 collective-permute-start.11
  145.2 1.3 collective-permute-start.13
  146.5 0.0 copy-done.2
  146.5 0.0 copy-done.3
  146.5 13.9 %trailing.4.rest_4_ = f32[12,1,24,1,128,128]{5,4,3,2,1,0:T(8,128)} custom-call(s32[4]{0:T(128)S(1)} %pad_add_fusion.place, s32[192]{0:T(256)S(1)} %copy-done.3, s32[256]{0:T(256)S(1)} %copy-done.2, s32[64]{0:T(128)S(1)} %get-tuple-element.46.order, s32[25]{0:T(128)S(1)} %get-tuple-element.47.starts, ...), custom_call_target="tpu_custom_call", output_to_operand_aliasing={{}: (12, {})} | custom-call | flops 14495514624 | bytes 14155776 | tf_op jit(solution)/shard_map/trailing/pallas_call | solution.py:430
  160.5 10.1 %trailing.5.rest_4_ = f32[12,1,24,1,128,128]{5,4,3,2,1,0:T(8,128)} custom-call(s32[4]{0:T(128)S(1)} %pad_add_fusion.place, s32[192]{0:T(256)S(1)} %copy-done.3, s32[256]{0:T(256)S(1)} %copy-done.2, s32[64]{0:T(128)S(1)} %get-tuple-element.46.order, s32[25]{0:T(128)S(1)} %get-tuple-element.47.starts, ...), custom_call_target="tpu_custom_call", output_to_operand_aliasing={{}: (11, {})} | custom-call | flops 9663676416 | bytes 9437184 | tf_op jit(solution)/shard_map/trailing/pallas_call | solution.py:430
  170.6 0.0 collective-permute-done.11.rest_0_
  170.6 0.8 collective-permute-start.12
  171.5 0.0 collective-permute-done.13.rest_1_
  171.5 1.3 collective-permute-start.14
  172.8 10.5 %trailing.6.rest_3_ = f32[12,1,24,1,128,128]{5,4,3,2,1,0:T(8,128)} custom-call(s32[4]{0:T(128)S(1)} %pad_add_fusion.place, s32[192]{0:T(256)S(1)} %copy-done.3, s32[256]{0:T(256)S(1)} %copy-done.2, s32[64]{0:T(128)S(1)} %get-tuple-element.46.order, s32[25]{0:T(128)S(1)} %get-tuple-element.47.starts, ...), custom_call_target="tpu_custom_call", output_to_operand_aliasing={{}: (11, {})} | custom-call | flops 9663676416 | bytes 9437184 | tf_op jit(solution)/shard_map/trailing/pallas_call | solution.py:430
  183.3 0.0 collective-permute-done.12
  183.4 0.0 collective-permute-done.14
  183.4 0.1 pad_maximum_fusion.1.rest_0_
  183.4 7.9 %trailing.7 = f32[12,1,24,1,128,128]{5,4,3,2,1,0:T(8,128)} custom-call(s32[4]{0:T(128)S(1)} %pad_add_fusion.place, s32[192]{0:T(256)S(1)} %copy-done.3, s32[256]{0:T(256)S(1)} %copy-done.2, s32[64]{0:T(128)S(1)} %get-tuple-element.46.order, s32[25]{0:T(128)S(1)} %get-tuple-element.47.starts, ...), custom_call_target="tpu_custom_call", output_to_operand_aliasing={{}: (10, {})} | custom-call | flops 4831838208 | bytes 4718592 | tf_op jit(solution)/shard_map/trailing/pallas_call | solution.py:430
  (2 shorter events, 0.1 us)
Async XLA Ops:
  0.7 1.2 copy-start
  2.0 0.7 copy-start.4
  2.6 0.7 copy-start.5
  6.5 129.9 %copy-start.1 = (f32[2,256,256]{2,1,0:T(8,128)S(1)}, f32[2,256,256]{2,1,0:T(8,128)}, u32[]{:S(2)}) copy-start(f32[2,256,256]{2,1,0:T(8,128)} %diag_ref.1) | copy-start | bytes 1572868
  6.5 140.1 %copy-start.2 = (s32[256]{0:T(256)S(1)}, s32[256]{0:T(256)}, u32[]{:S(2)}) copy-start(s32[256]{0:T(256)} %constant.18.clone.places_table) | copy-start | bytes 3076
  6.5 140.0 %copy-start.3 = (s32[192]{0:T(256)S(1)}, s32[192]{0:T(256)}, u32[]{:S(2)}) copy-start(s32[192]{0:T(256)} %constant.17.clone.columns_table) | copy-start | bytes 2308
  74.6 7.4 %collective-permute-start = (f32[3,128,128]{2,1,0:T(8,128)S(1)}, f32[3,128,128]{2,1,0:T(8,128)S(1)}, u32[]{:S(2)}, u32[]{:S(2)}) collective-permute-start(f32[3,128,128]{2,1,0:T(8,128)S(1)} %get-tuple-element.29), channel_id=1, source_target_pairs={{0,0},{1,4},{2,8},{3,12},{4,1},{5,5},{6,9},{7,13},{8,2},{9,6},{10,... | collective-permute-start | bytes 589832 | tf_op jit(solution)/shard_map/ppermute | solution.py:497
  75.2 11.6 %collective-permute-start.1 = (f32[3,128,128]{2,1,0:T(8,128)S(1)}, f32[3,128,128]{2,1,0:T(8,128)S(1)}, u32[]{:S(2)}, u32[]{:S(2)}) collective-permute-start(f32[3,128,128]{2,1,0:T(8,128)S(1)} %get-tuple-element.30), channel_id=1, source_target_pairs={{0,4},{1,8},{2,12},{3,0},{4,5},{5,9},{6,13},{7,1},{8,6},{9,10},{10... | collective-permute-start | bytes 589832 | tf_op jit(solution)/shard_map/ppermute | solution.py:497
  77.6 9.8 %collective-permute-start.2 = (f32[3,128,128]{2,1,0:T(8,128)S(1)}, f32[3,128,128]{2,1,0:T(8,128)S(1)}, u32[]{:S(2)}, u32[]{:S(2)}) collective-permute-start(f32[3,128,128]{2,1,0:T(8,128)S(1)} %get-tuple-element.31), channel_id=1, source_target_pairs={{0,8},{1,12},{2,0},{3,4},{4,9},{5,13},{6,1},{7,5},{8,10},{9,14},{1... | collective-permute-start | bytes 589832 | tf_op jit(solution)/shard_map/ppermute | solution.py:497
  80.9 6.9 %collective-permute-start.3 = (f32[3,128,128]{2,1,0:T(8,128)S(1)}, f32[3,128,128]{2,1,0:T(8,128)S(1)}, u32[]{:S(2)}, u32[]{:S(2)}) collective-permute-start(f32[3,128,128]{2,1,0:T(8,128)S(1)} %get-tuple-element.32), channel_id=1, source_target_pairs={{0,12},{1,0},{2,4},{3,8},{4,13},{5,1},{6,5},{7,9},{8,14},{9,2},{10... | collective-permute-start | bytes 589832 | tf_op jit(solution)/shard_map/ppermute | solution.py:497
  87.7 21.2 %collective-permute-start.9 = (f32[12,128,128]{2,1,0:T(8,128)S(1)}, f32[12,128,128]{2,1,0:T(8,128)S(1)}, u32[]{:S(2)}, u32[]{:S(2)}) collective-permute-start(f32[12,128,128]{2,1,0:T(8,128)S(1)} %get-tuple-element.39.t0), channel_id=1, source_target_pairs={{0,2},{1,3},{2,0},{3,1},{4,6},{5,7},{6,4},{7,5},{8,10},{9,11},{10,... | collective-permute-start | bytes 2359304 | tf_op jit(solution)/shard_map/ppermute | solution.py:481
  90.8 18.6 %collective-permute-start.6 = (f32[4,3,128,128]{3,2,1,0:T(8,128)S(1)}, f32[4,3,128,128]{3,2,1,0:T(8,128)S(1)}, u32[]{:S(2)}, u32[]{:S(2)}) collective-permute-start(f32[4,3,128,128]{3,2,1,0:T(8,128)S(1)} %pad_maximum_fusion.rest_0_), channel_id=1, source_target_pairs={{8,0},{16,8},{24,16},{28,24},{20,28},{12,20},{4,12},{0,4},{9,1},{1... | collective-permute-start | bytes 2359304 | tf_op jit(solution)/shard_map/ppermute | solution.py:508
  92.3 19.5 %collective-permute-start.4 = (f32[4,3,128,128]{3,2,1,0:T(8,128)S(1)}, f32[4,3,128,128]{3,2,1,0:T(8,128)S(1)}, u32[]{:S(2)}, u32[]{:S(2)}) collective-permute-start(f32[4,3,128,128]{3,2,1,0:T(8,128)S(1)} %pad_maximum_fusion.rest_0_), channel_id=1, source_target_pairs={{0,8},{8,16},{16,24},{24,28},{28,20},{20,12},{12,4},{4,0},{1,9},{9... | collective-permute-start | bytes 2359304 | tf_op jit(solution)/shard_map/ppermute | solution.py:507
  92.9 43.5 %collective-permute-start.8 = (f32[12,128,128]{2,1,0:T(8,128)S(1)}, f32[12,128,128]{2,1,0:T(8,128)S(1)}, u32[]{:S(2)}, u32[]{:S(2)}) collective-permute-start(f32[12,128,128]{2,1,0:T(8,128)S(1)} %get-tuple-element.39.t0), channel_id=1, source_target_pairs={{0,1},{1,0},{2,3},{3,2},{4,5},{5,4},{6,7},{7,6},{8,9},{9,8},{10,11... | collective-permute-start | bytes 2359304 | tf_op jit(solution)/shard_map/ppermute | solution.py:480
  108.9 27.5 %collective-permute-start.10 = (f32[12,128,128]{2,1,0:T(8,128)S(1)}, f32[12,128,128]{2,1,0:T(8,128)S(1)}, u32[]{:S(2)}, u32[]{:S(2)}) collective-permute-start(f32[12,128,128]{2,1,0:T(8,128)S(1)} %collective-permute-done.9.t2), channel_id=1, source_target_pairs={{0,1},{1,0},{2,3},{3,2},{4,5},{5,4},{6,7},{7,6},{8,9},{9,8},{10,11... | collective-permute-start | bytes 2359304 | tf_op jit(solution)/shard_map/ppermute | solution.py:482
  109.4 35.0 %collective-permute-start.7 = (f32[4,3,128,128]{3,2,1,0:T(8,128)S(1)}, f32[4,3,128,128]{3,2,1,0:T(8,128)S(1)}, u32[]{:S(2)}, u32[]{:S(2)}) collective-permute-start(f32[4,3,128,128]{3,2,1,0:T(8,128)S(1)} %collective-permute-done.6.rest_2_), channel_id=1, source_target_pairs={{8,0},{16,8},{24,16},{28,24},{20,28},{12,20},{4,12},{0,4},{9,1},{1... | collective-permute-start | bytes 2359304 | tf_op jit(solution)/shard_map/ppermute | solution.py:508
  111.8 32.7 %collective-permute-start.5 = (f32[4,3,128,128]{3,2,1,0:T(8,128)S(1)}, f32[4,3,128,128]{3,2,1,0:T(8,128)S(1)}, u32[]{:S(2)}, u32[]{:S(2)}) collective-permute-start(f32[4,3,128,128]{3,2,1,0:T(8,128)S(1)} %collective-permute-done.4.rest_1_), channel_id=1, source_target_pairs={{0,8},{8,16},{16,24},{24,28},{28,20},{20,12},{12,4},{4,0},{1,9},{9... | collective-permute-start | bytes 2359304 | tf_op jit(solution)/shard_map/ppermute | solution.py:507
  144.4 26.2 %collective-permute-start.11 = (f32[4,3,128,128]{3,2,1,0:T(8,128)S(1)}, f32[4,3,128,128]{3,2,1,0:T(8,128)S(1)}, u32[]{:S(2)}, u32[]{:S(2)}) collective-permute-start(f32[4,3,128,128]{3,2,1,0:T(8,128)S(1)} %collective-permute-done.5.rest_0_), channel_id=1, source_target_pairs={{0,8},{8,16},{16,24},{24,28},{28,20},{20,12},{12,4},{4,0},{1,9},{9... | collective-permute-start | bytes 2359304 | tf_op jit(solution)/shard_map/ppermute | solution.py:507
  145.2 26.2 %collective-permute-start.13 = (f32[4,3,128,128]{3,2,1,0:T(8,128)S(1)}, f32[4,3,128,128]{3,2,1,0:T(8,128)S(1)}, u32[]{:S(2)}, u32[]{:S(2)}) collective-permute-start(f32[4,3,128,128]{3,2,1,0:T(8,128)S(1)} %collective-permute-done.7.rest_1_), channel_id=1, source_target_pairs={{8,0},{16,8},{24,16},{28,24},{20,28},{12,20},{4,12},{0,4},{9,1},{1... | collective-permute-start | bytes 2359304 | tf_op jit(solution)/shard_map/ppermute | solution.py:508
  170.6 12.7 %collective-permute-start.12 = (f32[2,3,128,128]{3,2,1,0:T(8,128)S(1)}, f32[2,3,128,128]{3,2,1,0:T(8,128)S(1)}, u32[]{:S(2)}, u32[]{:S(2)}) collective-permute-start(f32[2,3,128,128]{3,2,1,0:T(8,128)S(1)} %slice.13), channel_id=1, source_target_pairs={{0,8},{8,16},{16,24},{24,28},{28,20},{20,12},{12,4},{4,0},{1,9},{9... | collective-permute-start | bytes 1179656 | tf_op jit(solution)/shard_map/ppermute | solution.py:513
  171.5 11.9 %collective-permute-start.14 = (f32[2,3,128,128]{3,2,1,0:T(8,128)S(1)}, f32[2,3,128,128]{3,2,1,0:T(8,128)S(1)}, u32[]{:S(2)}, u32[]{:S(2)}) collective-permute-start(f32[2,3,128,128]{3,2,1,0:T(8,128)S(1)} %slice.14), channel_id=1, source_target_pairs={{8,0},{16,8},{24,16},{28,24},{20,28},{12,20},{4,12},{0,4},{9,1},{1... | collective-permute-start | bytes 1179656 | tf_op jit(solution)/shard_map/ppermute | solution.py:513

commit v6 on v5

--- a/solution.py
+++ b/solution.py
@@ -58,92 +58,86 @@
     return 4 * TILE // height, height
 
 
-def pack_kernel(
-    owners, place, dest, slot, count, child_ref, front_ref, out_ref, notes_ref, lead_ref,
-    tile_ref, sems, notes_sem, lead_sem,
+def notes_kernel(
+    owners, place, dest, slot, count, child_ref, front_ref, out_ref, tile_ref, sem
 ):
+    slots = dest.shape[0]
+    height = out_ref.shape[1] - NOTE
+    each = TILE // height
+    live = jnp.minimum(count[0], slots)
+    out_ref[:, :NOTE] = jnp.full((out_ref.shape[0], NOTE, TILE), -1.0, jnp.float32)
+    out_ref[:, NOTE:] = jnp.zeros((out_ref.shape[0], height, TILE), jnp.float32)
+
+    @pl.loop(0, live)
+    def _(k):
+        out_ref[dest[k], :NOTE] = jnp.full((NOTE, TILE), slot[k].astype(jnp.float32))
+
+    def add(i, tile):
+        copy = pltpu.make_async_copy(tile, tile_ref, sem)
+        copy.start()
+        copy.wait()
+        span = pl.ds(i * each, each)
+        out_ref[span, NOTE:] = out_ref[span, NOTE:] + tile_ref[...].reshape(each, height, TILE)
+
+    for i, owner in enumerate(owners):
+        pl.when(place[3] == owner)(functools.partial(add, i, front_ref.at[0, 0, 0, 0]))
+
+    @pl.loop(0, live)
+    def _(k):
+        for i, owner in enumerate(owners):
+            wanted = jnp.logical_and(slot[k] == 0, dest[k] == owner)
+            pl.when(wanted)(functools.partial(add, i, child_ref.at[k]))
+
+
+def make_notes(child_tiles, front, place, dest, slot, count, devices, owners):
+    _, height = lead_slices(devices)
+    hbm = pl.BlockSpec(memory_space=pltpu.HBM)
+    return pl.pallas_call(
+        functools.partial(notes_kernel, owners),
+        in_specs=[pl.BlockSpec(memory_space=pltpu.SMEM)] * 4 + [hbm, hbm],
+        out_specs=pl.BlockSpec(memory_space=pltpu.VMEM),
+        scratch_shapes=[pltpu.VMEM((TILE, TILE), jnp.float32), pltpu.SemaphoreType.DMA],
+        out_shape=jax.ShapeDtypeStruct((devices, NOTE + height, TILE), jnp.float32),
+        compiler_params=pltpu.CompilerParams(vmem_limit_bytes=VMEM),
+        name="notes",
+    )(place, dest, slot, count, child_tiles, front)
+
+
+def pack_kernel(dest, count, child_ref, out_ref, sems):
     slots = child_ref.shape[0]
-    n_slices, height, _ = lead_ref.shape
-    each = n_slices // 4
+    live = jnp.minimum(count[0], slots)
 
     def copy(k):
-        return pltpu.make_async_copy(
-            child_ref.at[k], out_ref.at[dest[k], pl.ds(0, TILE)], sems.at[k]
-        )
-
-    notes_ref[...] = jnp.full_like(notes_ref, -1.0)
-    lead_ref[...] = jnp.zeros_like(lead_ref)
-    live = jnp.minimum(count[0], slots)
+        return pltpu.make_async_copy(child_ref.at[k], out_ref.at[dest[k]], sems.at[k])
 
     @pl.loop(0, live)
     def _(k):
         copy(k).start()
-        notes_ref[dest[k]] = jnp.full(notes_ref.shape[1:], slot[k].astype(jnp.float32))
-
-    notes = pltpu.make_async_copy(notes_ref, out_ref.at[:, pl.ds(TILE, NOTE)], notes_sem)
-    notes.start()
-
-    for i, owner in enumerate(owners):
-        span = pl.ds(i * each, each)
-
-        @pl.when(place[3] == owner)
-        def _():
-            own = pltpu.make_async_copy(front_ref.at[0, 0, 0, 0], tile_ref, lead_sem)
-            own.start()
-            own.wait()
-            lead_ref[span] = tile_ref[...].reshape(each, height, TILE)
-
-        @pl.loop(0, live)
-        def _(k):
-            @pl.when(jnp.logical_and(slot[k] == 0, dest[k] == owner))
-            def _():
-                lead_ref[span] = lead_ref[span] + child_ref[k].reshape(each, height, TILE)
-
-    lead = pltpu.make_async_copy(
-        lead_ref, out_ref.at[pl.ds(0, n_slices), pl.ds(TILE + NOTE, height)], lead_sem
-    )
-    lead.start()
-    notes.wait()
-    lead.wait()
 
     @pl.loop(0, live)
     def _(k):
         copy(k).wait()
 
 
-def pack(child_tiles, front, place, dest, slot, count, devices, owners):
+def pack(child_tiles, dest, count, devices):
     slots = child_tiles.shape[0]
-    n_slices, height = lead_slices(devices)
-    hbm = pl.BlockSpec(memory_space=pltpu.HBM)
     return pl.pallas_call(
-        functools.partial(pack_kernel, owners),
-        in_specs=[pl.BlockSpec(memory_space=pltpu.SMEM)] * 4
-        + [pl.BlockSpec(memory_space=pltpu.VMEM), hbm],
-        out_specs=hbm,
-        scratch_shapes=[
-            pltpu.VMEM((devices, NOTE, TILE), jnp.float32),
-            pltpu.VMEM((n_slices, height, TILE), jnp.float32),
-            pltpu.VMEM((TILE, TILE), jnp.float32),
-            pltpu.SemaphoreType.DMA((slots,)),
-            pltpu.SemaphoreType.DMA,
-            pltpu.SemaphoreType.DMA,
-        ],
-        out_shape=jax.ShapeDtypeStruct((devices, TILE + NOTE + height, TILE), jnp.float32),
+        pack_kernel,
+        in_specs=[pl.BlockSpec(memory_space=pltpu.SMEM)] * 2
+        + [pl.BlockSpec(memory_space=pltpu.VMEM)],
+        out_specs=pl.BlockSpec(memory_space=pltpu.HBM),
+        scratch_shapes=[pltpu.SemaphoreType.DMA((slots,))],
+        out_shape=jax.ShapeDtypeStruct((devices, TILE, TILE), jnp.float32),
         compiler_params=pltpu.CompilerParams(vmem_limit_bytes=VMEM),
         name="pack",
-    )(place, dest, slot, count, child_tiles, front)
-
-
-def columns_kernel(place, slot_in, front_ref, incoming_ref, out_ref, own_ref, *rest):
-    *parts, tile_ref, slices_ref, sem, slices_sem = rest
+    )(dest, count, child_tiles)
+
+
+def columns_kernel(place, slot_in, front_ref, incoming_ref, out_ref, *rest):
+    *parts, tile_ref, sem = rest
     cols = place[2]
-    height = own_ref.shape[1]
     strip = pltpu.make_async_copy(front_ref.at[:, 0, 0, 0], out_ref, sem)
     strip.start()
-    slices = pltpu.make_async_copy(
-        incoming_ref.at[:, pl.ds(TILE + NOTE, height)], slices_ref, slices_sem
-    )
-    slices.start()
     strip.wait()
 
     @pl.loop(0, incoming_ref.shape[0])
@@ -152,7 +146,7 @@
 
         @pl.when(jnp.logical_and(slot >= 0, lax.rem(slot, cols) == 0))
         def _():
-            copy = pltpu.make_async_copy(incoming_ref.at[s, pl.ds(0, TILE)], tile_ref, sem)
+            copy = pltpu.make_async_copy(incoming_ref.at[s], tile_ref, sem)
             copy.start()
             copy.wait()
             row = lax.div(slot, cols)
@@ -164,15 +158,10 @@
         for t in range(group):
             part_ref[t] = out_ref[lax.rem(place[1] + j, count) * group + t].T
 
-    slices.wait()
-    own_ref[...] = jnp.broadcast_to(jnp.sum(slices_ref[...], axis=0)[None], own_ref.shape)
-
 
 def assemble_columns(front, incoming, place, slot_in, parts):
-    rows, devices = front.shape[0], incoming.shape[0]
-    _, height = lead_slices(devices)
-    shapes = [(rows, TILE, TILE), (devices, height, TILE)]
-    shapes += [(rows // parts, TILE, TILE)] * parts
+    rows = front.shape[0]
+    shapes = [(rows, TILE, TILE)] + [(rows // parts, TILE, TILE)] * parts
     out_shape = [jax.ShapeDtypeStruct(shape, jnp.float32) for shape in shapes]
     return pl.pallas_call(
         columns_kernel,
@@ -183,8 +172,6 @@
             out_specs=[whole_spec(a) for a in out_shape],
             scratch_shapes=[
                 pltpu.VMEM((TILE, TILE), jnp.float32),
-                pltpu.VMEM((devices, height, TILE), jnp.float32),
-                pltpu.SemaphoreType.DMA,
                 pltpu.SemaphoreType.DMA,
             ],
         ),
@@ -256,8 +243,7 @@
 
     one, two = two_panels(columns, small_ref, mask)
     for i, panel in enumerate((mask(1, one), mask(2, two))):
-        high, low = halves(panel)
-        for k, half in enumerate((high, low, high)):
+        for k, half in enumerate(halves(panel)):
             pair_ref[:, k * WIDTH + i * PANEL : k * WIDTH + (i + 1) * PANEL] = half
     pieces = (one[:, :TILE], one[:, TILE:], two[:, :TILE], two[:, TILE:])
     for c in range(4):
@@ -273,7 +259,7 @@
     group = rows // 3
     height = group * TILE
     out_shape = [
-        jax.ShapeDtypeStruct((rows * TILE, 3 * WIDTH), jnp.bfloat16),
+        jax.ShapeDtypeStruct((rows * TILE, 2 * WIDTH), jnp.bfloat16),
         jax.ShapeDtypeStruct(front.shape, jnp.float32),
         jax.ShapeDtypeStruct((3, PANEL, 3 * PANEL), jnp.bfloat16),
         jax.ShapeDtypeStruct((2 * slot_in.shape[0],), jnp.int32),
@@ -287,7 +273,7 @@
             grid=(3,),
             in_specs=[strip] * 4 + [whole_spec(lead), whole_spec(diag)],
             out_specs=[
-                pl.BlockSpec((height, 3 * WIDTH), lambda i, *_: (i, 0)),
+                pl.BlockSpec((height, 2 * WIDTH), lambda i, *_: (i, 0)),
                 pl.BlockSpec((group, 1, 1, 1, TILE, TILE), lambda i, *_: (i, 0, 0, 0, 0, 0)),
                 whole_spec(out_shape[2]),
                 pl.BlockSpec(memory_space=pltpu.SMEM),
@@ -360,7 +346,7 @@
                 def _(i):
                     s = order[2 * i]
                     copy = pltpu.make_async_copy(
-                        incoming_ref.at[s, pl.ds(0, TILE)], child_ref.at[s], child_sems.at[s]
+                        incoming_ref.at[s], child_ref.at[s], child_sems.at[s]
                     )
                     act(copy, j, s, order[2 * i + 1])
 
@@ -396,10 +382,14 @@
 
         start = jnp.minimum(2 * step, count - 2)
         lanes = pl.ds(pl.multiple_of(start * TILE, TILE), 2 * TILE)
-        update = dot(pair_ref[...], right_ref[:, lanes])
-        for j in range(2):
-            part = update[:, j * TILE : (j + 1) * TILE].reshape(rows, TILE, TILE)
-            given[slot, j] = taken[slot, j] - part
+        block = rows // 3
+        for m in range(3):
+            left = pair_ref[m * block * TILE : (m + 1) * block * TILE]
+            update = dot(jnp.concatenate([left, left[:, :WIDTH]], axis=1), right_ref[:, lanes])
+            span = slice(m * block, (m + 1) * block)
+            for j in range(2):
+                part = update[:, j * TILE : (j + 1) * TILE].reshape(block, TILE, TILE)
+                given[slot, j, span] = taken[slot, j, span] - part
 
         def add(copy, j, s, a):
             copy.wait()
@@ -463,27 +453,29 @@
     owners = [r * n_col + c for r in (2, 3) for c in (0, 1)]
     place = jnp.stack([my_row, my_col, jnp.int32(cols_here), my_row * n_col + my_col])
 
-    outgoing = pack(
-        child_tiles, front, place, tile_dest[:, 0], tile_slot, tile_count, devices, owners
-    )
+    dest = tile_dest[:, 0]
+    notes = make_notes(child_tiles, front, place, dest, tile_slot, tile_count, devices, owners)
+    notes = lax.all_to_all(notes, BOTH, split_axis=0, concat_axis=0, tiled=True)
+    slot_in = notes[:, 0, 0].astype(jnp.int32)
+    lead = jnp.broadcast_to(jnp.sum(notes[:, NOTE:], axis=0)[None], notes[:, NOTE:].shape)
+    lead = lax.all_to_all(lead, BOTH, split_axis=0, concat_axis=0, tiled=True)
+    lead = lead[: lead_slices(devices)[0]].reshape(2, 2, TILE, TILE)
+
+    outgoing = pack(child_tiles, dest, tile_count, devices)
+    outgoing, slot_in = lax.optimization_barrier((outgoing, slot_in))
     incoming = lax.all_to_all(outgoing, BOTH, split_axis=0, concat_axis=0, tiled=True)
-    slot_in = lax.optimization_barrier(incoming[:, TILE, 0].astype(jnp.int32))
+    incoming, lead = lax.optimization_barrier((incoming, lead))
 
     ring = rows_here % n_col == 0
-    mine, own, *parts = assemble_columns(front, incoming, place, slot_in, n_col if ring else 1)
-
-    def hand_on(own):
-        lead = lax.all_to_all(own, BOTH, split_axis=0, concat_axis=0, tiled=True)
-        return lead[: lead_slices(devices)[0]].reshape(2, 2, TILE, TILE)
+    mine, *parts = assemble_columns(front, incoming, place, slot_in, n_col if ring else 1)
 
     def exchange(mine):
         near = lax.ppermute(mine, "col", [(c, c ^ 1) for c in range(n_col)])
         far = lax.ppermute(mine, "col", [(c, c ^ 2) for c in range(n_col)])
         return [near, far, lax.ppermute(far, "col", [(c, c ^ 1) for c in range(n_col)])]
 
-    def own_panels(mine, own):
-        tiles = exchange(mine)
-        return row_panels(mine, tiles, hand_on(own), diag_inverses, place, slot_in, front)
+    def own_panels(mine):
+        return row_panels(mine, exchange(mine), lead, diag_inverses, place, slot_in, front)
 
     sets = n_row // n_col
     if ring:
@@ -495,13 +487,13 @@
                 for c in range(n_col)
             ]
             arrived.append(lax.ppermute(part, BOTH, pairs))
-        arrived, own, mine = lax.optimization_barrier((arrived, own, mine))
+        arrived, mine = lax.optimization_barrier((arrived, mine))
         piece = jnp.stack(arrived)
         circle = list(range(0, n_row, 2)) + list(range(n_row - 1, 0, -2))
         up = [(circle[i], circle[(i + 1) % n_row]) for i in range(n_row)]
         down = [(b, a) for a, b in up]
         rounds = [[(piece, 0)]]
-        panels = own_panels(mine, own)
+        panels = own_panels(mine)
         ahead = behind = piece
         for step in range(1, n_row // 2):
             ahead = lax.ppermute(ahead, "row", up)
@@ -529,7 +521,7 @@
         ]
         moved = lax.all_gather(lax.ppermute(parts[0], BOTH, pairs), "row", axis=0, tiled=False)
         rounds = [[(moved[h * n_col : (h + 1) * n_col], h)] for h in range(sets)]
-        panels = own_panels(mine, own)
+        panels = own_panels(mine)
 
         def described(row, h):
             return [a * sets + h for a in range(rows_here)], list(range(n_col))

time: 192 us -> 191 us (level)
  blocking collectives: 90 us -> 71.4 us
  waiting for transfers between devices: 22.3 us -> 38.8 us
  Pallas kernels: 55.7 us -> 49.5 us
  local copies, waits for them, and re-layouts: 2.61 us -> 6.02 us
    all_to_all x1, blocking collectives: 65.4 us -> 50.9 us  [body(): lax.all_to_all(outgoing, BOTH, split_axis=0, concat_axis=0, tiled=True)]
    all_to_all x0 -> x1, waiting for transfers between devices: none -> 7.04 us  [body(): lead = lax.all_to_all(lead, BOTH, split_axis=0, concat_axis=0, tiled=True)]
    ppermute x3, waiting for transfers between devices: 0.48 us -> 7.46 us  [body(): behind = lax.ppermute(behind, 'row', down)]
    pallas_call x4, Pallas kernels: 42.5 us -> 36.8 us  [trailing(): pl.pallas_call(functools.partial(trailing_kernel, first, len(pieces)), in...]
    all_to_all x1, blocking collectives: 24.6 us -> 20.5 us  [body(): notes = lax.all_to_all(notes, BOTH, split_axis=0, concat_axis=0, tiled=True)]
    unnamed x12 -> x20, local copies, waits for them, and re-layouts: 2.56 us -> 5.24 us
    all_to_all x0 -> x1, starting transfers between devices: none -> 2.64 us  [body(): lead = lax.all_to_all(lead, BOTH, split_axis=0, concat_axis=0, tiled=True)]
  transfers between devices with their start and end apart: 15 -> 16, of which waited for: 5 -> 8; matrix products, arithmetic and copies ran while one was open for 0% -> 1% of each run, Pallas kernels for 22% -> 21%
where the time goes in v6:
time: 191 us; the launch traced here: 190 us
  blocking collectives  71.4 us (37%)
  Pallas kernels  49.5 us (26%)
  waiting for transfers between devices  38.8 us (20%)
  starting transfers between devices  20.8 us (11%)
  local copies, waits for them, and re-layouts  6.02 us (3%)
  other arithmetic  2.75 us (1%)
    all_to_all x1, blocking collectives, body(): lax.all_to_all(outgoing, BOTH, split_axis=0, concat_axis=0, tiled=True)  50.9 us
    pallas_call x4, Pallas kernels, trailing(): pl.pallas_call(functools.partial(trailing_kernel, first, len(pieces)), in...  36.8 us
    all_to_all x1, blocking collectives, body(): notes = lax.all_to_all(notes, BOTH, split_axis=0, concat_axis=0, tiled=True)  20.5 us
    ppermute x1, waiting for transfers between devices, exchange(): far = lax.ppermute(mine, 'col', [(c, c ^ 2) for c in range(n_col)])  16.1 us
    pallas_call x1, Pallas kernels, row_panels(): pl.pallas_call(row_panels_kernel, grid_spec=pltpu.PrefetchScalarGridSpec(...  7.47 us
    ppermute x3, waiting for transfers between devices, body(): behind = lax.ppermute(behind, 'row', down)  7.46 us
    ppermute x4, waiting for transfers between devices, body(): arrived.append(lax.ppermute(part, BOTH, pairs))  7.05 us
    all_to_all x1, waiting for transfers between devices, body(): lead = lax.all_to_all(lead, BOTH, split_axis=0, concat_axis=0, tiled=True)  7.04 us
  transfers between devices with their start and end apart: 16, of which 8 were waited for; matrix products, arithmetic and copies ran while one was open for 1% of the time, Pallas kernels for 21%

profile of v6, /device:TPU:0, one launch (start us, length us, event | category | flops | bytes accessed | tf_op | source)
XLA Modules:
  0.0 190.2 jit_solution(6684194609220658243)
XLA Ops:
  0.0 0.0 copy-start.8
  0.7 0.1 pad_add_fusion.place
  0.7 0.0 copy-start.2
  0.8 1.2 copy-done.2
  2.0 0.0 copy-start.7
  2.0 0.7 copy-done.7
  2.6 0.0 copy-start.9
  2.6 0.7 copy-done.9
  3.3 1.3 notes.1
  4.6 0.0 copy-start.5
  4.6 0.0 copy-start.6
  4.6 20.5 %all_to_all.15 = f32[32,24,128]{2,1,0:T(8,128)} all-to-all(f32[32,24,128]{2,1,0:T(8,128)S(1)} %notes.1), channel_id=1, replica_groups=mesh['row'=8,'col'=4] {'row','col'}, dimensions={0} | all-to-all | bytes 786432 | tf_op jit(solution)/shard_map/all_to_all | solution.py:458
  25.1 1.0 slice_reduce_fusion
  26.1 0.7 broadcast_in_dim.2
  26.8 2.6 %all-to-all-start.2 = ((f32[32,16,128]{2,1,0:T(8,128)}), f32[32,16,128]{2,1,0:T(8,128)S(1)}, u32[]{:S(2)}, u32[]{:S(2)}) async-start(f32[32,16,128]{2,1,0:T(8,128)} %broadcast_in_dim.2), calls=%async_computation.2 | async-start | bytes 524288 | tf_op jit(solution)/shard_map/all_to_all | solution.py:461
  29.4 0.0 copy-done.8
  29.4 0.0 copy-done.3
  29.4 2.0 %pack.1 = f32[32,128,128]{2,1,0:T(8,128)S(1)} custom-call(s32[16]{0:T(128)S(1)} %bitcast.11, s32[1]{0:T(128)S(6)} %copy.17.count, f32[16,128,128]{2,1,0:T(8,128)S(1)} %copy-done.3), custom_call_target="tpu_custom_call" | custom-call | tf_op jit(solution)/shard_map/pack/pallas_call | solution.py:124
  31.4 1.6 fusion.slot_in
  33.0 7.0 %all-to-all-done.2 = f32[32,16,128]{2,1,0:T(8,128)S(1)} async-done(((f32[32,16,128]{2,1,0:T(8,128)}), f32[32,16,128]{2,1,0:T(8,128)S(1)}, u32[]{:S(2)}, u32[]{:S(2)}) %all-to-all-start.2) | async-done | bytes 262176 | tf_op jit(solution)/shard_map/all_to_all | solution.py:461
  40.0 50.9 %all_to_all.16.incoming_ref.rest_4_.rest_3_.rest_2_ = f32[32,128,128]{2,1,0:T(8,128)S(1)} all-to-all(f32[32,128,128]{2,1,0:T(8,128)S(1)} %pack.1), channel_id=1, replica_groups=mesh['row'=8,'col'=4] {'row','col'}, dimensions={0} | all-to-all | bytes 4194304 | tf_op jit(solution)/shard_map/all_to_all | solution.py:466
  90.9 2.0 %panel_columns.1 = (f32[12,128,128]{2,1,0:T(8,128)S(1)}, f32[3,128,128]{2,1,0:T(8,128)S(1)}, f32[3,128,128]{2,1,0:T(8,128)S(1)}, f32[3,128,128]{2,1,0:T(8,128)S(1)}, f32[3,128,128]{2,1,0:T(8,128)S(1)}) custom-call(s32[4]{0:T(128)S(1)} %pad_add_fusion.place, s32[32]{0:T(128)S(1)} %fusion.slot_in, f32[12,1,24,1,128,128]{5,4,3,2,1,0:T(8,128)} %rest_1_.1, ...), custom_call_target="tpu_custom_call" | custom-call | tf_op jit(solution)/shard_map/panel_columns/pallas_call | solution.py:166
  92.9 0.7 collective-permute-start
  93.6 3.2 %collective-permute-start.1 = (f32[3,128,128]{2,1,0:T(8,128)S(1)}, f32[3,128,128]{2,1,0:T(8,128)S(1)}, u32[]{:S(2)}, u32[]{:S(2)}) collective-permute-start(f32[3,128,128]{2,1,0:T(8,128)S(1)} %get-tuple-element.35), channel_id=1, source_target_pairs={{0,4},{1,8},{2,12},{3,0},{4,5},{5,9},{6,13},{7,1},{8,6},{9,10},{10... | collective-permute-start | bytes 589832 | tf_op jit(solution)/shard_map/ppermute | solution.py:489
  96.8 2.5 %collective-permute-start.2 = (f32[3,128,128]{2,1,0:T(8,128)S(1)}, f32[3,128,128]{2,1,0:T(8,128)S(1)}, u32[]{:S(2)}, u32[]{:S(2)}) collective-permute-start(f32[3,128,128]{2,1,0:T(8,128)S(1)} %get-tuple-element.36), channel_id=1, source_target_pairs={{0,8},{1,12},{2,0},{3,4},{4,9},{5,13},{6,1},{7,5},{8,10},{9,14},{1... | collective-permute-start | bytes 589832 | tf_op jit(solution)/shard_map/ppermute | solution.py:489
  99.2 0.5 collective-permute-start.3
  99.7 0.0 collective-permute-done
  99.7 4.9 %collective-permute-done.1 = f32[3,128,128]{2,1,0:T(8,128)S(1)} collective-permute-done((f32[3,128,128]{2,1,0:T(8,128)S(1)}, f32[3,128,128]{2,1,0:T(8,128)S(1)}, u32[]{:S(2)}, u32[]{:S(2)}) %collective-permute-start.1) | collective-permute-done | bytes 196640 | tf_op jit(solution)/shard_map/ppermute | solution.py:489
  104.7 0.0 collective-permute-done.2
  104.7 2.1 %collective-permute-done.3 = f32[3,128,128]{2,1,0:T(8,128)S(1)} collective-permute-done((f32[3,128,128]{2,1,0:T(8,128)S(1)}, f32[3,128,128]{2,1,0:T(8,128)S(1)}, u32[]{:S(2)}, u32[]{:S(2)}) %collective-permute-start.3) | collective-permute-done | bytes 196640 | tf_op jit(solution)/shard_map/ppermute | solution.py:489
  106.8 2.7 %collective-permute-start.9 = (f32[12,128,128]{2,1,0:T(8,128)S(1)}, f32[12,128,128]{2,1,0:T(8,128)S(1)}, u32[]{:S(2)}, u32[]{:S(2)}) collective-permute-start(f32[12,128,128]{2,1,0:T(8,128)S(1)} %get-tuple-element.43.t0), channel_id=1, source_target_pairs={{0,2},{1,3},{2,0},{3,1},{4,6},{5,7},{6,4},{7,5},{8,10},{9,11},{10,... | collective-permute-start | bytes 2359304 | tf_op jit(solution)/shard_map/ppermute | solution.py:474
  109.5 0.1 pad_maximum_fusion.rest_0_
  109.5 1.3 collective-permute-start.6
  110.9 0.7 collective-permute-start.4
  111.6 0.0 collective-permute-start.8
  111.6 16.1 %collective-permute-done.9.t2 = f32[12,128,128]{2,1,0:T(8,128)S(1)} collective-permute-done((f32[12,128,128]{2,1,0:T(8,128)S(1)}, f32[12,128,128]{2,1,0:T(8,128)S(1)}, u32[]{:S(2)}, u32[]{:S(2)}) %collective-permute-start.9) | collective-permute-done | bytes 786464 | tf_op jit(solution)/shard_map/ppermute | solution.py:474
  127.7 0.3 collective-permute-start.10
  128.0 0.2 collective-permute-done.6.rest_2_
  128.2 1.6 collective-permute-start.7
  129.8 0.0 collective-permute-done.4.rest_1_
  129.8 0.5 collective-permute-start.5
  130.2 0.0 collective-permute-done.8.t1
  130.2 0.0 collective-permute-done.10.t3
  130.2 1.0 copy-done.4
  131.3 7.5 %row_panels.1 = (bf16[1536,1024]{1,0:T(8,128)(2,1)S(1)}, f32[12,1,24,1,128,128]{5,4,3,2,1,0:T(8,128)}, bf16[3,256,768]{2,1,0:T(8,128)(2,1)S(1)}, s32[64]{0:T(128)S(1)}, s32[25]{0:T(128)S(1)}) custom-call(s32[4]{0:T(128)S(1)} %pad_add_fusion.place, s32[32]{0:T(128)S(1)} %fusion.slot_in, f32[12,128,128]{2,1,0:T(8,128)S(1)} %get-tuple-element.43.t0, ...), custom_call_target="tpu_custom_call" | custom-call | tf_op jit(solution)/shard_map/row_panels/pallas_call | solution.py:269
  138.7 1.6 copy-done
  140.4 7.3 %collective-permute-done.7.rest_1_ = f32[4,3,128,128]{3,2,1,0:T(8,128)S(1)} collective-permute-done((f32[4,3,128,128]{3,2,1,0:T(8,128)S(1)}, f32[4,3,128,128]{3,2,1,0:T(8,128)S(1)}, u32[]{:S(2)}, u32[]{:S(2)}) %collective-permute-start.7) | collective-permute-done | bytes 786464 | tf_op jit(solution)/shard_map/ppermute | solution.py:500
  147.6 0.9 collective-permute-done.5.rest_0_
  148.6 0.8 collective-permute-start.11
  149.4 1.2 collective-permute-start.13
  150.6 0.0 copy-done.5
  150.6 0.0 copy-done.6
  150.6 13.2 %trailing.4.rest_4_ = f32[12,1,24,1,128,128]{5,4,3,2,1,0:T(8,128)} custom-call(s32[4]{0:T(128)S(1)} %pad_add_fusion.place, s32[192]{0:T(256)S(1)} %copy-done.6, s32[256]{0:T(256)S(1)} %copy-done.5, s32[64]{0:T(128)S(1)} %get-tuple-element.50.order, s32[25]{0:T(128)S(1)} %get-tuple-element.51.starts, ...), custom_call_target="tpu_custom_call", output_to_operand_aliasing={{}: (12, {})} | custom-call | flops 14495514624 | bytes 14155776 | tf_op jit(solution)/shard_map/trailing/pallas_call | solution.py:420
  163.8 0.0 copy-done.1
  163.8 8.4 %trailing.5.rest_4_ = f32[12,1,24,1,128,128]{5,4,3,2,1,0:T(8,128)} custom-call(s32[4]{0:T(128)S(1)} %pad_add_fusion.place, s32[192]{0:T(256)S(1)} %copy-done.6, s32[256]{0:T(256)S(1)} %copy-done.5, s32[64]{0:T(128)S(1)} %get-tuple-element.50.order, s32[25]{0:T(128)S(1)} %get-tuple-element.51.starts, ...), custom_call_target="tpu_custom_call", output_to_operand_aliasing={{}: (11, {})} | custom-call | flops 9663676416 | bytes 9437184 | tf_op jit(solution)/shard_map/trailing/pallas_call | solution.py:420
  172.3 0.0 collective-permute-done.11.rest_0_
  172.3 1.2 collective-permute-start.12
  173.5 0.0 collective-permute-done.13.rest_1_
  173.6 1.0 collective-permute-start.14
  174.6 8.9 %trailing.6.rest_3_ = f32[12,1,24,1,128,128]{5,4,3,2,1,0:T(8,128)} custom-call(s32[4]{0:T(128)S(1)} %pad_add_fusion.place, s32[192]{0:T(256)S(1)} %copy-done.6, s32[256]{0:T(256)S(1)} %copy-done.5, s32[64]{0:T(128)S(1)} %get-tuple-element.50.order, s32[25]{0:T(128)S(1)} %get-tuple-element.51.starts, ...), custom_call_target="tpu_custom_call", output_to_operand_aliasing={{}: (11, {})} | custom-call | flops 9663676416 | bytes 9437184 | tf_op jit(solution)/shard_map/trailing/pallas_call | solution.py:420
  183.5 0.3 collective-permute-done.12
  183.7 0.0 collective-permute-done.14
  183.8 0.1 pad_maximum_fusion.1.rest_0_
  183.8 6.3 %trailing.7 = f32[12,1,24,1,128,128]{5,4,3,2,1,0:T(8,128)} custom-call(s32[4]{0:T(128)S(1)} %pad_add_fusion.place, s32[192]{0:T(256)S(1)} %copy-done.6, s32[256]{0:T(256)S(1)} %copy-done.5, s32[64]{0:T(128)S(1)} %get-tuple-element.50.order, s32[25]{0:T(128)S(1)} %get-tuple-element.51.starts, ...), custom_call_target="tpu_custom_call", output_to_operand_aliasing={{}: (10, {})} | custom-call | flops 4831838208 | bytes 4718592 | tf_op jit(solution)/shard_map/trailing/pallas_call | solution.py:420
  (6 shorter events, 0.1 us)
Async XLA Ops:
  0.0 29.4 %copy-start.8 = (s32[16,1]{0,1:T(1,128)S(1)}, s32[16,1]{0,1:T(1,128)}, u32[]{:S(2)}) copy-start(s32[16,1]{0,1:T(1,128)} %param.10) | copy-start | bytes 196
  0.7 1.2 copy-start.2
  2.0 0.7 copy-start.7
  2.6 0.7 copy-start.9
  3.3 26.1 %copy-start.3 = (f32[16,128,128]{2,1,0:T(8,128)S(1)}, f32[16,128,128]{2,1,0:T(8,128)}, u32[]{:S(2)}) copy-start(f32[16,128,128]{2,1,0:T(8,128)} %child_ref.3) | copy-start | bytes 3145732
  4.6 146.1 %copy-start.5 = (s32[256]{0:T(256)S(1)}, s32[256]{0:T(256)}, u32[]{:S(2)}) copy-start(s32[256]{0:T(256)} %constant.20.clone.places_table) | copy-start | bytes 3076
  4.6 146.0 %copy-start.6 = (s32[192]{0:T(256)S(1)}, s32[192]{0:T(256)}, u32[]{:S(2)}) copy-start(s32[192]{0:T(256)} %constant.19.clone.columns_table) | copy-start | bytes 2308
  26.8 13.2 %all-to-all-start.2 = ((f32[32,16,128]{2,1,0:T(8,128)}), f32[32,16,128]{2,1,0:T(8,128)S(1)}, u32[]{:S(2)}, u32[]{:S(2)}) async-start(f32[32,16,128]{2,1,0:T(8,128)} %broadcast_in_dim.2), calls=%async_computation.2 | async-start | bytes 524288 | tf_op jit(solution)/shard_map/all_to_all | solution.py:461
  92.9 6.8 %collective-permute-start = (f32[3,128,128]{2,1,0:T(8,128)S(1)}, f32[3,128,128]{2,1,0:T(8,128)S(1)}, u32[]{:S(2)}, u32[]{:S(2)}) collective-permute-start(f32[3,128,128]{2,1,0:T(8,128)S(1)} %get-tuple-element.34), channel_id=1, source_target_pairs={{0,0},{1,4},{2,8},{3,12},{4,1},{5,5},{6,9},{7,13},{8,2},{9,6},{10,... | collective-permute-start | bytes 589832 | tf_op jit(solution)/shard_map/ppermute | solution.py:489
  93.6 11.1 %collective-permute-start.1 = (f32[3,128,128]{2,1,0:T(8,128)S(1)}, f32[3,128,128]{2,1,0:T(8,128)S(1)}, u32[]{:S(2)}, u32[]{:S(2)}) collective-permute-start(f32[3,128,128]{2,1,0:T(8,128)S(1)} %get-tuple-element.35), channel_id=1, source_target_pairs={{0,4},{1,8},{2,12},{3,0},{4,5},{5,9},{6,13},{7,1},{8,6},{9,10},{10... | collective-permute-start | bytes 589832 | tf_op jit(solution)/shard_map/ppermute | solution.py:489
  96.8 7.9 %collective-permute-start.2 = (f32[3,128,128]{2,1,0:T(8,128)S(1)}, f32[3,128,128]{2,1,0:T(8,128)S(1)}, u32[]{:S(2)}, u32[]{:S(2)}) collective-permute-start(f32[3,128,128]{2,1,0:T(8,128)S(1)} %get-tuple-element.36), channel_id=1, source_target_pairs={{0,8},{1,12},{2,0},{3,4},{4,9},{5,13},{6,1},{7,5},{8,10},{9,14},{1... | collective-permute-start | bytes 589832 | tf_op jit(solution)/shard_map/ppermute | solution.py:489
  99.2 7.6 %collective-permute-start.3 = (f32[3,128,128]{2,1,0:T(8,128)S(1)}, f32[3,128,128]{2,1,0:T(8,128)S(1)}, u32[]{:S(2)}, u32[]{:S(2)}) collective-permute-start(f32[3,128,128]{2,1,0:T(8,128)S(1)} %get-tuple-element.37), channel_id=1, source_target_pairs={{0,12},{1,0},{2,4},{3,8},{4,13},{5,1},{6,5},{7,9},{8,14},{9,2},{10... | collective-permute-start | bytes 589832 | tf_op jit(solution)/shard_map/ppermute | solution.py:489
  106.8 20.9 %collective-permute-start.9 = (f32[12,128,128]{2,1,0:T(8,128)S(1)}, f32[12,128,128]{2,1,0:T(8,128)S(1)}, u32[]{:S(2)}, u32[]{:S(2)}) collective-permute-start(f32[12,128,128]{2,1,0:T(8,128)S(1)} %get-tuple-element.43.t0), channel_id=1, source_target_pairs={{0,2},{1,3},{2,0},{3,1},{4,6},{5,7},{6,4},{7,5},{8,10},{9,11},{10,... | collective-permute-start | bytes 2359304 | tf_op jit(solution)/shard_map/ppermute | solution.py:474
  109.5 18.6 %collective-permute-start.6 = (f32[4,3,128,128]{3,2,1,0:T(8,128)S(1)}, f32[4,3,128,128]{3,2,1,0:T(8,128)S(1)}, u32[]{:S(2)}, u32[]{:S(2)}) collective-permute-start(f32[4,3,128,128]{3,2,1,0:T(8,128)S(1)} %pad_maximum_fusion.rest_0_), channel_id=1, source_target_pairs={{8,0},{16,8},{24,16},{28,24},{20,28},{12,20},{4,12},{0,4},{9,1},{1... | collective-permute-start | bytes 2359304 | tf_op jit(solution)/shard_map/ppermute | solution.py:500
  110.9 18.9 %collective-permute-start.4 = (f32[4,3,128,128]{3,2,1,0:T(8,128)S(1)}, f32[4,3,128,128]{3,2,1,0:T(8,128)S(1)}, u32[]{:S(2)}, u32[]{:S(2)}) collective-permute-start(f32[4,3,128,128]{3,2,1,0:T(8,128)S(1)} %pad_maximum_fusion.rest_0_), channel_id=1, source_target_pairs={{0,8},{8,16},{16,24},{24,28},{28,20},{20,12},{12,4},{4,0},{1,9},{9... | collective-permute-start | bytes 2359304 | tf_op jit(solution)/shard_map/ppermute | solution.py:499
  111.6 18.6 %collective-permute-start.8 = (f32[12,128,128]{2,1,0:T(8,128)S(1)}, f32[12,128,128]{2,1,0:T(8,128)S(1)}, u32[]{:S(2)}, u32[]{:S(2)}) collective-permute-start(f32[12,128,128]{2,1,0:T(8,128)S(1)} %get-tuple-element.43.t0), channel_id=1, source_target_pairs={{0,1},{1,0},{2,3},{3,2},{4,5},{5,4},{6,7},{7,6},{8,9},{9,8},{10,11... | collective-permute-start | bytes 2359304 | tf_op jit(solution)/shard_map/ppermute | solution.py:473
  127.7 2.5 %collective-permute-start.10 = (f32[12,128,128]{2,1,0:T(8,128)S(1)}, f32[12,128,128]{2,1,0:T(8,128)S(1)}, u32[]{:S(2)}, u32[]{:S(2)}) collective-permute-start(f32[12,128,128]{2,1,0:T(8,128)S(1)} %collective-permute-done.9.t2), channel_id=1, source_target_pairs={{0,1},{1,0},{2,3},{3,2},{4,5},{5,4},{6,7},{7,6},{8,9},{9,8},{10,11... | collective-permute-start | bytes 2359304 | tf_op jit(solution)/shard_map/ppermute | solution.py:475
  128.2 19.5 %collective-permute-start.7 = (f32[4,3,128,128]{3,2,1,0:T(8,128)S(1)}, f32[4,3,128,128]{3,2,1,0:T(8,128)S(1)}, u32[]{:S(2)}, u32[]{:S(2)}) collective-permute-start(f32[4,3,128,128]{3,2,1,0:T(8,128)S(1)} %collective-permute-done.6.rest_2_), channel_id=1, source_target_pairs={{8,0},{16,8},{24,16},{28,24},{20,28},{12,20},{4,12},{0,4},{9,1},{1... | collective-permute-start | bytes 2359304 | tf_op jit(solution)/shard_map/ppermute | solution.py:500
  129.8 18.8 %collective-permute-start.5 = (f32[4,3,128,128]{3,2,1,0:T(8,128)S(1)}, f32[4,3,128,128]{3,2,1,0:T(8,128)S(1)}, u32[]{:S(2)}, u32[]{:S(2)}) collective-permute-start(f32[4,3,128,128]{3,2,1,0:T(8,128)S(1)} %collective-permute-done.4.rest_1_), channel_id=1, source_target_pairs={{0,8},{8,16},{16,24},{24,28},{28,20},{20,12},{12,4},{4,0},{1,9},{9... | collective-permute-start | bytes 2359304 | tf_op jit(solution)/shard_map/ppermute | solution.py:499
  130.2 1.0 copy-start.4
  138.7 1.6 copy-start
  148.6 15.2 %copy-start.1 = (bf16[1536,1024]{1,0:T(8,128)(2,1)S(1)}, bf16[1536,1024]{1,0:T(8,128)(2,1)}, u32[]{:S(2)}) copy-start(bf16[1536,1024]{1,0:T(8,128)(2,1)} %copy-done) | copy-start | bytes 9437188
  148.6 23.7 %collective-permute-start.11 = (f32[4,3,128,128]{3,2,1,0:T(8,128)S(1)}, f32[4,3,128,128]{3,2,1,0:T(8,128)S(1)}, u32[]{:S(2)}, u32[]{:S(2)}) collective-permute-start(f32[4,3,128,128]{3,2,1,0:T(8,128)S(1)} %collective-permute-done.5.rest_0_), channel_id=1, source_target_pairs={{0,8},{8,16},{16,24},{24,28},{28,20},{20,12},{12,4},{4,0},{1,9},{9... | collective-permute-start | bytes 2359304 | tf_op jit(solution)/shard_map/ppermute | solution.py:499
  149.4 24.2 %collective-permute-start.13 = (f32[4,3,128,128]{3,2,1,0:T(8,128)S(1)}, f32[4,3,128,128]{3,2,1,0:T(8,128)S(1)}, u32[]{:S(2)}, u32[]{:S(2)}) collective-permute-start(f32[4,3,128,128]{3,2,1,0:T(8,128)S(1)} %collective-permute-done.7.rest_1_), channel_id=1, source_target_pairs={{8,0},{16,8},{24,16},{28,24},{20,28},{12,20},{4,12},{0,4},{9,1},{1... | collective-permute-start | bytes 2359304 | tf_op jit(solution)/shard_map/ppermute | solution.py:500
  172.3 11.4 %collective-permute-start.12 = (f32[2,3,128,128]{3,2,1,0:T(8,128)S(1)}, f32[2,3,128,128]{3,2,1,0:T(8,128)S(1)}, u32[]{:S(2)}, u32[]{:S(2)}) collective-permute-start(f32[2,3,128,128]{3,2,1,0:T(8,128)S(1)} %slice.18), channel_id=1, source_target_pairs={{0,8},{8,16},{16,24},{24,28},{28,20},{20,12},{12,4},{4,0},{1,9},{9... | collective-permute-start | bytes 1179656 | tf_op jit(solution)/shard_map/ppermute | solution.py:505
  173.6 10.2 %collective-permute-start.14 = (f32[2,3,128,128]{3,2,1,0:T(8,128)S(1)}, f32[2,3,128,128]{3,2,1,0:T(8,128)S(1)}, u32[]{:S(2)}, u32[]{:S(2)}) collective-permute-start(f32[2,3,128,128]{3,2,1,0:T(8,128)S(1)} %slice.19), channel_id=1, source_target_pairs={{8,0},{16,8},{24,16},{28,24},{20,28},{12,20},{4,12},{0,4},{9,1},{1... | collective-permute-start | bytes 1179656 | tf_op jit(solution)/shard_map/ppermute | solution.py:505

commit v7 on v6

--- a/solution.py
+++ b/solution.py
@@ -53,87 +53,50 @@
     return pl.BlockSpec(array.shape, lambda *_: (0,) * rank)
 
 
-def lead_slices(devices):
-    height = max(8, 4 * TILE // devices)
-    return 4 * TILE // height, height
-
-
-def notes_kernel(
-    owners, place, dest, slot, count, child_ref, front_ref, out_ref, tile_ref, sem
-):
-    slots = dest.shape[0]
-    height = out_ref.shape[1] - NOTE
-    each = TILE // height
-    live = jnp.minimum(count[0], slots)
-    out_ref[:, :NOTE] = jnp.full((out_ref.shape[0], NOTE, TILE), -1.0, jnp.float32)
-    out_ref[:, NOTE:] = jnp.zeros((out_ref.shape[0], height, TILE), jnp.float32)
-
-    @pl.loop(0, live)
-    def _(k):
-        out_ref[dest[k], :NOTE] = jnp.full((NOTE, TILE), slot[k].astype(jnp.float32))
-
-    def add(i, tile):
-        copy = pltpu.make_async_copy(tile, tile_ref, sem)
-        copy.start()
-        copy.wait()
-        span = pl.ds(i * each, each)
-        out_ref[span, NOTE:] = out_ref[span, NOTE:] + tile_ref[...].reshape(each, height, TILE)
-
-    for i, owner in enumerate(owners):
-        pl.when(place[3] == owner)(functools.partial(add, i, front_ref.at[0, 0, 0, 0]))
-
-    @pl.loop(0, live)
-    def _(k):
-        for i, owner in enumerate(owners):
-            wanted = jnp.logical_and(slot[k] == 0, dest[k] == owner)
-            pl.when(wanted)(functools.partial(add, i, child_ref.at[k]))
-
-
-def make_notes(child_tiles, front, place, dest, slot, count, devices, owners):
-    _, height = lead_slices(devices)
-    hbm = pl.BlockSpec(memory_space=pltpu.HBM)
-    return pl.pallas_call(
-        functools.partial(notes_kernel, owners),
-        in_specs=[pl.BlockSpec(memory_space=pltpu.SMEM)] * 4 + [hbm, hbm],
-        out_specs=pl.BlockSpec(memory_space=pltpu.VMEM),
-        scratch_shapes=[pltpu.VMEM((TILE, TILE), jnp.float32), pltpu.SemaphoreType.DMA],
-        out_shape=jax.ShapeDtypeStruct((devices, NOTE + height, TILE), jnp.float32),
-        compiler_params=pltpu.CompilerParams(vmem_limit_bytes=VMEM),
-        name="notes",
-    )(place, dest, slot, count, child_tiles, front)
-
-
-def pack_kernel(dest, count, child_ref, out_ref, sems):
+def pack_kernel(dest, slot, count, child_ref, out_ref, notes_ref, sems, notes_sem):
     slots = child_ref.shape[0]
     live = jnp.minimum(count[0], slots)
 
     def copy(k):
-        return pltpu.make_async_copy(child_ref.at[k], out_ref.at[dest[k]], sems.at[k])
+        return pltpu.make_async_copy(
+            child_ref.at[k], out_ref.at[dest[k], pl.ds(0, TILE)], sems.at[k]
+        )
+
+    notes_ref[...] = jnp.full_like(notes_ref, -1.0)
 
     @pl.loop(0, live)
     def _(k):
         copy(k).start()
+        notes_ref[dest[k]] = jnp.full(notes_ref.shape[1:], slot[k].astype(jnp.float32))
+
+    notes = pltpu.make_async_copy(notes_ref, out_ref.at[:, pl.ds(TILE, NOTE)], notes_sem)
+    notes.start()
+    notes.wait()
 
     @pl.loop(0, live)
     def _(k):
         copy(k).wait()
 
 
-def pack(child_tiles, dest, count, devices):
+def pack(child_tiles, dest, slot, count, devices):
     slots = child_tiles.shape[0]
     return pl.pallas_call(
         pack_kernel,
-        in_specs=[pl.BlockSpec(memory_space=pltpu.SMEM)] * 2
+        in_specs=[pl.BlockSpec(memory_space=pltpu.SMEM)] * 3
         + [pl.BlockSpec(memory_space=pltpu.VMEM)],
         out_specs=pl.BlockSpec(memory_space=pltpu.HBM),
-        scratch_shapes=[pltpu.SemaphoreType.DMA((slots,))],
-        out_shape=jax.ShapeDtypeStruct((devices, TILE, TILE), jnp.float32),
+        scratch_shapes=[
+            pltpu.VMEM((devices, NOTE, TILE), jnp.float32),
+            pltpu.SemaphoreType.DMA((slots,)),
+            pltpu.SemaphoreType.DMA,
+        ],
+        out_shape=jax.ShapeDtypeStruct((devices, TILE + NOTE, TILE), jnp.float32),
         compiler_params=pltpu.CompilerParams(vmem_limit_bytes=VMEM),
         name="pack",
-    )(dest, count, child_tiles)
-
-
-def columns_kernel(place, slot_in, front_ref, incoming_ref, out_ref, *rest):
+    )(dest, slot, count, child_tiles)
+
+
+def columns_kernel(place, slot_in, front_ref, incoming_ref, out_ref, top_ref, *rest):
     *parts, tile_ref, sem = rest
     cols = place[2]
     strip = pltpu.make_async_copy(front_ref.at[:, 0, 0, 0], out_ref, sem)
@@ -146,12 +109,13 @@
 
         @pl.when(jnp.logical_and(slot >= 0, lax.rem(slot, cols) == 0))
         def _():
-            copy = pltpu.make_async_copy(incoming_ref.at[s], tile_ref, sem)
+            copy = pltpu.make_async_copy(incoming_ref.at[s, pl.ds(0, TILE)], tile_ref, sem)
             copy.start()
             copy.wait()
             row = lax.div(slot, cols)
             out_ref[row] = out_ref[row] + tile_ref[...]
 
+    top_ref[...] = out_ref[0]
     count = len(parts)
     for j, part_ref in enumerate(parts):
         group = part_ref.shape[0]
@@ -161,7 +125,7 @@
 
 def assemble_columns(front, incoming, place, slot_in, parts):
     rows = front.shape[0]
-    shapes = [(rows, TILE, TILE)] + [(rows // parts, TILE, TILE)] * parts
+    shapes = [(rows, TILE, TILE), (TILE, TILE)] + [(rows // parts, TILE, TILE)] * parts
     out_shape = [jax.ShapeDtypeStruct(shape, jnp.float32) for shape in shapes]
     return pl.pallas_call(
         columns_kernel,
@@ -346,7 +310,7 @@
                 def _(i):
                     s = order[2 * i]
                     copy = pltpu.make_async_copy(
-                        incoming_ref.at[s], child_ref.at[s], child_sems.at[s]
+                        incoming_ref.at[s, pl.ds(0, TILE)], child_ref.at[s], child_sems.at[s]
                     )
                     act(copy, j, s, order[2 * i + 1])
 
@@ -453,28 +417,28 @@
     owners = [r * n_col + c for r in (2, 3) for c in (0, 1)]
     place = jnp.stack([my_row, my_col, jnp.int32(cols_here), my_row * n_col + my_col])
 
-    dest = tile_dest[:, 0]
-    notes = make_notes(child_tiles, front, place, dest, tile_slot, tile_count, devices, owners)
-    notes = lax.all_to_all(notes, BOTH, split_axis=0, concat_axis=0, tiled=True)
-    slot_in = notes[:, 0, 0].astype(jnp.int32)
-    lead = jnp.broadcast_to(jnp.sum(notes[:, NOTE:], axis=0)[None], notes[:, NOTE:].shape)
-    lead = lax.all_to_all(lead, BOTH, split_axis=0, concat_axis=0, tiled=True)
-    lead = lead[: lead_slices(devices)[0]].reshape(2, 2, TILE, TILE)
-
-    outgoing = pack(child_tiles, dest, tile_count, devices)
-    outgoing, slot_in = lax.optimization_barrier((outgoing, slot_in))
+    outgoing = pack(child_tiles, tile_dest[:, 0], tile_slot, tile_count, devices)
     incoming = lax.all_to_all(outgoing, BOTH, split_axis=0, concat_axis=0, tiled=True)
-    incoming, lead = lax.optimization_barrier((incoming, lead))
+    slot_in = lax.optimization_barrier(incoming[:, TILE, 0].astype(jnp.int32))
 
     ring = rows_here % n_col == 0
-    mine, *parts = assemble_columns(front, incoming, place, slot_in, n_col if ring else 1)
+    mine, top, *parts = assemble_columns(front, incoming, place, slot_in, n_col if ring else 1)
+
+    slices = top.reshape(devices, TILE // devices, TILE)
+    slices = lax.all_to_all(slices, BOTH, split_axis=0, concat_axis=0, tiled=True)
+    slices = jnp.stack([slices[owner] for owner in owners])
+    slices = jnp.broadcast_to(slices[None], (devices,) + slices.shape)
+
+    def hand_on(slices):
+        lead = lax.all_to_all(slices, BOTH, split_axis=0, concat_axis=0, tiled=True)
+        return lead.transpose(1, 0, 2, 3).reshape(2, 2, TILE, TILE)
 
     def exchange(mine):
         near = lax.ppermute(mine, "col", [(c, c ^ 1) for c in range(n_col)])
         far = lax.ppermute(mine, "col", [(c, c ^ 2) for c in range(n_col)])
         return [near, far, lax.ppermute(far, "col", [(c, c ^ 1) for c in range(n_col)])]
 
-    def own_panels(mine):
+    def own_panels(mine, lead):
         return row_panels(mine, exchange(mine), lead, diag_inverses, place, slot_in, front)
 
     sets = n_row // n_col
@@ -487,17 +451,20 @@
                 for c in range(n_col)
             ]
             arrived.append(lax.ppermute(part, BOTH, pairs))
-        arrived, mine = lax.optimization_barrier((arrived, mine))
+        arrived, mine, slices = lax.optimization_barrier((arrived, mine, slices))
         piece = jnp.stack(arrived)
         circle = list(range(0, n_row, 2)) + list(range(n_row - 1, 0, -2))
         up = [(circle[i], circle[(i + 1) % n_row]) for i in range(n_row)]
         down = [(b, a) for a, b in up]
         rounds = [[(piece, 0)]]
-        panels = own_panels(mine)
+        lead = hand_on(slices)
         ahead = behind = piece
         for step in range(1, n_row // 2):
             ahead = lax.ppermute(ahead, "row", up)
             behind = lax.ppermute(behind, "row", down)
+            if step == 1:
+                ahead, behind, lead = lax.optimization_barrier((ahead, behind, lead))
+                panels = own_panels(mine, lead)
             if step == 2:
                 ahead, behind, panels = lax.optimization_barrier((ahead, behind, panels))
             rounds.append([(ahead, -step), (behind, step)])
@@ -521,7 +488,7 @@
         ]
         moved = lax.all_gather(lax.ppermute(parts[0], BOTH, pairs), "row", axis=0, tiled=False)
         rounds = [[(moved[h * n_col : (h + 1) * n_col], h)] for h in range(sets)]
-        panels = own_panels(mine)
+        panels = own_panels(mine, hand_on(slices))
 
         def described(row, h):
             return [a * sets + h for a in range(rows_here)], list(range(n_col))

time: 191 us -> 184 us (0.963)
  blocking collectives: 71.4 us -> 0 us
  waiting for transfers between devices: 38.8 us -> 85.9 us
  starting transfers between devices: 20.8 us -> 35.5 us
  local copies, waits for them, and re-layouts: 6.02 us -> 7.99 us
    all_to_all x2 -> x0, blocking collectives: 71.4 us -> none  [the longest x1 50.9 us: body(): lax.all_to_all(outgoing, BOTH, split_axis=0, concat_axis=0, tiled=True)]
    all_to_all x1 -> x3, waiting for transfers between devices: 7.04 us -> 72.2 us  [the longest x1 51.5 us: body(): lax.all_to_all(outgoing, BOTH, split_axis=0, concat_axis=0, tiled=True)]
    ppermute x1, waiting for transfers between devices: 16.1 us -> 0.01 us  [exchange(): far = lax.ppermute(mine, 'col', [(c, c ^ 2) for c in range(n_col)])]
    all_to_all x1 -> x3, starting transfers between devices: 2.64 us -> 16.1 us  [the longest x1 7.1 us: body(): lax.all_to_all(outgoing, BOTH, split_axis=0, concat_axis=0, tiled=True)]
    ppermute x3, waiting for transfers between devices: 7.46 us -> 0.56 us  [body(): behind = lax.ppermute(behind, 'row', down)]
    ppermute x3, waiting for transfers between devices: 0.94 us -> 7.46 us  [body(): ahead = lax.ppermute(ahead, 'row', up)]
    unnamed x20 -> x18, local copies, waits for them, and re-layouts: 5.24 us -> 5.52 us
  transfers between devices with their start and end apart: 16 -> 18, of which waited for: 8 -> 8; matrix products, arithmetic and copies ran while one was open for 1% -> 2% of each run, Pallas kernels for 21% -> 22%
where the time goes in v7:
time: 184 us
  waiting for transfers between devices  85.9 us (47%)
  Pallas kernels  51 us (28%)
  starting transfers between devices  35.5 us (19%)
  local copies, waits for them, and re-layouts  7.99 us (4%)
  other arithmetic  2.07 us (1%)
    all_to_all x1, waiting for transfers between devices, body(): lax.all_to_all(outgoing, BOTH, split_axis=0, concat_axis=0, tiled=True)  51.5 us
    pallas_call x4, Pallas kernels, trailing(): pl.pallas_call(functools.partial(trailing_kernel, first, len(pieces)), in...  37.1 us
    all_to_all x1, waiting for transfers between devices, hand_on(): lead = lax.all_to_all(slices, BOTH, split_axis=0, concat_axis=0, tiled=True)  20.7 us
    pallas_call x1, Pallas kernels, row_panels(): pl.pallas_call(row_panels_kernel, grid_spec=pltpu.PrefetchScalarGridSpec(...  8.6 us
    ppermute x4, starting transfers between devices, body(): arrived.append(lax.ppermute(part, BOTH, pairs))  7.78 us
    ppermute x3, waiting for transfers between devices, body(): ahead = lax.ppermute(ahead, 'row', up)  7.46 us
    all_to_all x1, starting transfers between devices, body(): lax.all_to_all(outgoing, BOTH, split_axis=0, concat_axis=0, tiled=True)  7.1 us
    ppermute x4, waiting for transfers between devices, body(): arrived.append(lax.ppermute(part, BOTH, pairs))  5.59 us
  transfers between devices with their start and end apart: 18, of which 8 were waited for; matrix products, arithmetic and copies ran while one was open for 2% of the time, Pallas kernels for 22%

profile of v7, /device:TPU:0, one launch (start us, length us, event | category | flops | bytes accessed | tf_op | source)
XLA Modules:
  0.0 183.5 jit_solution(13804958807592105234)
XLA Ops:
  0.0 0.0 copy-start.5
  0.0 0.0 copy-start.6
  0.7 0.0 copy-start.3
  0.7 1.2 copy-done.3
  1.9 0.0 copy-start.7
  1.9 0.7 copy-done.7
  2.6 0.7 copy-done.8
  3.2 2.1 %pack.1 = f32[32,136,128]{2,1,0:T(8,128)S(1)} custom-call(s32[16]{0:T(128)S(1)} %bitcast.12, s32[16]{0:T(128)S(1)} %copy-done.8, s32[1]{0:T(128)S(6)} %copy.18.count, f32[16,128,128]{2,1,0:T(8,128)S(1)} %copy-done.3), custom_call_target="tpu_custom_call" | custom-call | tf_op jit(solution)/shard_map/pack/pallas_call | solution.py:83
  5.3 0.0 copy-start.2
  5.4 1.4 copy-done.2
  6.7 7.1 %all-to-all-start = ((f32[32,136,128]{2,1,0:T(8,128)}), f32[32,136,128]{2,1,0:T(8,128)S(1)}, u32[]{:S(2)}, u32[]{:S(2)}) async-start(f32[32,136,128]{2,1,0:T(8,128)} %copy-done.2), calls=%async_computation | async-start | bytes 4456448 | tf_op jit(solution)/shard_map/all_to_all | solution.py:421
  13.8 0.1 pad_add_fusion.place
  13.9 51.5 %all-to-all-done.incoming_ref.rest_4_.rest_3_.rest_2_ = f32[32,136,128]{2,1,0:T(8,128)S(1)} async-done(((f32[32,136,128]{2,1,0:T(8,128)}), f32[32,136,128]{2,1,0:T(8,128)S(1)}, u32[]{:S(2)}, u32[]{:S(2)}) %all-to-all-start) | async-done | bytes 2228256 | tf_op jit(solution)/shard_map/all_to_all | solution.py:421
  65.4 0.7 fusion.slot_in
  66.1 3.2 %panel_columns.1 = (f32[12,128,128]{2,1,0:T(8,128)}, f32[128,128]{1,0:T(8,128)}, f32[3,128,128]{2,1,0:T(8,128)S(1)}, f32[3,128,128]{2,1,0:T(8,128)S(1)}, f32[3,1...) custom-call(s32[4]{0:T(128)S(1)} %pad_add_fusion.place, s32[32]{0:T(128)S(1)} %fusion.slot_in, ...), custom_call_target="tpu_custom_call" | custom-call | tf_op jit(solution)/shard_map/panel_columns/pallas_call | solution.py:130
  69.3 4.4 %all-to-all-start.1 = ((f32[32,4,128]{2,1,0:T(4,128)}), f32[32,4,128]{2,1,0:T(4,128)}, u32[]{:S(2)}, u32[]{:S(2)}) async-start(f32[32,4,128]{2,1,0:T(4,128)} %bitcast.4), calls=%async_computation.1 | async-start | bytes 131072 | tf_op jit(solution)/shard_map/all_to_all | solution.py:428
  73.8 1.3 collective-permute-start
  75.1 2.4 %collective-permute-start.1 = (f32[3,128,128]{2,1,0:T(8,128)S(1)}, f32[3,128,128]{2,1,0:T(8,128)}, u32[]{:S(2)}, u32[]{:S(2)}) collective-permute-start(f32[3,128,128]{2,1,0:T(8,128)S(1)} %get-tuple-element.33), channel_id=1, source_target_pairs={{0,4},{1,8},{2,12},{3,0},{4,5},{5,9},{6,13},{7,1},{8,6},{9,10},{10... | collective-permute-start | bytes 589832 | tf_op jit(solution)/shard_map/ppermute | solution.py:453
  77.6 3.5 %collective-permute-start.2 = (f32[3,128,128]{2,1,0:T(8,128)S(1)}, f32[3,128,128]{2,1,0:T(8,128)}, u32[]{:S(2)}, u32[]{:S(2)}) collective-permute-start(f32[3,128,128]{2,1,0:T(8,128)S(1)} %get-tuple-element.34), channel_id=1, source_target_pairs={{0,8},{1,12},{2,0},{3,4},{4,9},{5,13},{6,1},{7,5},{8,10},{9,14},{1... | collective-permute-start | bytes 589832 | tf_op jit(solution)/shard_map/ppermute | solution.py:453
  81.0 0.5 collective-permute-start.3
  81.6 0.0 all-to-all-done.1
  81.6 0.7 fusion.1
  82.2 0.0 collective-permute-done
  82.3 4.3 %collective-permute-done.1 = f32[3,128,128]{2,1,0:T(8,128)} collective-permute-done((f32[3,128,128]{2,1,0:T(8,128)S(1)}, f32[3,128,128]{2,1,0:T(8,128)}, u32[]{:S(2)}, u32[]{:S(2)}) %collective-permute-start.1) | collective-permute-done | bytes 196640 | tf_op jit(solution)/shard_map/ppermute | solution.py:453
  86.6 0.6 collective-permute-done.2
  87.2 0.6 collective-permute-done.3
  87.8 0.7 broadcast_in_dim.2
  88.6 2.7 %collective-permute-start.9 = (f32[12,128,128]{2,1,0:T(8,128)}, f32[12,128,128]{2,1,0:T(8,128)}, u32[]{:S(2)}, u32[]{:S(2)}) collective-permute-start(f32[12,128,128]{2,1,0:T(8,128)} %get-tuple-element.45.t0), channel_id=1, source_target_pairs={{0,2},{1,3},{2,0},{3,1},{4,6},{5,7},{6,4},{7,5},{8,10},{9,11},{10,... | collective-permute-start | bytes 2359304 | tf_op jit(solution)/shard_map/ppermute | solution.py:438
  91.3 1.3 pad_maximum_fusion.rest_0_
  92.6 1.4 collective-permute-start.5
  94.0 0.7 collective-permute-start.4
  94.7 4.6 %all-to-all-start.2 = ((f32[32,4,4,128]{3,2,1,0:T(4,128)}), f32[32,4,4,128]{3,2,1,0:T(4,128)}, u32[]{:S(2)}, u32[]{:S(2)}) async-start(f32[32,4,4,128]{3,2,1,0:T(4,128)} %broadcast_in_dim.2), calls=%async_computation.2 | async-start | bytes 524288 | tf_op jit(solution)/shard_map/all_to_all | solution.py:433
  99.2 0.2 collective-permute-start.8
  99.5 20.7 %all-to-all-done.2 = f32[32,4,4,128]{3,2,1,0:T(4,128)} async-done(((f32[32,4,4,128]{3,2,1,0:T(4,128)}), f32[32,4,4,128]{3,2,1,0:T(4,128)}, u32[]{:S(2)}, u32[]{:S(2)}) %all-to-all-start.2) | async-done | bytes 262176 | tf_op jit(solution)/shard_map/all_to_all | solution.py:433
  120.1 1.0 copy.13
  121.1 0.0 collective-permute-done.9.t2
  121.1 0.4 collective-permute-start.10
  121.6 0.0 collective-permute-done.5.rest_2_
  121.6 0.0 collective-permute-done.4.rest_1_
  121.6 0.7 collective-permute-start.6
  122.3 1.3 collective-permute-start.7
  123.6 0.0 collective-permute-done.8.t1
  123.6 0.1 collective-permute-done.10.t3
  123.7 0.0 copy-done.4
  123.7 8.6 %row_panels.1 = (bf16[1536,1024]{1,0:T(8,128)(2,1)S(1)}, f32[12,1,24,1,128,128]{5,4,3,2,1,0:T(8,128)}, bf16[3,256,768]{2,1,0:T(8,128)(2,1)S(1)}, s32[64]{0:T(128)S(1)}, s32[25]{0:T(128)S(1)}) custom-call(s32[4]{0:T(128)S(1)} %pad_add_fusion.place, s32[32]{0:T(128)S(1)} %fusion.slot_in, f32[12,128,128]{2,1,0:T(8,128)} %get-tuple-element.45.t0, ...), custom_call_target="tpu_custom_call" | custom-call | tf_op jit(solution)/shard_map/row_panels/pallas_call | solution.py:233
  132.3 1.6 copy-done
  133.9 7.5 %collective-permute-done.6.rest_0_ = f32[4,3,128,128]{3,2,1,0:T(8,128)S(1)} collective-permute-done((f32[4,3,128,128]{3,2,1,0:T(8,128)}, f32[4,3,128,128]{3,2,1,0:T(8,128)S(1)}, u32[]{:S(2)}, u32[]{:S(2)}) %collective-permute-start.6) | collective-permute-done | bytes 786464 | tf_op jit(solution)/shard_map/ppermute | solution.py:463
  141.4 0.6 collective-permute-done.7.rest_1_
  141.9 0.3 collective-permute-start.11
  142.3 1.7 collective-permute-start.13
  144.0 0.0 copy-done.5
  144.0 0.0 copy-done.6
  144.0 13.7 %trailing.4.rest_4_ = f32[12,1,24,1,128,128]{5,4,3,2,1,0:T(8,128)} custom-call(s32[4]{0:T(128)S(1)} %pad_add_fusion.place, s32[192]{0:T(256)S(1)} %copy-done.6, s32[256]{0:T(256)S(1)} %copy-done.5, s32[64]{0:T(128)S(1)} %get-tuple-element.52.order, s32[25]{0:T(128)S(1)} %get-tuple-element.53.starts, ...), custom_call_target="tpu_custom_call", output_to_operand_aliasing={{}: (12, {})} | custom-call | flops 14495514624 | bytes 14155776 | tf_op jit(solution)/shard_map/trailing/pallas_call | solution.py:384
  157.7 0.0 copy-done.1
  157.7 8.5 %trailing.5.rest_4_ = f32[12,1,24,1,128,128]{5,4,3,2,1,0:T(8,128)} custom-call(s32[4]{0:T(128)S(1)} %pad_add_fusion.place, s32[192]{0:T(256)S(1)} %copy-done.6, s32[256]{0:T(256)S(1)} %copy-done.5, s32[64]{0:T(128)S(1)} %get-tuple-element.52.order, s32[25]{0:T(128)S(1)} %get-tuple-element.53.starts, ...), custom_call_target="tpu_custom_call", output_to_operand_aliasing={{}: (11, {})} | custom-call | flops 9663676416 | bytes 9437184 | tf_op jit(solution)/shard_map/trailing/pallas_call | solution.py:384
  166.2 0.0 collective-permute-done.11.rest_0_
  166.2 1.7 collective-permute-start.12
  168.0 0.0 collective-permute-done.13.rest_1_
  168.0 0.4 collective-permute-start.14
  168.4 8.8 %trailing.6.rest_3_ = f32[12,1,24,1,128,128]{5,4,3,2,1,0:T(8,128)} custom-call(s32[4]{0:T(128)S(1)} %pad_add_fusion.place, s32[192]{0:T(256)S(1)} %copy-done.6, s32[256]{0:T(256)S(1)} %copy-done.5, s32[64]{0:T(128)S(1)} %get-tuple-element.52.order, s32[25]{0:T(128)S(1)} %get-tuple-element.53.starts, ...), custom_call_target="tpu_custom_call", output_to_operand_aliasing={{}: (11, {})} | custom-call | flops 9663676416 | bytes 9437184 | tf_op jit(solution)/shard_map/trailing/pallas_call | solution.py:384
  177.2 0.0 collective-permute-done.12
  177.2 0.0 collective-permute-done.14
  177.2 0.1 pad_maximum_fusion.1.rest_0_
  177.3 6.1 %trailing.7 = f32[12,1,24,1,128,128]{5,4,3,2,1,0:T(8,128)} custom-call(s32[4]{0:T(128)S(1)} %pad_add_fusion.place, s32[192]{0:T(256)S(1)} %copy-done.6, s32[256]{0:T(256)S(1)} %copy-done.5, s32[64]{0:T(128)S(1)} %get-tuple-element.52.order, s32[25]{0:T(128)S(1)} %get-tuple-element.53.starts, ...), custom_call_target="tpu_custom_call", output_to_operand_aliasing={{}: (10, {})} | custom-call | flops 4831838208 | bytes 4718592 | tf_op jit(solution)/shard_map/trailing/pallas_call | solution.py:384
  (7 shorter events, 0.1 us)
Async XLA Ops:
  0.0 144.0 %copy-start.5 = (s32[256]{0:T(256)S(1)}, s32[256]{0:T(256)}, u32[]{:S(2)}) copy-start(s32[256]{0:T(256)} %constant.18.clone.places_table) | copy-start | bytes 3076
  0.0 144.0 %copy-start.6 = (s32[192]{0:T(256)S(1)}, s32[192]{0:T(256)}, u32[]{:S(2)}) copy-start(s32[192]{0:T(256)} %constant.17.clone.columns_table) | copy-start | bytes 2308
  0.7 1.2 copy-start.3
  1.9 0.7 copy-start.7
  2.6 0.7 copy-start.8
  3.2 120.5 %copy-start.4 = (f32[2,256,256]{2,1,0:T(8,128)S(1)}, f32[2,256,256]{2,1,0:T(8,128)}, u32[]{:S(2)}) copy-start(f32[2,256,256]{2,1,0:T(8,128)} %diag_ref.1) | copy-start | bytes 1572868
  5.3 1.4 copy-start.2
  6.7 58.7 %all-to-all-start = ((f32[32,136,128]{2,1,0:T(8,128)}), f32[32,136,128]{2,1,0:T(8,128)S(1)}, u32[]{:S(2)}, u32[]{:S(2)}) async-start(f32[32,136,128]{2,1,0:T(8,128)} %copy-done.2), calls=%async_computation | async-start | bytes 4456448 | tf_op jit(solution)/shard_map/all_to_all | solution.py:421
  69.3 12.2 %all-to-all-start.1 = ((f32[32,4,128]{2,1,0:T(4,128)}), f32[32,4,128]{2,1,0:T(4,128)}, u32[]{:S(2)}, u32[]{:S(2)}) async-start(f32[32,4,128]{2,1,0:T(4,128)} %bitcast.4), calls=%async_computation.1 | async-start | bytes 131072 | tf_op jit(solution)/shard_map/all_to_all | solution.py:428
  73.8 8.5 %collective-permute-start = (f32[3,128,128]{2,1,0:T(8,128)S(1)}, f32[3,128,128]{2,1,0:T(8,128)}, u32[]{:S(2)}, u32[]{:S(2)}) collective-permute-start(f32[3,128,128]{2,1,0:T(8,128)S(1)} %get-tuple-element.32), channel_id=1, source_target_pairs={{0,0},{1,4},{2,8},{3,12},{4,1},{5,5},{6,9},{7,13},{8,2},{9,6},{10,... | collective-permute-start | bytes 589832 | tf_op jit(solution)/shard_map/ppermute | solution.py:453
  75.1 11.4 %collective-permute-start.1 = (f32[3,128,128]{2,1,0:T(8,128)S(1)}, f32[3,128,128]{2,1,0:T(8,128)}, u32[]{:S(2)}, u32[]{:S(2)}) collective-permute-start(f32[3,128,128]{2,1,0:T(8,128)S(1)} %get-tuple-element.33), channel_id=1, source_target_pairs={{0,4},{1,8},{2,12},{3,0},{4,5},{5,9},{6,13},{7,1},{8,6},{9,10},{10... | collective-permute-start | bytes 589832 | tf_op jit(solution)/shard_map/ppermute | solution.py:453
  77.6 9.7 %collective-permute-start.2 = (f32[3,128,128]{2,1,0:T(8,128)S(1)}, f32[3,128,128]{2,1,0:T(8,128)}, u32[]{:S(2)}, u32[]{:S(2)}) collective-permute-start(f32[3,128,128]{2,1,0:T(8,128)S(1)} %get-tuple-element.34), channel_id=1, source_target_pairs={{0,8},{1,12},{2,0},{3,4},{4,9},{5,13},{6,1},{7,5},{8,10},{9,14},{1... | collective-permute-start | bytes 589832 | tf_op jit(solution)/shard_map/ppermute | solution.py:453
  81.0 6.8 %collective-permute-start.3 = (f32[3,128,128]{2,1,0:T(8,128)S(1)}, f32[3,128,128]{2,1,0:T(8,128)}, u32[]{:S(2)}, u32[]{:S(2)}) collective-permute-start(f32[3,128,128]{2,1,0:T(8,128)S(1)} %get-tuple-element.35), channel_id=1, source_target_pairs={{0,12},{1,0},{2,4},{3,8},{4,13},{5,1},{6,5},{7,9},{8,14},{9,2},{10... | collective-permute-start | bytes 589832 | tf_op jit(solution)/shard_map/ppermute | solution.py:453
  88.6 32.6 %collective-permute-start.9 = (f32[12,128,128]{2,1,0:T(8,128)}, f32[12,128,128]{2,1,0:T(8,128)}, u32[]{:S(2)}, u32[]{:S(2)}) collective-permute-start(f32[12,128,128]{2,1,0:T(8,128)} %get-tuple-element.45.t0), channel_id=1, source_target_pairs={{0,2},{1,3},{2,0},{3,1},{4,6},{5,7},{6,4},{7,5},{8,10},{9,11},{10,... | collective-permute-start | bytes 2359304 | tf_op jit(solution)/shard_map/ppermute | solution.py:438
  92.6 29.0 %collective-permute-start.5 = (f32[4,3,128,128]{3,2,1,0:T(8,128)S(1)}, f32[4,3,128,128]{3,2,1,0:T(8,128)}, u32[]{:S(2)}, u32[]{:S(2)}) collective-permute-start(f32[4,3,128,128]{3,2,1,0:T(8,128)S(1)} %pad_maximum_fusion.rest_0_), channel_id=1, source_target_pairs={{8,0},{16,8},{24,16},{28,24},{20,28},{12,20},{4,12},{0,4},{9,1},{1... | collective-permute-start | bytes 2359304 | tf_op jit(solution)/shard_map/ppermute | solution.py:464
  94.0 27.6 %collective-permute-start.4 = (f32[4,3,128,128]{3,2,1,0:T(8,128)S(1)}, f32[4,3,128,128]{3,2,1,0:T(8,128)}, u32[]{:S(2)}, u32[]{:S(2)}) collective-permute-start(f32[4,3,128,128]{3,2,1,0:T(8,128)S(1)} %pad_maximum_fusion.rest_0_), channel_id=1, source_target_pairs={{0,8},{8,16},{16,24},{24,28},{28,20},{20,12},{12,4},{4,0},{1,9},{9... | collective-permute-start | bytes 2359304 | tf_op jit(solution)/shard_map/ppermute | solution.py:463
  94.7 25.5 %all-to-all-start.2 = ((f32[32,4,4,128]{3,2,1,0:T(4,128)}), f32[32,4,4,128]{3,2,1,0:T(4,128)}, u32[]{:S(2)}, u32[]{:S(2)}) async-start(f32[32,4,4,128]{3,2,1,0:T(4,128)} %broadcast_in_dim.2), calls=%async_computation.2 | async-start | bytes 524288 | tf_op jit(solution)/shard_map/all_to_all | solution.py:433
  99.2 24.4 %collective-permute-start.8 = (f32[12,128,128]{2,1,0:T(8,128)}, f32[12,128,128]{2,1,0:T(8,128)}, u32[]{:S(2)}, u32[]{:S(2)}) collective-permute-start(f32[12,128,128]{2,1,0:T(8,128)} %get-tuple-element.45.t0), channel_id=1, source_target_pairs={{0,1},{1,0},{2,3},{3,2},{4,5},{5,4},{6,7},{7,6},{8,9},{9,8},{10,11... | collective-permute-start | bytes 2359304 | tf_op jit(solution)/shard_map/ppermute | solution.py:437
  121.1 2.6 %collective-permute-start.10 = (f32[12,128,128]{2,1,0:T(8,128)}, f32[12,128,128]{2,1,0:T(8,128)S(1)}, u32[]{:S(2)}, u32[]{:S(2)}) collective-permute-start(f32[12,128,128]{2,1,0:T(8,128)} %collective-permute-done.9.t2), channel_id=1, source_target_pairs={{0,1},{1,0},{2,3},{3,2},{4,5},{5,4},{6,7},{7,6},{8,9},{9,8},{10,11... | collective-permute-start | bytes 2359304 | tf_op jit(solution)/shard_map/ppermute | solution.py:439
  121.6 19.8 %collective-permute-start.6 = (f32[4,3,128,128]{3,2,1,0:T(8,128)}, f32[4,3,128,128]{3,2,1,0:T(8,128)S(1)}, u32[]{:S(2)}, u32[]{:S(2)}) collective-permute-start(f32[4,3,128,128]{3,2,1,0:T(8,128)} %collective-permute-done.4.rest_1_), channel_id=1, source_target_pairs={{0,8},{8,16},{16,24},{24,28},{28,20},{20,12},{12,4},{4,0},{1,9},{9... | collective-permute-start | bytes 2359304 | tf_op jit(solution)/shard_map/ppermute | solution.py:463
  122.3 19.6 %collective-permute-start.7 = (f32[4,3,128,128]{3,2,1,0:T(8,128)}, f32[4,3,128,128]{3,2,1,0:T(8,128)S(1)}, u32[]{:S(2)}, u32[]{:S(2)}) collective-permute-start(f32[4,3,128,128]{3,2,1,0:T(8,128)} %collective-permute-done.5.rest_2_), channel_id=1, source_target_pairs={{8,0},{16,8},{24,16},{28,24},{20,28},{12,20},{4,12},{0,4},{9,1},{1... | collective-permute-start | bytes 2359304 | tf_op jit(solution)/shard_map/ppermute | solution.py:464
  132.3 1.6 copy-start
  141.9 15.7 %copy-start.1 = (bf16[1536,1024]{1,0:T(8,128)(2,1)S(1)}, bf16[1536,1024]{1,0:T(8,128)(2,1)}, u32[]{:S(2)}) copy-start(bf16[1536,1024]{1,0:T(8,128)(2,1)} %copy-done) | copy-start | bytes 9437188
  141.9 24.3 %collective-permute-start.11 = (f32[4,3,128,128]{3,2,1,0:T(8,128)S(1)}, f32[4,3,128,128]{3,2,1,0:T(8,128)S(1)}, u32[]{:S(2)}, u32[]{:S(2)}) collective-permute-start(f32[4,3,128,128]{3,2,1,0:T(8,128)S(1)} %collective-permute-done.6.rest_0_), channel_id=1, source_target_pairs={{0,8},{8,16},{16,24},{24,28},{28,20},{20,12},{12,4},{4,0},{1,9},{9... | collective-permute-start | bytes 2359304 | tf_op jit(solution)/shard_map/ppermute | solution.py:463
  142.3 25.7 %collective-permute-start.13 = (f32[4,3,128,128]{3,2,1,0:T(8,128)S(1)}, f32[4,3,128,128]{3,2,1,0:T(8,128)S(1)}, u32[]{:S(2)}, u32[]{:S(2)}) collective-permute-start(f32[4,3,128,128]{3,2,1,0:T(8,128)S(1)} %collective-permute-done.7.rest_1_), channel_id=1, source_target_pairs={{8,0},{16,8},{24,16},{28,24},{20,28},{12,20},{4,12},{0,4},{9,1},{1... | collective-permute-start | bytes 2359304 | tf_op jit(solution)/shard_map/ppermute | solution.py:464
  166.2 11.0 %collective-permute-start.12 = (f32[2,3,128,128]{3,2,1,0:T(8,128)S(1)}, f32[2,3,128,128]{3,2,1,0:T(8,128)S(1)}, u32[]{:S(2)}, u32[]{:S(2)}) collective-permute-start(f32[2,3,128,128]{3,2,1,0:T(8,128)S(1)} %slice.27), channel_id=1, source_target_pairs={{0,8},{8,16},{16,24},{24,28},{28,20},{20,12},{12,4},{4,0},{1,9},{9... | collective-permute-start | bytes 1179656 | tf_op jit(solution)/shard_map/ppermute | solution.py:472
  168.0 9.2 %collective-permute-start.14 = (f32[2,3,128,128]{3,2,1,0:T(8,128)S(1)}, f32[2,3,128,128]{3,2,1,0:T(8,128)S(1)}, u32[]{:S(2)}, u32[]{:S(2)}) collective-permute-start(f32[2,3,128,128]{3,2,1,0:T(8,128)S(1)} %slice.28), channel_id=1, source_target_pairs={{8,0},{16,8},{24,16},{28,24},{20,28},{12,20},{4,12},{0,4},{9,1},{1... | collective-permute-start | bytes 1179656 | tf_op jit(solution)/shard_map/ppermute | solution.py:472

commit v8 on v7

--- a/solution.py
+++ b/solution.py
@@ -53,50 +53,36 @@
     return pl.BlockSpec(array.shape, lambda *_: (0,) * rank)
 
 
-def pack_kernel(dest, slot, count, child_ref, out_ref, notes_ref, sems, notes_sem):
-    slots = child_ref.shape[0]
-    live = jnp.minimum(count[0], slots)
-
-    def copy(k):
-        return pltpu.make_async_copy(
-            child_ref.at[k], out_ref.at[dest[k], pl.ds(0, TILE)], sems.at[k]
-        )
-
-    notes_ref[...] = jnp.full_like(notes_ref, -1.0)
-
-    @pl.loop(0, live)
+def pack_kernel(owners, me, dest, slot, count, child_ref, top_ref, out_ref, lead_ref):
+    out_ref[:, TILE:] = jnp.full((out_ref.shape[0], NOTE, TILE), -1.0, jnp.float32)
+    for i, owner in enumerate(owners):
+        lead_ref[i] = jnp.where(me[0] == owner, top_ref[...], 0.0)
+
+    @pl.loop(0, jnp.minimum(count[0], child_ref.shape[0]))
     def _(k):
-        copy(k).start()
-        notes_ref[dest[k]] = jnp.full(notes_ref.shape[1:], slot[k].astype(jnp.float32))
-
-    notes = pltpu.make_async_copy(notes_ref, out_ref.at[:, pl.ds(TILE, NOTE)], notes_sem)
-    notes.start()
-    notes.wait()
-
-    @pl.loop(0, live)
-    def _(k):
-        copy(k).wait()
-
-
-def pack(child_tiles, dest, slot, count, devices):
-    slots = child_tiles.shape[0]
+        out_ref[dest[k], :TILE] = child_ref[k]
+        out_ref[dest[k], TILE:] = jnp.full((NOTE, TILE), slot[k].astype(jnp.float32))
+        for i, owner in enumerate(owners):
+
+            @pl.when(jnp.logical_and(slot[k] == 0, dest[k] == owner))
+            def _():
+                lead_ref[i] = lead_ref[i] + child_ref[k]
+
+
+def pack(child_tiles, top, me, dest, slot, count, devices, owners):
+    shapes = [(devices, TILE + NOTE, TILE), (len(owners), TILE, TILE)]
+    spec = lambda space, n: [pl.BlockSpec(memory_space=space)] * n
     return pl.pallas_call(
-        pack_kernel,
-        in_specs=[pl.BlockSpec(memory_space=pltpu.SMEM)] * 3
-        + [pl.BlockSpec(memory_space=pltpu.VMEM)],
-        out_specs=pl.BlockSpec(memory_space=pltpu.HBM),
-        scratch_shapes=[
-            pltpu.VMEM((devices, NOTE, TILE), jnp.float32),
-            pltpu.SemaphoreType.DMA((slots,)),
-            pltpu.SemaphoreType.DMA,
-        ],
-        out_shape=jax.ShapeDtypeStruct((devices, TILE + NOTE, TILE), jnp.float32),
+        functools.partial(pack_kernel, owners),
+        in_specs=spec(pltpu.SMEM, 4) + spec(pltpu.VMEM, 2),
+        out_specs=spec(pltpu.VMEM, 2),
+        out_shape=[jax.ShapeDtypeStruct(shape, jnp.float32) for shape in shapes],
         compiler_params=pltpu.CompilerParams(vmem_limit_bytes=VMEM),
         name="pack",
-    )(dest, slot, count, child_tiles)
-
-
-def columns_kernel(place, slot_in, front_ref, incoming_ref, out_ref, top_ref, *rest):
+    )(me, dest, slot, count, child_tiles, top)
+
+
+def columns_kernel(place, slot_in, front_ref, incoming_ref, out_ref, *rest):
     *parts, tile_ref, sem = rest
     cols = place[2]
     strip = pltpu.make_async_copy(front_ref.at[:, 0, 0, 0], out_ref, sem)
@@ -115,7 +101,6 @@
             row = lax.div(slot, cols)
             out_ref[row] = out_ref[row] + tile_ref[...]
 
-    top_ref[...] = out_ref[0]
     count = len(parts)
     for j, part_ref in enumerate(parts):
         group = part_ref.shape[0]
@@ -125,7 +110,7 @@
 
 def assemble_columns(front, incoming, place, slot_in, parts):
     rows = front.shape[0]
-    shapes = [(rows, TILE, TILE), (TILE, TILE)] + [(rows // parts, TILE, TILE)] * parts
+    shapes = [(rows, TILE, TILE)] + [(rows // parts, TILE, TILE)] * parts
     out_shape = [jax.ShapeDtypeStruct(shape, jnp.float32) for shape in shapes]
     return pl.pallas_call(
         columns_kernel,
@@ -146,20 +131,20 @@
 
 
 def row_panels_kernel(
-    place, slot_in, t0, t1, t2, t3, lead_ref, diag_ref, pair_ref, out_ref, across_ref, order,
-    starts, small_ref, tiles_ref, cursor,
+    place, slot_in, tiles_ref, lead_ref, diag_ref, pair_ref, out_ref, across_ref, order, starts,
+    small_ref, cursor,
 ):
     step = pl.program_id(0)
     cols = starts.shape[0] - 1
     my_row, my_col = place[0], place[1]
-    group = t0.shape[0]
+    group = tiles_ref.shape[1]
     height = group * TILE
 
     @pl.when(step == 0)
     def _():
         small_ref[0] = stacked(diag_ref[0])
         lead = jnp.concatenate(
-            [jnp.concatenate([lead_ref[i, 0], lead_ref[i, 1]], axis=1) for i in range(2)], axis=0
+            [jnp.concatenate([lead_ref[i], lead_ref[i + 1]], axis=1) for i in (0, 2)], axis=0
         )
         lead = dot(deep(lead), small_ref[0])
         small_ref[1] = stacked(lead.T)
@@ -195,8 +180,6 @@
                 cursor[b] = i + 1
 
 
-    for i, tile_ref in enumerate((t0, t1, t2, t3)):
-        tiles_ref[jnp.bitwise_xor(my_col, i)] = tile_ref[...]
     columns = [tiles_ref[c].reshape(height, TILE) for c in range(4)]
     tile_row = lax.broadcasted_iota(jnp.int32, (height, PANEL), 0) // TILE
     first = jnp.logical_and(step == 0, tile_row == 0)
@@ -217,7 +200,7 @@
             out_ref[:, 0, 0, 0] = pieces[c].reshape(group, TILE, TILE)
 
 
-def row_panels(mine, others, lead, diag, place, slot_in, front):
+def row_panels(tiles, lead, diag, place, slot_in, front):
     rows = front.shape[0]
     cols = front.shape[2]
     group = rows // 3
@@ -229,13 +212,16 @@
         jax.ShapeDtypeStruct((2 * slot_in.shape[0],), jnp.int32),
         jax.ShapeDtypeStruct((cols + 1,), jnp.int32),
     ]
-    strip = pl.BlockSpec((group, TILE, TILE), lambda i, *_: (i, 0, 0))
     return pl.pallas_call(
         row_panels_kernel,
         grid_spec=pltpu.PrefetchScalarGridSpec(
             num_scalar_prefetch=2,
             grid=(3,),
-            in_specs=[strip] * 4 + [whole_spec(lead), whole_spec(diag)],
+            in_specs=[
+                pl.BlockSpec((4, group, TILE, TILE), lambda i, *_: (0, i, 0, 0)),
+                whole_spec(lead),
+                whole_spec(diag),
+            ],
             out_specs=[
                 pl.BlockSpec((height, 2 * WIDTH), lambda i, *_: (i, 0)),
                 pl.BlockSpec((group, 1, 1, 1, TILE, TILE), lambda i, *_: (i, 0, 0, 0, 0, 0)),
@@ -245,22 +231,26 @@
             ],
             scratch_shapes=[
                 pltpu.VMEM((3, 3 * PANEL, PANEL), jnp.bfloat16),
-                pltpu.VMEM((4, group, TILE, TILE), jnp.float32),
                 pltpu.SMEM((cols,), jnp.int32),
             ],
         ),
         out_shape=out_shape,
         compiler_params=pltpu.CompilerParams(vmem_limit_bytes=VMEM),
         name="row_panels",
-    )(place, slot_in, mine, *others, lead, diag)
+    )(place, slot_in, tiles, lead, diag)
 
 
 def trailing_kernel(
-    first, n_pieces, place, columns_table, places_table, order, starts, pair_ref, small_ref, *rest
+    first, n_held, halved, place, columns_table, places_table, order, starts, pair_ref, small_ref, *rest
 ):
-    piece_refs = rest[:n_pieces]
-    front_ref, incoming_ref, _, out_ref, right_ref, taken, given, child_ref = rest[n_pieces:-3]
-    take_sems, give_sems, child_sems = rest[-3:]
+    piece_refs = rest[:n_held]
+    front_ref, incoming_ref, _, out_ref, right_ref, taken, given, child_ref, *rest = rest[n_held:]
+    take_sems, give_sems, child_sems, *joined = rest
+    if halved:
+        joined[0][:2] = piece_refs[0][...]
+        joined[0][2:] = piece_refs[1][...]
+        piece_refs = joined
+    n_pieces = len(piece_refs)
     group = piece_refs[0].shape[1]
     count = n_pieces * group
     steps = (count + 1) // 2
@@ -374,7 +364,8 @@
     rows = front.shape[0]
     pair, out, small, order, starts = panels
     group = pieces[0].shape[1]
-    count = len(pieces) * group
+    halved = pieces[0].shape[0] == 2
+    count = group if halved else len(pieces) * group
     scalars = [place, *tables, order, starts]
     held = [pair, small, *pieces]
     distant = [front, incoming, out]
@@ -382,7 +373,7 @@
     height = rows * TILE
     devices = incoming.shape[0]
     return pl.pallas_call(
-        functools.partial(trailing_kernel, first, len(pieces)),
+        functools.partial(trailing_kernel, first, len(pieces), halved),
         in_specs=spec(pltpu.SMEM, 5) + spec(pltpu.VMEM, len(held)) + spec(pltpu.HBM, 3),
         out_specs=pl.BlockSpec(memory_space=pltpu.HBM),
         scratch_shapes=[
@@ -393,7 +384,8 @@
             pltpu.SemaphoreType.DMA((2, 2)),
             pltpu.SemaphoreType.DMA((2, 2)),
             pltpu.SemaphoreType.DMA((devices,)),
-        ],
+        ]
+        + [pltpu.VMEM((4, group, TILE, TILE), jnp.float32)] * halved,
         out_shape=jax.ShapeDtypeStruct(front.shape, jnp.float32),
         input_output_aliases={len(held) + 7: 0},
         compiler_params=pltpu.CompilerParams(vmem_limit_bytes=VMEM),
@@ -417,29 +409,19 @@
     owners = [r * n_col + c for r in (2, 3) for c in (0, 1)]
     place = jnp.stack([my_row, my_col, jnp.int32(cols_here), my_row * n_col + my_col])
 
-    outgoing = pack(child_tiles, tile_dest[:, 0], tile_slot, tile_count, devices)
+    outgoing, lead = pack(
+        child_tiles, front[0, 0, 0, 0], place[3:], tile_dest[:, 0], tile_slot, tile_count,
+        devices, owners,
+    )
+    lead = lax.optimization_barrier(lax.psum(lead, "col"))
+    lead = lax.psum(lead, "row")
     incoming = lax.all_to_all(outgoing, BOTH, split_axis=0, concat_axis=0, tiled=True)
     slot_in = lax.optimization_barrier(incoming[:, TILE, 0].astype(jnp.int32))
 
     ring = rows_here % n_col == 0
-    mine, top, *parts = assemble_columns(front, incoming, place, slot_in, n_col if ring else 1)
-
-    slices = top.reshape(devices, TILE // devices, TILE)
-    slices = lax.all_to_all(slices, BOTH, split_axis=0, concat_axis=0, tiled=True)
-    slices = jnp.stack([slices[owner] for owner in owners])
-    slices = jnp.broadcast_to(slices[None], (devices,) + slices.shape)
-
-    def hand_on(slices):
-        lead = lax.all_to_all(slices, BOTH, split_axis=0, concat_axis=0, tiled=True)
-        return lead.transpose(1, 0, 2, 3).reshape(2, 2, TILE, TILE)
-
-    def exchange(mine):
-        near = lax.ppermute(mine, "col", [(c, c ^ 1) for c in range(n_col)])
-        far = lax.ppermute(mine, "col", [(c, c ^ 2) for c in range(n_col)])
-        return [near, far, lax.ppermute(far, "col", [(c, c ^ 1) for c in range(n_col)])]
-
-    def own_panels(mine, lead):
-        return row_panels(mine, exchange(mine), lead, diag_inverses, place, slot_in, front)
+    mine, *parts = assemble_columns(front, incoming, place, slot_in, n_col if ring else 1)
+    tiles = lax.all_gather(mine, "col", axis=0, tiled=False)
+    panels = row_panels(tiles, lead, diag_inverses, place, slot_in, front)
 
     sets = n_row // n_col
     if ring:
@@ -451,28 +433,21 @@
                 for c in range(n_col)
             ]
             arrived.append(lax.ppermute(part, BOTH, pairs))
-        arrived, mine, slices = lax.optimization_barrier((arrived, mine, slices))
         piece = jnp.stack(arrived)
         circle = list(range(0, n_row, 2)) + list(range(n_row - 1, 0, -2))
         up = [(circle[i], circle[(i + 1) % n_row]) for i in range(n_row)]
         down = [(b, a) for a, b in up]
         rounds = [[(piece, 0)]]
-        lead = hand_on(slices)
         ahead = behind = piece
         for step in range(1, n_row // 2):
             ahead = lax.ppermute(ahead, "row", up)
             behind = lax.ppermute(behind, "row", down)
-            if step == 1:
-                ahead, behind, lead = lax.optimization_barrier((ahead, behind, lead))
-                panels = own_panels(mine, lead)
             if step == 2:
                 ahead, behind, panels = lax.optimization_barrier((ahead, behind, panels))
             rounds.append([(ahead, -step), (behind, step)])
-        last = jnp.concatenate(
-            [lax.ppermute(ahead[:2], "row", up), lax.ppermute(behind[2:], "row", down)]
-        )
-        rounds.append([(last, n_row // 2)])
-        rounds = [rounds[0] + rounds[1]] + rounds[2:]
+        last = [lax.ppermute(ahead[:2], "row", up), lax.ppermute(behind[2:], "row", down)]
+        whole = [entry for entries in rounds for entry in entries]
+        rounds = [whole[:2], whole[2:4], whole[4:5], *rounds[3:], [(last, n_row // 2)]]
 
         def described(row, shift):
             origin = circle[(circle.index(row) + shift) % n_row]
@@ -488,7 +463,6 @@
         ]
         moved = lax.all_gather(lax.ppermute(parts[0], BOTH, pairs), "row", axis=0, tiled=False)
         rounds = [[(moved[h * n_col : (h + 1) * n_col], h)] for h in range(sets)]
-        panels = own_panels(mine, hand_on(slices))
 
         def described(row, h):
             return [a * sets + h for a in range(rows_here)], list(range(n_col))
@@ -504,9 +478,10 @@
     first = 0
     for entries in rounds:
         pieces = [piece for piece, _ in entries]
+        pieces = pieces[0] if isinstance(pieces[0], list) else pieces
         out = trailing(front, pieces, first, place, tables, panels, incoming)
         panels = [panels[0], out, *panels[2:]]
-        first += len(pieces)
+        first += len(entries)
     return panels[1]
 
 

time: 184 us -> 235 us (1.28)
  waiting for transfers between devices: 85.9 us -> 139 us
  starting transfers between devices: 35.5 us -> 21.5 us
  between operations: 1.02 us -> 13.9 us
    psum x0 -> x2, waiting for transfers between devices: none -> 73 us  [the longest x1 44.2 us: body(): lead = lax.optimization_barrier(lax.psum(lead, 'col'))]
    all_to_all x1, waiting for transfers between devices: 51.5 us -> 6.51 us  [body(): lax.all_to_all(outgoing, BOTH, split_axis=0, concat_axis=0, tiled=True)]
    all_gather x0 -> x1, waiting for transfers between devices: none -> 29.4 us  [body(): tiles = lax.all_gather(mine, 'col', axis=0, tiled=False)]
    all_to_all x2 -> x0, waiting for transfers between devices: 20.7 us -> none  [the longest x1 20.7 us: hand_on(): lead = lax.all_to_all(slices, BOTH, split_axis=0, concat_axis=0, tiled=True)]
    ppermute x3, waiting for transfers between devices: 0.56 us -> 18.3 us  [body(): behind = lax.ppermute(behind, 'row', down)]
    all_to_all x2 -> x0, starting transfers between devices: 9.01 us -> none  [the longest x1 4.57 us: hand_on(): lead = lax.all_to_all(slices, BOTH, split_axis=0, concat_axis=0, tiled=True)]
    ppermute x3, waiting for transfers between devices: 7.46 us -> 0.01 us  [body(): ahead = lax.ppermute(ahead, 'row', up)]
    ppermute x3 -> x0, starting transfers between devices: 3.38 us -> none  [the longest x1 2.72 us: exchange(): far = lax.ppermute(mine, 'col', [(c, c ^ 2) for c in range(n_col)])]
  transfers between devices with their start and end apart: 18 -> 16, of which waited for: 8 -> 10; matrix products, arithmetic and copies ran while one was open for 2% -> 0% of each run, Pallas kernels for 22% -> 19%
where the time goes in v8:
time: 235 us
  waiting for transfers between devices  139 us (59%)
  Pallas kernels  52.2 us (22%)
  starting transfers between devices  21.5 us (9%)
  between operations  13.9 us (6%)
  local copies, waits for them, and re-layouts  7.65 us (3%)
    psum x1, waiting for transfers between devices, body(): lead = lax.optimization_barrier(lax.psum(lead, 'col'))  44.2 us
    pallas_call x5, Pallas kernels, trailing(): pl.pallas_call(functools.partial(trailing_kernel, first, len(pieces), hal...  39.5 us
    all_gather x1, waiting for transfers between devices, body(): tiles = lax.all_gather(mine, 'col', axis=0, tiled=False)  29.4 us
    psum x1, waiting for transfers between devices, body(): lead = lax.psum(lead, 'row')  28.8 us
    ppermute x3, waiting for transfers between devices, body(): behind = lax.ppermute(behind, 'row', down)  18.3 us
    ppermute x4, waiting for transfers between devices, body(): arrived.append(lax.ppermute(part, BOTH, pairs))  8.96 us
    pallas_call x1, Pallas kernels, row_panels(): pl.pallas_call(row_panels_kernel, grid_spec=pltpu.PrefetchScalarGridSpec(...  7.54 us
    all_to_all x1, starting transfers between devices, body(): lax.all_to_all(outgoing, BOTH, split_axis=0, concat_axis=0, tiled=True)  7.42 us
  transfers between devices with their start and end apart: 16, of which 10 were waited for; matrix products, arithmetic and copies ran while one was open for 0% of the time, Pallas kernels for 19%

profile of v8, /device:TPU:0, one launch (start us, length us, event | category | flops | bytes accessed | tf_op | source)
XLA Modules:
  0.0 234.6 jit_solution(16655672424143724623)
XLA Ops:
  6.5 0.0 copy-start.5
  6.5 0.0 copy-start.6
  7.2 0.8 slice_bitcast_fusion.top_ref
  8.1 0.0 copy-start.2
  8.1 1.2 copy-done.2
  9.3 0.0 copy-start.7
  9.3 0.7 copy-done.7
  9.9 0.0 copy-start.8
  9.9 0.7 copy-done.8
  10.6 0.0 copy-start.3
  10.6 1.8 pack.1
  12.4 0.0 copy-start.1
  12.4 1.4 copy-done.1
  13.8 7.4 %all-to-all-start = ((f32[32,136,128]{2,1,0:T(8,128)}), f32[32,136,128]{2,1,0:T(8,128)S(1)}, u32[]{:S(2)}, u32[]{:S(2)}) async-start(f32[32,136,128]{2,1,0:T(8,128)} %copy-done.1), calls=%async_computation | async-start | bytes 4456448 | tf_op jit(solution)/shard_map/all_to_all | solution.py:418
  21.2 0.0 all-reduce.3.cloned.1.call-start
  21.3 0.7 all-reduce.3.cloned.1.call-update
  22.0 0.0 all-reduce.5.cloned.1.call-start
  22.0 44.2 %all-reduce.3.cloned.1.call-done = f32[4,128,128]{2,1,0:T(8,128)} async-done(((f32[4,128,128]{2,1,0:T(8,128)}), f32[4,128,128]{2,1,0:T(8,128)}) %all-reduce.3.cloned.1.call-update) | async-done | bytes 262160 | tf_op jit(solution)/shard_map/psum | solution.py:416
  66.2 0.0 all-reduce.5.cloned.1.call-update
  66.2 0.0 all-gather.3.cloned.1.call-start
  66.2 0.1 pad_add_fusion.place
  66.3 6.5 %all-to-all-done.incoming_ref.rest_3_.rest_2_ = f32[32,136,128]{2,1,0:T(8,128)S(1)} async-done(((f32[32,136,128]{2,1,0:T(8,128)}), f32[32,136,128]{2,1,0:T(8,128)S(1)}, u32[]{:S(2)}, u32[]{:S(2)}) %all-to-all-start) | async-done | bytes 2228256 | tf_op jit(solution)/shard_map/all_to_all | solution.py:418
  72.8 0.7 fusion.slot_in
  73.5 3.3 %panel_columns.1 = (f32[12,128,128]{2,1,0:T(8,128)}, f32[3,128,128]{2,1,0:T(8,128)S(1)}, f32[3,128,128]{2,1,0:T(8,128)S(1)}, f32[3,128,128]{2,1,0:T(8,128)S(1)}, f32[3,128,128]{2,1,0:T(8,128)S(1)}) custom-call(s32[4]{0:T(128)S(1)} %pad_add_fusion.place, s32[32]{0:T(128)S(1)} %fusion.slot_in, f32[12,1,24,1,128,128]{5,4,3,2,1,0:T(8,128)} %rest_2_.7, ...), custom_call_target="tpu_custom_call" | custom-call | tf_op jit(solution)/shard_map/panel_columns/pallas_call | solution.py:115
  76.8 0.0 all-gather.3.cloned.1.call-update
  76.8 0.7 collective-permute-start
  77.5 1.9 collective-permute-start.1
  79.5 2.4 %collective-permute-start.2 = (f32[3,128,128]{2,1,0:T(8,128)S(1)}, f32[3,128,128]{2,1,0:T(8,128)S(1)}, u32[]{:S(2)}, u32[]{:S(2)}) collective-permute-start(f32[3,128,128]{2,1,0:T(8,128)S(1)} %get-tuple-element.27), channel_id=1, source_target_pairs={{0,8},{1,12},{2,0},{3,4},{4,9},{5,13},{6,1},{7,5},{8,10},{9,14},{1... | collective-permute-start | bytes 589832 | tf_op jit(solution)/shard_map/ppermute | solution.py:435
  81.9 0.6 collective-permute-start.3
  82.5 0.0 collective-permute-done
  82.5 2.8 %collective-permute-done.1 = f32[3,128,128]{2,1,0:T(8,128)S(1)} collective-permute-done((f32[3,128,128]{2,1,0:T(8,128)S(1)}, f32[3,128,128]{2,1,0:T(8,128)S(1)}, u32[]{:S(2)}, u32[]{:S(2)}) %collective-permute-start.1) | collective-permute-done | bytes 196640 | tf_op jit(solution)/shard_map/ppermute | solution.py:435
  85.3 2.7 %collective-permute-done.2 = f32[3,128,128]{2,1,0:T(8,128)S(1)} collective-permute-done((f32[3,128,128]{2,1,0:T(8,128)S(1)}, f32[3,128,128]{2,1,0:T(8,128)S(1)}, u32[]{:S(2)}, u32[]{:S(2)}) %collective-permute-start.2) | collective-permute-done | bytes 196640 | tf_op jit(solution)/shard_map/ppermute | solution.py:435
  87.9 3.5 %collective-permute-done.3 = f32[3,128,128]{2,1,0:T(8,128)S(1)} collective-permute-done((f32[3,128,128]{2,1,0:T(8,128)S(1)}, f32[3,128,128]{2,1,0:T(8,128)S(1)}, u32[]{:S(2)}, u32[]{:S(2)}) %collective-permute-start.3) | collective-permute-done | bytes 196640 | tf_op jit(solution)/shard_map/ppermute | solution.py:435
  91.4 0.1 pad_maximum_fusion.rest_0_
  91.5 1.8 collective-permute-start.6
  93.3 0.3 collective-permute-start.4
  93.6 18.3 %collective-permute-done.6.rest_0_ = f32[4,3,128,128]{3,2,1,0:T(8,128)} collective-permute-done((f32[4,3,128,128]{3,2,1,0:T(8,128)S(1)}, f32[4,3,128,128]{3,2,1,0:T(8,128)}, u32[]{:S(2)}, u32[]{:S(2)}) %collective-permute-start.6) | collective-permute-done | bytes 786464 | tf_op jit(solution)/shard_map/ppermute | solution.py:444
  111.9 1.5 collective-permute-start.7
  113.3 0.0 collective-permute-done.4.rest_1_
  113.3 0.6 collective-permute-start.5
  113.9 28.8 %all-reduce.5.cloned.1.call-done.lead_ref = f32[4,128,128]{2,1,0:T(8,128)} async-done(((f32[4,128,128]{2,1,0:T(8,128)}), f32[4,128,128]{2,1,0:T(8,128)}) %all-reduce.5.cloned.1.call-update) | async-done | bytes 262160 | tf_op jit(solution)/shard_map/psum | solution.py:417
  142.7 29.4 %all-gather.3.cloned.1.call-done = f32[48,128,128]{2,1,0:T(8,128)} async-done(((f32[12,128,128]{2,1,0:T(8,128)}), f32[48,128,128]{2,1,0:T(8,128)}) %all-gather.3.cloned.1.call-update) | async-done | bytes 3145744 | tf_op jit(solution)/shard_map/all_gather | solution.py:423
  172.1 0.0 copy-done.3
  172.1 0.0 copy-start
  172.2 1.9 copy-done
  174.0 0.9 copy-done.4
  175.0 7.5 %row_panels.1 = (bf16[1536,1024]{1,0:T(8,128)(2,1)S(1)}, f32[12,1,24,1,128,128]{5,4,3,2,1,0:T(8,128)}, bf16[3,256,768]{2,1,0:T(8,128)(2,1)S(1)}, s32[64]{0:T(128)S(1)}, s32[25]{0:T(128)S(1)}) custom-call(s32[4]{0:T(128)S(1)} %pad_add_fusion.place, s32[32]{0:T(128)S(1)} %fusion.slot_in, f32[4,12,128,128]{3,2,1,0:T(8,128)S(1)} %bitcast.11, ...), custom_call_target="tpu_custom_call" | custom-call | tf_op jit(solution)/shard_map/row_panels/pallas_call | solution.py:215
  182.5 0.0 collective-permute-done.7.rest_0_
  182.5 0.0 collective-permute-done.5.rest_1_
  182.5 1.5 collective-permute-start.8
  184.1 0.5 collective-permute-start.10
  184.6 0.0 copy-done.5
  184.6 0.0 copy-done.6
  184.6 8.6 %trailing.5.rest_4_ = f32[12,1,24,1,128,128]{5,4,3,2,1,0:T(8,128)} custom-call(s32[4]{0:T(128)S(1)} %pad_add_fusion.place, s32[192]{0:T(256)S(1)} %copy-done.6, s32[256]{0:T(256)S(1)} %copy-done.5, s32[64]{0:T(128)S(1)} %get-tuple-element.36.order, s32[25]{0:T(128)S(1)} %get-tuple-element.37.starts, ...), custom_call_target="tpu_custom_call", output_to_operand_aliasing={{}: (11, {})} | custom-call | flops 9663676416 | bytes 9437184 | tf_op jit(solution)/shard_map/trailing/pallas_call | solution.py:375
  193.2 9.3 %trailing.6.rest_3_ = f32[12,1,24,1,128,128]{5,4,3,2,1,0:T(8,128)} custom-call(s32[4]{0:T(128)S(1)} %pad_add_fusion.place, s32[192]{0:T(256)S(1)} %copy-done.6, s32[256]{0:T(256)S(1)} %copy-done.5, s32[64]{0:T(128)S(1)} %get-tuple-element.36.order, s32[25]{0:T(128)S(1)} %get-tuple-element.37.starts, ...), custom_call_target="tpu_custom_call", output_to_operand_aliasing={{}: (11, {})} | custom-call | flops 9663676416 | bytes 9437184 | tf_op jit(solution)/shard_map/trailing/pallas_call | solution.py:375
  202.5 6.7 %trailing.7.rest_4_ = f32[12,1,24,1,128,128]{5,4,3,2,1,0:T(8,128)} custom-call(s32[4]{0:T(128)S(1)} %pad_add_fusion.place, s32[192]{0:T(256)S(1)} %copy-done.6, s32[256]{0:T(256)S(1)} %copy-done.5, s32[64]{0:T(128)S(1)} %get-tuple-element.36.order, s32[25]{0:T(128)S(1)} %get-tuple-element.37.starts, ...), custom_call_target="tpu_custom_call", output_to_operand_aliasing={{}: (10, {})} | custom-call | flops 4831838208 | bytes 4718592 | tf_op jit(solution)/shard_map/trailing/pallas_call | solution.py:375
  209.2 0.0 collective-permute-done.8.rest_0_
  209.3 2.1 collective-permute-start.9
  211.4 0.0 collective-permute-done.10.rest_1_
  211.4 0.1 collective-permute-start.11
  211.5 8.8 %trailing.8.rest_4_ = f32[12,1,24,1,128,128]{5,4,3,2,1,0:T(8,128)} custom-call(s32[4]{0:T(128)S(1)} %pad_add_fusion.place, s32[192]{0:T(256)S(1)} %copy-done.6, s32[256]{0:T(256)S(1)} %copy-done.5, s32[64]{0:T(128)S(1)} %get-tuple-element.36.order, s32[25]{0:T(128)S(1)} %get-tuple-element.37.starts, ...), custom_call_target="tpu_custom_call", output_to_operand_aliasing={{}: (11, {})} | custom-call | flops 9663676416 | bytes 9437184 | tf_op jit(solution)/shard_map/trailing/pallas_call | solution.py:375
  220.3 0.1 collective-permute-done.9.rest_0_
  220.4 1.6 collective-permute-done.11.rest_1_
  222.0 6.1 %trailing.9 = f32[12,1,24,1,128,128]{5,4,3,2,1,0:T(8,128)} custom-call(s32[4]{0:T(128)S(1)} %pad_add_fusion.place, s32[192]{0:T(256)S(1)} %copy-done.6, s32[256]{0:T(256)S(1)} %copy-done.5, s32[64]{0:T(128)S(1)} %get-tuple-element.36.order, s32[25]{0:T(128)S(1)} %get-tuple-element.37.starts, ...), custom_call_target="tpu_custom_call", output_to_operand_aliasing={{}: (11, {})} | custom-call | flops 4831838208 | bytes 4718592 | tf_op jit(solution)/shard_map/trailing/pallas_call | solution.py:375
  (3 shorter events, 0.1 us)
Async XLA Ops:
  6.5 178.1 %copy-start.5 = (s32[256]{0:T(256)S(1)}, s32[256]{0:T(256)}, u32[]{:S(2)}) copy-start(s32[256]{0:T(256)} %constant.18.clone.places_table) | copy-start | bytes 3076
  6.5 178.1 %copy-start.6 = (s32[192]{0:T(256)S(1)}, s32[192]{0:T(256)}, u32[]{:S(2)}) copy-start(s32[192]{0:T(256)} %constant.17.clone.columns_table) | copy-start | bytes 2308
  8.1 1.2 copy-start.2
  9.3 0.7 copy-start.7
  9.9 0.7 copy-start.8
  10.6 161.5 %copy-start.3 = (f32[2,256,256]{2,1,0:T(8,128)S(1)}, f32[2,256,256]{2,1,0:T(8,128)}, u32[]{:S(2)}) copy-start(f32[2,256,256]{2,1,0:T(8,128)} %diag_ref.1) | copy-start | bytes 1572868
  12.4 1.4 copy-start.1
  13.8 59.0 %all-to-all-start = ((f32[32,136,128]{2,1,0:T(8,128)}), f32[32,136,128]{2,1,0:T(8,128)S(1)}, u32[]{:S(2)}, u32[]{:S(2)}) async-start(f32[32,136,128]{2,1,0:T(8,128)} %copy-done.1), calls=%async_computation | async-start | bytes 4456448 | tf_op jit(solution)/shard_map/all_to_all | solution.py:418
  21.2 44.9 %all-reduce.3.cloned.1.call-start = ((), (), s32[]{:S(2)}) async-start(), calls=%async_computation.1 | async-start | bytes 524288 | tf_op jit(solution)/shard_map/psum | solution.py:416
  22.0 120.8 %all-reduce.5.cloned.1.call-start = ((), (), s32[]{:S(2)}) async-start(), calls=%async_computation.2 | async-start | bytes 524288 | tf_op jit(solution)/shard_map/psum | solution.py:417
  66.2 106.0 %all-gather.3.cloned.1.call-start = ((), (), s32[]{:S(2)}) async-start(), calls=%async_computation.3 | async-start | bytes 3932160 | tf_op jit(solution)/shard_map/all_gather | solution.py:423
  76.8 5.6 %collective-permute-start = (f32[3,128,128]{2,1,0:T(8,128)S(1)}, f32[3,128,128]{2,1,0:T(8,128)S(1)}, u32[]{:S(2)}, u32[]{:S(2)}) collective-permute-start(f32[3,128,128]{2,1,0:T(8,128)S(1)} %get-tuple-element.25), channel_id=1, source_target_pairs={{0,0},{1,4},{2,8},{3,12},{4,1},{5,5},{6,9},{7,13},{8,2},{9,6},{10,... | collective-permute-start | bytes 589832 | tf_op jit(solution)/shard_map/ppermute | solution.py:435
  77.5 7.8 %collective-permute-start.1 = (f32[3,128,128]{2,1,0:T(8,128)S(1)}, f32[3,128,128]{2,1,0:T(8,128)S(1)}, u32[]{:S(2)}, u32[]{:S(2)}) collective-permute-start(f32[3,128,128]{2,1,0:T(8,128)S(1)} %get-tuple-element.26), channel_id=1, source_target_pairs={{0,4},{1,8},{2,12},{3,0},{4,5},{5,9},{6,13},{7,1},{8,6},{9,10},{10... | collective-permute-start | bytes 589832 | tf_op jit(solution)/shard_map/ppermute | solution.py:435
  79.5 8.5 %collective-permute-start.2 = (f32[3,128,128]{2,1,0:T(8,128)S(1)}, f32[3,128,128]{2,1,0:T(8,128)S(1)}, u32[]{:S(2)}, u32[]{:S(2)}) collective-permute-start(f32[3,128,128]{2,1,0:T(8,128)S(1)} %get-tuple-element.27), channel_id=1, source_target_pairs={{0,8},{1,12},{2,0},{3,4},{4,9},{5,13},{6,1},{7,5},{8,10},{9,14},{1... | collective-permute-start | bytes 589832 | tf_op jit(solution)/shard_map/ppermute | solution.py:435
  81.9 9.6 %collective-permute-start.3 = (f32[3,128,128]{2,1,0:T(8,128)S(1)}, f32[3,128,128]{2,1,0:T(8,128)S(1)}, u32[]{:S(2)}, u32[]{:S(2)}) collective-permute-start(f32[3,128,128]{2,1,0:T(8,128)S(1)} %get-tuple-element.28), channel_id=1, source_target_pairs={{0,12},{1,0},{2,4},{3,8},{4,13},{5,1},{6,5},{7,9},{8,14},{9,2},{10... | collective-permute-start | bytes 589832 | tf_op jit(solution)/shard_map/ppermute | solution.py:435
  91.5 20.4 %collective-permute-start.6 = (f32[4,3,128,128]{3,2,1,0:T(8,128)S(1)}, f32[4,3,128,128]{3,2,1,0:T(8,128)}, u32[]{:S(2)}, u32[]{:S(2)}) collective-permute-start(f32[4,3,128,128]{3,2,1,0:T(8,128)S(1)} %pad_maximum_fusion.rest_0_), channel_id=1, source_target_pairs={{8,0},{16,8},{24,16},{28,24},{20,28},{12,20},{4,12},{0,4},{9,1},{1... | collective-permute-start | bytes 2359304 | tf_op jit(solution)/shard_map/ppermute | solution.py:444
  93.3 20.1 %collective-permute-start.4 = (f32[4,3,128,128]{3,2,1,0:T(8,128)S(1)}, f32[4,3,128,128]{3,2,1,0:T(8,128)}, u32[]{:S(2)}, u32[]{:S(2)}) collective-permute-start(f32[4,3,128,128]{3,2,1,0:T(8,128)S(1)} %pad_maximum_fusion.rest_0_), channel_id=1, source_target_pairs={{0,8},{8,16},{16,24},{24,28},{28,20},{20,12},{12,4},{4,0},{1,9},{9... | collective-permute-start | bytes 2359304 | tf_op jit(solution)/shard_map/ppermute | solution.py:443
  111.9 70.6 %collective-permute-start.7 = (f32[4,3,128,128]{3,2,1,0:T(8,128)}, f32[4,3,128,128]{3,2,1,0:T(8,128)}, u32[]{:S(2)}, u32[]{:S(2)}) collective-permute-start(f32[4,3,128,128]{3,2,1,0:T(8,128)} %collective-permute-done.6.rest_0_), channel_id=1, source_target_pairs={{8,0},{16,8},{24,16},{28,24},{20,28},{12,20},{4,12},{0,4},{9,1},{1... | collective-permute-start | bytes 2359304 | tf_op jit(solution)/shard_map/ppermute | solution.py:444
  113.3 69.2 %collective-permute-start.5 = (f32[4,3,128,128]{3,2,1,0:T(8,128)}, f32[4,3,128,128]{3,2,1,0:T(8,128)}, u32[]{:S(2)}, u32[]{:S(2)}) collective-permute-start(f32[4,3,128,128]{3,2,1,0:T(8,128)} %collective-permute-done.4.rest_1_), channel_id=1, source_target_pairs={{0,8},{8,16},{16,24},{24,28},{28,20},{20,12},{12,4},{4,0},{1,9},{9... | collective-permute-start | bytes 2359304 | tf_op jit(solution)/shard_map/ppermute | solution.py:443
  172.1 1.9 copy-start
  174.0 0.9 copy-start.4
  182.5 26.7 %collective-permute-start.8 = (f32[4,3,128,128]{3,2,1,0:T(8,128)}, f32[4,3,128,128]{3,2,1,0:T(8,128)S(1)}, u32[]{:S(2)}, u32[]{:S(2)}) collective-permute-start(f32[4,3,128,128]{3,2,1,0:T(8,128)} %collective-permute-done.5.rest_1_), channel_id=1, source_target_pairs={{0,8},{8,16},{16,24},{24,28},{28,20},{20,12},{12,4},{4,0},{1,9},{9... | collective-permute-start | bytes 2359304 | tf_op jit(solution)/shard_map/ppermute | solution.py:443
  184.1 27.3 %collective-permute-start.10 = (f32[4,3,128,128]{3,2,1,0:T(8,128)}, f32[4,3,128,128]{3,2,1,0:T(8,128)S(1)}, u32[]{:S(2)}, u32[]{:S(2)}) collective-permute-start(f32[4,3,128,128]{3,2,1,0:T(8,128)} %collective-permute-done.7.rest_0_), channel_id=1, source_target_pairs={{8,0},{16,8},{24,16},{28,24},{20,28},{12,20},{4,12},{0,4},{9,1},{1... | collective-permute-start | bytes 2359304 | tf_op jit(solution)/shard_map/ppermute | solution.py:444
  209.3 11.1 %collective-permute-start.9 = (f32[2,3,128,128]{3,2,1,0:T(8,128)S(1)}, f32[2,3,128,128]{3,2,1,0:T(8,128)S(1)}, u32[]{:S(2)}, u32[]{:S(2)}) collective-permute-start(f32[2,3,128,128]{3,2,1,0:T(8,128)S(1)} %slice.17), channel_id=1, source_target_pairs={{0,8},{8,16},{16,24},{24,28},{28,20},{20,12},{12,4},{4,0},{1,9},{9... | collective-permute-start | bytes 1179656 | tf_op jit(solution)/shard_map/ppermute | solution.py:448
  211.4 10.6 %collective-permute-start.11 = (f32[2,3,128,128]{3,2,1,0:T(8,128)S(1)}, f32[2,3,128,128]{3,2,1,0:T(8,128)S(1)}, u32[]{:S(2)}, u32[]{:S(2)}) collective-permute-start(f32[2,3,128,128]{3,2,1,0:T(8,128)S(1)} %slice.18), channel_id=1, source_target_pairs={{8,0},{16,8},{24,16},{28,24},{20,28},{12,20},{4,12},{0,4},{9,1},{1... | collective-permute-start | bytes 1179656 | tf_op jit(solution)/shard_map/ppermute | solution.py:448
Sparse Core Ops, SparseCore 0:
  24.4 41.7 all-reduce.2
  69.9 72.7 all-reduce.4
  144.3 27.8 all-gather.2

commit v9 on v5

--- a/solution.py
+++ b/solution.py
@@ -59,56 +59,60 @@
 
 
 def pack_kernel(
-    owners, place, dest, slot, count, child_ref, front_ref, out_ref, notes_ref, lead_ref,
-    tile_ref, sems, notes_sem, lead_sem,
+    owners, place, dest, slot, count, child_ref, front_ref, out_ref, held_ref, notes_ref,
+    lead_ref, tile_ref, in_sems, out_sems, sem,
 ):
-    slots = child_ref.shape[0]
     n_slices, height, _ = lead_ref.shape
     each = n_slices // 4
-
-    def copy(k):
+    live = jnp.minimum(count[0], child_ref.shape[0])
+
+    def arrive(k):
+        return pltpu.make_async_copy(child_ref.at[k], held_ref.at[k], in_sems.at[k])
+
+    def leave(k):
         return pltpu.make_async_copy(
-            child_ref.at[k], out_ref.at[dest[k], pl.ds(0, TILE)], sems.at[k]
+            held_ref.at[k], out_ref.at[dest[k], pl.ds(0, TILE)], out_sems.at[k]
         )
+
+    @pl.loop(0, live)
+    def _(k):
+        arrive(k).start()
 
     notes_ref[...] = jnp.full_like(notes_ref, -1.0)
     lead_ref[...] = jnp.zeros_like(lead_ref)
-    live = jnp.minimum(count[0], slots)
+    for i, owner in enumerate(owners):
+
+        @pl.when(place[3] == owner)
+        def _():
+            own = pltpu.make_async_copy(front_ref.at[0, 0, 0, 0], tile_ref, sem)
+            own.start()
+            own.wait()
+            lead_ref[i * each : (i + 1) * each] = tile_ref[...].reshape(each, height, TILE)
 
     @pl.loop(0, live)
     def _(k):
-        copy(k).start()
         notes_ref[dest[k]] = jnp.full(notes_ref.shape[1:], slot[k].astype(jnp.float32))
-
-    notes = pltpu.make_async_copy(notes_ref, out_ref.at[:, pl.ds(TILE, NOTE)], notes_sem)
-    notes.start()
-
-    for i, owner in enumerate(owners):
-        span = pl.ds(i * each, each)
-
-        @pl.when(place[3] == owner)
-        def _():
-            own = pltpu.make_async_copy(front_ref.at[0, 0, 0, 0], tile_ref, lead_sem)
-            own.start()
-            own.wait()
-            lead_ref[span] = tile_ref[...].reshape(each, height, TILE)
-
-        @pl.loop(0, live)
-        def _(k):
+        arrive(k).wait()
+        leave(k).start()
+        for i, owner in enumerate(owners):
+
             @pl.when(jnp.logical_and(slot[k] == 0, dest[k] == owner))
             def _():
-                lead_ref[span] = lead_ref[span] + child_ref[k].reshape(each, height, TILE)
-
+                span = pl.ds(i * each, each)
+                lead_ref[span] = lead_ref[span] + held_ref[k].reshape(each, height, TILE)
+
+    notes = pltpu.make_async_copy(notes_ref, out_ref.at[:, pl.ds(TILE, NOTE)], sem)
+    notes.start()
+    notes.wait()
     lead = pltpu.make_async_copy(
-        lead_ref, out_ref.at[pl.ds(0, n_slices), pl.ds(TILE + NOTE, height)], lead_sem
+        lead_ref, out_ref.at[pl.ds(0, n_slices), pl.ds(TILE + NOTE, height)], sem
     )
     lead.start()
-    notes.wait()
     lead.wait()
 
     @pl.loop(0, live)
     def _(k):
-        copy(k).wait()
+        leave(k).wait()
 
 
 def pack(child_tiles, front, place, dest, slot, count, devices, owners):
@@ -117,19 +121,19 @@
     hbm = pl.BlockSpec(memory_space=pltpu.HBM)
     return pl.pallas_call(
         functools.partial(pack_kernel, owners),
-        in_specs=[pl.BlockSpec(memory_space=pltpu.SMEM)] * 4
-        + [pl.BlockSpec(memory_space=pltpu.VMEM), hbm],
+        in_specs=[pl.BlockSpec(memory_space=pltpu.SMEM)] * 4 + [hbm, hbm],
         out_specs=hbm,
         scratch_shapes=[
+            pltpu.VMEM((slots, TILE, TILE), jnp.float32),
             pltpu.VMEM((devices, NOTE, TILE), jnp.float32),
             pltpu.VMEM((n_slices, height, TILE), jnp.float32),
             pltpu.VMEM((TILE, TILE), jnp.float32),
             pltpu.SemaphoreType.DMA((slots,)),
-            pltpu.SemaphoreType.DMA,
+            pltpu.SemaphoreType.DMA((slots,)),
             pltpu.SemaphoreType.DMA,
         ],
         out_shape=jax.ShapeDtypeStruct((devices, TILE + NOTE + height, TILE), jnp.float32),
-        compiler_params=pltpu.CompilerParams(vmem_limit_bytes=VMEM),
+        compiler_params=pltpu.CompilerParams(vmem_limit_bytes=62 * 1024 * 1024),
         name="pack",
     )(place, dest, slot, count, child_tiles, front)
 
@@ -306,30 +310,31 @@
 
 
 def trailing_kernel(
-    first, n_pieces, place, columns_table, places_table, order, starts, pair_ref, small_ref, *rest
+    first, n_held, halved, place, columns_table, places_table, order, starts, small_ref, *rest
 ):
-    piece_refs = rest[:n_pieces]
-    front_ref, incoming_ref, _, out_ref, right_ref, taken, given, child_ref = rest[n_pieces:-3]
-    take_sems, give_sems, child_sems = rest[-3:]
+    piece_refs = rest[:n_held]
+    pair_hbm, front_ref, incoming_ref, _, out_ref, *rest = rest[n_held:]
+    pair_ref, right_ref, taken, given, child_ref, *rest = rest
+    pair_sem, take_sems, give_sems, child_sems, *joined = rest
+    if halved:
+        joined[0][:2] = piece_refs[0][...]
+        joined[0][2:] = piece_refs[1][...]
+        piece_refs = joined
     group = piece_refs[0].shape[1]
-    count = n_pieces * group
-    steps = (count + 1) // 2
+    count = len(piece_refs) * group
+    pairs, single = count // 2, count % 2
     rows, cols = front_ref.shape[0], front_ref.shape[2]
     columns_base = place[0] * cols + first * group
     places_base = (place[0] * (cols // group) + first) * 4
 
-    def columns_of(step):
-        for j in range(2):
-            index = jnp.minimum(2 * step, count - 2) + j
-            b = columns_table[columns_base + index]
-            wanted = b > 0
-            if count % 2 and j == 0:
-                wanted = jnp.logical_and(wanted, step < steps - 1)
-            yield j, b, wanted
-
-    def each_take(step, act):
+    def columns_of(step, width):
+        for j in range(width):
+            b = columns_table[columns_base + 2 * step + j]
+            yield j, b, b > 0
+
+    def each_take(step, width, act):
         slot = lax.rem(step, 2)
-        for j, b, wanted in columns_of(step):
+        for j, b, wanted in columns_of(step, width):
 
             @pl.when(wanted)
             def _():
@@ -339,9 +344,9 @@
                     )
                 )
 
-    def each_give(step, act):
+    def each_give(step, width, act):
         slot = lax.rem(step, 2)
-        for j, b, wanted in columns_of(step):
+        for j, b, wanted in columns_of(step, width):
 
             @pl.when(wanted)
             def _():
@@ -351,8 +356,8 @@
                     )
                 )
 
-    def each_child(step, act):
-        for j, b, wanted in columns_of(step):
+    def each_child(step, width, act):
+        for j, b, wanted in columns_of(step, width):
 
             @pl.when(wanted)
             def _():
@@ -364,10 +369,14 @@
                     )
                     act(copy, j, s, order[2 * i + 1])
 
-    for step in range(min(steps, 2)):
-        each_take(step, lambda copy: copy.start())
-    for step in range(steps):
-        each_child(step, lambda copy, *_: copy.start())
+    start, wait = (lambda copy, *_: copy.start()), (lambda copy, *_: copy.wait())
+    steps = [(step, 2) for step in range(pairs)] + [(pairs, 1)] * single
+    pair_copy = pltpu.make_async_copy(pair_hbm, pair_ref, pair_sem)
+    pair_copy.start()
+    for step, width in steps[:2]:
+        each_take(step, width, start)
+    for step, width in steps:
+        each_child(step, width, start)
 
     tile_columns = [
         jnp.concatenate(
@@ -384,64 +393,68 @@
         high, low = halves(panel)
         for k, half in enumerate((high, high, low)):
             right_ref[k * WIDTH + i * PANEL : k * WIDTH + (i + 1) * PANEL] = half
-
-    @pl.loop(0, steps)
-    def _(step):
+    pair_copy.wait()
+
+    def update(step, width):
         slot = lax.rem(step, 2)
-        each_take(step, lambda copy: copy.wait())
-
-        @pl.when(step >= 2)
-        def _():
-            each_give(step - 2, lambda copy: copy.wait())
-
-        start = jnp.minimum(2 * step, count - 2)
-        lanes = pl.ds(pl.multiple_of(start * TILE, TILE), 2 * TILE)
-        update = dot(pair_ref[...], right_ref[:, lanes])
-        for j in range(2):
-            part = update[:, j * TILE : (j + 1) * TILE].reshape(rows, TILE, TILE)
+        each_take(step, width, wait)
+        pl.when(step >= 2)(lambda: each_give(step - 2, 2, wait))
+        lanes = pl.ds(pl.multiple_of(2 * step * TILE, TILE), width * TILE)
+        change = dot(pair_ref[...], right_ref[:, lanes])
+        for j in range(width):
+            part = change[:, j * TILE : (j + 1) * TILE].reshape(rows, TILE, TILE)
             given[slot, j] = taken[slot, j] - part
 
         def add(copy, j, s, a):
             copy.wait()
             given[slot, j, a] = given[slot, j, a] + child_ref[s]
 
-        each_child(step, add)
-        each_give(step, lambda copy: copy.start())
-
-        @pl.when(step + 2 < steps)
-        def _():
-            each_take(step + 2, lambda copy: copy.start())
-
-    for step in range(max(steps - 2, 0), steps):
-        each_give(step, lambda copy: copy.wait())
+        each_child(step, width, add)
+        each_give(step, width, start)
+
+    @pl.loop(0, pairs)
+    def _(step):
+        update(step, 2)
+        pl.when(step + 2 < pairs)(lambda: each_take(step + 2, 2, start))
+        if single:
+            pl.when(step + 2 == pairs)(lambda: each_take(step + 2, 1, start))
+
+    if single:
+        update(jnp.int32(pairs), 1)
+    for step, width in steps[-2:]:
+        each_give(step, width, wait)
 
 
 def trailing(front, pieces, first, place, tables, panels, incoming):
     rows = front.shape[0]
     pair, out, small, order, starts = panels
     group = pieces[0].shape[1]
-    count = len(pieces) * group
+    halved = pieces[0].shape[0] == 2
+    count = group if halved else len(pieces) * group
     scalars = [place, *tables, order, starts]
-    held = [pair, small, *pieces]
-    distant = [front, incoming, out]
+    held = [small, *pieces]
+    distant = [pair, front, incoming, out]
     spec = lambda space, n: [pl.BlockSpec(memory_space=space)] * n
     height = rows * TILE
     devices = incoming.shape[0]
     return pl.pallas_call(
-        functools.partial(trailing_kernel, first, len(pieces)),
-        in_specs=spec(pltpu.SMEM, 5) + spec(pltpu.VMEM, len(held)) + spec(pltpu.HBM, 3),
+        functools.partial(trailing_kernel, first, len(pieces), halved),
+        in_specs=spec(pltpu.SMEM, 5) + spec(pltpu.VMEM, len(held)) + spec(pltpu.HBM, 4),
         out_specs=pl.BlockSpec(memory_space=pltpu.HBM),
         scratch_shapes=[
+            pltpu.VMEM(pair.shape, jnp.bfloat16),
             pltpu.VMEM((3 * WIDTH, count * TILE), jnp.bfloat16),
             pltpu.VMEM((2, 2, rows, TILE, TILE), jnp.float32),
             pltpu.VMEM((2, 2, rows, TILE, TILE), jnp.float32),
             pltpu.VMEM((devices, TILE, TILE), jnp.float32),
+            pltpu.SemaphoreType.DMA,
             pltpu.SemaphoreType.DMA((2, 2)),
             pltpu.SemaphoreType.DMA((2, 2)),
             pltpu.SemaphoreType.DMA((devices,)),
-        ],
+        ]
+        + [pltpu.VMEM((4, group, TILE, TILE), jnp.float32)] * halved,
         out_shape=jax.ShapeDtypeStruct(front.shape, jnp.float32),
-        input_output_aliases={len(held) + 7: 0},
+        input_output_aliases={5 + len(held) + 3: 0},
         compiler_params=pltpu.CompilerParams(vmem_limit_bytes=VMEM),
         cost_estimate=pl.CostEstimate(
             flops=8 * count * 2 * height * TILE * WIDTH,
@@ -471,19 +484,16 @@
 
     ring = rows_here % n_col == 0
     mine, own, *parts = assemble_columns(front, incoming, place, slot_in, n_col if ring else 1)
-
-    def hand_on(own):
-        lead = lax.all_to_all(own, BOTH, split_axis=0, concat_axis=0, tiled=True)
-        return lead[: lead_slices(devices)[0]].reshape(2, 2, TILE, TILE)
+    lead = lax.all_to_all(own, BOTH, split_axis=0, concat_axis=0, tiled=True)
+    lead = lead[: lead_slices(devices)[0]].reshape(2, 2, TILE, TILE)
 
     def exchange(mine):
         near = lax.ppermute(mine, "col", [(c, c ^ 1) for c in range(n_col)])
         far = lax.ppermute(mine, "col", [(c, c ^ 2) for c in range(n_col)])
         return [near, far, lax.ppermute(far, "col", [(c, c ^ 1) for c in range(n_col)])]
 
-    def own_panels(mine, own):
-        tiles = exchange(mine)
-        return row_panels(mine, tiles, hand_on(own), diag_inverses, place, slot_in, front)
+    def own_panels(mine, lead):
+        return row_panels(mine, exchange(mine), lead, diag_inverses, place, slot_in, front)
 
     sets = n_row // n_col
     if ring:
@@ -495,13 +505,13 @@
                 for c in range(n_col)
             ]
             arrived.append(lax.ppermute(part, BOTH, pairs))
-        arrived, own, mine = lax.optimization_barrier((arrived, own, mine))
+        arrived, mine, lead = lax.optimization_barrier((arrived, mine, lead))
         piece = jnp.stack(arrived)
         circle = list(range(0, n_row, 2)) + list(range(n_row - 1, 0, -2))
         up = [(circle[i], circle[(i + 1) % n_row]) for i in range(n_row)]
         down = [(b, a) for a, b in up]
         rounds = [[(piece, 0)]]
-        panels = own_panels(mine, own)
+        panels = own_panels(mine, lead)
         ahead = behind = piece
         for step in range(1, n_row // 2):
             ahead = lax.ppermute(ahead, "row", up)
@@ -509,11 +519,9 @@
             if step == 2:
                 ahead, behind, panels = lax.optimization_barrier((ahead, behind, panels))
             rounds.append([(ahead, -step), (behind, step)])
-        last = jnp.concatenate(
-            [lax.ppermute(ahead[:2], "row", up), lax.ppermute(behind[2:], "row", down)]
-        )
-        rounds.append([(last, n_row // 2)])
-        rounds = [rounds[0] + rounds[1]] + rounds[2:]
+        last = [lax.ppermute(ahead[:2], "row", up), lax.ppermute(behind[2:], "row", down)]
+        whole = [entry for entries in rounds for entry in entries]
+        rounds = [whole[:2], whole[2:4], whole[4:5], *rounds[3:], [(last, n_row // 2)]]
 
         def described(row, shift):
             origin = circle[(circle.index(row) + shift) % n_row]
@@ -529,7 +537,7 @@
         ]
         moved = lax.all_gather(lax.ppermute(parts[0], BOTH, pairs), "row", axis=0, tiled=False)
         rounds = [[(moved[h * n_col : (h + 1) * n_col], h)] for h in range(sets)]
-        panels = own_panels(mine, own)
+        panels = own_panels(mine, lead)
 
         def described(row, h):
             return [a * sets + h for a in range(rows_here)], list(range(n_col))
@@ -545,9 +553,10 @@
     first = 0
     for entries in rounds:
         pieces = [piece for piece, _ in entries]
+        pieces = pieces[0] if isinstance(pieces[0], list) else pieces
         out = trailing(front, pieces, first, place, tables, panels, incoming)
         panels = [panels[0], out, *panels[2:]]
-        first += len(pieces)
+        first += len(entries)
     return panels[1]
 
 

time: 192 us -> 192 us (level)
  blocking collectives: 90 us -> 65.5 us
  waiting for transfers between devices: 22.3 us -> 31.6 us
  Pallas kernels: 55.7 us -> 62.7 us
  starting transfers between devices: 19.1 us -> 22.7 us
  local copies, waits for them, and re-layouts: 2.61 us -> 5.6 us
    all_to_all x1 -> x0, blocking collectives: 24.6 us -> none  [hand_on(): lead = lax.all_to_all(own, BOTH, split_axis=0, concat_axis=0, tiled=True)]
    ppermute x3, waiting for transfers between devices: 0.48 us -> 9.88 us  [body(): behind = lax.ppermute(behind, 'row', down)]
    pallas_call x4 -> x5, Pallas kernels: 42.5 us -> 48.2 us  [trailing(): pl.pallas_call(functools.partial(trailing_kernel, first, len(pieces), hal...]
    unnamed x12 -> x24, local copies, waits for them, and re-layouts: 2.56 us -> 5.54 us
    all_to_all x0 -> x1, starting transfers between devices: none -> 2.59 us  [body(): lead = lax.all_to_all(own, BOTH, split_axis=0, concat_axis=0, tiled=True)]
  transfers between devices with their start and end apart: 15 -> 16, of which waited for: 5 -> 6; matrix products, arithmetic and copies ran while one was open for 0% -> 1% of each run, Pallas kernels for 22% -> 24%
where the time goes in v9:
time: 192 us
  blocking collectives  65.5 us (34%)
  Pallas kernels  62.7 us (33%)
  waiting for transfers between devices  31.6 us (16%)
  starting transfers between devices  22.7 us (12%)
  local copies, waits for them, and re-layouts  5.6 us (3%)
  other arithmetic  2.55 us (1%)
    all_to_all x1, blocking collectives, body(): lax.all_to_all(outgoing, BOTH, split_axis=0, concat_axis=0, tiled=True)  65.5 us
    pallas_call x5, Pallas kernels, trailing(): pl.pallas_call(functools.partial(trailing_kernel, first, len(pieces), hal...  48.2 us
    ppermute x1, waiting for transfers between devices, exchange(): far = lax.ppermute(mine, 'col', [(c, c ^ 2) for c in range(n_col)])  14.6 us
    ppermute x3, waiting for transfers between devices, body(): behind = lax.ppermute(behind, 'row', down)  9.88 us
    pallas_call x1, Pallas kernels, row_panels(): pl.pallas_call(row_panels_kernel, grid_spec=pltpu.PrefetchScalarGridSpec(...  8.01 us
    ppermute x4, starting transfers between devices, body(): arrived.append(lax.ppermute(part, BOTH, pairs))  7.77 us
    ppermute x4, waiting for transfers between devices, body(): arrived.append(lax.ppermute(part, BOTH, pairs))  6.31 us
    ppermute x3, starting transfers between devices, body(): behind = lax.ppermute(behind, 'row', down)  5.81 us
  transfers between devices with their start and end apart: 16, of which 6 were waited for; matrix products, arithmetic and copies ran while one was open for 1% of the time, Pallas kernels for 24%

profile of v9, /device:TPU:0, one launch (start us, length us, event | category | flops | bytes accessed | tf_op | source)
XLA Modules:
  0.0 191.6 jit_solution(1043047908593945833)
XLA Ops:
  0.7 0.6 pad_add_fusion.place
  1.3 0.0 copy-start.2
  1.3 3.7 %pack.1 = f32[32,152,128]{2,1,0:T(8,128)} custom-call(s32[4]{0:T(128)} %pad_add_fusion.place, s32[16]{0:T(128)} %bitcast.13, s32[16]{0:T(128)} %slot.1, s32[1]{0:T(128)S(6)} %copy.19.count, f32[16,128,128]{2,1,0:T(8,128)} %child_ref.1, f32[12,1,24,1,128,128]{5,4,3,2,1,0:T(8,128)} %rest_3_.7), custom_call_target="tpu_custom_call" | custom-call | tf_op jit(solution)/shard_map/pack/pallas_call | solution.py:122
  5.0 0.0 copy-start.3
  5.0 0.0 copy-start.4
  5.0 65.5 %all_to_all.10.incoming_ref.rest_4_.rest_3_ = f32[32,152,128]{2,1,0:T(8,128)S(1)} all-to-all(f32[32,152,128]{2,1,0:T(8,128)} %pack.1), channel_id=1, replica_groups=mesh['row'=8,'col'=4] {'row','col'}, dimensions={0} | all-to-all | bytes 4980736 | tf_op jit(solution)/shard_map/all_to_all | solution.py:482
  70.5 0.7 fusion.slot_in
  71.2 0.0 copy-done.2
  71.2 2.8 %panel_columns.1 = (f32[12,128,128]{2,1,0:T(8,128)S(1)}, f32[32,16,128]{2,1,0:T(8,128)S(1)}, f32[3,128,128]{2,1,0:T(8,128)S(1)}, f32[3,128,128]{2,1,0:T(8,128)S(...) custom-call(s32[4]{0:T(128)S(1)} %copy-done.2, s32[32]{0:T(128)S(1)} %fusion.slot_in, ...), custom_call_target="tpu_custom_call" | custom-call | tf_op jit(solution)/shard_map/panel_columns/pallas_call | solution.py:181
  74.0 0.0 copy-start.1
  74.0 0.7 copy-done.1
  74.7 0.0 copy-start.5
  74.7 0.7 copy-done.5
  75.4 0.0 copy-start.6
  75.4 0.7 copy-done.6
  76.0 0.0 copy-start.7
  76.0 0.7 copy-done.7
  76.7 0.7 copy-done.8
  77.4 2.6 %all-to-all-start.1 = ((f32[32,16,128]{2,1,0:T(8,128)}), f32[32,16,128]{2,1,0:T(8,128)S(1)}, u32[]{:S(2)}, u32[]{:S(2)}) async-start(f32[32,16,128]{2,1,0:T(8,128)} %copy-done.1), calls=%async_computation.1 | async-start | bytes 524288 | tf_op jit(solution)/shard_map/all_to_all | solution.py:487
  80.0 1.6 collective-permute-start
  81.6 2.1 %collective-permute-start.1 = (f32[3,128,128]{2,1,0:T(8,128)}, f32[3,128,128]{2,1,0:T(8,128)S(1)}, u32[]{:S(2)}, u32[]{:S(2)}) collective-permute-start(f32[3,128,128]{2,1,0:T(8,128)} %copy-done.7), channel_id=1, source_target_pairs={{0,4},{1,8},{2,12},{3,0},{4,5},{5,9},{6,13},{7,1},{8,6},{9,10},{10... | collective-permute-start | bytes 589832 | tf_op jit(solution)/shard_map/ppermute | solution.py:507
  83.7 3.5 %collective-permute-start.2 = (f32[3,128,128]{2,1,0:T(8,128)}, f32[3,128,128]{2,1,0:T(8,128)S(1)}, u32[]{:S(2)}, u32[]{:S(2)}) collective-permute-start(f32[3,128,128]{2,1,0:T(8,128)} %copy-done.6), channel_id=1, source_target_pairs={{0,8},{1,12},{2,0},{3,4},{4,9},{5,13},{6,1},{7,5},{8,10},{9,14},{1... | collective-permute-start | bytes 589832 | tf_op jit(solution)/shard_map/ppermute | solution.py:507
  87.2 0.5 collective-permute-start.3
  87.8 0.0 collective-permute-done
  87.8 6.0 %collective-permute-done.1 = f32[3,128,128]{2,1,0:T(8,128)S(1)} collective-permute-done((f32[3,128,128]{2,1,0:T(8,128)}, f32[3,128,128]{2,1,0:T(8,128)S(1)}, u32[]{:S(2)}, u32[]{:S(2)}) %collective-permute-start.1) | collective-permute-done | bytes 196640 | tf_op jit(solution)/shard_map/ppermute | solution.py:507
  93.8 0.3 collective-permute-done.2
  94.1 0.0 copy-done.9
  94.1 0.4 copy-done.10
  94.5 0.7 copy-done.11
  95.1 0.0 collective-permute-done.3
  95.1 0.0 all-to-all-done.1
  95.1 3.3 %collective-permute-start.9 = (f32[12,128,128]{2,1,0:T(8,128)S(1)}, f32[12,128,128]{2,1,0:T(8,128)S(1)}, u32[]{:S(2)}, u32[]{:S(2)}) collective-permute-start(f32[12,128,128]{2,1,0:T(8,128)S(1)} %get-tuple-element.39.t0), channel_id=1, source_target_pairs={{0,2},{1,3},{2,0},{3,1},{4,6},{5,7},{6,4},{7,5},{8,10},{9,11},{10,... | collective-permute-start | bytes 2359304 | tf_op jit(solution)/shard_map/ppermute | solution.py:492
  98.4 1.3 pad_maximum_fusion.rest_0_
  99.7 2.5 %collective-permute-start.6 = (f32[4,3,128,128]{3,2,1,0:T(8,128)S(1)}, f32[4,3,128,128]{3,2,1,0:T(8,128)S(1)}, u32[]{:S(2)}, u32[]{:S(2)}) collective-permute-start(f32[4,3,128,128]{3,2,1,0:T(8,128)S(1)} %pad_maximum_fusion.rest_0_), channel_id=1, source_target_pairs={{8,0},{16,8},{24,16},{28,24},{20,28},{12,20},{4,12},{0,4},{9,1},{1... | collective-permute-start | bytes 2359304 | tf_op jit(solution)/shard_map/ppermute | solution.py:518
  102.1 0.0 collective-permute-start.4
  102.2 0.0 collective-permute-start.8
  102.2 14.6 %collective-permute-done.9.t2 = f32[12,128,128]{2,1,0:T(8,128)S(1)} collective-permute-done((f32[12,128,128]{2,1,0:T(8,128)S(1)}, f32[12,128,128]{2,1,0:T(8,128)S(1)}, u32[]{:S(2)}, u32[]{:S(2)}) %collective-permute-start.9) | collective-permute-done | bytes 786464 | tf_op jit(solution)/shard_map/ppermute | solution.py:492
  116.8 0.1 collective-permute-start.10
  116.9 1.9 %collective-permute-done.6.rest_0_ = f32[4,3,128,128]{3,2,1,0:T(8,128)S(1)} collective-permute-done((f32[4,3,128,128]{3,2,1,0:T(8,128)S(1)}, f32[4,3,128,128]{3,2,1,0:T(8,128)S(1)}, u32[]{:S(2)}, u32[]{:S(2)}) %collective-permute-start.6) | collective-permute-done | bytes 786464 | tf_op jit(solution)/shard_map/ppermute | solution.py:518
  118.9 2.3 %collective-permute-start.7 = (f32[4,3,128,128]{3,2,1,0:T(8,128)S(1)}, f32[4,3,128,128]{3,2,1,0:T(8,128)S(1)}, u32[]{:S(2)}, u32[]{:S(2)}) collective-permute-start(f32[4,3,128,128]{3,2,1,0:T(8,128)S(1)} %collective-permute-done.6.rest_0_), channel_id=1, source_target_pairs={{8,0},{16,8},{24,16},{28,24},{20,28},{12,20},{4,12},{0,4},{9,1},{1... | collective-permute-start | bytes 2359304 | tf_op jit(solution)/shard_map/ppermute | solution.py:518
  121.1 0.0 collective-permute-done.4.rest_1_
  121.1 0.0 collective-permute-start.5
  121.1 0.0 collective-permute-done.8.t1
  121.2 0.0 collective-permute-done.10.t3
  121.2 0.0 copy-start
  121.2 1.0 copy-done
  122.2 8.0 %row_panels.1 = (bf16[1536,1536]{1,0:T(8,128)(2,1)}, f32[12,1,24,1,128,128]{5,4,3,2,1,0:T(8,128)}, bf16[3,256,768]{2,1,0:T(8,128)(2,1)S(1)}, s32[64]{0:T(128)S(1)}, s32[25]{0:T(128)S(1)}) custom-call(s32[4]{0:T(128)S(1)} %copy-done.2, s32[32]{0:T(128)S(1)} %fusion.slot_in, f32[12,128,128]{2,1,0:T(8,128)S(1)} %get-tuple-element.39.t0, ...), custom_call_target="tpu_custom_call" | custom-call | tf_op jit(solution)/shard_map/row_panels/pallas_call | solution.py:287
  130.2 7.9 %collective-permute-done.7.rest_0_ = f32[4,3,128,128]{3,2,1,0:T(8,128)S(1)} collective-permute-done((f32[4,3,128,128]{3,2,1,0:T(8,128)S(1)}, f32[4,3,128,128]{3,2,1,0:T(8,128)S(1)}, u32[]{:S(2)}, u32[]{:S(2)}) %collective-permute-start.7) | collective-permute-done | bytes 786464 | tf_op jit(solution)/shard_map/ppermute | solution.py:518
  138.2 0.8 collective-permute-done.5.rest_1_
  138.9 1.0 collective-permute-start.11
  139.9 1.1 collective-permute-start.13
  141.0 0.0 copy-done.3
  141.0 0.0 copy-done.4
  141.0 9.1 %trailing.5.rest_5_ = f32[12,1,24,1,128,128]{5,4,3,2,1,0:T(8,128)} custom-call(s32[4]{0:T(128)S(1)} %copy-done.2, s32[192]{0:T(256)S(1)} %copy-done.4, s32[256]{0:T(256)S(1)} %copy-done.3, s32[64]{0:T(128)S(1)} %get-tuple-element.46.order, s32[25]{0:T(128)S(1)} %get-tuple-element.47.starts, ...), custom_call_target="tpu_custom_call", output_to_operand_aliasing={{}: (11, {})} | custom-call | flops 9663676416 | bytes 9437184 | tf_op jit(solution)/shard_map/trailing/pallas_call | solution.py:440
  150.1 9.7 %trailing.6.rest_4_ = f32[12,1,24,1,128,128]{5,4,3,2,1,0:T(8,128)} custom-call(s32[4]{0:T(128)S(1)} %copy-done.2, s32[192]{0:T(256)S(1)} %copy-done.4, s32[256]{0:T(256)S(1)} %copy-done.3, s32[64]{0:T(128)S(1)} %get-tuple-element.46.order, s32[25]{0:T(128)S(1)} %get-tuple-element.47.starts, ...), custom_call_target="tpu_custom_call", output_to_operand_aliasing={{}: (11, {})} | custom-call | flops 9663676416 | bytes 9437184 | tf_op jit(solution)/shard_map/trailing/pallas_call | solution.py:440
  159.8 9.8 %trailing.7.rest_5_ = f32[12,1,24,1,128,128]{5,4,3,2,1,0:T(8,128)} custom-call(s32[4]{0:T(128)S(1)} %copy-done.2, s32[192]{0:T(256)S(1)} %copy-done.4, s32[256]{0:T(256)S(1)} %copy-done.3, s32[64]{0:T(128)S(1)} %get-tuple-element.46.order, s32[25]{0:T(128)S(1)} %get-tuple-element.47.starts, ...), custom_call_target="tpu_custom_call", output_to_operand_aliasing={{}: (10, {})} | custom-call | flops 4831838208 | bytes 4718592 | tf_op jit(solution)/shard_map/trailing/pallas_call | solution.py:440
  169.7 0.0 collective-permute-done.11.rest_0_
  169.7 1.5 collective-permute-start.12
  171.2 0.0 collective-permute-done.13.rest_1_
  171.3 0.6 collective-permute-start.14
  171.9 9.7 %trailing.8.rest_5_ = f32[12,1,24,1,128,128]{5,4,3,2,1,0:T(8,128)} custom-call(s32[4]{0:T(128)S(1)} %copy-done.2, s32[192]{0:T(256)S(1)} %copy-done.4, s32[256]{0:T(256)S(1)} %copy-done.3, s32[64]{0:T(128)S(1)} %get-tuple-element.46.order, s32[25]{0:T(128)S(1)} %get-tuple-element.47.starts, ...), custom_call_target="tpu_custom_call", output_to_operand_aliasing={{}: (11, {})} | custom-call | flops 9663676416 | bytes 9437184 | tf_op jit(solution)/shard_map/trailing/pallas_call | solution.py:440
  181.6 0.0 collective-permute-done.12.rest_0_
  181.6 0.0 collective-permute-done.14.rest_1_
  181.6 9.8 %trailing.9 = f32[12,1,24,1,128,128]{5,4,3,2,1,0:T(8,128)} custom-call(s32[4]{0:T(128)S(1)} %copy-done.2, s32[192]{0:T(256)S(1)} %copy-done.4, s32[256]{0:T(256)S(1)} %copy-done.3, s32[64]{0:T(128)S(1)} %get-tuple-element.46.order, s32[25]{0:T(128)S(1)} %get-tuple-element.47.starts, ...), custom_call_target="tpu_custom_call", output_to_operand_aliasing={{}: (11, {})} | custom-call | flops 4831838208 | bytes 4718592 | tf_op jit(solution)/shard_map/trailing/pallas_call | solution.py:440
  (6 shorter events, 0.1 us)
Async XLA Ops:
  1.3 69.9 %copy-start.2 = (s32[4]{0:T(128)S(1)}, s32[4]{0:T(128)}, u32[]{:S(2)}) copy-start(s32[4]{0:T(128)} %pad_add_fusion.place) | copy-start | bytes 52
  5.0 136.0 %copy-start.3 = (s32[256]{0:T(256)S(1)}, s32[256]{0:T(256)}, u32[]{:S(2)}) copy-start(s32[256]{0:T(256)} %constant.18.clone.places_table) | copy-start | bytes 3076
  5.0 136.0 %copy-start.4 = (s32[192]{0:T(256)S(1)}, s32[192]{0:T(256)}, u32[]{:S(2)}) copy-start(s32[192]{0:T(256)} %constant.17.clone.columns_table) | copy-start | bytes 2308
  74.0 0.7 copy-start.1
  74.7 0.7 copy-start.5
  75.4 0.7 copy-start.6
  76.0 0.7 copy-start.7
  76.7 0.7 copy-start.8
  77.4 17.7 %all-to-all-start.1 = ((f32[32,16,128]{2,1,0:T(8,128)}), f32[32,16,128]{2,1,0:T(8,128)S(1)}, u32[]{:S(2)}, u32[]{:S(2)}) async-start(f32[32,16,128]{2,1,0:T(8,128)} %copy-done.1), calls=%async_computation.1 | async-start | bytes 524288 | tf_op jit(solution)/shard_map/all_to_all | solution.py:487
  80.0 7.8 %collective-permute-start = (f32[3,128,128]{2,1,0:T(8,128)}, f32[3,128,128]{2,1,0:T(8,128)S(1)}, u32[]{:S(2)}, u32[]{:S(2)}) collective-permute-start(f32[3,128,128]{2,1,0:T(8,128)} %copy-done.8), channel_id=1, source_target_pairs={{0,0},{1,4},{2,8},{3,12},{4,1},{5,5},{6,9},{7,13},{8,2},{9,6},{10,... | collective-permute-start | bytes 589832 | tf_op jit(solution)/shard_map/ppermute | solution.py:507
  81.6 12.2 %collective-permute-start.1 = (f32[3,128,128]{2,1,0:T(8,128)}, f32[3,128,128]{2,1,0:T(8,128)S(1)}, u32[]{:S(2)}, u32[]{:S(2)}) collective-permute-start(f32[3,128,128]{2,1,0:T(8,128)} %copy-done.7), channel_id=1, source_target_pairs={{0,4},{1,8},{2,12},{3,0},{4,5},{5,9},{6,13},{7,1},{8,6},{9,10},{10... | collective-permute-start | bytes 589832 | tf_op jit(solution)/shard_map/ppermute | solution.py:507
  83.7 10.4 %collective-permute-start.2 = (f32[3,128,128]{2,1,0:T(8,128)}, f32[3,128,128]{2,1,0:T(8,128)S(1)}, u32[]{:S(2)}, u32[]{:S(2)}) collective-permute-start(f32[3,128,128]{2,1,0:T(8,128)} %copy-done.6), channel_id=1, source_target_pairs={{0,8},{1,12},{2,0},{3,4},{4,9},{5,13},{6,1},{7,5},{8,10},{9,14},{1... | collective-permute-start | bytes 589832 | tf_op jit(solution)/shard_map/ppermute | solution.py:507
  87.2 7.9 %collective-permute-start.3 = (f32[3,128,128]{2,1,0:T(8,128)}, f32[3,128,128]{2,1,0:T(8,128)}, u32[]{:S(2)}, u32[]{:S(2)}) collective-permute-start(f32[3,128,128]{2,1,0:T(8,128)} %copy-done.5), channel_id=1, source_target_pairs={{0,12},{1,0},{2,4},{3,8},{4,13},{5,1},{6,5},{7,9},{8,14},{9,2},{10... | collective-permute-start | bytes 589832 | tf_op jit(solution)/shard_map/ppermute | solution.py:507
  87.8 6.3 %copy-start.9 = (f32[3,128,128]{2,1,0:T(8,128)}, f32[3,128,128]{2,1,0:T(8,128)S(1)}, u32[]{:S(2)}) copy-start(f32[3,128,128]{2,1,0:T(8,128)S(1)} %collective-permute-done) | copy-start | bytes 589828
  93.8 0.7 copy-start.10
  94.5 0.7 copy-start.11
  95.1 21.6 %collective-permute-start.9 = (f32[12,128,128]{2,1,0:T(8,128)S(1)}, f32[12,128,128]{2,1,0:T(8,128)S(1)}, u32[]{:S(2)}, u32[]{:S(2)}) collective-permute-start(f32[12,128,128]{2,1,0:T(8,128)S(1)} %get-tuple-element.39.t0), channel_id=1, source_target_pairs={{0,2},{1,3},{2,0},{3,1},{4,6},{5,7},{6,4},{7,5},{8,10},{9,11},{10,... | collective-permute-start | bytes 2359304 | tf_op jit(solution)/shard_map/ppermute | solution.py:492
  99.7 19.2 %collective-permute-start.6 = (f32[4,3,128,128]{3,2,1,0:T(8,128)S(1)}, f32[4,3,128,128]{3,2,1,0:T(8,128)S(1)}, u32[]{:S(2)}, u32[]{:S(2)}) collective-permute-start(f32[4,3,128,128]{3,2,1,0:T(8,128)S(1)} %pad_maximum_fusion.rest_0_), channel_id=1, source_target_pairs={{8,0},{16,8},{24,16},{28,24},{20,28},{12,20},{4,12},{0,4},{9,1},{1... | collective-permute-start | bytes 2359304 | tf_op jit(solution)/shard_map/ppermute | solution.py:518
  102.1 19.0 %collective-permute-start.4 = (f32[4,3,128,128]{3,2,1,0:T(8,128)S(1)}, f32[4,3,128,128]{3,2,1,0:T(8,128)S(1)}, u32[]{:S(2)}, u32[]{:S(2)}) collective-permute-start(f32[4,3,128,128]{3,2,1,0:T(8,128)S(1)} %pad_maximum_fusion.rest_0_), channel_id=1, source_target_pairs={{0,8},{8,16},{16,24},{24,28},{28,20},{20,12},{12,4},{4,0},{1,9},{9... | collective-permute-start | bytes 2359304 | tf_op jit(solution)/shard_map/ppermute | solution.py:517
  102.2 19.0 %collective-permute-start.8 = (f32[12,128,128]{2,1,0:T(8,128)S(1)}, f32[12,128,128]{2,1,0:T(8,128)S(1)}, u32[]{:S(2)}, u32[]{:S(2)}) collective-permute-start(f32[12,128,128]{2,1,0:T(8,128)S(1)} %get-tuple-element.39.t0), channel_id=1, source_target_pairs={{0,1},{1,0},{2,3},{3,2},{4,5},{5,4},{6,7},{7,6},{8,9},{9,8},{10,11... | collective-permute-start | bytes 2359304 | tf_op jit(solution)/shard_map/ppermute | solution.py:491
  116.8 4.4 %collective-permute-start.10 = (f32[12,128,128]{2,1,0:T(8,128)S(1)}, f32[12,128,128]{2,1,0:T(8,128)S(1)}, u32[]{:S(2)}, u32[]{:S(2)}) collective-permute-start(f32[12,128,128]{2,1,0:T(8,128)S(1)} %collective-permute-done.9.t2), channel_id=1, source_target_pairs={{0,1},{1,0},{2,3},{3,2},{4,5},{5,4},{6,7},{7,6},{8,9},{9,8},{10,11... | collective-permute-start | bytes 2359304 | tf_op jit(solution)/shard_map/ppermute | solution.py:493
  118.9 19.3 %collective-permute-start.7 = (f32[4,3,128,128]{3,2,1,0:T(8,128)S(1)}, f32[4,3,128,128]{3,2,1,0:T(8,128)S(1)}, u32[]{:S(2)}, u32[]{:S(2)}) collective-permute-start(f32[4,3,128,128]{3,2,1,0:T(8,128)S(1)} %collective-permute-done.6.rest_0_), channel_id=1, source_target_pairs={{8,0},{16,8},{24,16},{28,24},{20,28},{12,20},{4,12},{0,4},{9,1},{1... | collective-permute-start | bytes 2359304 | tf_op jit(solution)/shard_map/ppermute | solution.py:518
  121.1 17.8 %collective-permute-start.5 = (f32[4,3,128,128]{3,2,1,0:T(8,128)S(1)}, f32[4,3,128,128]{3,2,1,0:T(8,128)S(1)}, u32[]{:S(2)}, u32[]{:S(2)}) collective-permute-start(f32[4,3,128,128]{3,2,1,0:T(8,128)S(1)} %collective-permute-done.4.rest_1_), channel_id=1, source_target_pairs={{0,8},{8,16},{16,24},{24,28},{28,20},{20,12},{12,4},{4,0},{1,9},{9... | collective-permute-start | bytes 2359304 | tf_op jit(solution)/shard_map/ppermute | solution.py:517
  121.2 1.0 copy-start
  138.9 30.7 %collective-permute-start.11 = (f32[4,3,128,128]{3,2,1,0:T(8,128)S(1)}, f32[4,3,128,128]{3,2,1,0:T(8,128)S(1)}, u32[]{:S(2)}, u32[]{:S(2)}) collective-permute-start(f32[4,3,128,128]{3,2,1,0:T(8,128)S(1)} %collective-permute-done.5.rest_1_), channel_id=1, source_target_pairs={{0,8},{8,16},{16,24},{24,28},{28,20},{20,12},{12,4},{4,0},{1,9},{9... | collective-permute-start | bytes 2359304 | tf_op jit(solution)/shard_map/ppermute | solution.py:517
  139.9 31.3 %collective-permute-start.13 = (f32[4,3,128,128]{3,2,1,0:T(8,128)S(1)}, f32[4,3,128,128]{3,2,1,0:T(8,128)S(1)}, u32[]{:S(2)}, u32[]{:S(2)}) collective-permute-start(f32[4,3,128,128]{3,2,1,0:T(8,128)S(1)} %collective-permute-done.7.rest_0_), channel_id=1, source_target_pairs={{8,0},{16,8},{24,16},{28,24},{20,28},{12,20},{4,12},{0,4},{9,1},{1... | collective-permute-start | bytes 2359304 | tf_op jit(solution)/shard_map/ppermute | solution.py:518
  169.7 11.8 %collective-permute-start.12 = (f32[2,3,128,128]{3,2,1,0:T(8,128)S(1)}, f32[2,3,128,128]{3,2,1,0:T(8,128)S(1)}, u32[]{:S(2)}, u32[]{:S(2)}) collective-permute-start(f32[2,3,128,128]{3,2,1,0:T(8,128)S(1)} %slice.13), channel_id=1, source_target_pairs={{0,8},{8,16},{16,24},{24,28},{28,20},{20,12},{12,4},{4,0},{1,9},{9... | collective-permute-start | bytes 1179656 | tf_op jit(solution)/shard_map/ppermute | solution.py:522
  171.3 10.3 %collective-permute-start.14 = (f32[2,3,128,128]{3,2,1,0:T(8,128)S(1)}, f32[2,3,128,128]{3,2,1,0:T(8,128)S(1)}, u32[]{:S(2)}, u32[]{:S(2)}) collective-permute-start(f32[2,3,128,128]{3,2,1,0:T(8,128)S(1)} %slice.14), channel_id=1, source_target_pairs={{8,0},{16,8},{24,16},{28,24},{20,28},{12,20},{4,12},{0,4},{9,1},{1... | collective-permute-start | bytes 1179656 | tf_op jit(solution)/shard_map/ppermute | solution.py:522

commit v10 on v9

--- a/solution.py
+++ b/solution.py
@@ -13,6 +13,8 @@
 WIDTH = 2 * PANEL
 NOTE = 8
 VMEM = 46 * 1024 * 1024
+ALL_VMEM = 63 * 1024 * 1024
+PARTS = 3
 BOTH = ("row", "col")
 
 
@@ -133,22 +135,27 @@
             pltpu.SemaphoreType.DMA,
         ],
         out_shape=jax.ShapeDtypeStruct((devices, TILE + NOTE + height, TILE), jnp.float32),
-        compiler_params=pltpu.CompilerParams(vmem_limit_bytes=62 * 1024 * 1024),
+        compiler_params=pltpu.CompilerParams(vmem_limit_bytes=ALL_VMEM),
         name="pack",
     )(place, dest, slot, count, child_tiles, front)
 
 
 def columns_kernel(place, slot_in, front_ref, incoming_ref, out_ref, own_ref, *rest):
-    *parts, tile_ref, slices_ref, sem, slices_sem = rest
+    *parts, tile_ref, slices_ref, sem, slices_sem, strip_sems = rest
     cols = place[2]
     height = own_ref.shape[1]
-    strip = pltpu.make_async_copy(front_ref.at[:, 0, 0, 0], out_ref, sem)
-    strip.start()
+    strips = [
+        pltpu.make_async_copy(front_ref.at[a, 0, 0, 0], out_ref.at[a], strip_sems.at[a])
+        for a in range(out_ref.shape[0])
+    ]
+    for strip in strips:
+        strip.start()
     slices = pltpu.make_async_copy(
         incoming_ref.at[:, pl.ds(TILE + NOTE, height)], slices_ref, slices_sem
     )
     slices.start()
-    strip.wait()
+    for strip in strips:
+        strip.wait()
 
     @pl.loop(0, incoming_ref.shape[0])
     def _(s):
@@ -190,17 +197,23 @@
                 pltpu.VMEM((devices, height, TILE), jnp.float32),
                 pltpu.SemaphoreType.DMA,
                 pltpu.SemaphoreType.DMA,
+                pltpu.SemaphoreType.DMA((rows,)),
             ],
         ),
         out_shape=out_shape,
-        compiler_params=pltpu.CompilerParams(vmem_limit_bytes=VMEM),
+        compiler_params=pltpu.CompilerParams(vmem_limit_bytes=ALL_VMEM),
         name="panel_columns",
     )(place, slot_in, front, incoming)
 
 
+def panel_rows(source, target, sems, t):
+    span = pl.ds(pl.multiple_of(t * TILE, TILE), TILE)
+    return pltpu.make_async_copy(source.at[span], target.at[span], sems.at[t])
+
+
 def row_panels_kernel(
-    place, slot_in, t0, t1, t2, t3, lead_ref, diag_ref, pair_ref, out_ref, across_ref, order,
-    starts, small_ref, tiles_ref, cursor,
+    place, slot_in, t0, t1, t2, t3, lead_ref, diag_ref, pair_hbm, out_ref, across_ref, order,
+    starts, small_ref, tiles_ref, cursor, pair_ref, pair_sems,
 ):
     step = pl.program_id(0)
     cols = starts.shape[0] - 1
@@ -262,7 +275,16 @@
     for i, panel in enumerate((mask(1, one), mask(2, two))):
         high, low = halves(panel)
         for k, half in enumerate((high, low, high)):
-            pair_ref[:, k * WIDTH + i * PANEL : k * WIDTH + (i + 1) * PANEL] = half
+            lanes = slice(k * WIDTH + i * PANEL, k * WIDTH + (i + 1) * PANEL)
+            pair_ref[pl.ds(pl.multiple_of(step * height, height), height), lanes] = half
+    for t in range(group):
+        panel_rows(pair_ref, pair_hbm, pair_sems, step * group + t).start()
+
+    @pl.when(step == pl.num_programs(0) - 1)
+    def _():
+        for t in range(pair_sems.shape[0]):
+            panel_rows(pair_ref, pair_hbm, pair_sems, t).wait()
+
     pieces = (one[:, :TILE], one[:, TILE:], two[:, :TILE], two[:, TILE:])
     for c in range(4):
 
@@ -291,7 +313,7 @@
             grid=(3,),
             in_specs=[strip] * 4 + [whole_spec(lead), whole_spec(diag)],
             out_specs=[
-                pl.BlockSpec((height, 3 * WIDTH), lambda i, *_: (i, 0)),
+                pl.BlockSpec(memory_space=pltpu.HBM),
                 pl.BlockSpec((group, 1, 1, 1, TILE, TILE), lambda i, *_: (i, 0, 0, 0, 0, 0)),
                 whole_spec(out_shape[2]),
                 pl.BlockSpec(memory_space=pltpu.SMEM),
@@ -301,6 +323,8 @@
                 pltpu.VMEM((3, 3 * PANEL, PANEL), jnp.bfloat16),
                 pltpu.VMEM((4, group, TILE, TILE), jnp.float32),
                 pltpu.SMEM((cols,), jnp.int32),
+                pltpu.VMEM(out_shape[0].shape, jnp.bfloat16),
+                pltpu.SemaphoreType.DMA((rows,)),
             ],
         ),
         out_shape=out_shape,
@@ -315,7 +339,7 @@
     piece_refs = rest[:n_held]
     pair_hbm, front_ref, incoming_ref, _, out_ref, *rest = rest[n_held:]
     pair_ref, right_ref, taken, given, child_ref, *rest = rest
-    pair_sem, take_sems, give_sems, child_sems, *joined = rest
+    pair_sems, take_sems, give_sems, child_sems, *joined = rest
     if halved:
         joined[0][:2] = piece_refs[0][...]
         joined[0][2:] = piece_refs[1][...]
@@ -338,11 +362,13 @@
 
             @pl.when(wanted)
             def _():
-                act(
-                    pltpu.make_async_copy(
-                        front_ref.at[:, 0, b, 0], taken.at[slot, j], take_sems.at[slot, j]
+                for p in range(PARTS):
+                    span = pl.ds(p * (rows // PARTS), rows // PARTS)
+                    act(
+                        pltpu.make_async_copy(
+                            front_ref.at[span, 0, b, 0], taken.at[slot, j, span], take_sems.at[slot, j, p]
+                        )
                     )
-                )
 
     def each_give(step, width, act):
         slot = lax.rem(step, 2)
@@ -350,11 +376,13 @@
 
             @pl.when(wanted)
             def _():
-                act(
-                    pltpu.make_async_copy(
-                        given.at[slot, j], out_ref.at[:, 0, b, 0], give_sems.at[slot, j]
+                for p in range(PARTS):
+                    span = pl.ds(p * (rows // PARTS), rows // PARTS)
+                    act(
+                        pltpu.make_async_copy(
+                            given.at[slot, j, span], out_ref.at[span, 0, b, 0], give_sems.at[slot, j, p]
+                        )
                     )
-                )
 
     def each_child(step, width, act):
         for j, b, wanted in columns_of(step, width):
@@ -371,8 +399,8 @@
 
     start, wait = (lambda copy, *_: copy.start()), (lambda copy, *_: copy.wait())
     steps = [(step, 2) for step in range(pairs)] + [(pairs, 1)] * single
-    pair_copy = pltpu.make_async_copy(pair_hbm, pair_ref, pair_sem)
-    pair_copy.start()
+    for t in range(rows):
+        panel_rows(pair_hbm, pair_ref, pair_sems, t).start()
     for step, width in steps[:2]:
         each_take(step, width, start)
     for step, width in steps:
@@ -393,7 +421,8 @@
         high, low = halves(panel)
         for k, half in enumerate((high, high, low)):
             right_ref[k * WIDTH + i * PANEL : k * WIDTH + (i + 1) * PANEL] = half
-    pair_copy.wait()
+    for t in range(rows):
+        panel_rows(pair_hbm, pair_ref, pair_sems, t).wait()
 
     def update(step, width):
         slot = lax.rem(step, 2)
@@ -447,9 +476,9 @@
             pltpu.VMEM((2, 2, rows, TILE, TILE), jnp.float32),
             pltpu.VMEM((2, 2, rows, TILE, TILE), jnp.float32),
             pltpu.VMEM((devices, TILE, TILE), jnp.float32),
-            pltpu.SemaphoreType.DMA,
-            pltpu.SemaphoreType.DMA((2, 2)),
-            pltpu.SemaphoreType.DMA((2, 2)),
+            pltpu.SemaphoreType.DMA((rows,)),
+            pltpu.SemaphoreType.DMA((2, 2, PARTS)),
+            pltpu.SemaphoreType.DMA((2, 2, PARTS)),
             pltpu.SemaphoreType.DMA((devices,)),
         ]
         + [pltpu.VMEM((4, group, TILE, TILE), jnp.float32)] * halved,

time: 192 us -> 196 us (1.021)
  Pallas kernels: 62.7 us -> 67.1 us
    pallas_call x5, Pallas kernels: 48.2 us -> 50.6 us  [trailing(): pl.pallas_call(functools.partial(trailing_kernel, first, len(pieces), hal...]
    ppermute x3, starting transfers between devices: 5.81 us -> 3.82 us  [body(): behind = lax.ppermute(behind, 'row', down)]
    unnamed x24 -> x16, local copies, waits for them, and re-layouts: 5.54 us -> 4.34 us
  transfers between devices with their start and end apart: 16 -> 16, of which waited for: 6 -> 7; matrix products, arithmetic and copies ran while one was open for 1% -> 0% of each run, Pallas kernels for 24% -> 25%
where the time goes in v10:
time: 196 us
  Pallas kernels  67.1 us (34%)
  blocking collectives  65.5 us (33%)
  waiting for transfers between devices  31.5 us (16%)
  starting transfers between devices  24.1 us (12%)
  local copies, waits for them, and re-layouts  4.4 us (2%)
    all_to_all x1, blocking collectives, body(): lax.all_to_all(outgoing, BOTH, split_axis=0, concat_axis=0, tiled=True)  65.5 us
    pallas_call x5, Pallas kernels, trailing(): pl.pallas_call(functools.partial(trailing_kernel, first, len(pieces), hal...  50.6 us
    ppermute x1, waiting for transfers between devices, exchange(): far = lax.ppermute(mine, 'col', [(c, c ^ 2) for c in range(n_col)])  16 us
    pallas_call x1, Pallas kernels, row_panels(): pl.pallas_call(row_panels_kernel, grid_spec=pltpu.PrefetchScalarGridSpec(...  8.81 us
    ppermute x3, waiting for transfers between devices, body(): behind = lax.ppermute(behind, 'row', down)  7.94 us
    ppermute x4, starting transfers between devices, body(): arrived.append(lax.ppermute(part, BOTH, pairs))  7.86 us
    ppermute x4, waiting for transfers between devices, body(): arrived.append(lax.ppermute(part, BOTH, pairs))  6.65 us
    unnamed x16, local copies, waits for them, and re-layouts  4.34 us
  transfers between devices with their start and end apart: 16, of which 7 were waited for; matrix products, arithmetic and copies ran while one was open for 0% of the time, Pallas kernels for 25%

profile of v10, /device:TPU:0, one launch (start us, length us, event | category | flops | bytes accessed | tf_op | source)
XLA Modules:
  0.0 195.5 jit_solution(4550915765634495221)
XLA Ops:
  0.7 0.7 pad_add_fusion.place
  1.3 3.7 %pack.1 = f32[32,152,128]{2,1,0:T(8,128)} custom-call(s32[4]{0:T(128)} %pad_add_fusion.place, s32[16]{0:T(128)} %bitcast.14, s32[16]{0:T(128)} %slot.1, s32[1]{0:T(128)S(6)} %copy.19.count, f32[16,128,128]{2,1,0:T(8,128)} %child_ref.1, f32[12,1,24,1,128,128]{5,4,3,2,1,0:T(8,128)} %rest_3_.7), custom_call_target="tpu_custom_call" | custom-call | tf_op jit(solution)/shard_map/pack/pallas_call | solution.py:124
  5.0 0.0 copy-start.3
  5.0 0.0 copy-start.4
  5.0 0.0 copy-start.5
  5.1 0.0 copy-start.6
  5.1 65.5 %all_to_all.10.incoming_ref.rest_4_.rest_3_ = f32[32,152,128]{2,1,0:T(8,128)S(1)} all-to-all(f32[32,152,128]{2,1,0:T(8,128)} %pack.1), channel_id=1, replica_groups=mesh['row'=8,'col'=4] {'row','col'}, dimensions={0} | all-to-all | bytes 4980736 | tf_op jit(solution)/shard_map/all_to_all | solution.py:511
  70.6 0.0 copy-start
  70.6 1.5 copy-done
  72.1 1.2 fusion.slot_in
  73.3 0.0 copy-start.7
  73.3 4.0 %panel_columns.1 = (f32[12,128,128]{2,1,0:T(8,128)}, f32[32,16,128]{2,1,0:T(8,128)}, f32[3,128,128]{2,1,0:T(8,128)}, f32[3,128,128]{2,1,0:T(8,128)}, f32[3,128,128]{2,1,0:T(8,128)}, /*index=5*/f32[3,128,128]{2,1,0:T(8,128)}) custom-call(s32[4]{0:T(128)} %pad_add_fusion.place, s32[32]{0:T(128)} %fusion.slot_in, f32[12,1,24,1,128,128]{5,4,3,2,1,0:T(8,128)} %rest_3_.7, ...), custom_call_target="tpu_custom_call" | custom-call | tf_op jit(solution)/shard_map/panel_columns/pallas_call | solution.py:188
  77.3 4.2 %all-to-all-start.1 = ((f32[32,16,128]{2,1,0:T(8,128)}), f32[32,16,128]{2,1,0:T(8,128)S(1)}, u32[]{:S(2)}, u32[]{:S(2)}) async-start(f32[32,16,128]{2,1,0:T(8,128)} %get-tuple-element.34), calls=%async_computation.1 | async-start | bytes 524288 | tf_op jit(solution)/shard_map/all_to_all | solution.py:516
  81.5 1.6 collective-permute-start
  83.1 2.3 %collective-permute-start.1 = (f32[3,128,128]{2,1,0:T(8,128)}, f32[3,128,128]{2,1,0:T(8,128)S(1)}, u32[]{:S(2)}, u32[]{:S(2)}) collective-permute-start(f32[3,128,128]{2,1,0:T(8,128)} %get-tuple-element.30), channel_id=1, source_target_pairs={{0,4},{1,8},{2,12},{3,0},{4,5},{5,9},{6,13},{7,1},{8,6},{9,10},{10... | collective-permute-start | bytes 589832 | tf_op jit(solution)/shard_map/ppermute | solution.py:536
  85.4 3.5 %collective-permute-start.2 = (f32[3,128,128]{2,1,0:T(8,128)}, f32[3,128,128]{2,1,0:T(8,128)S(1)}, u32[]{:S(2)}, u32[]{:S(2)}) collective-permute-start(f32[3,128,128]{2,1,0:T(8,128)} %get-tuple-element.31), channel_id=1, source_target_pairs={{0,8},{1,12},{2,0},{3,4},{4,9},{5,13},{6,1},{7,5},{8,10},{9,14},{1... | collective-permute-start | bytes 589832 | tf_op jit(solution)/shard_map/ppermute | solution.py:536
  88.8 0.5 collective-permute-start.3
  89.4 0.0 collective-permute-done
  89.4 5.8 %collective-permute-done.1 = f32[3,128,128]{2,1,0:T(8,128)S(1)} collective-permute-done((f32[3,128,128]{2,1,0:T(8,128)}, f32[3,128,128]{2,1,0:T(8,128)S(1)}, u32[]{:S(2)}, u32[]{:S(2)}) %collective-permute-start.1) | collective-permute-done | bytes 196640 | tf_op jit(solution)/shard_map/ppermute | solution.py:536
  95.1 0.4 collective-permute-done.2
  95.6 0.5 collective-permute-done.3
  96.0 0.0 all-to-all-done.1
  96.0 3.8 %collective-permute-start.9 = (f32[12,128,128]{2,1,0:T(8,128)}, f32[12,128,128]{2,1,0:T(8,128)S(1)}, u32[]{:S(2)}, u32[]{:S(2)}) collective-permute-start(f32[12,128,128]{2,1,0:T(8,128)} %get-tuple-element.39.t0), channel_id=1, source_target_pairs={{0,2},{1,3},{2,0},{3,1},{4,6},{5,7},{6,4},{7,5},{8,10},{9,11},{10,... | collective-permute-start | bytes 2359304 | tf_op jit(solution)/shard_map/ppermute | solution.py:521
  99.8 0.1 pad_maximum_fusion.rest_0_
  99.9 1.3 collective-permute-start.6
  101.2 0.8 collective-permute-start.4
  102.0 0.0 collective-permute-start.8
  102.0 16.0 %collective-permute-done.9.t2 = f32[12,128,128]{2,1,0:T(8,128)S(1)} collective-permute-done((f32[12,128,128]{2,1,0:T(8,128)}, f32[12,128,128]{2,1,0:T(8,128)S(1)}, u32[]{:S(2)}, u32[]{:S(2)}) %collective-permute-start.9) | collective-permute-done | bytes 786464 | tf_op jit(solution)/shard_map/ppermute | solution.py:521
  118.0 0.0 collective-permute-start.10
  118.0 1.1 collective-permute-done.6.rest_0_
  119.1 1.4 collective-permute-start.7
  120.5 0.0 collective-permute-done.4.rest_1_
  120.5 0.6 collective-permute-start.5
  121.1 0.0 collective-permute-done.8.t1
  121.1 0.0 collective-permute-done.10.t3
  121.1 0.0 copy-done.3
  121.1 0.0 copy-done.4
  121.2 0.0 copy-done.7
  121.2 0.0 copy-start.2
  121.2 1.1 copy-done.2
  122.3 8.8 %row_panels.1 = (bf16[1536,1536]{1,0:T(8,128)(2,1)}, f32[12,1,24,1,128,128]{5,4,3,2,1,0:T(8,128)}, bf16[3,256,768]{2,1,0:T(8,128)(2,1)S(1)}, s32[64]{0:T(128)S(1)}, s32[25]{0:T(128)S(1)}) custom-call(s32[4]{0:T(128)S(1)} %copy-done.4, s32[32]{0:T(128)S(1)} %copy-done.7, f32[12,128,128]{2,1,0:T(8,128)S(1)} %copy-done.2, ...), custom_call_target="tpu_custom_call" | custom-call | tf_op jit(solution)/shard_map/row_panels/pallas_call | solution.py:309
  131.1 6.8 %collective-permute-done.7.rest_0_ = f32[4,3,128,128]{3,2,1,0:T(8,128)S(1)} collective-permute-done((f32[4,3,128,128]{3,2,1,0:T(8,128)S(1)}, f32[4,3,128,128]{3,2,1,0:T(8,128)S(1)}, u32[]{:S(2)}, u32[]{:S(2)}) %collective-permute-start.7) | collective-permute-done | bytes 786464 | tf_op jit(solution)/shard_map/ppermute | solution.py:547
  138.0 0.9 collective-permute-done.5.rest_1_
  138.8 0.9 collective-permute-start.11
  139.7 1.1 collective-permute-start.13
  140.8 0.0 copy-done.5
  140.8 0.0 copy-done.6
  140.8 0.0 copy-start.1
  140.8 1.7 copy-done.1
  142.5 9.7 %trailing.5.rest_5_ = f32[12,1,24,1,128,128]{5,4,3,2,1,0:T(8,128)} custom-call(s32[4]{0:T(128)S(1)} %copy-done.4, s32[192]{0:T(256)S(1)} %copy-done.6, s32[256]{0:T(256)S(1)} %copy-done.5, s32[64]{0:T(128)S(1)} %get-tuple-element.46.order, s32[25]{0:T(128)S(1)} %get-tuple-element.47.starts, ...), custom_call_target="tpu_custom_call", output_to_operand_aliasing={{}: (11, {})} | custom-call | flops 9663676416 | bytes 9437184 | tf_op jit(solution)/shard_map/trailing/pallas_call | solution.py:469
  152.3 10.3 %trailing.6.rest_4_ = f32[12,1,24,1,128,128]{5,4,3,2,1,0:T(8,128)} custom-call(s32[4]{0:T(128)S(1)} %copy-done.4, s32[192]{0:T(256)S(1)} %copy-done.6, s32[256]{0:T(256)S(1)} %copy-done.5, s32[64]{0:T(128)S(1)} %get-tuple-element.46.order, s32[25]{0:T(128)S(1)} %get-tuple-element.47.starts, ...), custom_call_target="tpu_custom_call", output_to_operand_aliasing={{}: (11, {})} | custom-call | flops 9663676416 | bytes 9437184 | tf_op jit(solution)/shard_map/trailing/pallas_call | solution.py:469
  162.5 10.2 %trailing.7.rest_5_ = f32[12,1,24,1,128,128]{5,4,3,2,1,0:T(8,128)} custom-call(s32[4]{0:T(128)S(1)} %copy-done.4, s32[192]{0:T(256)S(1)} %copy-done.6, s32[256]{0:T(256)S(1)} %copy-done.5, s32[64]{0:T(128)S(1)} %get-tuple-element.46.order, s32[25]{0:T(128)S(1)} %get-tuple-element.47.starts, ...), custom_call_target="tpu_custom_call", output_to_operand_aliasing={{}: (10, {})} | custom-call | flops 4831838208 | bytes 4718592 | tf_op jit(solution)/shard_map/trailing/pallas_call | solution.py:469
  172.8 0.0 collective-permute-done.11.rest_0_
  172.8 1.2 collective-permute-start.12
  174.1 0.0 collective-permute-done.13.rest_1_
  174.1 0.9 collective-permute-start.14
  175.0 10.2 %trailing.8.rest_5_ = f32[12,1,24,1,128,128]{5,4,3,2,1,0:T(8,128)} custom-call(s32[4]{0:T(128)S(1)} %copy-done.4, s32[192]{0:T(256)S(1)} %copy-done.6, s32[256]{0:T(256)S(1)} %copy-done.5, s32[64]{0:T(128)S(1)} %get-tuple-element.46.order, s32[25]{0:T(128)S(1)} %get-tuple-element.47.starts, ...), custom_call_target="tpu_custom_call", output_to_operand_aliasing={{}: (11, {})} | custom-call | flops 9663676416 | bytes 9437184 | tf_op jit(solution)/shard_map/trailing/pallas_call | solution.py:469
  185.3 0.0 collective-permute-done.12.rest_0_
  185.3 0.0 collective-permute-done.14.rest_1_
  185.3 10.1 %trailing.9 = f32[12,1,24,1,128,128]{5,4,3,2,1,0:T(8,128)} custom-call(s32[4]{0:T(128)S(1)} %copy-done.4, s32[192]{0:T(256)S(1)} %copy-done.6, s32[256]{0:T(256)S(1)} %copy-done.5, s32[64]{0:T(128)S(1)} %get-tuple-element.46.order, s32[25]{0:T(128)S(1)} %get-tuple-element.47.starts, ...), custom_call_target="tpu_custom_call", output_to_operand_aliasing={{}: (11, {})} | custom-call | flops 4831838208 | bytes 4718592 | tf_op jit(solution)/shard_map/trailing/pallas_call | solution.py:469
  (2 shorter events, 0.1 us)
Async XLA Ops:
  5.0 116.1 %copy-start.3 = (f32[2,256,256]{2,1,0:T(8,128)S(1)}, f32[2,256,256]{2,1,0:T(8,128)}, u32[]{:S(2)}) copy-start(f32[2,256,256]{2,1,0:T(8,128)} %diag_ref.1) | copy-start | bytes 1572868
  5.0 116.1 %copy-start.4 = (s32[4]{0:T(128)S(1)}, s32[4]{0:T(128)}, u32[]{:S(2)}) copy-start(s32[4]{0:T(128)} %pad_add_fusion.place) | copy-start | bytes 52
  5.0 135.8 %copy-start.5 = (s32[256]{0:T(256)S(1)}, s32[256]{0:T(256)}, u32[]{:S(2)}) copy-start(s32[256]{0:T(256)} %constant.18.clone.places_table) | copy-start | bytes 3076
  5.1 135.8 %copy-start.6 = (s32[192]{0:T(256)S(1)}, s32[192]{0:T(256)}, u32[]{:S(2)}) copy-start(s32[192]{0:T(256)} %constant.17.clone.columns_table) | copy-start | bytes 2308
  70.6 1.5 copy-start
  73.3 47.9 %copy-start.7 = (s32[32]{0:T(128)S(1)}, s32[32]{0:T(128)}, u32[]{:S(2)}) copy-start(s32[32]{0:T(128)} %fusion.slot_in) | copy-start | bytes 388
  77.3 18.7 %all-to-all-start.1 = ((f32[32,16,128]{2,1,0:T(8,128)}), f32[32,16,128]{2,1,0:T(8,128)S(1)}, u32[]{:S(2)}, u32[]{:S(2)}) async-start(f32[32,16,128]{2,1,0:T(8,128)} %get-tuple-element.34), calls=%async_computation.1 | async-start | bytes 524288 | tf_op jit(solution)/shard_map/all_to_all | solution.py:516
  81.5 7.9 %collective-permute-start = (f32[3,128,128]{2,1,0:T(8,128)}, f32[3,128,128]{2,1,0:T(8,128)S(1)}, u32[]{:S(2)}, u32[]{:S(2)}) collective-permute-start(f32[3,128,128]{2,1,0:T(8,128)} %get-tuple-element.29), channel_id=1, source_target_pairs={{0,0},{1,4},{2,8},{3,12},{4,1},{5,5},{6,9},{7,13},{8,2},{9,6},{10,... | collective-permute-start | bytes 589832 | tf_op jit(solution)/shard_map/ppermute | solution.py:536
  83.1 12.0 %collective-permute-start.1 = (f32[3,128,128]{2,1,0:T(8,128)}, f32[3,128,128]{2,1,0:T(8,128)S(1)}, u32[]{:S(2)}, u32[]{:S(2)}) collective-permute-start(f32[3,128,128]{2,1,0:T(8,128)} %get-tuple-element.30), channel_id=1, source_target_pairs={{0,4},{1,8},{2,12},{3,0},{4,5},{5,9},{6,13},{7,1},{8,6},{9,10},{10... | collective-permute-start | bytes 589832 | tf_op jit(solution)/shard_map/ppermute | solution.py:536
  85.4 10.2 %collective-permute-start.2 = (f32[3,128,128]{2,1,0:T(8,128)}, f32[3,128,128]{2,1,0:T(8,128)S(1)}, u32[]{:S(2)}, u32[]{:S(2)}) collective-permute-start(f32[3,128,128]{2,1,0:T(8,128)} %get-tuple-element.31), channel_id=1, source_target_pairs={{0,8},{1,12},{2,0},{3,4},{4,9},{5,13},{6,1},{7,5},{8,10},{9,14},{1... | collective-permute-start | bytes 589832 | tf_op jit(solution)/shard_map/ppermute | solution.py:536
  88.8 7.2 %collective-permute-start.3 = (f32[3,128,128]{2,1,0:T(8,128)}, f32[3,128,128]{2,1,0:T(8,128)S(1)}, u32[]{:S(2)}, u32[]{:S(2)}) collective-permute-start(f32[3,128,128]{2,1,0:T(8,128)} %get-tuple-element.32), channel_id=1, source_target_pairs={{0,12},{1,0},{2,4},{3,8},{4,13},{5,1},{6,5},{7,9},{8,14},{9,2},{10... | collective-permute-start | bytes 589832 | tf_op jit(solution)/shard_map/ppermute | solution.py:536
  96.0 22.0 %collective-permute-start.9 = (f32[12,128,128]{2,1,0:T(8,128)}, f32[12,128,128]{2,1,0:T(8,128)S(1)}, u32[]{:S(2)}, u32[]{:S(2)}) collective-permute-start(f32[12,128,128]{2,1,0:T(8,128)} %get-tuple-element.39.t0), channel_id=1, source_target_pairs={{0,2},{1,3},{2,0},{3,1},{4,6},{5,7},{6,4},{7,5},{8,10},{9,11},{10,... | collective-permute-start | bytes 2359304 | tf_op jit(solution)/shard_map/ppermute | solution.py:521
  99.9 19.2 %collective-permute-start.6 = (f32[4,3,128,128]{3,2,1,0:T(8,128)S(1)}, f32[4,3,128,128]{3,2,1,0:T(8,128)S(1)}, u32[]{:S(2)}, u32[]{:S(2)}) collective-permute-start(f32[4,3,128,128]{3,2,1,0:T(8,128)S(1)} %pad_maximum_fusion.rest_0_), channel_id=1, source_target_pairs={{8,0},{16,8},{24,16},{28,24},{20,28},{12,20},{4,12},{0,4},{9,1},{1... | collective-permute-start | bytes 2359304 | tf_op jit(solution)/shard_map/ppermute | solution.py:547
  101.2 19.3 %collective-permute-start.4 = (f32[4,3,128,128]{3,2,1,0:T(8,128)S(1)}, f32[4,3,128,128]{3,2,1,0:T(8,128)S(1)}, u32[]{:S(2)}, u32[]{:S(2)}) collective-permute-start(f32[4,3,128,128]{3,2,1,0:T(8,128)S(1)} %pad_maximum_fusion.rest_0_), channel_id=1, source_target_pairs={{0,8},{8,16},{16,24},{24,28},{28,20},{20,12},{12,4},{4,0},{1,9},{9... | collective-permute-start | bytes 2359304 | tf_op jit(solution)/shard_map/ppermute | solution.py:546
  102.0 19.2 %collective-permute-start.8 = (f32[12,128,128]{2,1,0:T(8,128)}, f32[12,128,128]{2,1,0:T(8,128)S(1)}, u32[]{:S(2)}, u32[]{:S(2)}) collective-permute-start(f32[12,128,128]{2,1,0:T(8,128)} %get-tuple-element.39.t0), channel_id=1, source_target_pairs={{0,1},{1,0},{2,3},{3,2},{4,5},{5,4},{6,7},{7,6},{8,9},{9,8},{10,11... | collective-permute-start | bytes 2359304 | tf_op jit(solution)/shard_map/ppermute | solution.py:520
  118.0 3.1 %collective-permute-start.10 = (f32[12,128,128]{2,1,0:T(8,128)S(1)}, f32[12,128,128]{2,1,0:T(8,128)S(1)}, u32[]{:S(2)}, u32[]{:S(2)}) collective-permute-start(f32[12,128,128]{2,1,0:T(8,128)S(1)} %collective-permute-done.9.t2), channel_id=1, source_target_pairs={{0,1},{1,0},{2,3},{3,2},{4,5},{5,4},{6,7},{7,6},{8,9},{9,8},{10,11... | collective-permute-start | bytes 2359304 | tf_op jit(solution)/shard_map/ppermute | solution.py:522
  119.1 18.8 %collective-permute-start.7 = (f32[4,3,128,128]{3,2,1,0:T(8,128)S(1)}, f32[4,3,128,128]{3,2,1,0:T(8,128)S(1)}, u32[]{:S(2)}, u32[]{:S(2)}) collective-permute-start(f32[4,3,128,128]{3,2,1,0:T(8,128)S(1)} %collective-permute-done.6.rest_0_), channel_id=1, source_target_pairs={{8,0},{16,8},{24,16},{28,24},{20,28},{12,20},{4,12},{0,4},{9,1},{1... | collective-permute-start | bytes 2359304 | tf_op jit(solution)/shard_map/ppermute | solution.py:547
  120.5 18.3 %collective-permute-start.5 = (f32[4,3,128,128]{3,2,1,0:T(8,128)S(1)}, f32[4,3,128,128]{3,2,1,0:T(8,128)S(1)}, u32[]{:S(2)}, u32[]{:S(2)}) collective-permute-start(f32[4,3,128,128]{3,2,1,0:T(8,128)S(1)} %collective-permute-done.4.rest_1_), channel_id=1, source_target_pairs={{0,8},{8,16},{16,24},{24,28},{28,20},{20,12},{12,4},{4,0},{1,9},{9... | collective-permute-start | bytes 2359304 | tf_op jit(solution)/shard_map/ppermute | solution.py:546
  121.2 1.1 copy-start.2
  138.8 34.0 %collective-permute-start.11 = (f32[4,3,128,128]{3,2,1,0:T(8,128)S(1)}, f32[4,3,128,128]{3,2,1,0:T(8,128)S(1)}, u32[]{:S(2)}, u32[]{:S(2)}) collective-permute-start(f32[4,3,128,128]{3,2,1,0:T(8,128)S(1)} %collective-permute-done.5.rest_1_), channel_id=1, source_target_pairs={{0,8},{8,16},{16,24},{24,28},{28,20},{20,12},{12,4},{4,0},{1,9},{9... | collective-permute-start | bytes 2359304 | tf_op jit(solution)/shard_map/ppermute | solution.py:546
  139.7 34.4 %collective-permute-start.13 = (f32[4,3,128,128]{3,2,1,0:T(8,128)S(1)}, f32[4,3,128,128]{3,2,1,0:T(8,128)S(1)}, u32[]{:S(2)}, u32[]{:S(2)}) collective-permute-start(f32[4,3,128,128]{3,2,1,0:T(8,128)S(1)} %collective-permute-done.7.rest_0_), channel_id=1, source_target_pairs={{8,0},{16,8},{24,16},{28,24},{20,28},{12,20},{4,12},{0,4},{9,1},{1... | collective-permute-start | bytes 2359304 | tf_op jit(solution)/shard_map/ppermute | solution.py:547
  140.8 1.7 copy-start.1
  172.8 12.4 %collective-permute-start.12 = (f32[2,3,128,128]{3,2,1,0:T(8,128)S(1)}, f32[2,3,128,128]{3,2,1,0:T(8,128)S(1)}, u32[]{:S(2)}, u32[]{:S(2)}) collective-permute-start(f32[2,3,128,128]{3,2,1,0:T(8,128)S(1)} %slice.13), channel_id=1, source_target_pairs={{0,8},{8,16},{16,24},{24,28},{28,20},{20,12},{12,4},{4,0},{1,9},{9... | collective-permute-start | bytes 1179656 | tf_op jit(solution)/shard_map/ppermute | solution.py:551
  174.1 11.2 %collective-permute-start.14 = (f32[2,3,128,128]{3,2,1,0:T(8,128)S(1)}, f32[2,3,128,128]{3,2,1,0:T(8,128)S(1)}, u32[]{:S(2)}, u32[]{:S(2)}) collective-permute-start(f32[2,3,128,128]{3,2,1,0:T(8,128)S(1)} %slice.14), channel_id=1, source_target_pairs={{8,0},{16,8},{24,16},{28,24},{20,28},{12,20},{4,12},{0,4},{9,1},{1... | collective-permute-start | bytes 1179656 | tf_op jit(solution)/shard_map/ppermute | solution.py:551

commit v11 on v10

--- a/solution.py
+++ b/solution.py
@@ -14,7 +14,6 @@
 NOTE = 8
 VMEM = 46 * 1024 * 1024
 ALL_VMEM = 63 * 1024 * 1024
-PARTS = 3
 BOTH = ("row", "col")
 
 
@@ -201,7 +200,7 @@
             ],
         ),
         out_shape=out_shape,
-        compiler_params=pltpu.CompilerParams(vmem_limit_bytes=ALL_VMEM),
+        compiler_params=pltpu.CompilerParams(vmem_limit_bytes=VMEM),
         name="panel_columns",
     )(place, slot_in, front, incoming)
 
@@ -294,9 +293,8 @@
 
 
 def row_panels(mine, others, lead, diag, place, slot_in, front):
-    rows = front.shape[0]
-    cols = front.shape[2]
-    group = rows // 3
+    rows, cols = front.shape[0], front.shape[2]
+    group = 2 - rows % 2
     height = group * TILE
     out_shape = [
         jax.ShapeDtypeStruct((rows * TILE, 3 * WIDTH), jnp.bfloat16),
@@ -310,7 +308,7 @@
         row_panels_kernel,
         grid_spec=pltpu.PrefetchScalarGridSpec(
             num_scalar_prefetch=2,
-            grid=(3,),
+            grid=(rows // group,),
             in_specs=[strip] * 4 + [whole_spec(lead), whole_spec(diag)],
             out_specs=[
                 pl.BlockSpec(memory_space=pltpu.HBM),
@@ -346,46 +344,39 @@
         piece_refs = joined
     group = piece_refs[0].shape[1]
     count = len(piece_refs) * group
-    pairs, single = count // 2, count % 2
+    steps = (count + 1) // 2
     rows, cols = front_ref.shape[0], front_ref.shape[2]
     columns_base = place[0] * cols + first * group
     places_base = (place[0] * (cols // group) + first) * 4
 
-    def columns_of(step, width):
-        for j in range(width):
-            b = columns_table[columns_base + 2 * step + j]
-            yield j, b, b > 0
-
-    def each_take(step, width, act):
+    def columns_of(step):
+        for j in range(2):
+            b = columns_table[columns_base + jnp.minimum(2 * step, count - 2) + j]
+            wanted = b > 0
+            if count % 2 and j == 0:
+                wanted = jnp.logical_and(wanted, step < steps - 1)
+            yield j, b, wanted
+
+    def each_take(step, act):
         slot = lax.rem(step, 2)
-        for j, b, wanted in columns_of(step, width):
+        for j, b, wanted in columns_of(step):
 
             @pl.when(wanted)
             def _():
-                for p in range(PARTS):
-                    span = pl.ds(p * (rows // PARTS), rows // PARTS)
-                    act(
-                        pltpu.make_async_copy(
-                            front_ref.at[span, 0, b, 0], taken.at[slot, j, span], take_sems.at[slot, j, p]
-                        )
-                    )
-
-    def each_give(step, width, act):
+                source = front_ref.at[:, 0, b, 0]
+                act(pltpu.make_async_copy(source, taken.at[slot, j], take_sems.at[slot, j]))
+
+    def each_give(step, act):
         slot = lax.rem(step, 2)
-        for j, b, wanted in columns_of(step, width):
+        for j, b, wanted in columns_of(step):
 
             @pl.when(wanted)
             def _():
-                for p in range(PARTS):
-                    span = pl.ds(p * (rows // PARTS), rows // PARTS)
-                    act(
-                        pltpu.make_async_copy(
-                            given.at[slot, j, span], out_ref.at[span, 0, b, 0], give_sems.at[slot, j, p]
-                        )
-                    )
-
-    def each_child(step, width, act):
-        for j, b, wanted in columns_of(step, width):
+                target = out_ref.at[:, 0, b, 0]
+                act(pltpu.make_async_copy(given.at[slot, j], target, give_sems.at[slot, j]))
+
+    def each_child(step, act):
+        for j, b, wanted in columns_of(step):
 
             @pl.when(wanted)
             def _():
@@ -398,13 +389,12 @@
                     act(copy, j, s, order[2 * i + 1])
 
     start, wait = (lambda copy, *_: copy.start()), (lambda copy, *_: copy.wait())
-    steps = [(step, 2) for step in range(pairs)] + [(pairs, 1)] * single
     for t in range(rows):
         panel_rows(pair_hbm, pair_ref, pair_sems, t).start()
-    for step, width in steps[:2]:
-        each_take(step, width, start)
-    for step, width in steps:
-        each_child(step, width, start)
+    for step in range(min(steps, 2)):
+        each_take(step, start)
+    for step in range(steps):
+        each_child(step, start)
 
     tile_columns = [
         jnp.concatenate(
@@ -424,34 +414,35 @@
     for t in range(rows):
         panel_rows(pair_hbm, pair_ref, pair_sems, t).wait()
 
-    def update(step, width):
+    block = rows // 3
+    height = block * TILE
+
+    @pl.loop(0, steps)
+    def _(step):
         slot = lax.rem(step, 2)
-        each_take(step, width, wait)
-        pl.when(step >= 2)(lambda: each_give(step - 2, 2, wait))
-        lanes = pl.ds(pl.multiple_of(2 * step * TILE, TILE), width * TILE)
-        change = dot(pair_ref[...], right_ref[:, lanes])
-        for j in range(width):
-            part = change[:, j * TILE : (j + 1) * TILE].reshape(rows, TILE, TILE)
-            given[slot, j] = taken[slot, j] - part
+        each_take(step, wait)
+        pl.when(step >= 2)(lambda: each_give(step - 2, wait))
+        lanes = pl.ds(pl.multiple_of(jnp.minimum(2 * step, count - 2) * TILE, TILE), 2 * TILE)
+
+        @pl.loop(0, 3)
+        def _(m):
+            left = pair_ref[pl.ds(pl.multiple_of(m * height, height), height)]
+            change = dot(left, right_ref[:, lanes])
+            span = pl.ds(m * block, block)
+            for j in range(2):
+                part = change[:, j * TILE : (j + 1) * TILE].reshape(block, TILE, TILE)
+                given[slot, j, span] = taken[slot, j, span] - part
 
         def add(copy, j, s, a):
             copy.wait()
             given[slot, j, a] = given[slot, j, a] + child_ref[s]
 
-        each_child(step, width, add)
-        each_give(step, width, start)
-
-    @pl.loop(0, pairs)
-    def _(step):
-        update(step, 2)
-        pl.when(step + 2 < pairs)(lambda: each_take(step + 2, 2, start))
-        if single:
-            pl.when(step + 2 == pairs)(lambda: each_take(step + 2, 1, start))
-
-    if single:
-        update(jnp.int32(pairs), 1)
-    for step, width in steps[-2:]:
-        each_give(step, width, wait)
+        each_child(step, add)
+        each_give(step, start)
+        pl.when(step + 2 < steps)(lambda: each_take(step + 2, start))
+
+    for step in range(max(steps - 2, 0), steps):
+        each_give(step, wait)
 
 
 def trailing(front, pieces, first, place, tables, panels, incoming):
@@ -477,8 +468,8 @@
             pltpu.VMEM((2, 2, rows, TILE, TILE), jnp.float32),
             pltpu.VMEM((devices, TILE, TILE), jnp.float32),
             pltpu.SemaphoreType.DMA((rows,)),
-            pltpu.SemaphoreType.DMA((2, 2, PARTS)),
-            pltpu.SemaphoreType.DMA((2, 2, PARTS)),
+            pltpu.SemaphoreType.DMA((2, 2)),
+            pltpu.SemaphoreType.DMA((2, 2)),
             pltpu.SemaphoreType.DMA((devices,)),
         ]
         + [pltpu.VMEM((4, group, TILE, TILE), jnp.float32)] * halved,

time: 196 us -> 191 us (0.974)
  Pallas kernels: 67.1 us -> 63.9 us
    pallas_call x5, Pallas kernels: 50.6 us -> 47.6 us  [trailing(): pl.pallas_call(functools.partial(trailing_kernel, first, len(pieces), hal...]
    ppermute x3, starting transfers between devices: 3.82 us -> 6.05 us  [body(): behind = lax.ppermute(behind, 'row', down)]
    unnamed x16 -> x24, local copies, waits for them, and re-layouts: 4.34 us -> 5.42 us
  transfers between devices with their start and end apart: 16 -> 16, of which waited for: 7 -> 6; matrix products, arithmetic and copies ran while one was open for 0% -> 1% of each run, Pallas kernels for 25% -> 26%
where the time goes in v11:
time: 191 us
  blocking collectives  65.3 us (34%)
  Pallas kernels  63.9 us (33%)
  waiting for transfers between devices  29.7 us (16%)
  starting transfers between devices  23.2 us (12%)
  local copies, waits for them, and re-layouts  5.47 us (3%)
  other arithmetic  2.55 us (1%)
    all_to_all x1, blocking collectives, body(): lax.all_to_all(outgoing, BOTH, split_axis=0, concat_axis=0, tiled=True)  65.3 us
    pallas_call x5, Pallas kernels, trailing(): pl.pallas_call(functools.partial(trailing_kernel, first, len(pieces), hal...  47.6 us
    ppermute x1, waiting for transfers between devices, exchange(): far = lax.ppermute(mine, 'col', [(c, c ^ 2) for c in range(n_col)])  14.5 us
    pallas_call x1, Pallas kernels, row_panels(): pl.pallas_call(row_panels_kernel, grid_spec=pltpu.PrefetchScalarGridSpec(...  9.79 us
    ppermute x3, waiting for transfers between devices, body(): behind = lax.ppermute(behind, 'row', down)  8.02 us
    ppermute x4, starting transfers between devices, body(): arrived.append(lax.ppermute(part, BOTH, pairs))  7.86 us
    ppermute x4, waiting for transfers between devices, body(): arrived.append(lax.ppermute(part, BOTH, pairs))  6.18 us
    ppermute x3, starting transfers between devices, body(): behind = lax.ppermute(behind, 'row', down)  6.05 us
  transfers between devices with their start and end apart: 16, of which 6 were waited for; matrix products, arithmetic and copies ran while one was open for 1% of the time, Pallas kernels for 26%

profile of v11, /device:TPU:0, one launch (start us, length us, event | category | flops | bytes accessed | tf_op | source)
XLA Modules:
  0.0 190.9 jit_solution(5116794124412059112)
XLA Ops:
  0.7 0.6 pad_add_fusion.place
  1.3 0.0 copy-start.2
  1.3 3.9 %pack.1 = f32[32,152,128]{2,1,0:T(8,128)} custom-call(s32[4]{0:T(128)} %pad_add_fusion.place, s32[16]{0:T(128)} %bitcast.13, s32[16]{0:T(128)} %slot.1, s32[1]{0:T(128)S(6)} %copy.19.count, f32[16,128,128]{2,1,0:T(8,128)} %child_ref.1, f32[12,1,24,1,128,128]{5,4,3,2,1,0:T(8,128)} %rest_3_.7), custom_call_target="tpu_custom_call" | custom-call | tf_op jit(solution)/shard_map/pack/pallas_call | solution.py:123
  5.2 0.0 copy-start.3
  5.2 0.0 copy-start.4
  5.2 65.3 %all_to_all.10.incoming_ref.rest_4_.rest_3_ = f32[32,152,128]{2,1,0:T(8,128)S(1)} all-to-all(f32[32,152,128]{2,1,0:T(8,128)} %pack.1), channel_id=1, replica_groups=mesh['row'=8,'col'=4] {'row','col'}, dimensions={0} | all-to-all | bytes 4980736 | tf_op jit(solution)/shard_map/all_to_all | solution.py:502
  70.5 0.7 fusion.slot_in
  71.1 0.0 copy-done.2
  71.1 2.6 %panel_columns.1 = (f32[12,128,128]{2,1,0:T(8,128)S(1)}, f32[32,16,128]{2,1,0:T(8,128)S(1)}, f32[3,128,128]{2,1,0:T(8,128)S(1)}, f32[3,128,128]{2,1,0:T(8,128)S(...) custom-call(s32[4]{0:T(128)S(1)} %copy-done.2, s32[32]{0:T(128)S(1)} %fusion.slot_in, ...), custom_call_target="tpu_custom_call" | custom-call | tf_op jit(solution)/shard_map/panel_columns/pallas_call | solution.py:187
  73.8 0.0 copy-start.1
  73.8 0.7 copy-done.1
  74.5 0.0 copy-start.5
  74.5 0.7 copy-done.5
  75.2 0.0 copy-start.6
  75.2 0.7 copy-done.6
  75.8 0.0 copy-start.7
  75.8 0.7 copy-done.7
  76.5 0.7 copy-done.8
  77.2 2.7 %all-to-all-start.1 = ((f32[32,16,128]{2,1,0:T(8,128)}), f32[32,16,128]{2,1,0:T(8,128)S(1)}, u32[]{:S(2)}, u32[]{:S(2)}) async-start(f32[32,16,128]{2,1,0:T(8,128)} %copy-done.1), calls=%async_computation.1 | async-start | bytes 524288 | tf_op jit(solution)/shard_map/all_to_all | solution.py:507
  79.9 1.6 collective-permute-start
  81.5 2.3 %collective-permute-start.1 = (f32[3,128,128]{2,1,0:T(8,128)}, f32[3,128,128]{2,1,0:T(8,128)S(1)}, u32[]{:S(2)}, u32[]{:S(2)}) collective-permute-start(f32[3,128,128]{2,1,0:T(8,128)} %copy-done.7), channel_id=1, source_target_pairs={{0,4},{1,8},{2,12},{3,0},{4,5},{5,9},{6,13},{7,1},{8,6},{9,10},{10... | collective-permute-start | bytes 589832 | tf_op jit(solution)/shard_map/ppermute | solution.py:527
  83.8 3.5 %collective-permute-start.2 = (f32[3,128,128]{2,1,0:T(8,128)}, f32[3,128,128]{2,1,0:T(8,128)S(1)}, u32[]{:S(2)}, u32[]{:S(2)}) collective-permute-start(f32[3,128,128]{2,1,0:T(8,128)} %copy-done.6), channel_id=1, source_target_pairs={{0,8},{1,12},{2,0},{3,4},{4,9},{5,13},{6,1},{7,5},{8,10},{9,14},{1... | collective-permute-start | bytes 589832 | tf_op jit(solution)/shard_map/ppermute | solution.py:527
  87.2 0.5 collective-permute-start.3
  87.7 0.0 collective-permute-done
  87.8 5.8 %collective-permute-done.1 = f32[3,128,128]{2,1,0:T(8,128)S(1)} collective-permute-done((f32[3,128,128]{2,1,0:T(8,128)}, f32[3,128,128]{2,1,0:T(8,128)S(1)}, u32[]{:S(2)}, u32[]{:S(2)}) %collective-permute-start.1) | collective-permute-done | bytes 196640 | tf_op jit(solution)/shard_map/ppermute | solution.py:527
  93.5 0.4 collective-permute-done.2
  93.9 0.0 copy-done.9
  93.9 0.3 copy-done.10
  94.2 0.7 copy-done.11
  94.9 0.0 collective-permute-done.3
  94.9 0.0 all-to-all-done.1
  94.9 3.4 %collective-permute-start.9 = (f32[12,128,128]{2,1,0:T(8,128)S(1)}, f32[12,128,128]{2,1,0:T(8,128)S(1)}, u32[]{:S(2)}, u32[]{:S(2)}) collective-permute-start(f32[12,128,128]{2,1,0:T(8,128)S(1)} %get-tuple-element.39.t0), channel_id=1, source_target_pairs={{0,2},{1,3},{2,0},{3,1},{4,6},{5,7},{6,4},{7,5},{8,10},{9,11},{10,... | collective-permute-start | bytes 2359304 | tf_op jit(solution)/shard_map/ppermute | solution.py:512
  98.3 1.3 pad_maximum_fusion.rest_0_
  99.6 2.5 %collective-permute-start.6 = (f32[4,3,128,128]{3,2,1,0:T(8,128)S(1)}, f32[4,3,128,128]{3,2,1,0:T(8,128)S(1)}, u32[]{:S(2)}, u32[]{:S(2)}) collective-permute-start(f32[4,3,128,128]{3,2,1,0:T(8,128)S(1)} %pad_maximum_fusion.rest_0_), channel_id=1, source_target_pairs={{8,0},{16,8},{24,16},{28,24},{20,28},{12,20},{4,12},{0,4},{9,1},{1... | collective-permute-start | bytes 2359304 | tf_op jit(solution)/shard_map/ppermute | solution.py:538
  102.1 0.0 collective-permute-start.4
  102.1 0.0 collective-permute-start.8
  102.1 14.5 %collective-permute-done.9.t2 = f32[12,128,128]{2,1,0:T(8,128)S(1)} collective-permute-done((f32[12,128,128]{2,1,0:T(8,128)S(1)}, f32[12,128,128]{2,1,0:T(8,128)S(1)}, u32[]{:S(2)}, u32[]{:S(2)}) %collective-permute-start.9) | collective-permute-done | bytes 786464 | tf_op jit(solution)/shard_map/ppermute | solution.py:512
  116.6 0.2 collective-permute-start.10
  116.8 2.0 %collective-permute-done.6.rest_0_ = f32[4,3,128,128]{3,2,1,0:T(8,128)S(1)} collective-permute-done((f32[4,3,128,128]{3,2,1,0:T(8,128)S(1)}, f32[4,3,128,128]{3,2,1,0:T(8,128)S(1)}, u32[]{:S(2)}, u32[]{:S(2)}) %collective-permute-start.6) | collective-permute-done | bytes 786464 | tf_op jit(solution)/shard_map/ppermute | solution.py:538
  118.8 2.3 %collective-permute-start.7 = (f32[4,3,128,128]{3,2,1,0:T(8,128)S(1)}, f32[4,3,128,128]{3,2,1,0:T(8,128)S(1)}, u32[]{:S(2)}, u32[]{:S(2)}) collective-permute-start(f32[4,3,128,128]{3,2,1,0:T(8,128)S(1)} %collective-permute-done.6.rest_0_), channel_id=1, source_target_pairs={{8,0},{16,8},{24,16},{28,24},{20,28},{12,20},{4,12},{0,4},{9,1},{1... | collective-permute-start | bytes 2359304 | tf_op jit(solution)/shard_map/ppermute | solution.py:538
  121.1 0.0 collective-permute-done.4.rest_1_
  121.1 0.0 collective-permute-start.5
  121.1 0.0 collective-permute-done.8.t1
  121.1 0.0 collective-permute-done.10.t3
  121.2 0.0 copy-start
  121.2 1.0 copy-done
  122.2 9.8 %row_panels.1 = (bf16[1536,1536]{1,0:T(8,128)(2,1)}, f32[12,1,24,1,128,128]{5,4,3,2,1,0:T(8,128)}, bf16[3,256,768]{2,1,0:T(8,128)(2,1)S(1)}, s32[64]{0:T(128)S(1)}, s32[25]{0:T(128)S(1)}) custom-call(s32[4]{0:T(128)S(1)} %copy-done.2, s32[32]{0:T(128)S(1)} %fusion.slot_in, f32[12,128,128]{2,1,0:T(8,128)S(1)} %get-tuple-element.39.t0, ...), custom_call_target="tpu_custom_call" | custom-call | tf_op jit(solution)/shard_map/row_panels/pallas_call | solution.py:307
  132.0 6.0 %collective-permute-done.7.rest_0_ = f32[4,3,128,128]{3,2,1,0:T(8,128)S(1)} collective-permute-done((f32[4,3,128,128]{3,2,1,0:T(8,128)S(1)}, f32[4,3,128,128]{3,2,1,0:T(8,128)S(1)}, u32[]{:S(2)}, u32[]{:S(2)}) %collective-permute-start.7) | collective-permute-done | bytes 786464 | tf_op jit(solution)/shard_map/ppermute | solution.py:538
  138.0 1.0 collective-permute-done.5.rest_1_
  139.0 0.8 collective-permute-start.11
  139.8 1.2 collective-permute-start.13
  141.0 0.0 copy-done.3
  141.0 0.0 copy-done.4
  141.0 10.1 %trailing.5.rest_5_ = f32[12,1,24,1,128,128]{5,4,3,2,1,0:T(8,128)} custom-call(s32[4]{0:T(128)S(1)} %copy-done.2, s32[192]{0:T(256)S(1)} %copy-done.4, s32[256]{0:T(256)S(1)} %copy-done.3, s32[64]{0:T(128)S(1)} %get-tuple-element.46.order, s32[25]{0:T(128)S(1)} %get-tuple-element.47.starts, ...), custom_call_target="tpu_custom_call", output_to_operand_aliasing={{}: (11, {})} | custom-call | flops 9663676416 | bytes 9437184 | tf_op jit(solution)/shard_map/trailing/pallas_call | solution.py:460
  151.2 10.4 %trailing.6.rest_4_ = f32[12,1,24,1,128,128]{5,4,3,2,1,0:T(8,128)} custom-call(s32[4]{0:T(128)S(1)} %copy-done.2, s32[192]{0:T(256)S(1)} %copy-done.4, s32[256]{0:T(256)S(1)} %copy-done.3, s32[64]{0:T(128)S(1)} %get-tuple-element.46.order, s32[25]{0:T(128)S(1)} %get-tuple-element.47.starts, ...), custom_call_target="tpu_custom_call", output_to_operand_aliasing={{}: (11, {})} | custom-call | flops 9663676416 | bytes 9437184 | tf_op jit(solution)/shard_map/trailing/pallas_call | solution.py:460
  161.6 8.3 %trailing.7.rest_5_ = f32[12,1,24,1,128,128]{5,4,3,2,1,0:T(8,128)} custom-call(s32[4]{0:T(128)S(1)} %copy-done.2, s32[192]{0:T(256)S(1)} %copy-done.4, s32[256]{0:T(256)S(1)} %copy-done.3, s32[64]{0:T(128)S(1)} %get-tuple-element.46.order, s32[25]{0:T(128)S(1)} %get-tuple-element.47.starts, ...), custom_call_target="tpu_custom_call", output_to_operand_aliasing={{}: (10, {})} | custom-call | flops 4831838208 | bytes 4718592 | tf_op jit(solution)/shard_map/trailing/pallas_call | solution.py:460
  169.9 0.0 collective-permute-done.11.rest_0_
  169.9 1.2 collective-permute-start.12
  171.1 0.0 collective-permute-done.13.rest_1_
  171.2 0.9 collective-permute-start.14
  172.1 10.4 %trailing.8.rest_5_ = f32[12,1,24,1,128,128]{5,4,3,2,1,0:T(8,128)} custom-call(s32[4]{0:T(128)S(1)} %copy-done.2, s32[192]{0:T(256)S(1)} %copy-done.4, s32[256]{0:T(256)S(1)} %copy-done.3, s32[64]{0:T(128)S(1)} %get-tuple-element.46.order, s32[25]{0:T(128)S(1)} %get-tuple-element.47.starts, ...), custom_call_target="tpu_custom_call", output_to_operand_aliasing={{}: (11, {})} | custom-call | flops 9663676416 | bytes 9437184 | tf_op jit(solution)/shard_map/trailing/pallas_call | solution.py:460
  182.5 0.0 collective-permute-done.12.rest_0_
  182.5 0.0 collective-permute-done.14.rest_1_
  182.6 8.3 %trailing.9 = f32[12,1,24,1,128,128]{5,4,3,2,1,0:T(8,128)} custom-call(s32[4]{0:T(128)S(1)} %copy-done.2, s32[192]{0:T(256)S(1)} %copy-done.4, s32[256]{0:T(256)S(1)} %copy-done.3, s32[64]{0:T(128)S(1)} %get-tuple-element.46.order, s32[25]{0:T(128)S(1)} %get-tuple-element.47.starts, ...), custom_call_target="tpu_custom_call", output_to_operand_aliasing={{}: (11, {})} | custom-call | flops 4831838208 | bytes 4718592 | tf_op jit(solution)/shard_map/trailing/pallas_call | solution.py:460
  (6 shorter events, 0.1 us)
Async XLA Ops:
  1.3 69.8 %copy-start.2 = (s32[4]{0:T(128)S(1)}, s32[4]{0:T(128)}, u32[]{:S(2)}) copy-start(s32[4]{0:T(128)} %pad_add_fusion.place) | copy-start | bytes 52
  5.2 135.9 %copy-start.3 = (s32[256]{0:T(256)S(1)}, s32[256]{0:T(256)}, u32[]{:S(2)}) copy-start(s32[256]{0:T(256)} %constant.18.clone.places_table) | copy-start | bytes 3076
  5.2 135.9 %copy-start.4 = (s32[192]{0:T(256)S(1)}, s32[192]{0:T(256)}, u32[]{:S(2)}) copy-start(s32[192]{0:T(256)} %constant.17.clone.columns_table) | copy-start | bytes 2308
  73.8 0.7 copy-start.1
  74.5 0.7 copy-start.5
  75.2 0.7 copy-start.6
  75.8 0.7 copy-start.7
  76.5 0.7 copy-start.8
  77.2 17.7 %all-to-all-start.1 = ((f32[32,16,128]{2,1,0:T(8,128)}), f32[32,16,128]{2,1,0:T(8,128)S(1)}, u32[]{:S(2)}, u32[]{:S(2)}) async-start(f32[32,16,128]{2,1,0:T(8,128)} %copy-done.1), calls=%async_computation.1 | async-start | bytes 524288 | tf_op jit(solution)/shard_map/all_to_all | solution.py:507
  79.9 7.9 %collective-permute-start = (f32[3,128,128]{2,1,0:T(8,128)}, f32[3,128,128]{2,1,0:T(8,128)S(1)}, u32[]{:S(2)}, u32[]{:S(2)}) collective-permute-start(f32[3,128,128]{2,1,0:T(8,128)} %copy-done.8), channel_id=1, source_target_pairs={{0,0},{1,4},{2,8},{3,12},{4,1},{5,5},{6,9},{7,13},{8,2},{9,6},{10,... | collective-permute-start | bytes 589832 | tf_op jit(solution)/shard_map/ppermute | solution.py:527
  81.5 12.0 %collective-permute-start.1 = (f32[3,128,128]{2,1,0:T(8,128)}, f32[3,128,128]{2,1,0:T(8,128)S(1)}, u32[]{:S(2)}, u32[]{:S(2)}) collective-permute-start(f32[3,128,128]{2,1,0:T(8,128)} %copy-done.7), channel_id=1, source_target_pairs={{0,4},{1,8},{2,12},{3,0},{4,5},{5,9},{6,13},{7,1},{8,6},{9,10},{10... | collective-permute-start | bytes 589832 | tf_op jit(solution)/shard_map/ppermute | solution.py:527
  83.8 10.2 %collective-permute-start.2 = (f32[3,128,128]{2,1,0:T(8,128)}, f32[3,128,128]{2,1,0:T(8,128)S(1)}, u32[]{:S(2)}, u32[]{:S(2)}) collective-permute-start(f32[3,128,128]{2,1,0:T(8,128)} %copy-done.6), channel_id=1, source_target_pairs={{0,8},{1,12},{2,0},{3,4},{4,9},{5,13},{6,1},{7,5},{8,10},{9,14},{1... | collective-permute-start | bytes 589832 | tf_op jit(solution)/shard_map/ppermute | solution.py:527
  87.2 7.7 %collective-permute-start.3 = (f32[3,128,128]{2,1,0:T(8,128)}, f32[3,128,128]{2,1,0:T(8,128)}, u32[]{:S(2)}, u32[]{:S(2)}) collective-permute-start(f32[3,128,128]{2,1,0:T(8,128)} %copy-done.5), channel_id=1, source_target_pairs={{0,12},{1,0},{2,4},{3,8},{4,13},{5,1},{6,5},{7,9},{8,14},{9,2},{10... | collective-permute-start | bytes 589832 | tf_op jit(solution)/shard_map/ppermute | solution.py:527
  87.8 6.2 %copy-start.9 = (f32[3,128,128]{2,1,0:T(8,128)}, f32[3,128,128]{2,1,0:T(8,128)S(1)}, u32[]{:S(2)}) copy-start(f32[3,128,128]{2,1,0:T(8,128)S(1)} %collective-permute-done) | copy-start | bytes 589828
  93.5 0.7 copy-start.10
  94.2 0.7 copy-start.11
  94.9 21.7 %collective-permute-start.9 = (f32[12,128,128]{2,1,0:T(8,128)S(1)}, f32[12,128,128]{2,1,0:T(8,128)S(1)}, u32[]{:S(2)}, u32[]{:S(2)}) collective-permute-start(f32[12,128,128]{2,1,0:T(8,128)S(1)} %get-tuple-element.39.t0), channel_id=1, source_target_pairs={{0,2},{1,3},{2,0},{3,1},{4,6},{5,7},{6,4},{7,5},{8,10},{9,11},{10,... | collective-permute-start | bytes 2359304 | tf_op jit(solution)/shard_map/ppermute | solution.py:512
  99.6 19.2 %collective-permute-start.6 = (f32[4,3,128,128]{3,2,1,0:T(8,128)S(1)}, f32[4,3,128,128]{3,2,1,0:T(8,128)S(1)}, u32[]{:S(2)}, u32[]{:S(2)}) collective-permute-start(f32[4,3,128,128]{3,2,1,0:T(8,128)S(1)} %pad_maximum_fusion.rest_0_), channel_id=1, source_target_pairs={{8,0},{16,8},{24,16},{28,24},{20,28},{12,20},{4,12},{0,4},{9,1},{1... | collective-permute-start | bytes 2359304 | tf_op jit(solution)/shard_map/ppermute | solution.py:538
  102.1 19.1 %collective-permute-start.4 = (f32[4,3,128,128]{3,2,1,0:T(8,128)S(1)}, f32[4,3,128,128]{3,2,1,0:T(8,128)S(1)}, u32[]{:S(2)}, u32[]{:S(2)}) collective-permute-start(f32[4,3,128,128]{3,2,1,0:T(8,128)S(1)} %pad_maximum_fusion.rest_0_), channel_id=1, source_target_pairs={{0,8},{8,16},{16,24},{24,28},{28,20},{20,12},{12,4},{4,0},{1,9},{9... | collective-permute-start | bytes 2359304 | tf_op jit(solution)/shard_map/ppermute | solution.py:537
  102.1 19.1 %collective-permute-start.8 = (f32[12,128,128]{2,1,0:T(8,128)S(1)}, f32[12,128,128]{2,1,0:T(8,128)S(1)}, u32[]{:S(2)}, u32[]{:S(2)}) collective-permute-start(f32[12,128,128]{2,1,0:T(8,128)S(1)} %get-tuple-element.39.t0), channel_id=1, source_target_pairs={{0,1},{1,0},{2,3},{3,2},{4,5},{5,4},{6,7},{7,6},{8,9},{9,8},{10,11... | collective-permute-start | bytes 2359304 | tf_op jit(solution)/shard_map/ppermute | solution.py:511
  116.6 4.6 %collective-permute-start.10 = (f32[12,128,128]{2,1,0:T(8,128)S(1)}, f32[12,128,128]{2,1,0:T(8,128)S(1)}, u32[]{:S(2)}, u32[]{:S(2)}) collective-permute-start(f32[12,128,128]{2,1,0:T(8,128)S(1)} %collective-permute-done.9.t2), channel_id=1, source_target_pairs={{0,1},{1,0},{2,3},{3,2},{4,5},{5,4},{6,7},{7,6},{8,9},{9,8},{10,11... | collective-permute-start | bytes 2359304 | tf_op jit(solution)/shard_map/ppermute | solution.py:513
  118.8 19.2 %collective-permute-start.7 = (f32[4,3,128,128]{3,2,1,0:T(8,128)S(1)}, f32[4,3,128,128]{3,2,1,0:T(8,128)S(1)}, u32[]{:S(2)}, u32[]{:S(2)}) collective-permute-start(f32[4,3,128,128]{3,2,1,0:T(8,128)S(1)} %collective-permute-done.6.rest_0_), channel_id=1, source_target_pairs={{8,0},{16,8},{24,16},{28,24},{20,28},{12,20},{4,12},{0,4},{9,1},{1... | collective-permute-start | bytes 2359304 | tf_op jit(solution)/shard_map/ppermute | solution.py:538
  121.1 17.9 %collective-permute-start.5 = (f32[4,3,128,128]{3,2,1,0:T(8,128)S(1)}, f32[4,3,128,128]{3,2,1,0:T(8,128)S(1)}, u32[]{:S(2)}, u32[]{:S(2)}) collective-permute-start(f32[4,3,128,128]{3,2,1,0:T(8,128)S(1)} %collective-permute-done.4.rest_1_), channel_id=1, source_target_pairs={{0,8},{8,16},{16,24},{24,28},{28,20},{20,12},{12,4},{4,0},{1,9},{9... | collective-permute-start | bytes 2359304 | tf_op jit(solution)/shard_map/ppermute | solution.py:537
  121.2 1.0 copy-start
  139.0 30.9 %collective-permute-start.11 = (f32[4,3,128,128]{3,2,1,0:T(8,128)S(1)}, f32[4,3,128,128]{3,2,1,0:T(8,128)S(1)}, u32[]{:S(2)}, u32[]{:S(2)}) collective-permute-start(f32[4,3,128,128]{3,2,1,0:T(8,128)S(1)} %collective-permute-done.5.rest_1_), channel_id=1, source_target_pairs={{0,8},{8,16},{16,24},{24,28},{28,20},{20,12},{12,4},{4,0},{1,9},{9... | collective-permute-start | bytes 2359304 | tf_op jit(solution)/shard_map/ppermute | solution.py:537
  139.8 31.3 %collective-permute-start.13 = (f32[4,3,128,128]{3,2,1,0:T(8,128)S(1)}, f32[4,3,128,128]{3,2,1,0:T(8,128)S(1)}, u32[]{:S(2)}, u32[]{:S(2)}) collective-permute-start(f32[4,3,128,128]{3,2,1,0:T(8,128)S(1)} %collective-permute-done.7.rest_0_), channel_id=1, source_target_pairs={{8,0},{16,8},{24,16},{28,24},{20,28},{12,20},{4,12},{0,4},{9,1},{1... | collective-permute-start | bytes 2359304 | tf_op jit(solution)/shard_map/ppermute | solution.py:538
  169.9 12.6 %collective-permute-start.12 = (f32[2,3,128,128]{3,2,1,0:T(8,128)S(1)}, f32[2,3,128,128]{3,2,1,0:T(8,128)S(1)}, u32[]{:S(2)}, u32[]{:S(2)}) collective-permute-start(f32[2,3,128,128]{3,2,1,0:T(8,128)S(1)} %slice.13), channel_id=1, source_target_pairs={{0,8},{8,16},{16,24},{24,28},{28,20},{20,12},{12,4},{4,0},{1,9},{9... | collective-permute-start | bytes 1179656 | tf_op jit(solution)/shard_map/ppermute | solution.py:542
  171.2 11.4 %collective-permute-start.14 = (f32[2,3,128,128]{3,2,1,0:T(8,128)S(1)}, f32[2,3,128,128]{3,2,1,0:T(8,128)S(1)}, u32[]{:S(2)}, u32[]{:S(2)}) collective-permute-start(f32[2,3,128,128]{3,2,1,0:T(8,128)S(1)} %slice.14), channel_id=1, source_target_pairs={{8,0},{16,8},{24,16},{28,24},{20,28},{12,20},{4,12},{0,4},{9,1},{1... | collective-permute-start | bytes 1179656 | tf_op jit(solution)/shard_map/ppermute | solution.py:542

commit v12 on v9

--- a/solution.py
+++ b/solution.py
@@ -260,8 +260,7 @@
 
     one, two = two_panels(columns, small_ref, mask)
     for i, panel in enumerate((mask(1, one), mask(2, two))):
-        high, low = halves(panel)
-        for k, half in enumerate((high, low, high)):
+        for k, half in enumerate(halves(panel)):
             pair_ref[:, k * WIDTH + i * PANEL : k * WIDTH + (i + 1) * PANEL] = half
     pieces = (one[:, :TILE], one[:, TILE:], two[:, :TILE], two[:, TILE:])
     for c in range(4):
@@ -277,7 +276,7 @@
     group = rows // 3
     height = group * TILE
     out_shape = [
-        jax.ShapeDtypeStruct((rows * TILE, 3 * WIDTH), jnp.bfloat16),
+        jax.ShapeDtypeStruct((rows * TILE, 2 * WIDTH), jnp.bfloat16),
         jax.ShapeDtypeStruct(front.shape, jnp.float32),
         jax.ShapeDtypeStruct((3, PANEL, 3 * PANEL), jnp.bfloat16),
         jax.ShapeDtypeStruct((2 * slot_in.shape[0],), jnp.int32),
@@ -291,7 +290,7 @@
             grid=(3,),
             in_specs=[strip] * 4 + [whole_spec(lead), whole_spec(diag)],
             out_specs=[
-                pl.BlockSpec((height, 3 * WIDTH), lambda i, *_: (i, 0)),
+                pl.BlockSpec((height, 2 * WIDTH), lambda i, *_: (i, 0)),
                 pl.BlockSpec((group, 1, 1, 1, TILE, TILE), lambda i, *_: (i, 0, 0, 0, 0, 0)),
                 whole_spec(out_shape[2]),
                 pl.BlockSpec(memory_space=pltpu.SMEM),
@@ -310,31 +309,36 @@
 
 
 def trailing_kernel(
-    first, n_held, halved, place, columns_table, places_table, order, starts, small_ref, *rest
+    first, n_held, halved, place, columns_table, places_table, order, starts, pair_ref, small_ref,
+    *rest,
 ):
     piece_refs = rest[:n_held]
-    pair_hbm, front_ref, incoming_ref, _, out_ref, *rest = rest[n_held:]
-    pair_ref, right_ref, taken, given, child_ref, *rest = rest
-    pair_sem, take_sems, give_sems, child_sems, *joined = rest
+    front_ref, incoming_ref, _, out_ref, right_ref, taken, given, child_ref, *rest = rest[n_held:]
+    take_sems, give_sems, child_sems, *joined = rest
     if halved:
         joined[0][:2] = piece_refs[0][...]
         joined[0][2:] = piece_refs[1][...]
         piece_refs = joined
+    n_pieces = len(piece_refs)
     group = piece_refs[0].shape[1]
-    count = len(piece_refs) * group
-    pairs, single = count // 2, count % 2
+    count = n_pieces * group
+    steps = (count + 1) // 2
     rows, cols = front_ref.shape[0], front_ref.shape[2]
     columns_base = place[0] * cols + first * group
     places_base = (place[0] * (cols // group) + first) * 4
 
-    def columns_of(step, width):
-        for j in range(width):
-            b = columns_table[columns_base + 2 * step + j]
-            yield j, b, b > 0
-
-    def each_take(step, width, act):
+    def columns_of(step):
+        for j in range(2):
+            index = jnp.minimum(2 * step, count - 2) + j
+            b = columns_table[columns_base + index]
+            wanted = b > 0
+            if count % 2 and j == 0:
+                wanted = jnp.logical_and(wanted, step < steps - 1)
+            yield j, b, wanted
+
+    def each_take(step, act):
         slot = lax.rem(step, 2)
-        for j, b, wanted in columns_of(step, width):
+        for j, b, wanted in columns_of(step):
 
             @pl.when(wanted)
             def _():
@@ -344,9 +348,9 @@
                     )
                 )
 
-    def each_give(step, width, act):
+    def each_give(step, act):
         slot = lax.rem(step, 2)
-        for j, b, wanted in columns_of(step, width):
+        for j, b, wanted in columns_of(step):
 
             @pl.when(wanted)
             def _():
@@ -356,8 +360,8 @@
                     )
                 )
 
-    def each_child(step, width, act):
-        for j, b, wanted in columns_of(step, width):
+    def each_child(step, act):
+        for j, b, wanted in columns_of(step):
 
             @pl.when(wanted)
             def _():
@@ -369,14 +373,10 @@
                     )
                     act(copy, j, s, order[2 * i + 1])
 
-    start, wait = (lambda copy, *_: copy.start()), (lambda copy, *_: copy.wait())
-    steps = [(step, 2) for step in range(pairs)] + [(pairs, 1)] * single
-    pair_copy = pltpu.make_async_copy(pair_hbm, pair_ref, pair_sem)
-    pair_copy.start()
-    for step, width in steps[:2]:
-        each_take(step, width, start)
-    for step, width in steps:
-        each_child(step, width, start)
+    for step in range(min(steps, 2)):
+        each_take(step, lambda copy: copy.start())
+    for step in range(steps):
+        each_child(step, lambda copy, *_: copy.start())
 
     tile_columns = [
         jnp.concatenate(
@@ -393,36 +393,40 @@
         high, low = halves(panel)
         for k, half in enumerate((high, high, low)):
             right_ref[k * WIDTH + i * PANEL : k * WIDTH + (i + 1) * PANEL] = half
-    pair_copy.wait()
-
-    def update(step, width):
+
+    @pl.loop(0, steps)
+    def _(step):
         slot = lax.rem(step, 2)
-        each_take(step, width, wait)
-        pl.when(step >= 2)(lambda: each_give(step - 2, 2, wait))
-        lanes = pl.ds(pl.multiple_of(2 * step * TILE, TILE), width * TILE)
-        change = dot(pair_ref[...], right_ref[:, lanes])
-        for j in range(width):
-            part = change[:, j * TILE : (j + 1) * TILE].reshape(rows, TILE, TILE)
-            given[slot, j] = taken[slot, j] - part
+        each_take(step, lambda copy: copy.wait())
+
+        @pl.when(step >= 2)
+        def _():
+            each_give(step - 2, lambda copy: copy.wait())
+
+        start = jnp.minimum(2 * step, count - 2)
+        lanes = pl.ds(pl.multiple_of(start * TILE, TILE), 2 * TILE)
+        block = rows // 3
+        for m in range(3):
+            left = pair_ref[m * block * TILE : (m + 1) * block * TILE]
+            update = dot(jnp.concatenate([left, left[:, :WIDTH]], axis=1), right_ref[:, lanes])
+            span = slice(m * block, (m + 1) * block)
+            for j in range(2):
+                part = update[:, j * TILE : (j + 1) * TILE].reshape(block, TILE, TILE)
+                given[slot, j, span] = taken[slot, j, span] - part
 
         def add(copy, j, s, a):
             copy.wait()
             given[slot, j, a] = given[slot, j, a] + child_ref[s]
 
-        each_child(step, width, add)
-        each_give(step, width, start)
-
-    @pl.loop(0, pairs)
-    def _(step):
-        update(step, 2)
-        pl.when(step + 2 < pairs)(lambda: each_take(step + 2, 2, start))
-        if single:
-            pl.when(step + 2 == pairs)(lambda: each_take(step + 2, 1, start))
-
-    if single:
-        update(jnp.int32(pairs), 1)
-    for step, width in steps[-2:]:
-        each_give(step, width, wait)
+        each_child(step, add)
+        each_give(step, lambda copy: copy.start())
+
+        @pl.when(step + 2 < steps)
+        def _():
+            each_take(step + 2, lambda copy: copy.start())
+
+    for step in range(max(steps - 2, 0), steps):
+        each_give(step, lambda copy: copy.wait())
 
 
 def trailing(front, pieces, first, place, tables, panels, incoming):
@@ -432,29 +436,27 @@
     halved = pieces[0].shape[0] == 2
     count = group if halved else len(pieces) * group
     scalars = [place, *tables, order, starts]
-    held = [small, *pieces]
-    distant = [pair, front, incoming, out]
+    held = [pair, small, *pieces]
+    distant = [front, incoming, out]
     spec = lambda space, n: [pl.BlockSpec(memory_space=space)] * n
     height = rows * TILE
     devices = incoming.shape[0]
     return pl.pallas_call(
         functools.partial(trailing_kernel, first, len(pieces), halved),
-        in_specs=spec(pltpu.SMEM, 5) + spec(pltpu.VMEM, len(held)) + spec(pltpu.HBM, 4),
+        in_specs=spec(pltpu.SMEM, 5) + spec(pltpu.VMEM, len(held)) + spec(pltpu.HBM, 3),
         out_specs=pl.BlockSpec(memory_space=pltpu.HBM),
         scratch_shapes=[
-            pltpu.VMEM(pair.shape, jnp.bfloat16),
             pltpu.VMEM((3 * WIDTH, count * TILE), jnp.bfloat16),
             pltpu.VMEM((2, 2, rows, TILE, TILE), jnp.float32),
             pltpu.VMEM((2, 2, rows, TILE, TILE), jnp.float32),
             pltpu.VMEM((devices, TILE, TILE), jnp.float32),
-            pltpu.SemaphoreType.DMA,
             pltpu.SemaphoreType.DMA((2, 2)),
             pltpu.SemaphoreType.DMA((2, 2)),
             pltpu.SemaphoreType.DMA((devices,)),
         ]
         + [pltpu.VMEM((4, group, TILE, TILE), jnp.float32)] * halved,
         out_shape=jax.ShapeDtypeStruct(front.shape, jnp.float32),
-        input_output_aliases={5 + len(held) + 3: 0},
+        input_output_aliases={len(held) + 7: 0},
         compiler_params=pltpu.CompilerParams(vmem_limit_bytes=VMEM),
         cost_estimate=pl.CostEstimate(
             flops=8 * count * 2 * height * TILE * WIDTH,
@@ -496,6 +498,34 @@
         return row_panels(mine, exchange(mine), lead, diag_inverses, place, slot_in, front)
 
     sets = n_row // n_col
+    circle = list(range(0, n_row, 2)) + list(range(n_row - 1, 0, -2))
+    around = [0] + [sign * step for step in range(1, n_row // 2) for sign in (-1, 1)]
+    shifts = around + [n_row // 2] if ring else list(range(sets))
+
+    def described(row, shift):
+        if not ring:
+            return [a * sets + shift for a in range(rows_here)], list(range(n_col))
+        origin = circle[(circle.index(row) + shift) % n_row]
+        part, group = origin % n_col, rows_here // n_col
+        columns = [(part * group + t) * sets + origin // n_col for t in range(group)]
+        return columns, [(part - c) % n_col for c in range(n_col)]
+
+    tables = [
+        jnp.asarray(
+            np.concatenate([described(row, shift)[k] for row in range(n_row) for shift in shifts]),
+            jnp.int32,
+        )
+        for k in range(2)
+    ]
+
+    def updated(entries, panels, first):
+        assert [shift for _, shift in entries] == shifts[first : first + len(entries)]
+        pieces = [piece for piece, _ in entries]
+        pieces = pieces[0] if isinstance(pieces[0], list) else pieces
+        out = trailing(front, pieces, first, place, tables, panels, incoming)
+        return [panels[0], out, *panels[2:]]
+
+    first = 0
     if ring:
         arrived = []
         for j, part in enumerate(parts):
@@ -505,9 +535,9 @@
                 for c in range(n_col)
             ]
             arrived.append(lax.ppermute(part, BOTH, pairs))
-        arrived, mine, lead = lax.optimization_barrier((arrived, mine, lead))
+        arrived[0], mine = lax.optimization_barrier((arrived[0], mine))
+        arrived, lead = lax.optimization_barrier((arrived, lead))
         piece = jnp.stack(arrived)
-        circle = list(range(0, n_row, 2)) + list(range(n_row - 1, 0, -2))
         up = [(circle[i], circle[(i + 1) % n_row]) for i in range(n_row)]
         down = [(b, a) for a, b in up]
         rounds = [[(piece, 0)]]
@@ -517,17 +547,13 @@
             ahead = lax.ppermute(ahead, "row", up)
             behind = lax.ppermute(behind, "row", down)
             if step == 2:
+                panels = updated([(piece, 0), rounds[1][0]], panels, 0)
                 ahead, behind, panels = lax.optimization_barrier((ahead, behind, panels))
             rounds.append([(ahead, -step), (behind, step)])
         last = [lax.ppermute(ahead[:2], "row", up), lax.ppermute(behind[2:], "row", down)]
-        whole = [entry for entries in rounds for entry in entries]
-        rounds = [whole[:2], whole[2:4], whole[4:5], *rounds[3:], [(last, n_row // 2)]]
-
-        def described(row, shift):
-            origin = circle[(circle.index(row) + shift) % n_row]
-            part, group = origin % n_col, rows_here // n_col
-            columns = [(part * group + t) * sets + origin // n_col for t in range(group)]
-            return columns, [(part - c) % n_col for c in range(n_col)]
+        late = [entry for entries in rounds for entry in entries][2:]
+        rounds = [late[:2], late[2:3], *rounds[3:], [(last, n_row // 2)]]
+        first = 2
 
     else:
         pairs = [
@@ -539,23 +565,8 @@
         rounds = [[(moved[h * n_col : (h + 1) * n_col], h)] for h in range(sets)]
         panels = own_panels(mine, lead)
 
-        def described(row, h):
-            return [a * sets + h for a in range(rows_here)], list(range(n_col))
-
-    shifts = [shift for entries in rounds for _, shift in entries]
-    tables = [
-        jnp.asarray(
-            np.concatenate([described(row, shift)[k] for row in range(n_row) for shift in shifts]),
-            jnp.int32,
-        )
-        for k in range(2)
-    ]
-    first = 0
     for entries in rounds:
-        pieces = [piece for piece, _ in entries]
-        pieces = pieces[0] if isinstance(pieces[0], list) else pieces
-        out = trailing(front, pieces, first, place, tables, panels, incoming)
-        panels = [panels[0], out, *panels[2:]]
+        panels = updated(entries, panels, first)
         first += len(entries)
     return panels[1]
 

time: 192 us -> 193 us (level)
  Pallas kernels: 62.7 us -> 56.1 us
  starting transfers between devices: 22.7 us -> 27.6 us
  waiting for transfers between devices: 31.6 us -> 34.8 us
    ppermute x4, waiting for transfers between devices: 6.31 us -> 21 us  [body(): arrived.append(lax.ppermute(part, BOTH, pairs))]
    ppermute x1, waiting for transfers between devices: 14.6 us -> 0.01 us  [exchange(): far = lax.ppermute(mine, 'col', [(c, c ^ 2) for c in range(n_col)])]
    ppermute x3, waiting for transfers between devices: 0.8 us -> 13.8 us  [body(): ahead = lax.ppermute(ahead, 'row', up)]
    ppermute x3, waiting for transfers between devices: 9.88 us -> 0.01 us  [body(): behind = lax.ppermute(behind, 'row', down)]
    ppermute x1, starting transfers between devices: 3.26 us -> 9.54 us  [exchange(): far = lax.ppermute(mine, 'col', [(c, c ^ 2) for c in range(n_col)])]
    pallas_call x5, Pallas kernels: 48.2 us -> 41.9 us  [trailing(): pl.pallas_call(functools.partial(trailing_kernel, first, len(pieces), hal...]
    ppermute x3, starting transfers between devices: 5.81 us -> 2.83 us  [body(): behind = lax.ppermute(behind, 'row', down)]
    ppermute x4, starting transfers between devices: 7.77 us -> 5.15 us  [body(): arrived.append(lax.ppermute(part, BOTH, pairs))]
  transfers between devices with their start and end apart: 16 -> 16, of which waited for: 6 -> 3; matrix products, arithmetic and copies ran while one was open for 1% -> 1% of each run, Pallas kernels for 24% -> 23%
where the time goes in v12:
time: 193 us; the launch traced here: 192 us
  blocking collectives  65.5 us (34%)
  Pallas kernels  56.1 us (29%)
  waiting for transfers between devices  34.8 us (18%)
  starting transfers between devices  27.6 us (14%)
  local copies, waits for them, and re-layouts  4.18 us (2%)
  other arithmetic  2.51 us (1%)
    all_to_all x1, blocking collectives, body(): lax.all_to_all(outgoing, BOTH, split_axis=0, concat_axis=0, tiled=True)  65.5 us
    pallas_call x5, Pallas kernels, trailing(): pl.pallas_call(functools.partial(trailing_kernel, first, len(pieces), hal...  41.9 us
    ppermute x4, waiting for transfers between devices, body(): arrived.append(lax.ppermute(part, BOTH, pairs))  21 us
    ppermute x3, waiting for transfers between devices, body(): ahead = lax.ppermute(ahead, 'row', up)  13.8 us
    ppermute x1, starting transfers between devices, exchange(): far = lax.ppermute(mine, 'col', [(c, c ^ 2) for c in range(n_col)])  9.54 us
    pallas_call x1, Pallas kernels, row_panels(): pl.pallas_call(row_panels_kernel, grid_spec=pltpu.PrefetchScalarGridSpec(...  8.41 us
    ppermute x4, starting transfers between devices, body(): arrived.append(lax.ppermute(part, BOTH, pairs))  5.15 us
    all_to_all x1, starting transfers between devices, body(): lead = lax.all_to_all(own, BOTH, split_axis=0, concat_axis=0, tiled=True)  4.14 us
  transfers between devices with their start and end apart: 16, of which 3 were waited for; matrix products, arithmetic and copies ran while one was open for 1% of the time, Pallas kernels for 23%

profile of v12, /device:TPU:0, one launch (start us, length us, event | category | flops | bytes accessed | tf_op | source)
XLA Modules:
  0.0 191.8 jit_solution(12886683381274153943)
XLA Ops:
  0.7 0.6 pad_add_fusion.place
  1.2 3.8 %pack.1 = f32[32,152,128]{2,1,0:T(8,128)} custom-call(s32[4]{0:T(128)} %pad_add_fusion.place, s32[16]{0:T(128)} %bitcast.13, s32[16]{0:T(128)} %slot.1, s32[1]{0:T(128)S(6)} %copy.19.count, f32[16,128,128]{2,1,0:T(8,128)} %child_ref.1, f32[12,1,24,1,128,128]{5,4,3,2,1,0:T(8,128)} %rest_2_.7), custom_call_target="tpu_custom_call" | custom-call | tf_op jit(solution)/shard_map/pack/pallas_call | solution.py:122
  5.0 0.0 copy-start.6
  5.0 0.0 copy-start.7
  5.0 65.5 %all_to_all.10.incoming_ref.rest_3_.rest_2_ = f32[32,152,128]{2,1,0:T(8,128)S(1)} all-to-all(f32[32,152,128]{2,1,0:T(8,128)} %pack.1), channel_id=1, replica_groups=mesh['row'=8,'col'=4] {'row','col'}, dimensions={0} | all-to-all | bytes 4980736 | tf_op jit(solution)/shard_map/all_to_all | solution.py:484
  70.5 0.7 fusion.slot_in
  71.2 0.0 copy-done.5
  71.2 2.0 %panel_columns.1 = (f32[12,128,128]{2,1,0:T(8,128)S(1)}, f32[32,16,128]{2,1,0:T(8,128)S(1)}, f32[3,128,128]{2,1,0:T(8,128)S(1)}, f32[3,128,128]{2,1,0:T(8,128)S(...) custom-call(s32[4]{0:T(128)S(1)} %copy-done.5, s32[32]{0:T(128)S(1)} %fusion.slot_in, ...), custom_call_target="tpu_custom_call" | custom-call | tf_op jit(solution)/shard_map/panel_columns/pallas_call | solution.py:181
  73.2 0.0 copy-start.8
  73.2 0.0 copy-start.9
  73.2 0.0 copy-start.4
  73.3 0.0 copy-start.10
  73.3 0.7 collective-permute-start
  73.9 0.0 collective-permute-done
  74.0 0.0 copy-done.8
  74.0 0.0 copy-start.11
  74.0 0.0 copy-done.9
  74.0 9.5 %collective-permute-start.9 = (f32[12,128,128]{2,1,0:T(8,128)S(1)}, f32[12,128,128]{2,1,0:T(8,128)}, u32[]{:S(2)}, u32[]{:S(2)}) collective-permute-start(f32[12,128,128]{2,1,0:T(8,128)S(1)} %get-tuple-element.41.t0), channel_id=1, source_target_pairs={{0,2},{1,3},{2,0},{3,1},{4,6},{5,7},{6,4},{7,5},{8,10},{9,11},{10,... | collective-permute-start | bytes 2359304 | tf_op jit(solution)/shard_map/ppermute | solution.py:494
  83.5 0.0 copy-done.4
  83.5 0.0 copy-done.10
  83.5 0.0 copy-done.11
  83.5 4.1 %all-to-all-start.1 = ((f32[32,16,128]{2,1,0:T(8,128)}), f32[32,16,128]{2,1,0:T(8,128)S(1)}, u32[]{:S(2)}, u32[]{:S(2)}) async-start(f32[32,16,128]{2,1,0:T(8,128)} %copy-done.4), calls=%async_computation.1 | async-start | bytes 524288 | tf_op jit(solution)/shard_map/all_to_all | solution.py:489
  87.7 1.8 collective-permute-start.1
  89.5 2.4 %collective-permute-start.2 = (f32[3,128,128]{2,1,0:T(8,128)}, f32[3,128,128]{2,1,0:T(8,128)S(1)}, u32[]{:S(2)}, u32[]{:S(2)}) collective-permute-start(f32[3,128,128]{2,1,0:T(8,128)} %copy-done.9), channel_id=1, source_target_pairs={{0,8},{1,12},{2,0},{3,4},{4,9},{5,13},{6,1},{7,5},{8,10},{9,14},{1... | collective-permute-start | bytes 589832 | tf_op jit(solution)/shard_map/ppermute | solution.py:537
  91.9 0.3 collective-permute-start.3
  92.2 21.0 %collective-permute-done.1 = f32[3,128,128]{2,1,0:T(8,128)S(1)} collective-permute-done((f32[3,128,128]{2,1,0:T(8,128)}, f32[3,128,128]{2,1,0:T(8,128)S(1)}, u32[]{:S(2)}, u32[]{:S(2)}) %collective-permute-start.1) | collective-permute-done | bytes 196640 | tf_op jit(solution)/shard_map/ppermute | solution.py:537
  113.2 0.0 collective-permute-done.2
  113.2 0.7 copy-done.12
  113.9 0.7 copy-done.13
  114.6 0.0 collective-permute-done.3
  114.6 0.0 all-to-all-done.1
  114.6 1.3 pad_maximum_fusion.rest_0_
  115.8 0.1 collective-permute-start.4
  115.9 2.0 %collective-permute-start.6 = (f32[4,3,128,128]{3,2,1,0:T(8,128)S(1)}, f32[4,3,128,128]{3,2,1,0:T(8,128)S(1)}, u32[]{:S(2)}, u32[]{:S(2)}) collective-permute-start(f32[4,3,128,128]{3,2,1,0:T(8,128)S(1)} %pad_maximum_fusion.rest_0_), channel_id=1, source_target_pairs={{8,0},{16,8},{24,16},{28,24},{20,28},{12,20},{4,12},{0,4},{9,1},{1... | collective-permute-start | bytes 2359304 | tf_op jit(solution)/shard_map/ppermute | solution.py:548
  117.9 0.0 collective-permute-start.8
  117.9 0.0 collective-permute-done.9.t2
  117.9 0.5 collective-permute-start.10
  118.4 13.7 %collective-permute-done.4.rest_1_ = f32[4,3,128,128]{3,2,1,0:T(8,128)S(1)} collective-permute-done((f32[4,3,128,128]{3,2,1,0:T(8,128)S(1)}, f32[4,3,128,128]{3,2,1,0:T(8,128)S(1)}, u32[]{:S(2)}, u32[]{:S(2)}) %collective-permute-start.4) | collective-permute-done | bytes 786464 | tf_op jit(solution)/shard_map/ppermute | solution.py:547
  132.1 1.5 collective-permute-start.5
  133.6 0.0 collective-permute-done.6.rest_0_
  133.6 0.5 collective-permute-start.7
  134.1 0.0 collective-permute-done.8.t1
  134.1 0.0 collective-permute-done.10.t3
  134.1 1.0 copy-done.3
  135.2 8.4 %row_panels.1 = (bf16[1536,1024]{1,0:T(8,128)(2,1)S(1)}, f32[12,1,24,1,128,128]{5,4,3,2,1,0:T(8,128)}, bf16[3,256,768]{2,1,0:T(8,128)(2,1)S(1)}, s32[64]{0:T(128)S(1)}, s32[25]{0:T(128)S(1)}) custom-call(s32[4]{0:T(128)S(1)} %copy-done.5, s32[32]{0:T(128)S(1)} %fusion.slot_in, f32[12,128,128]{2,1,0:T(8,128)S(1)} %get-tuple-element.41.t0, ...), custom_call_target="tpu_custom_call" | custom-call | tf_op jit(solution)/shard_map/row_panels/pallas_call | solution.py:286
  143.6 1.6 copy-done
  145.2 0.0 copy-done.6
  145.2 0.0 copy-done.7
  145.2 9.5 %trailing.5.rest_4_ = f32[12,1,24,1,128,128]{5,4,3,2,1,0:T(8,128)} custom-call(s32[4]{0:T(128)S(1)} %copy-done.5, s32[192]{0:T(256)S(1)} %copy-done.6, s32[256]{0:T(256)S(1)} %copy-done.7, s32[64]{0:T(128)S(1)} %get-tuple-element.48.order, s32[25]{0:T(128)S(1)} %get-tuple-element.49.starts, ...), custom_call_target="tpu_custom_call", output_to_operand_aliasing={{}: (11, {})} | custom-call | flops 9663676416 | bytes 9437184 | tf_op jit(solution)/shard_map/trailing/pallas_call | solution.py:444
  154.7 0.0 copy-start.1
  154.7 0.0 collective-permute-done.5.rest_1_
  154.7 0.0 collective-permute-done.7.rest_0_
  154.7 1.8 collective-permute-start.11
  156.5 0.3 collective-permute-start.13
  156.8 10.1 %trailing.6.rest_3_ = f32[12,1,24,1,128,128]{5,4,3,2,1,0:T(8,128)} custom-call(s32[4]{0:T(128)S(1)} %copy-done.5, s32[192]{0:T(256)S(1)} %copy-done.6, s32[256]{0:T(256)S(1)} %copy-done.7, s32[64]{0:T(128)S(1)} %get-tuple-element.48.order, s32[25]{0:T(128)S(1)} %get-tuple-element.49.starts, ...), custom_call_target="tpu_custom_call", output_to_operand_aliasing={{}: (11, {})} | custom-call | flops 9663676416 | bytes 9437184 | tf_op jit(solution)/shard_map/trailing/pallas_call | solution.py:444
  166.9 6.1 %trailing.7.rest_4_ = f32[12,1,24,1,128,128]{5,4,3,2,1,0:T(8,128)} custom-call(s32[4]{0:T(128)S(1)} %copy-done.5, s32[192]{0:T(256)S(1)} %copy-done.6, s32[256]{0:T(256)S(1)} %copy-done.7, s32[64]{0:T(128)S(1)} %get-tuple-element.48.order, s32[25]{0:T(128)S(1)} %get-tuple-element.49.starts, ...), custom_call_target="tpu_custom_call", output_to_operand_aliasing={{}: (10, {})} | custom-call | flops 4831838208 | bytes 4718592 | tf_op jit(solution)/shard_map/trailing/pallas_call | solution.py:444
  173.0 0.1 collective-permute-done.11.rest_0_
  173.2 1.3 collective-permute-start.12
  174.4 0.0 collective-permute-done.13.rest_1_
  174.5 0.8 collective-permute-start.14
  175.3 10.0 %trailing.8.rest_4_ = f32[12,1,24,1,128,128]{5,4,3,2,1,0:T(8,128)} custom-call(s32[4]{0:T(128)S(1)} %copy-done.5, s32[192]{0:T(256)S(1)} %copy-done.6, s32[256]{0:T(256)S(1)} %copy-done.7, s32[64]{0:T(128)S(1)} %get-tuple-element.48.order, s32[25]{0:T(128)S(1)} %get-tuple-element.49.starts, ...), custom_call_target="tpu_custom_call", output_to_operand_aliasing={{}: (11, {})} | custom-call | flops 9663676416 | bytes 9437184 | tf_op jit(solution)/shard_map/trailing/pallas_call | solution.py:444
  185.4 0.0 collective-permute-done.12.rest_0_
  185.4 0.0 collective-permute-done.14.rest_1_
  185.4 6.2 %trailing.9 = f32[12,1,24,1,128,128]{5,4,3,2,1,0:T(8,128)} custom-call(s32[4]{0:T(128)S(1)} %copy-done.5, s32[192]{0:T(256)S(1)} %copy-done.6, s32[256]{0:T(256)S(1)} %copy-done.7, s32[64]{0:T(128)S(1)} %get-tuple-element.48.order, s32[25]{0:T(128)S(1)} %get-tuple-element.49.starts, ...), custom_call_target="tpu_custom_call", output_to_operand_aliasing={{}: (11, {})} | custom-call | flops 4831838208 | bytes 4718592 | tf_op jit(solution)/shard_map/trailing/pallas_call | solution.py:444
  (10 shorter events, 0.1 us)
Async XLA Ops:
  1.2 70.0 %copy-start.5 = (s32[4]{0:T(128)S(1)}, s32[4]{0:T(128)}, u32[]{:S(2)}) copy-start(s32[4]{0:T(128)} %pad_add_fusion.place) | copy-start | bytes 52
  5.0 140.2 %copy-start.6 = (s32[192]{0:T(256)S(1)}, s32[192]{0:T(256)}, u32[]{:S(2)}) copy-start(s32[192]{0:T(256)} %constant.17.clone.columns_table) | copy-start | bytes 2308
  5.0 140.2 %copy-start.7 = (s32[256]{0:T(256)S(1)}, s32[256]{0:T(256)}, u32[]{:S(2)}) copy-start(s32[256]{0:T(256)} %constant.18.clone.places_table) | copy-start | bytes 3076
  73.2 0.7 copy-start.8
  73.2 0.8 copy-start.9
  73.2 10.3 %copy-start.4 = (f32[32,16,128]{2,1,0:T(8,128)}, f32[32,16,128]{2,1,0:T(8,128)S(1)}, u32[]{:S(2)}) copy-start(f32[32,16,128]{2,1,0:T(8,128)S(1)} %get-tuple-element.36) | copy-start | bytes 786436
  73.3 10.3 %copy-start.10 = (f32[3,128,128]{2,1,0:T(8,128)}, f32[3,128,128]{2,1,0:T(8,128)S(1)}, u32[]{:S(2)}) copy-start(f32[3,128,128]{2,1,0:T(8,128)S(1)} %get-tuple-element.33) | copy-start | bytes 589828
  73.3 0.7 collective-permute-start
  74.0 9.6 %copy-start.11 = (f32[3,128,128]{2,1,0:T(8,128)}, f32[3,128,128]{2,1,0:T(8,128)S(1)}, u32[]{:S(2)}) copy-start(f32[3,128,128]{2,1,0:T(8,128)S(1)} %collective-permute-done) | copy-start | bytes 589828
  74.0 43.9 %collective-permute-start.9 = (f32[12,128,128]{2,1,0:T(8,128)S(1)}, f32[12,128,128]{2,1,0:T(8,128)}, u32[]{:S(2)}, u32[]{:S(2)}) collective-permute-start(f32[12,128,128]{2,1,0:T(8,128)S(1)} %get-tuple-element.41.t0), channel_id=1, source_target_pairs={{0,2},{1,3},{2,0},{3,1},{4,6},{5,7},{6,4},{7,5},{8,10},{9,11},{10,... | collective-permute-start | bytes 2359304 | tf_op jit(solution)/shard_map/ppermute | solution.py:494
  83.5 31.0 %all-to-all-start.1 = ((f32[32,16,128]{2,1,0:T(8,128)}), f32[32,16,128]{2,1,0:T(8,128)S(1)}, u32[]{:S(2)}, u32[]{:S(2)}) async-start(f32[32,16,128]{2,1,0:T(8,128)} %copy-done.4), calls=%async_computation.1 | async-start | bytes 524288 | tf_op jit(solution)/shard_map/all_to_all | solution.py:489
  87.7 25.5 %collective-permute-start.1 = (f32[3,128,128]{2,1,0:T(8,128)}, f32[3,128,128]{2,1,0:T(8,128)S(1)}, u32[]{:S(2)}, u32[]{:S(2)}) collective-permute-start(f32[3,128,128]{2,1,0:T(8,128)} %copy-done.10), channel_id=1, source_target_pairs={{0,4},{1,8},{2,12},{3,0},{4,5},{5,9},{6,13},{7,1},{8,6},{9,10},{10... | collective-permute-start | bytes 589832 | tf_op jit(solution)/shard_map/ppermute | solution.py:537
  89.5 23.7 %collective-permute-start.2 = (f32[3,128,128]{2,1,0:T(8,128)}, f32[3,128,128]{2,1,0:T(8,128)S(1)}, u32[]{:S(2)}, u32[]{:S(2)}) collective-permute-start(f32[3,128,128]{2,1,0:T(8,128)} %copy-done.9), channel_id=1, source_target_pairs={{0,8},{1,12},{2,0},{3,4},{4,9},{5,13},{6,1},{7,5},{8,10},{9,14},{1... | collective-permute-start | bytes 589832 | tf_op jit(solution)/shard_map/ppermute | solution.py:537
  91.9 22.7 %collective-permute-start.3 = (f32[3,128,128]{2,1,0:T(8,128)}, f32[3,128,128]{2,1,0:T(8,128)}, u32[]{:S(2)}, u32[]{:S(2)}) collective-permute-start(f32[3,128,128]{2,1,0:T(8,128)} %copy-done.8), channel_id=1, source_target_pairs={{0,12},{1,0},{2,4},{3,8},{4,13},{5,1},{6,5},{7,9},{8,14},{9,2},{10... | collective-permute-start | bytes 589832 | tf_op jit(solution)/shard_map/ppermute | solution.py:537
  113.2 0.7 copy-start.12
  113.9 0.7 copy-start.13
  115.8 16.2 %collective-permute-start.4 = (f32[4,3,128,128]{3,2,1,0:T(8,128)S(1)}, f32[4,3,128,128]{3,2,1,0:T(8,128)S(1)}, u32[]{:S(2)}, u32[]{:S(2)}) collective-permute-start(f32[4,3,128,128]{3,2,1,0:T(8,128)S(1)} %pad_maximum_fusion.rest_0_), channel_id=1, source_target_pairs={{0,8},{8,16},{16,24},{24,28},{28,20},{20,12},{12,4},{4,0},{1,9},{9... | collective-permute-start | bytes 2359304 | tf_op jit(solution)/shard_map/ppermute | solution.py:547
  115.9 17.7 %collective-permute-start.6 = (f32[4,3,128,128]{3,2,1,0:T(8,128)S(1)}, f32[4,3,128,128]{3,2,1,0:T(8,128)S(1)}, u32[]{:S(2)}, u32[]{:S(2)}) collective-permute-start(f32[4,3,128,128]{3,2,1,0:T(8,128)S(1)} %pad_maximum_fusion.rest_0_), channel_id=1, source_target_pairs={{8,0},{16,8},{24,16},{28,24},{20,28},{12,20},{4,12},{0,4},{9,1},{1... | collective-permute-start | bytes 2359304 | tf_op jit(solution)/shard_map/ppermute | solution.py:548
  117.9 16.2 %collective-permute-start.8 = (f32[12,128,128]{2,1,0:T(8,128)S(1)}, f32[12,128,128]{2,1,0:T(8,128)S(1)}, u32[]{:S(2)}, u32[]{:S(2)}) collective-permute-start(f32[12,128,128]{2,1,0:T(8,128)S(1)} %get-tuple-element.41.t0), channel_id=1, source_target_pairs={{0,1},{1,0},{2,3},{3,2},{4,5},{5,4},{6,7},{7,6},{8,9},{9,8},{10,11... | collective-permute-start | bytes 2359304 | tf_op jit(solution)/shard_map/ppermute | solution.py:493
  117.9 16.2 %collective-permute-start.10 = (f32[12,128,128]{2,1,0:T(8,128)}, f32[12,128,128]{2,1,0:T(8,128)S(1)}, u32[]{:S(2)}, u32[]{:S(2)}) collective-permute-start(f32[12,128,128]{2,1,0:T(8,128)} %collective-permute-done.9.t2), channel_id=1, source_target_pairs={{0,1},{1,0},{2,3},{3,2},{4,5},{5,4},{6,7},{7,6},{8,9},{9,8},{10,11... | collective-permute-start | bytes 2359304 | tf_op jit(solution)/shard_map/ppermute | solution.py:495
  132.1 22.6 %collective-permute-start.5 = (f32[4,3,128,128]{3,2,1,0:T(8,128)S(1)}, f32[4,3,128,128]{3,2,1,0:T(8,128)S(1)}, u32[]{:S(2)}, u32[]{:S(2)}) collective-permute-start(f32[4,3,128,128]{3,2,1,0:T(8,128)S(1)} %collective-permute-done.4.rest_1_), channel_id=1, source_target_pairs={{0,8},{8,16},{16,24},{24,28},{28,20},{20,12},{12,4},{4,0},{1,9},{9... | collective-permute-start | bytes 2359304 | tf_op jit(solution)/shard_map/ppermute | solution.py:547
  133.6 21.1 %collective-permute-start.7 = (f32[4,3,128,128]{3,2,1,0:T(8,128)S(1)}, f32[4,3,128,128]{3,2,1,0:T(8,128)S(1)}, u32[]{:S(2)}, u32[]{:S(2)}) collective-permute-start(f32[4,3,128,128]{3,2,1,0:T(8,128)S(1)} %collective-permute-done.6.rest_0_), channel_id=1, source_target_pairs={{8,0},{16,8},{24,16},{28,24},{20,28},{12,20},{4,12},{0,4},{9,1},{1... | collective-permute-start | bytes 2359304 | tf_op jit(solution)/shard_map/ppermute | solution.py:548
  134.1 1.0 copy-start.3
  143.6 1.6 copy-start
  154.7 12.2 %copy-start.1 = (bf16[1536,1024]{1,0:T(8,128)(2,1)S(1)}, bf16[1536,1024]{1,0:T(8,128)(2,1)}, u32[]{:S(2)}) copy-start(bf16[1536,1024]{1,0:T(8,128)(2,1)} %copy-done) | copy-start | bytes 9437188
  154.7 18.4 %collective-permute-start.11 = (f32[4,3,128,128]{3,2,1,0:T(8,128)S(1)}, f32[4,3,128,128]{3,2,1,0:T(8,128)S(1)}, u32[]{:S(2)}, u32[]{:S(2)}) collective-permute-start(f32[4,3,128,128]{3,2,1,0:T(8,128)S(1)} %collective-permute-done.5.rest_1_), channel_id=1, source_target_pairs={{0,8},{8,16},{16,24},{24,28},{28,20},{20,12},{12,4},{4,0},{1,9},{9... | collective-permute-start | bytes 2359304 | tf_op jit(solution)/shard_map/ppermute | solution.py:547
  156.5 17.9 %collective-permute-start.13 = (f32[4,3,128,128]{3,2,1,0:T(8,128)S(1)}, f32[4,3,128,128]{3,2,1,0:T(8,128)S(1)}, u32[]{:S(2)}, u32[]{:S(2)}) collective-permute-start(f32[4,3,128,128]{3,2,1,0:T(8,128)S(1)} %collective-permute-done.7.rest_0_), channel_id=1, source_target_pairs={{8,0},{16,8},{24,16},{28,24},{20,28},{12,20},{4,12},{0,4},{9,1},{1... | collective-permute-start | bytes 2359304 | tf_op jit(solution)/shard_map/ppermute | solution.py:548
  173.2 12.2 %collective-permute-start.12 = (f32[2,3,128,128]{3,2,1,0:T(8,128)S(1)}, f32[2,3,128,128]{3,2,1,0:T(8,128)S(1)}, u32[]{:S(2)}, u32[]{:S(2)}) collective-permute-start(f32[2,3,128,128]{3,2,1,0:T(8,128)S(1)} %slice.13), channel_id=1, source_target_pairs={{0,8},{8,16},{16,24},{24,28},{28,20},{20,12},{12,4},{4,0},{1,9},{9... | collective-permute-start | bytes 1179656 | tf_op jit(solution)/shard_map/ppermute | solution.py:553
  174.5 10.9 %copy-start.2 = (bf16[1536,1024]{1,0:T(8,128)(2,1)S(1)}, bf16[1536,1024]{1,0:T(8,128)(2,1)}, u32[]{:S(2)}) copy-start(bf16[1536,1024]{1,0:T(8,128)(2,1)} %copy-done) | copy-start | bytes 9437188
  174.5 10.9 %collective-permute-start.14 = (f32[2,3,128,128]{3,2,1,0:T(8,128)S(1)}, f32[2,3,128,128]{3,2,1,0:T(8,128)S(1)}, u32[]{:S(2)}, u32[]{:S(2)}) collective-permute-start(f32[2,3,128,128]{3,2,1,0:T(8,128)S(1)} %slice.14), channel_id=1, source_target_pairs={{8,0},{16,8},{24,16},{28,24},{20,28},{12,20},{4,12},{0,4},{9,1},{1... | collective-permute-start | bytes 1179656 | tf_op jit(solution)/shard_map/ppermute | solution.py:553

commit v13 on v12

--- a/solution.py
+++ b/solution.py
@@ -535,7 +535,7 @@
                 for c in range(n_col)
             ]
             arrived.append(lax.ppermute(part, BOTH, pairs))
-        arrived[0], mine = lax.optimization_barrier((arrived[0], mine))
+        arrived, mine = lax.optimization_barrier((arrived, mine))
         arrived, lead = lax.optimization_barrier((arrived, lead))
         piece = jnp.stack(arrived)
         up = [(circle[i], circle[(i + 1) % n_row]) for i in range(n_row)]

time: 193 us -> 188 us (0.974)
  blocking collectives: 65.5 us -> 86.5 us
  waiting for transfers between devices: 34.8 us -> 22.7 us
  starting transfers between devices: 27.6 us -> 18.8 us
  local copies, waits for them, and re-layouts: 4.18 us -> 1.73 us
    all_to_all x0 -> x1, blocking collectives: none -> 21.1 us  [body(): lead = lax.all_to_all(own, BOTH, split_axis=0, concat_axis=0, tiled=True)]
    ppermute x4, waiting for transfers between devices: 21 us -> 5.41 us  [body(): arrived.append(lax.ppermute(part, BOTH, pairs))]
    ppermute x1, starting transfers between devices: 9.54 us -> 2.85 us  [exchange(): far = lax.ppermute(mine, 'col', [(c, c ^ 2) for c in range(n_col)])]
    all_to_all x1 -> x0, starting transfers between devices: 4.14 us -> none  [body(): lead = lax.all_to_all(own, BOTH, split_axis=0, concat_axis=0, tiled=True)]
    ppermute x3, waiting for transfers between devices: 13.8 us -> 17.3 us  [body(): ahead = lax.ppermute(ahead, 'row', up)]
    unnamed x28 -> x14, local copies, waits for them, and re-layouts: 4.13 us -> 1.68 us
    ppermute x4, starting transfers between devices: 5.15 us -> 7.13 us  [body(): arrived.append(lax.ppermute(part, BOTH, pairs))]
  transfers between devices with their start and end apart: 16 -> 15, of which waited for: 3 -> 4; matrix products, arithmetic and copies ran while one was open for 1% -> 0% of each run, Pallas kernels for 23% -> 23%
where the time goes in v13:
time: 188 us
  blocking collectives  86.5 us (46%)
  Pallas kernels  55.7 us (30%)
  waiting for transfers between devices  22.7 us (12%)
  starting transfers between devices  18.8 us (10%)
    all_to_all x1, blocking collectives, body(): lax.all_to_all(outgoing, BOTH, split_axis=0, concat_axis=0, tiled=True)  65.4 us
    pallas_call x5, Pallas kernels, trailing(): pl.pallas_call(functools.partial(trailing_kernel, first, len(pieces), hal...  42 us
    all_to_all x1, blocking collectives, body(): lead = lax.all_to_all(own, BOTH, split_axis=0, concat_axis=0, tiled=True)  21.1 us
    ppermute x3, waiting for transfers between devices, body(): ahead = lax.ppermute(ahead, 'row', up)  17.3 us
    pallas_call x1, Pallas kernels, row_panels(): pl.pallas_call(row_panels_kernel, grid_spec=pltpu.PrefetchScalarGridSpec(...  7.51 us
    ppermute x4, starting transfers between devices, body(): arrived.append(lax.ppermute(part, BOTH, pairs))  7.13 us
    ppermute x4, waiting for transfers between devices, body(): arrived.append(lax.ppermute(part, BOTH, pairs))  5.41 us
    pallas_call x1, Pallas kernels, pack(): pl.pallas_call(functools.partial(pack_kernel, owners), in_specs=[pl.Block...  3.88 us
  transfers between devices with their start and end apart: 15, of which 4 were waited for; matrix products, arithmetic and copies ran while one was open for 0% of the time, Pallas kernels for 23%

profile of v13, /device:TPU:0, one launch (start us, length us, event | category | flops | bytes accessed | tf_op | source)
XLA Modules:
  0.0 187.8 jit_solution(13688656481987996492)
XLA Ops:
  0.7 0.7 pad_add_fusion.place
  1.3 0.0 copy-start.4
  1.3 3.9 %pack.1 = f32[32,152,128]{2,1,0:T(8,128)} custom-call(s32[4]{0:T(128)} %pad_add_fusion.place, s32[16]{0:T(128)} %bitcast.14, s32[16]{0:T(128)} %slot.1, s32[1]{0:T(128)S(6)} %copy.19.count, f32[16,128,128]{2,1,0:T(8,128)} %child_ref.1, f32[12,1,24,1,128,128]{5,4,3,2,1,0:T(8,128)} %rest_2_.7), custom_call_target="tpu_custom_call" | custom-call | tf_op jit(solution)/shard_map/pack/pallas_call | solution.py:122
  5.2 0.0 copy-start.3
  5.2 0.0 copy-start.5
  5.2 0.0 copy-start.6
  5.2 65.4 %all_to_all.10.incoming_ref.rest_3_.rest_2_ = f32[32,152,128]{2,1,0:T(8,128)S(1)} all-to-all(f32[32,152,128]{2,1,0:T(8,128)} %pack.1), channel_id=1, replica_groups=mesh['row'=8,'col'=4] {'row','col'}, dimensions={0} | all-to-all | bytes 4980736 | tf_op jit(solution)/shard_map/all_to_all | solution.py:484
  70.6 0.7 fusion.slot_in
  71.3 0.0 copy-done.4
  71.3 2.4 %panel_columns.1 = (f32[12,128,128]{2,1,0:T(8,128)S(1)}, f32[32,16,128]{2,1,0:T(8,128)S(1)}, f32[3,128,128]{2,1,0:T(8,128)S(1)}, f32[3,128,128]{2,1,0:T(8,128)S(...) custom-call(s32[4]{0:T(128)S(1)} %copy-done.4, s32[32]{0:T(128)S(1)} %fusion.slot_in, ...), custom_call_target="tpu_custom_call" | custom-call | tf_op jit(solution)/shard_map/panel_columns/pallas_call | solution.py:181
  73.7 0.7 collective-permute-start
  74.3 2.8 %collective-permute-start.1 = (f32[3,128,128]{2,1,0:T(8,128)S(1)}, f32[3,128,128]{2,1,0:T(8,128)S(1)}, u32[]{:S(2)}, u32[]{:S(2)}) collective-permute-start(f32[3,128,128]{2,1,0:T(8,128)S(1)} %get-tuple-element.34), channel_id=1, source_target_pairs={{0,4},{1,8},{2,12},{3,0},{4,5},{5,9},{6,13},{7,1},{8,6},{9,10},{10... | collective-permute-start | bytes 589832 | tf_op jit(solution)/shard_map/ppermute | solution.py:537
  77.2 1.7 collective-permute-start.2
  78.9 1.9 %collective-permute-start.3 = (f32[3,128,128]{2,1,0:T(8,128)S(1)}, f32[3,128,128]{2,1,0:T(8,128)S(1)}, u32[]{:S(2)}, u32[]{:S(2)}) collective-permute-start(f32[3,128,128]{2,1,0:T(8,128)S(1)} %get-tuple-element.36), channel_id=1, source_target_pairs={{0,12},{1,0},{2,4},{3,8},{4,13},{5,1},{6,5},{7,9},{8,14},{9,2},{10... | collective-permute-start | bytes 589832 | tf_op jit(solution)/shard_map/ppermute | solution.py:537
  80.8 0.0 collective-permute-done
  80.8 5.2 %collective-permute-done.1 = f32[3,128,128]{2,1,0:T(8,128)S(1)} collective-permute-done((f32[3,128,128]{2,1,0:T(8,128)S(1)}, f32[3,128,128]{2,1,0:T(8,128)S(1)}, u32[]{:S(2)}, u32[]{:S(2)}) %collective-permute-start.1) | collective-permute-done | bytes 196640 | tf_op jit(solution)/shard_map/ppermute | solution.py:537
  86.0 0.0 collective-permute-done.2
  86.0 0.2 collective-permute-done.3
  86.2 2.8 %collective-permute-start.9 = (f32[12,128,128]{2,1,0:T(8,128)S(1)}, f32[12,128,128]{2,1,0:T(8,128)S(1)}, u32[]{:S(2)}, u32[]{:S(2)}) collective-permute-start(f32[12,128,128]{2,1,0:T(8,128)S(1)} %get-tuple-element.47.t0), channel_id=1, source_target_pairs={{0,2},{1,3},{2,0},{3,1},{4,6},{5,7},{6,4},{7,5},{8,10},{9,11},{10,... | collective-permute-start | bytes 2359304 | tf_op jit(solution)/shard_map/ppermute | solution.py:494
  89.1 21.1 %all_to_all.11 = f32[32,16,128]{2,1,0:T(8,128)S(1)} all-to-all(f32[32,16,128]{2,1,0:T(8,128)S(1)} %get-tuple-element.42), channel_id=1, replica_groups=mesh['row'=8,'col'=4] {'row','col'}, dimensions={0} | all-to-all | bytes 524288 | tf_op jit(solution)/shard_map/all_to_all | solution.py:489
  110.2 0.1 pad_maximum_fusion.rest_0_
  110.2 1.0 collective-permute-start.4
  111.2 1.1 collective-permute-start.6
  112.3 0.0 collective-permute-start.8
  112.3 0.0 collective-permute-done.9.t2
  112.3 0.5 collective-permute-start.10
  112.8 17.0 %collective-permute-done.4.rest_1_ = f32[4,3,128,128]{3,2,1,0:T(8,128)S(1)} collective-permute-done((f32[4,3,128,128]{3,2,1,0:T(8,128)S(1)}, f32[4,3,128,128]{3,2,1,0:T(8,128)S(1)}, u32[]{:S(2)}, u32[]{:S(2)}) %collective-permute-start.4) | collective-permute-done | bytes 786464 | tf_op jit(solution)/shard_map/ppermute | solution.py:547
  129.9 0.9 collective-permute-start.5
  130.8 0.0 collective-permute-done.6.rest_0_
  130.8 1.1 collective-permute-start.7
  131.9 0.0 collective-permute-done.8.t1
  131.9 0.0 collective-permute-done.10.t3
  131.9 0.0 copy-done.3
  131.9 7.5 %row_panels.1 = (bf16[1536,1024]{1,0:T(8,128)(2,1)S(1)}, f32[12,1,24,1,128,128]{5,4,3,2,1,0:T(8,128)}, bf16[3,256,768]{2,1,0:T(8,128)(2,1)S(1)}, s32[64]{0:T(128)S(1)}, s32[25]{0:T(128)S(1)}) custom-call(s32[4]{0:T(128)S(1)} %copy-done.4, s32[32]{0:T(128)S(1)} %fusion.slot_in, f32[12,128,128]{2,1,0:T(8,128)S(1)} %get-tuple-element.47.t0, ...), custom_call_target="tpu_custom_call" | custom-call | tf_op jit(solution)/shard_map/row_panels/pallas_call | solution.py:286
  139.4 0.0 copy-start
  139.4 1.6 copy-done
  141.1 0.0 copy-done.5
  141.1 0.0 copy-done.6
  141.1 9.5 %trailing.5.rest_4_ = f32[12,1,24,1,128,128]{5,4,3,2,1,0:T(8,128)} custom-call(s32[4]{0:T(128)S(1)} %copy-done.4, s32[192]{0:T(256)S(1)} %copy-done.5, s32[256]{0:T(256)S(1)} %copy-done.6, s32[64]{0:T(128)S(1)} %get-tuple-element.54.order, s32[25]{0:T(128)S(1)} %get-tuple-element.55.starts, ...), custom_call_target="tpu_custom_call", output_to_operand_aliasing={{}: (11, {})} | custom-call | flops 9663676416 | bytes 9437184 | tf_op jit(solution)/shard_map/trailing/pallas_call | solution.py:444
  150.6 0.0 copy-start.1
  150.6 0.0 collective-permute-done.5.rest_1_
  150.6 0.0 collective-permute-done.7.rest_0_
  150.6 1.3 collective-permute-start.11
  151.9 0.8 collective-permute-start.13
  152.7 9.9 %trailing.6.rest_3_ = f32[12,1,24,1,128,128]{5,4,3,2,1,0:T(8,128)} custom-call(s32[4]{0:T(128)S(1)} %copy-done.4, s32[192]{0:T(256)S(1)} %copy-done.5, s32[256]{0:T(256)S(1)} %copy-done.6, s32[64]{0:T(128)S(1)} %get-tuple-element.54.order, s32[25]{0:T(128)S(1)} %get-tuple-element.55.starts, ...), custom_call_target="tpu_custom_call", output_to_operand_aliasing={{}: (11, {})} | custom-call | flops 9663676416 | bytes 9437184 | tf_op jit(solution)/shard_map/trailing/pallas_call | solution.py:444
  162.6 0.0 copy-done.1
  162.6 6.1 %trailing.7.rest_4_ = f32[12,1,24,1,128,128]{5,4,3,2,1,0:T(8,128)} custom-call(s32[4]{0:T(128)S(1)} %copy-done.4, s32[192]{0:T(256)S(1)} %copy-done.5, s32[256]{0:T(256)S(1)} %copy-done.6, s32[64]{0:T(128)S(1)} %get-tuple-element.54.order, s32[25]{0:T(128)S(1)} %get-tuple-element.55.starts, ...), custom_call_target="tpu_custom_call", output_to_operand_aliasing={{}: (10, {})} | custom-call | flops 4831838208 | bytes 4718592 | tf_op jit(solution)/shard_map/trailing/pallas_call | solution.py:444
  168.7 0.3 collective-permute-done.11.rest_0_
  169.0 1.3 collective-permute-start.12
  170.3 0.0 collective-permute-done.13.rest_1_
  170.4 0.0 copy-start.2
  170.4 0.8 collective-permute-start.14
  171.2 10.3 %trailing.8.rest_4_ = f32[12,1,24,1,128,128]{5,4,3,2,1,0:T(8,128)} custom-call(s32[4]{0:T(128)S(1)} %copy-done.4, s32[192]{0:T(256)S(1)} %copy-done.5, s32[256]{0:T(256)S(1)} %copy-done.6, s32[64]{0:T(128)S(1)} %get-tuple-element.54.order, s32[25]{0:T(128)S(1)} %get-tuple-element.55.starts, ...), custom_call_target="tpu_custom_call", output_to_operand_aliasing={{}: (11, {})} | custom-call | flops 9663676416 | bytes 9437184 | tf_op jit(solution)/shard_map/trailing/pallas_call | solution.py:444
  181.5 0.0 collective-permute-done.12.rest_0_
  181.5 0.0 collective-permute-done.14.rest_1_
  181.5 0.0 copy-done.2
  181.5 6.1 %trailing.9 = f32[12,1,24,1,128,128]{5,4,3,2,1,0:T(8,128)} custom-call(s32[4]{0:T(128)S(1)} %copy-done.4, s32[192]{0:T(256)S(1)} %copy-done.5, s32[256]{0:T(256)S(1)} %copy-done.6, s32[64]{0:T(128)S(1)} %get-tuple-element.54.order, s32[25]{0:T(128)S(1)} %get-tuple-element.55.starts, ...), custom_call_target="tpu_custom_call", output_to_operand_aliasing={{}: (11, {})} | custom-call | flops 4831838208 | bytes 4718592 | tf_op jit(solution)/shard_map/trailing/pallas_call | solution.py:444
  (2 shorter events, 0.1 us)
Async XLA Ops:
  1.3 70.0 %copy-start.4 = (s32[4]{0:T(128)S(1)}, s32[4]{0:T(128)}, u32[]{:S(2)}) copy-start(s32[4]{0:T(128)} %pad_add_fusion.place) | copy-start | bytes 52
  5.2 126.7 %copy-start.3 = (f32[2,256,256]{2,1,0:T(8,128)S(1)}, f32[2,256,256]{2,1,0:T(8,128)}, u32[]{:S(2)}) copy-start(f32[2,256,256]{2,1,0:T(8,128)} %diag_ref.1) | copy-start | bytes 1572868
  5.2 135.9 %copy-start.5 = (s32[192]{0:T(256)S(1)}, s32[192]{0:T(256)}, u32[]{:S(2)}) copy-start(s32[192]{0:T(256)} %constant.17.clone.columns_table) | copy-start | bytes 2308
  5.2 135.8 %copy-start.6 = (s32[256]{0:T(256)S(1)}, s32[256]{0:T(256)}, u32[]{:S(2)}) copy-start(s32[256]{0:T(256)} %constant.18.clone.places_table) | copy-start | bytes 3076
  73.7 7.1 %collective-permute-start = (f32[3,128,128]{2,1,0:T(8,128)S(1)}, f32[3,128,128]{2,1,0:T(8,128)S(1)}, u32[]{:S(2)}, u32[]{:S(2)}) collective-permute-start(f32[3,128,128]{2,1,0:T(8,128)S(1)} %get-tuple-element.33), channel_id=1, source_target_pairs={{0,0},{1,4},{2,8},{3,12},{4,1},{5,5},{6,9},{7,13},{8,2},{9,6},{10,... | collective-permute-start | bytes 589832 | tf_op jit(solution)/shard_map/ppermute | solution.py:537
  74.3 11.7 %collective-permute-start.1 = (f32[3,128,128]{2,1,0:T(8,128)S(1)}, f32[3,128,128]{2,1,0:T(8,128)S(1)}, u32[]{:S(2)}, u32[]{:S(2)}) collective-permute-start(f32[3,128,128]{2,1,0:T(8,128)S(1)} %get-tuple-element.34), channel_id=1, source_target_pairs={{0,4},{1,8},{2,12},{3,0},{4,5},{5,9},{6,13},{7,1},{8,6},{9,10},{10... | collective-permute-start | bytes 589832 | tf_op jit(solution)/shard_map/ppermute | solution.py:537
  77.2 8.9 %collective-permute-start.2 = (f32[3,128,128]{2,1,0:T(8,128)S(1)}, f32[3,128,128]{2,1,0:T(8,128)S(1)}, u32[]{:S(2)}, u32[]{:S(2)}) collective-permute-start(f32[3,128,128]{2,1,0:T(8,128)S(1)} %get-tuple-element.35), channel_id=1, source_target_pairs={{0,8},{1,12},{2,0},{3,4},{4,9},{5,13},{6,1},{7,5},{8,10},{9,14},{1... | collective-permute-start | bytes 589832 | tf_op jit(solution)/shard_map/ppermute | solution.py:537
  78.9 7.3 %collective-permute-start.3 = (f32[3,128,128]{2,1,0:T(8,128)S(1)}, f32[3,128,128]{2,1,0:T(8,128)S(1)}, u32[]{:S(2)}, u32[]{:S(2)}) collective-permute-start(f32[3,128,128]{2,1,0:T(8,128)S(1)} %get-tuple-element.36), channel_id=1, source_target_pairs={{0,12},{1,0},{2,4},{3,8},{4,13},{5,1},{6,5},{7,9},{8,14},{9,2},{10... | collective-permute-start | bytes 589832 | tf_op jit(solution)/shard_map/ppermute | solution.py:537
  86.2 26.1 %collective-permute-start.9 = (f32[12,128,128]{2,1,0:T(8,128)S(1)}, f32[12,128,128]{2,1,0:T(8,128)S(1)}, u32[]{:S(2)}, u32[]{:S(2)}) collective-permute-start(f32[12,128,128]{2,1,0:T(8,128)S(1)} %get-tuple-element.47.t0), channel_id=1, source_target_pairs={{0,2},{1,3},{2,0},{3,1},{4,6},{5,7},{6,4},{7,5},{8,10},{9,11},{10,... | collective-permute-start | bytes 2359304 | tf_op jit(solution)/shard_map/ppermute | solution.py:494
  110.2 19.6 %collective-permute-start.4 = (f32[4,3,128,128]{3,2,1,0:T(8,128)S(1)}, f32[4,3,128,128]{3,2,1,0:T(8,128)S(1)}, u32[]{:S(2)}, u32[]{:S(2)}) collective-permute-start(f32[4,3,128,128]{3,2,1,0:T(8,128)S(1)} %pad_maximum_fusion.rest_0_), channel_id=1, source_target_pairs={{0,8},{8,16},{16,24},{24,28},{28,20},{20,12},{12,4},{4,0},{1,9},{9... | collective-permute-start | bytes 2359304 | tf_op jit(solution)/shard_map/ppermute | solution.py:547
  111.2 19.6 %collective-permute-start.6 = (f32[4,3,128,128]{3,2,1,0:T(8,128)S(1)}, f32[4,3,128,128]{3,2,1,0:T(8,128)S(1)}, u32[]{:S(2)}, u32[]{:S(2)}) collective-permute-start(f32[4,3,128,128]{3,2,1,0:T(8,128)S(1)} %pad_maximum_fusion.rest_0_), channel_id=1, source_target_pairs={{8,0},{16,8},{24,16},{28,24},{20,28},{12,20},{4,12},{0,4},{9,1},{1... | collective-permute-start | bytes 2359304 | tf_op jit(solution)/shard_map/ppermute | solution.py:548
  112.3 19.6 %collective-permute-start.8 = (f32[12,128,128]{2,1,0:T(8,128)S(1)}, f32[12,128,128]{2,1,0:T(8,128)S(1)}, u32[]{:S(2)}, u32[]{:S(2)}) collective-permute-start(f32[12,128,128]{2,1,0:T(8,128)S(1)} %get-tuple-element.47.t0), channel_id=1, source_target_pairs={{0,1},{1,0},{2,3},{3,2},{4,5},{5,4},{6,7},{7,6},{8,9},{9,8},{10,11... | collective-permute-start | bytes 2359304 | tf_op jit(solution)/shard_map/ppermute | solution.py:493
  112.3 19.6 %collective-permute-start.10 = (f32[12,128,128]{2,1,0:T(8,128)S(1)}, f32[12,128,128]{2,1,0:T(8,128)S(1)}, u32[]{:S(2)}, u32[]{:S(2)}) collective-permute-start(f32[12,128,128]{2,1,0:T(8,128)S(1)} %collective-permute-done.9.t2), channel_id=1, source_target_pairs={{0,1},{1,0},{2,3},{3,2},{4,5},{5,4},{6,7},{7,6},{8,9},{9,8},{10,11... | collective-permute-start | bytes 2359304 | tf_op jit(solution)/shard_map/ppermute | solution.py:495
  129.9 20.7 %collective-permute-start.5 = (f32[4,3,128,128]{3,2,1,0:T(8,128)S(1)}, f32[4,3,128,128]{3,2,1,0:T(8,128)S(1)}, u32[]{:S(2)}, u32[]{:S(2)}) collective-permute-start(f32[4,3,128,128]{3,2,1,0:T(8,128)S(1)} %collective-permute-done.4.rest_1_), channel_id=1, source_target_pairs={{0,8},{8,16},{16,24},{24,28},{28,20},{20,12},{12,4},{4,0},{1,9},{9... | collective-permute-start | bytes 2359304 | tf_op jit(solution)/shard_map/ppermute | solution.py:547
  130.8 19.8 %collective-permute-start.7 = (f32[4,3,128,128]{3,2,1,0:T(8,128)S(1)}, f32[4,3,128,128]{3,2,1,0:T(8,128)S(1)}, u32[]{:S(2)}, u32[]{:S(2)}) collective-permute-start(f32[4,3,128,128]{3,2,1,0:T(8,128)S(1)} %collective-permute-done.6.rest_0_), channel_id=1, source_target_pairs={{8,0},{16,8},{24,16},{28,24},{20,28},{12,20},{4,12},{0,4},{9,1},{1... | collective-permute-start | bytes 2359304 | tf_op jit(solution)/shard_map/ppermute | solution.py:548
  139.4 1.6 copy-start
  150.6 12.0 %copy-start.1 = (bf16[1536,1024]{1,0:T(8,128)(2,1)S(1)}, bf16[1536,1024]{1,0:T(8,128)(2,1)}, u32[]{:S(2)}) copy-start(bf16[1536,1024]{1,0:T(8,128)(2,1)} %copy-done) | copy-start | bytes 9437188
  150.6 18.4 %collective-permute-start.11 = (f32[4,3,128,128]{3,2,1,0:T(8,128)S(1)}, f32[4,3,128,128]{3,2,1,0:T(8,128)S(1)}, u32[]{:S(2)}, u32[]{:S(2)}) collective-permute-start(f32[4,3,128,128]{3,2,1,0:T(8,128)S(1)} %collective-permute-done.5.rest_1_), channel_id=1, source_target_pairs={{0,8},{8,16},{16,24},{24,28},{28,20},{20,12},{12,4},{4,0},{1,9},{9... | collective-permute-start | bytes 2359304 | tf_op jit(solution)/shard_map/ppermute | solution.py:547
  151.9 18.5 %collective-permute-start.13 = (f32[4,3,128,128]{3,2,1,0:T(8,128)S(1)}, f32[4,3,128,128]{3,2,1,0:T(8,128)S(1)}, u32[]{:S(2)}, u32[]{:S(2)}) collective-permute-start(f32[4,3,128,128]{3,2,1,0:T(8,128)S(1)} %collective-permute-done.7.rest_0_), channel_id=1, source_target_pairs={{8,0},{16,8},{24,16},{28,24},{20,28},{12,20},{4,12},{0,4},{9,1},{1... | collective-permute-start | bytes 2359304 | tf_op jit(solution)/shard_map/ppermute | solution.py:548
  169.0 12.5 %collective-permute-start.12 = (f32[2,3,128,128]{3,2,1,0:T(8,128)S(1)}, f32[2,3,128,128]{3,2,1,0:T(8,128)S(1)}, u32[]{:S(2)}, u32[]{:S(2)}) collective-permute-start(f32[2,3,128,128]{3,2,1,0:T(8,128)S(1)} %slice.13), channel_id=1, source_target_pairs={{0,8},{8,16},{16,24},{24,28},{28,20},{20,12},{12,4},{4,0},{1,9},{9... | collective-permute-start | bytes 1179656 | tf_op jit(solution)/shard_map/ppermute | solution.py:553
  170.4 11.2 %copy-start.2 = (bf16[1536,1024]{1,0:T(8,128)(2,1)S(1)}, bf16[1536,1024]{1,0:T(8,128)(2,1)}, u32[]{:S(2)}) copy-start(bf16[1536,1024]{1,0:T(8,128)(2,1)} %copy-done) | copy-start | bytes 9437188
  170.4 11.1 %collective-permute-start.14 = (f32[2,3,128,128]{3,2,1,0:T(8,128)S(1)}, f32[2,3,128,128]{3,2,1,0:T(8,128)S(1)}, u32[]{:S(2)}, u32[]{:S(2)}) collective-permute-start(f32[2,3,128,128]{3,2,1,0:T(8,128)S(1)} %slice.14), channel_id=1, source_target_pairs={{8,0},{16,8},{24,16},{28,24},{20,28},{12,20},{4,12},{0,4},{9,1},{1... | collective-permute-start | bytes 1179656 | tf_op jit(solution)/shard_map/ppermute | solution.py:553

commit v14 on v13

--- a/solution.py
+++ b/solution.py
@@ -535,8 +535,7 @@
                 for c in range(n_col)
             ]
             arrived.append(lax.ppermute(part, BOTH, pairs))
-        arrived, mine = lax.optimization_barrier((arrived, mine))
-        arrived, lead = lax.optimization_barrier((arrived, lead))
+        arrived, mine, lead = lax.optimization_barrier((arrived, mine, lead))
         piece = jnp.stack(arrived)
         up = [(circle[i], circle[(i + 1) % n_row]) for i in range(n_row)]
         down = [(b, a) for a, b in up]

time: 188 us -> 179 us (0.952)
  blocking collectives: 86.5 us -> 65.3 us
  local copies, waits for them, and re-layouts: 1.73 us -> 7.09 us
  starting transfers between devices: 18.8 us -> 22.8 us
    all_to_all x1 -> x0, blocking collectives: 21.1 us -> none  [body(): lead = lax.all_to_all(own, BOTH, split_axis=0, concat_axis=0, tiled=True)]
    ppermute x3, waiting for transfers between devices: 17.3 us -> 2.68 us  [body(): ahead = lax.ppermute(ahead, 'row', up)]
    ppermute x1, waiting for transfers between devices: 0.01 us -> 14.4 us  [exchange(): far = lax.ppermute(mine, 'col', [(c, c ^ 2) for c in range(n_col)])]
    unnamed x14 -> x30, local copies, waits for them, and re-layouts: 1.68 us -> 7.04 us
    all_to_all x0 -> x1, starting transfers between devices: none -> 2.79 us  [body(): lead = lax.all_to_all(own, BOTH, split_axis=0, concat_axis=0, tiled=True)]
  transfers between devices with their start and end apart: 15 -> 16, of which waited for: 4 -> 6; matrix products, arithmetic and copies ran while one was open for 0% -> 1% of each run, Pallas kernels for 23% -> 24%
where the time goes in v14:
time: 179 us; the launch traced here: 178 us
  blocking collectives  65.3 us (36%)
  Pallas kernels  55.4 us (31%)
  waiting for transfers between devices  23.7 us (13%)
  starting transfers between devices  22.8 us (13%)
  local copies, waits for them, and re-layouts  7.09 us (4%)
  other arithmetic  2.59 us (1%)
    all_to_all x1, blocking collectives, body(): lax.all_to_all(outgoing, BOTH, split_axis=0, concat_axis=0, tiled=True)  65.3 us
    pallas_call x5, Pallas kernels, trailing(): pl.pallas_call(functools.partial(trailing_kernel, first, len(pieces), hal...  42 us
    ppermute x1, waiting for transfers between devices, exchange(): far = lax.ppermute(mine, 'col', [(c, c ^ 2) for c in range(n_col)])  14.4 us
    ppermute x4, starting transfers between devices, body(): arrived.append(lax.ppermute(part, BOTH, pairs))  7.86 us
    pallas_call x1, Pallas kernels, row_panels(): pl.pallas_call(row_panels_kernel, grid_spec=pltpu.PrefetchScalarGridSpec(...  7.49 us
    unnamed x30, local copies, waits for them, and re-layouts  7.04 us
    ppermute x4, waiting for transfers between devices, body(): arrived.append(lax.ppermute(part, BOTH, pairs))  6.18 us
    ppermute x3, starting transfers between devices, body(): behind = lax.ppermute(behind, 'row', down)  4.51 us
  transfers between devices with their start and end apart: 16, of which 6 were waited for; matrix products, arithmetic and copies ran while one was open for 1% of the time, Pallas kernels for 24%

profile of v14, /device:TPU:0, one launch (start us, length us, event | category | flops | bytes accessed | tf_op | source)
XLA Modules:
  0.0 177.9 jit_solution(14745337901901947943)
XLA Ops:
  0.7 0.7 pad_add_fusion.place
  1.3 3.9 %pack.1 = f32[32,152,128]{2,1,0:T(8,128)} custom-call(s32[4]{0:T(128)} %pad_add_fusion.place, s32[16]{0:T(128)} %bitcast.13, s32[16]{0:T(128)} %slot.1, s32[1]{0:T(128)S(6)} %copy.19.count, f32[16,128,128]{2,1,0:T(8,128)} %child_ref.1, f32[12,1,24,1,128,128]{5,4,3,2,1,0:T(8,128)} %rest_2_.7), custom_call_target="tpu_custom_call" | custom-call | tf_op jit(solution)/shard_map/pack/pallas_call | solution.py:122
  5.3 0.0 copy-start.6
  5.3 0.0 copy-start.7
  5.3 65.3 %all_to_all.10.incoming_ref.rest_3_.rest_2_ = f32[32,152,128]{2,1,0:T(8,128)S(1)} all-to-all(f32[32,152,128]{2,1,0:T(8,128)} %pack.1), channel_id=1, replica_groups=mesh['row'=8,'col'=4] {'row','col'}, dimensions={0} | all-to-all | bytes 4980736 | tf_op jit(solution)/shard_map/all_to_all | solution.py:484
  70.6 0.7 fusion.slot_in
  71.3 0.0 copy-done.5
  71.3 2.0 %panel_columns.1 = (f32[12,128,128]{2,1,0:T(8,128)S(1)}, f32[32,16,128]{2,1,0:T(8,128)S(1)}, f32[3,128,128]{2,1,0:T(8,128)S(1)}, f32[3,128,128]{2,1,0:T(8,128)S(...) custom-call(s32[4]{0:T(128)S(1)} %copy-done.5, s32[32]{0:T(128)S(1)} %fusion.slot_in, ...), custom_call_target="tpu_custom_call" | custom-call | tf_op jit(solution)/shard_map/panel_columns/pallas_call | solution.py:181
  73.3 0.0 copy-start.4
  73.3 0.7 copy-done.4
  74.0 0.7 copy-done.8
  74.7 0.7 copy-done.9
  75.4 0.7 copy-done.10
  76.0 0.7 copy-done.11
  76.7 2.8 %all-to-all-start.1 = ((f32[32,16,128]{2,1,0:T(8,128)}), f32[32,16,128]{2,1,0:T(8,128)S(1)}, u32[]{:S(2)}, u32[]{:S(2)}) async-start(f32[32,16,128]{2,1,0:T(8,128)} %copy-done.4), calls=%async_computation.1 | async-start | bytes 524288 | tf_op jit(solution)/shard_map/all_to_all | solution.py:489
  79.5 1.6 collective-permute-start
  81.1 2.3 %collective-permute-start.1 = (f32[3,128,128]{2,1,0:T(8,128)}, f32[3,128,128]{2,1,0:T(8,128)S(1)}, u32[]{:S(2)}, u32[]{:S(2)}) collective-permute-start(f32[3,128,128]{2,1,0:T(8,128)} %copy-done.10), channel_id=1, source_target_pairs={{0,4},{1,8},{2,12},{3,0},{4,5},{5,9},{6,13},{7,1},{8,6},{9,10},{10... | collective-permute-start | bytes 589832 | tf_op jit(solution)/shard_map/ppermute | solution.py:537
  83.4 3.5 %collective-permute-start.2 = (f32[3,128,128]{2,1,0:T(8,128)}, f32[3,128,128]{2,1,0:T(8,128)S(1)}, u32[]{:S(2)}, u32[]{:S(2)}) collective-permute-start(f32[3,128,128]{2,1,0:T(8,128)} %copy-done.9), channel_id=1, source_target_pairs={{0,8},{1,12},{2,0},{3,4},{4,9},{5,13},{6,1},{7,5},{8,10},{9,14},{1... | collective-permute-start | bytes 589832 | tf_op jit(solution)/shard_map/ppermute | solution.py:537
  86.8 0.5 collective-permute-start.3
  87.4 0.0 collective-permute-done
  87.4 5.8 %collective-permute-done.1 = f32[3,128,128]{2,1,0:T(8,128)S(1)} collective-permute-done((f32[3,128,128]{2,1,0:T(8,128)}, f32[3,128,128]{2,1,0:T(8,128)S(1)}, u32[]{:S(2)}, u32[]{:S(2)}) %collective-permute-start.1) | collective-permute-done | bytes 196640 | tf_op jit(solution)/shard_map/ppermute | solution.py:537
  93.1 0.4 collective-permute-done.2
  93.6 0.0 copy-done.12
  93.6 0.2 copy-done.13
  93.8 0.7 copy-done.14
  94.5 0.0 collective-permute-done.3
  94.5 0.0 all-to-all-done.1
  94.5 3.4 %collective-permute-start.9 = (f32[12,128,128]{2,1,0:T(8,128)S(1)}, f32[12,128,128]{2,1,0:T(8,128)S(1)}, u32[]{:S(2)}, u32[]{:S(2)}) collective-permute-start(f32[12,128,128]{2,1,0:T(8,128)S(1)} %get-tuple-element.39.t0), channel_id=1, source_target_pairs={{0,2},{1,3},{2,0},{3,1},{4,6},{5,7},{6,4},{7,5},{8,10},{9,11},{10,... | collective-permute-start | bytes 2359304 | tf_op jit(solution)/shard_map/ppermute | solution.py:494
  97.9 1.3 pad_maximum_fusion.rest_0_
  99.2 0.1 collective-permute-start.4
  99.3 2.5 %collective-permute-start.6 = (f32[4,3,128,128]{3,2,1,0:T(8,128)S(1)}, f32[4,3,128,128]{3,2,1,0:T(8,128)S(1)}, u32[]{:S(2)}, u32[]{:S(2)}) collective-permute-start(f32[4,3,128,128]{3,2,1,0:T(8,128)S(1)} %pad_maximum_fusion.rest_0_), channel_id=1, source_target_pairs={{8,0},{16,8},{24,16},{28,24},{20,28},{12,20},{4,12},{0,4},{9,1},{1... | collective-permute-start | bytes 2359304 | tf_op jit(solution)/shard_map/ppermute | solution.py:547
  101.8 0.0 collective-permute-start.8
  101.8 14.4 %collective-permute-done.9.t2 = f32[12,128,128]{2,1,0:T(8,128)S(1)} collective-permute-done((f32[12,128,128]{2,1,0:T(8,128)S(1)}, f32[12,128,128]{2,1,0:T(8,128)S(1)}, u32[]{:S(2)}, u32[]{:S(2)}) %collective-permute-start.9) | collective-permute-done | bytes 786464 | tf_op jit(solution)/shard_map/ppermute | solution.py:494
  116.2 0.2 collective-permute-start.10
  116.5 2.6 %collective-permute-done.4.rest_1_ = f32[4,3,128,128]{3,2,1,0:T(8,128)S(1)} collective-permute-done((f32[4,3,128,128]{3,2,1,0:T(8,128)S(1)}, f32[4,3,128,128]{3,2,1,0:T(8,128)S(1)}, u32[]{:S(2)}, u32[]{:S(2)}) %collective-permute-start.4) | collective-permute-done | bytes 786464 | tf_op jit(solution)/shard_map/ppermute | solution.py:546
  119.0 0.4 collective-permute-start.5
  119.4 0.4 collective-permute-done.6.rest_0_
  119.7 1.3 collective-permute-start.7
  121.0 0.0 collective-permute-done.8.t1
  121.0 0.0 collective-permute-done.10.t3
  121.1 1.0 copy-done.3
  122.1 7.5 %row_panels.1 = (bf16[1536,1024]{1,0:T(8,128)(2,1)S(1)}, f32[12,1,24,1,128,128]{5,4,3,2,1,0:T(8,128)}, bf16[3,256,768]{2,1,0:T(8,128)(2,1)S(1)}, s32[64]{0:T(128)S(1)}, s32[25]{0:T(128)S(1)}) custom-call(s32[4]{0:T(128)S(1)} %copy-done.5, s32[32]{0:T(128)S(1)} %fusion.slot_in, f32[12,128,128]{2,1,0:T(8,128)S(1)} %get-tuple-element.39.t0, ...), custom_call_target="tpu_custom_call" | custom-call | tf_op jit(solution)/shard_map/row_panels/pallas_call | solution.py:286
  129.6 1.6 copy-done
  131.2 0.0 copy-done.6
  131.2 0.0 copy-done.7
  131.2 9.5 %trailing.5.rest_4_ = f32[12,1,24,1,128,128]{5,4,3,2,1,0:T(8,128)} custom-call(s32[4]{0:T(128)S(1)} %copy-done.5, s32[192]{0:T(256)S(1)} %copy-done.6, s32[256]{0:T(256)S(1)} %copy-done.7, s32[64]{0:T(128)S(1)} %get-tuple-element.46.order, s32[25]{0:T(128)S(1)} %get-tuple-element.47.starts, ...), custom_call_target="tpu_custom_call", output_to_operand_aliasing={{}: (11, {})} | custom-call | flops 9663676416 | bytes 9437184 | tf_op jit(solution)/shard_map/trailing/pallas_call | solution.py:444
  140.7 0.0 copy-start.1
  140.7 0.0 collective-permute-done.5.rest_1_
  140.7 0.0 collective-permute-done.7.rest_0_
  140.7 1.4 collective-permute-start.11
  142.1 0.7 collective-permute-start.13
  142.8 10.0 %trailing.6.rest_3_ = f32[12,1,24,1,128,128]{5,4,3,2,1,0:T(8,128)} custom-call(s32[4]{0:T(128)S(1)} %copy-done.5, s32[192]{0:T(256)S(1)} %copy-done.6, s32[256]{0:T(256)S(1)} %copy-done.7, s32[64]{0:T(128)S(1)} %get-tuple-element.46.order, s32[25]{0:T(128)S(1)} %get-tuple-element.47.starts, ...), custom_call_target="tpu_custom_call", output_to_operand_aliasing={{}: (11, {})} | custom-call | flops 9663676416 | bytes 9437184 | tf_op jit(solution)/shard_map/trailing/pallas_call | solution.py:444
  152.8 0.0 copy-done.1
  152.8 6.1 %trailing.7.rest_4_ = f32[12,1,24,1,128,128]{5,4,3,2,1,0:T(8,128)} custom-call(s32[4]{0:T(128)S(1)} %copy-done.5, s32[192]{0:T(256)S(1)} %copy-done.6, s32[256]{0:T(256)S(1)} %copy-done.7, s32[64]{0:T(128)S(1)} %get-tuple-element.46.order, s32[25]{0:T(128)S(1)} %get-tuple-element.47.starts, ...), custom_call_target="tpu_custom_call", output_to_operand_aliasing={{}: (10, {})} | custom-call | flops 4831838208 | bytes 4718592 | tf_op jit(solution)/shard_map/trailing/pallas_call | solution.py:444
  158.9 0.1 collective-permute-done.11.rest_0_
  159.1 2.0 %collective-permute-start.12 = (f32[2,3,128,128]{3,2,1,0:T(8,128)S(1)}, f32[2,3,128,128]{3,2,1,0:T(8,128)S(1)}, u32[]{:S(2)}, u32[]{:S(2)}) collective-permute-start(f32[2,3,128,128]{3,2,1,0:T(8,128)S(1)} %slice.13), channel_id=1, source_target_pairs={{0,8},{8,16},{16,24},{24,28},{28,20},{20,12},{12,4},{4,0},{1,9},{9... | collective-permute-start | bytes 1179656 | tf_op jit(solution)/shard_map/ppermute | solution.py:552
  161.1 0.0 collective-permute-done.13.rest_1_
  161.1 0.0 copy-start.2
  161.1 0.1 collective-permute-start.14
  161.2 10.3 %trailing.8.rest_4_ = f32[12,1,24,1,128,128]{5,4,3,2,1,0:T(8,128)} custom-call(s32[4]{0:T(128)S(1)} %copy-done.5, s32[192]{0:T(256)S(1)} %copy-done.6, s32[256]{0:T(256)S(1)} %copy-done.7, s32[64]{0:T(128)S(1)} %get-tuple-element.46.order, s32[25]{0:T(128)S(1)} %get-tuple-element.47.starts, ...), custom_call_target="tpu_custom_call", output_to_operand_aliasing={{}: (11, {})} | custom-call | flops 9663676416 | bytes 9437184 | tf_op jit(solution)/shard_map/trailing/pallas_call | solution.py:444
  171.5 0.0 collective-permute-done.12.rest_0_
  171.6 0.0 collective-permute-done.14.rest_1_
  171.6 0.0 copy-done.2
  171.6 6.1 %trailing.9 = f32[12,1,24,1,128,128]{5,4,3,2,1,0:T(8,128)} custom-call(s32[4]{0:T(128)S(1)} %copy-done.5, s32[192]{0:T(256)S(1)} %copy-done.6, s32[256]{0:T(256)S(1)} %copy-done.7, s32[64]{0:T(128)S(1)} %get-tuple-element.46.order, s32[25]{0:T(128)S(1)} %get-tuple-element.47.starts, ...), custom_call_target="tpu_custom_call", output_to_operand_aliasing={{}: (11, {})} | custom-call | flops 4831838208 | bytes 4718592 | tf_op jit(solution)/shard_map/trailing/pallas_call | solution.py:444
  (12 shorter events, 0.1 us)
Async XLA Ops:
  1.3 70.0 %copy-start.5 = (s32[4]{0:T(128)S(1)}, s32[4]{0:T(128)}, u32[]{:S(2)}) copy-start(s32[4]{0:T(128)} %pad_add_fusion.place) | copy-start | bytes 52
  5.3 126.0 %copy-start.6 = (s32[192]{0:T(256)S(1)}, s32[192]{0:T(256)}, u32[]{:S(2)}) copy-start(s32[192]{0:T(256)} %constant.17.clone.columns_table) | copy-start | bytes 2308
  5.3 126.0 %copy-start.7 = (s32[256]{0:T(256)S(1)}, s32[256]{0:T(256)}, u32[]{:S(2)}) copy-start(s32[256]{0:T(256)} %constant.18.clone.places_table) | copy-start | bytes 3076
  73.3 0.7 copy-start.4
  74.0 0.7 copy-start.8
  74.7 0.7 copy-start.9
  75.4 0.7 copy-start.10
  76.0 0.7 copy-start.11
  76.7 17.8 %all-to-all-start.1 = ((f32[32,16,128]{2,1,0:T(8,128)}), f32[32,16,128]{2,1,0:T(8,128)S(1)}, u32[]{:S(2)}, u32[]{:S(2)}) async-start(f32[32,16,128]{2,1,0:T(8,128)} %copy-done.4), calls=%async_computation.1 | async-start | bytes 524288 | tf_op jit(solution)/shard_map/all_to_all | solution.py:489
  79.5 7.9 %collective-permute-start = (f32[3,128,128]{2,1,0:T(8,128)}, f32[3,128,128]{2,1,0:T(8,128)S(1)}, u32[]{:S(2)}, u32[]{:S(2)}) collective-permute-start(f32[3,128,128]{2,1,0:T(8,128)} %copy-done.11), channel_id=1, source_target_pairs={{0,0},{1,4},{2,8},{3,12},{4,1},{5,5},{6,9},{7,13},{8,2},{9,6},{10,... | collective-permute-start | bytes 589832 | tf_op jit(solution)/shard_map/ppermute | solution.py:537
  81.1 12.0 %collective-permute-start.1 = (f32[3,128,128]{2,1,0:T(8,128)}, f32[3,128,128]{2,1,0:T(8,128)S(1)}, u32[]{:S(2)}, u32[]{:S(2)}) collective-permute-start(f32[3,128,128]{2,1,0:T(8,128)} %copy-done.10), channel_id=1, source_target_pairs={{0,4},{1,8},{2,12},{3,0},{4,5},{5,9},{6,13},{7,1},{8,6},{9,10},{10... | collective-permute-start | bytes 589832 | tf_op jit(solution)/shard_map/ppermute | solution.py:537
  83.4 10.2 %collective-permute-start.2 = (f32[3,128,128]{2,1,0:T(8,128)}, f32[3,128,128]{2,1,0:T(8,128)S(1)}, u32[]{:S(2)}, u32[]{:S(2)}) collective-permute-start(f32[3,128,128]{2,1,0:T(8,128)} %copy-done.9), channel_id=1, source_target_pairs={{0,8},{1,12},{2,0},{3,4},{4,9},{5,13},{6,1},{7,5},{8,10},{9,14},{1... | collective-permute-start | bytes 589832 | tf_op jit(solution)/shard_map/ppermute | solution.py:537
  86.8 7.6 %collective-permute-start.3 = (f32[3,128,128]{2,1,0:T(8,128)}, f32[3,128,128]{2,1,0:T(8,128)}, u32[]{:S(2)}, u32[]{:S(2)}) collective-permute-start(f32[3,128,128]{2,1,0:T(8,128)} %copy-done.8), channel_id=1, source_target_pairs={{0,12},{1,0},{2,4},{3,8},{4,13},{5,1},{6,5},{7,9},{8,14},{9,2},{10... | collective-permute-start | bytes 589832 | tf_op jit(solution)/shard_map/ppermute | solution.py:537
  87.4 6.2 %copy-start.12 = (f32[3,128,128]{2,1,0:T(8,128)}, f32[3,128,128]{2,1,0:T(8,128)S(1)}, u32[]{:S(2)}) copy-start(f32[3,128,128]{2,1,0:T(8,128)S(1)} %collective-permute-done) | copy-start | bytes 589828
  93.1 0.7 copy-start.13
  93.8 0.7 copy-start.14
  94.5 21.7 %collective-permute-start.9 = (f32[12,128,128]{2,1,0:T(8,128)S(1)}, f32[12,128,128]{2,1,0:T(8,128)S(1)}, u32[]{:S(2)}, u32[]{:S(2)}) collective-permute-start(f32[12,128,128]{2,1,0:T(8,128)S(1)} %get-tuple-element.39.t0), channel_id=1, source_target_pairs={{0,2},{1,3},{2,0},{3,1},{4,6},{5,7},{6,4},{7,5},{8,10},{9,11},{10,... | collective-permute-start | bytes 2359304 | tf_op jit(solution)/shard_map/ppermute | solution.py:494
  99.2 19.8 %collective-permute-start.4 = (f32[4,3,128,128]{3,2,1,0:T(8,128)S(1)}, f32[4,3,128,128]{3,2,1,0:T(8,128)S(1)}, u32[]{:S(2)}, u32[]{:S(2)}) collective-permute-start(f32[4,3,128,128]{3,2,1,0:T(8,128)S(1)} %pad_maximum_fusion.rest_0_), channel_id=1, source_target_pairs={{0,8},{8,16},{16,24},{24,28},{28,20},{20,12},{12,4},{4,0},{1,9},{9... | collective-permute-start | bytes 2359304 | tf_op jit(solution)/shard_map/ppermute | solution.py:546
  99.3 20.4 %collective-permute-start.6 = (f32[4,3,128,128]{3,2,1,0:T(8,128)S(1)}, f32[4,3,128,128]{3,2,1,0:T(8,128)S(1)}, u32[]{:S(2)}, u32[]{:S(2)}) collective-permute-start(f32[4,3,128,128]{3,2,1,0:T(8,128)S(1)} %pad_maximum_fusion.rest_0_), channel_id=1, source_target_pairs={{8,0},{16,8},{24,16},{28,24},{20,28},{12,20},{4,12},{0,4},{9,1},{1... | collective-permute-start | bytes 2359304 | tf_op jit(solution)/shard_map/ppermute | solution.py:547
  101.8 19.3 %collective-permute-start.8 = (f32[12,128,128]{2,1,0:T(8,128)S(1)}, f32[12,128,128]{2,1,0:T(8,128)S(1)}, u32[]{:S(2)}, u32[]{:S(2)}) collective-permute-start(f32[12,128,128]{2,1,0:T(8,128)S(1)} %get-tuple-element.39.t0), channel_id=1, source_target_pairs={{0,1},{1,0},{2,3},{3,2},{4,5},{5,4},{6,7},{7,6},{8,9},{9,8},{10,11... | collective-permute-start | bytes 2359304 | tf_op jit(solution)/shard_map/ppermute | solution.py:493
  116.2 4.8 %collective-permute-start.10 = (f32[12,128,128]{2,1,0:T(8,128)S(1)}, f32[12,128,128]{2,1,0:T(8,128)S(1)}, u32[]{:S(2)}, u32[]{:S(2)}) collective-permute-start(f32[12,128,128]{2,1,0:T(8,128)S(1)} %collective-permute-done.9.t2), channel_id=1, source_target_pairs={{0,1},{1,0},{2,3},{3,2},{4,5},{5,4},{6,7},{7,6},{8,9},{9,8},{10,11... | collective-permute-start | bytes 2359304 | tf_op jit(solution)/shard_map/ppermute | solution.py:495
  119.0 21.7 %collective-permute-start.5 = (f32[4,3,128,128]{3,2,1,0:T(8,128)S(1)}, f32[4,3,128,128]{3,2,1,0:T(8,128)S(1)}, u32[]{:S(2)}, u32[]{:S(2)}) collective-permute-start(f32[4,3,128,128]{3,2,1,0:T(8,128)S(1)} %collective-permute-done.4.rest_1_), channel_id=1, source_target_pairs={{0,8},{8,16},{16,24},{24,28},{28,20},{20,12},{12,4},{4,0},{1,9},{9... | collective-permute-start | bytes 2359304 | tf_op jit(solution)/shard_map/ppermute | solution.py:546
  119.7 21.0 %collective-permute-start.7 = (f32[4,3,128,128]{3,2,1,0:T(8,128)S(1)}, f32[4,3,128,128]{3,2,1,0:T(8,128)S(1)}, u32[]{:S(2)}, u32[]{:S(2)}) collective-permute-start(f32[4,3,128,128]{3,2,1,0:T(8,128)S(1)} %collective-permute-done.6.rest_0_), channel_id=1, source_target_pairs={{8,0},{16,8},{24,16},{28,24},{20,28},{12,20},{4,12},{0,4},{9,1},{1... | collective-permute-start | bytes 2359304 | tf_op jit(solution)/shard_map/ppermute | solution.py:547
  121.0 1.0 copy-start.3
  129.6 1.6 copy-start
  140.7 12.1 %copy-start.1 = (bf16[1536,1024]{1,0:T(8,128)(2,1)S(1)}, bf16[1536,1024]{1,0:T(8,128)(2,1)}, u32[]{:S(2)}) copy-start(bf16[1536,1024]{1,0:T(8,128)(2,1)} %copy-done) | copy-start | bytes 9437188
  140.7 18.3 %collective-permute-start.11 = (f32[4,3,128,128]{3,2,1,0:T(8,128)S(1)}, f32[4,3,128,128]{3,2,1,0:T(8,128)S(1)}, u32[]{:S(2)}, u32[]{:S(2)}) collective-permute-start(f32[4,3,128,128]{3,2,1,0:T(8,128)S(1)} %collective-permute-done.5.rest_1_), channel_id=1, source_target_pairs={{0,8},{8,16},{16,24},{24,28},{28,20},{20,12},{12,4},{4,0},{1,9},{9... | collective-permute-start | bytes 2359304 | tf_op jit(solution)/shard_map/ppermute | solution.py:546
  142.1 18.9 %collective-permute-start.13 = (f32[4,3,128,128]{3,2,1,0:T(8,128)S(1)}, f32[4,3,128,128]{3,2,1,0:T(8,128)S(1)}, u32[]{:S(2)}, u32[]{:S(2)}) collective-permute-start(f32[4,3,128,128]{3,2,1,0:T(8,128)S(1)} %collective-permute-done.7.rest_0_), channel_id=1, source_target_pairs={{8,0},{16,8},{24,16},{28,24},{20,28},{12,20},{4,12},{0,4},{9,1},{1... | collective-permute-start | bytes 2359304 | tf_op jit(solution)/shard_map/ppermute | solution.py:547
  159.1 12.5 %collective-permute-start.12 = (f32[2,3,128,128]{3,2,1,0:T(8,128)S(1)}, f32[2,3,128,128]{3,2,1,0:T(8,128)S(1)}, u32[]{:S(2)}, u32[]{:S(2)}) collective-permute-start(f32[2,3,128,128]{3,2,1,0:T(8,128)S(1)} %slice.13), channel_id=1, source_target_pairs={{0,8},{8,16},{16,24},{24,28},{28,20},{20,12},{12,4},{4,0},{1,9},{9... | collective-permute-start | bytes 1179656 | tf_op jit(solution)/shard_map/ppermute | solution.py:552
  161.1 10.5 %copy-start.2 = (bf16[1536,1024]{1,0:T(8,128)(2,1)S(1)}, bf16[1536,1024]{1,0:T(8,128)(2,1)}, u32[]{:S(2)}) copy-start(bf16[1536,1024]{1,0:T(8,128)(2,1)} %copy-done) | copy-start | bytes 9437188
  161.1 10.5 %collective-permute-start.14 = (f32[2,3,128,128]{3,2,1,0:T(8,128)S(1)}, f32[2,3,128,128]{3,2,1,0:T(8,128)S(1)}, u32[]{:S(2)}, u32[]{:S(2)}) collective-permute-start(f32[2,3,128,128]{3,2,1,0:T(8,128)S(1)} %slice.14), channel_id=1, source_target_pairs={{8,0},{16,8},{24,16},{28,24},{20,28},{12,20},{4,12},{0,4},{9,1},{1... | collective-permute-start | bytes 1179656 | tf_op jit(solution)/shard_map/ppermute | solution.py:552

commit v15 on v14

--- a/solution.py
+++ b/solution.py
@@ -60,7 +60,7 @@
 
 def pack_kernel(
     owners, place, dest, slot, count, child_ref, front_ref, out_ref, held_ref, notes_ref,
-    lead_ref, tile_ref, in_sems, out_sems, sem,
+    lead_ref, tile_ref, in_sems, out_sems, sem, lead_sem,
 ):
     n_slices, height, _ = lead_ref.shape
     each = n_slices // 4
@@ -74,19 +74,20 @@
             held_ref.at[k], out_ref.at[dest[k], pl.ds(0, TILE)], out_sems.at[k]
         )
 
+    own = pltpu.make_async_copy(front_ref.at[0, 0, 0, 0], tile_ref, sem)
+    own.start()
+
     @pl.loop(0, live)
     def _(k):
         arrive(k).start()
 
     notes_ref[...] = jnp.full_like(notes_ref, -1.0)
     lead_ref[...] = jnp.zeros_like(lead_ref)
+    own.wait()
     for i, owner in enumerate(owners):
 
         @pl.when(place[3] == owner)
         def _():
-            own = pltpu.make_async_copy(front_ref.at[0, 0, 0, 0], tile_ref, sem)
-            own.start()
-            own.wait()
             lead_ref[i * each : (i + 1) * each] = tile_ref[...].reshape(each, height, TILE)
 
     @pl.loop(0, live)
@@ -103,11 +104,11 @@
 
     notes = pltpu.make_async_copy(notes_ref, out_ref.at[:, pl.ds(TILE, NOTE)], sem)
     notes.start()
-    notes.wait()
     lead = pltpu.make_async_copy(
-        lead_ref, out_ref.at[pl.ds(0, n_slices), pl.ds(TILE + NOTE, height)], sem
+        lead_ref, out_ref.at[pl.ds(0, n_slices), pl.ds(TILE + NOTE, height)], lead_sem
     )
     lead.start()
+    notes.wait()
     lead.wait()
 
     @pl.loop(0, live)
@@ -130,6 +131,7 @@
             pltpu.VMEM((TILE, TILE), jnp.float32),
             pltpu.SemaphoreType.DMA((slots,)),
             pltpu.SemaphoreType.DMA((slots,)),
+            pltpu.SemaphoreType.DMA,
             pltpu.SemaphoreType.DMA,
         ],
         out_shape=jax.ShapeDtypeStruct((devices, TILE + NOTE + height, TILE), jnp.float32),
@@ -408,7 +410,8 @@
         block = rows // 3
         for m in range(3):
             left = pair_ref[m * block * TILE : (m + 1) * block * TILE]
-            update = dot(jnp.concatenate([left, left[:, :WIDTH]], axis=1), right_ref[:, lanes])
+            update = dot(left, right_ref[: 2 * WIDTH, lanes])
+            update = update + dot(left[:, :WIDTH], right_ref[2 * WIDTH :, lanes])
             span = slice(m * block, (m + 1) * block)
             for j in range(2):
                 part = update[:, j * TILE : (j + 1) * TILE].reshape(block, TILE, TILE)
@@ -546,13 +549,12 @@
             ahead = lax.ppermute(ahead, "row", up)
             behind = lax.ppermute(behind, "row", down)
             if step == 2:
-                panels = updated([(piece, 0), rounds[1][0]], panels, 0)
+                panels = updated(rounds[0], panels, 0)
                 ahead, behind, panels = lax.optimization_barrier((ahead, behind, panels))
             rounds.append([(ahead, -step), (behind, step)])
         last = [lax.ppermute(ahead[:2], "row", up), lax.ppermute(behind[2:], "row", down)]
-        late = [entry for entries in rounds for entry in entries][2:]
-        rounds = [late[:2], late[2:3], *rounds[3:], [(last, n_row // 2)]]
-        first = 2
+        rounds = [*rounds[1:], [(last, n_row // 2)]]
+        first = 1
 
     else:
         pairs = [

time: 179 us -> 180 us (level)
  waiting for transfers between devices: 23.7 us -> 27.3 us
    ppermute x3, waiting for transfers between devices: 0.37 us -> 2.52 us  [body(): behind = lax.ppermute(behind, 'row', down)]
    unnamed x30 -> x28, local copies, waits for them, and re-layouts: 7.04 us -> 5.55 us
  transfers between devices with their start and end apart: 16 -> 16, of which waited for: 6 -> 7; matrix products, arithmetic and copies ran while one was open for 1% -> 1% of each run, Pallas kernels for 24% -> 24%
where the time goes in v15:
time: 180 us; the launch traced here: 179 us
  blocking collectives  65.6 us (36%)
  Pallas kernels  55.3 us (31%)
  waiting for transfers between devices  27.3 us (15%)
  starting transfers between devices  22 us (12%)
  local copies, waits for them, and re-layouts  5.61 us (3%)
  other arithmetic  2.51 us (1%)
    all_to_all x1, blocking collectives, body(): lax.all_to_all(outgoing, BOTH, split_axis=0, concat_axis=0, tiled=True)  65.6 us
    pallas_call x5, Pallas kernels, trailing(): pl.pallas_call(functools.partial(trailing_kernel, first, len(pieces), hal...  42.1 us
    ppermute x1, waiting for transfers between devices, exchange(): far = lax.ppermute(mine, 'col', [(c, c ^ 2) for c in range(n_col)])  14.6 us
    ppermute x4, starting transfers between devices, body(): arrived.append(lax.ppermute(part, BOTH, pairs))  7.77 us
    pallas_call x1, Pallas kernels, row_panels(): pl.pallas_call(row_panels_kernel, grid_spec=pltpu.PrefetchScalarGridSpec(...  7.48 us
    ppermute x4, waiting for transfers between devices, body(): arrived.append(lax.ppermute(part, BOTH, pairs))  6.31 us
    unnamed x28, local copies, waits for them, and re-layouts  5.55 us
    ppermute x3, starting transfers between devices, body(): behind = lax.ppermute(behind, 'row', down)  5.14 us
  transfers between devices with their start and end apart: 16, of which 7 were waited for; matrix products, arithmetic and copies ran while one was open for 1% of the time, Pallas kernels for 24%

profile of v15, /device:TPU:0, one launch (start us, length us, event | category | flops | bytes accessed | tf_op | source)
XLA Modules:
  0.0 179.4 jit_solution(13219060192007051246)
XLA Ops:
  0.7 0.6 pad_add_fusion.place
  1.2 0.0 copy-start.4
  1.2 3.2 %pack.1 = f32[32,152,128]{2,1,0:T(8,128)} custom-call(s32[4]{0:T(128)} %pad_add_fusion.place, s32[16]{0:T(128)} %bitcast.13, s32[16]{0:T(128)} %slot.1, s32[1]{0:T(128)S(6)} %copy.19.count, f32[16,128,128]{2,1,0:T(8,128)} %child_ref.1, f32[12,1,24,1,128,128]{5,4,3,2,1,0:T(8,128)} %rest_2_.7), custom_call_target="tpu_custom_call" | custom-call | tf_op jit(solution)/shard_map/pack/pallas_call | solution.py:123
  4.5 0.0 copy-start.5
  4.5 0.0 copy-start.6
  4.5 65.6 %all_to_all.10.incoming_ref.rest_2_.rest_3_ = f32[32,152,128]{2,1,0:T(8,128)S(1)} all-to-all(f32[32,152,128]{2,1,0:T(8,128)} %pack.1), channel_id=1, replica_groups=mesh['row'=8,'col'=4] {'row','col'}, dimensions={0} | all-to-all | bytes 4980736 | tf_op jit(solution)/shard_map/all_to_all | solution.py:487
  70.1 0.7 fusion.slot_in
  70.7 0.0 copy-done.4
  70.7 2.5 %panel_columns.1 = (f32[12,128,128]{2,1,0:T(8,128)S(1)}, f32[32,16,128]{2,1,0:T(8,128)S(1)}, f32[3,128,128]{2,1,0:T(8,128)S(1)}, f32[3,128,128]{2,1,0:T(8,128)S(...) custom-call(s32[4]{0:T(128)S(1)} %copy-done.4, s32[32]{0:T(128)S(1)} %fusion.slot_in, ...), custom_call_target="tpu_custom_call" | custom-call | tf_op jit(solution)/shard_map/panel_columns/pallas_call | solution.py:183
  73.2 0.0 copy-start.3
  73.3 0.7 copy-done.3
  74.0 0.0 copy-start.7
  74.0 0.7 copy-done.7
  74.6 0.7 copy-done.8
  75.3 0.7 copy-done.9
  76.0 0.7 copy-done.10
  76.7 2.6 %all-to-all-start.1 = ((f32[32,16,128]{2,1,0:T(8,128)}), f32[32,16,128]{2,1,0:T(8,128)S(1)}, u32[]{:S(2)}, u32[]{:S(2)}) async-start(f32[32,16,128]{2,1,0:T(8,128)} %copy-done.3), calls=%async_computation.1 | async-start | bytes 524288 | tf_op jit(solution)/shard_map/all_to_all | solution.py:492
  79.3 1.6 collective-permute-start
  80.9 2.1 %collective-permute-start.1 = (f32[3,128,128]{2,1,0:T(8,128)}, f32[3,128,128]{2,1,0:T(8,128)S(1)}, u32[]{:S(2)}, u32[]{:S(2)}) collective-permute-start(f32[3,128,128]{2,1,0:T(8,128)} %copy-done.9), channel_id=1, source_target_pairs={{0,4},{1,8},{2,12},{3,0},{4,5},{5,9},{6,13},{7,1},{8,6},{9,10},{10... | collective-permute-start | bytes 589832 | tf_op jit(solution)/shard_map/ppermute | solution.py:540
  83.0 3.5 %collective-permute-start.2 = (f32[3,128,128]{2,1,0:T(8,128)}, f32[3,128,128]{2,1,0:T(8,128)S(1)}, u32[]{:S(2)}, u32[]{:S(2)}) collective-permute-start(f32[3,128,128]{2,1,0:T(8,128)} %copy-done.8), channel_id=1, source_target_pairs={{0,8},{1,12},{2,0},{3,4},{4,9},{5,13},{6,1},{7,5},{8,10},{9,14},{1... | collective-permute-start | bytes 589832 | tf_op jit(solution)/shard_map/ppermute | solution.py:540
  86.5 0.5 collective-permute-start.3
  87.0 0.0 collective-permute-done
  87.1 6.0 %collective-permute-done.1 = f32[3,128,128]{2,1,0:T(8,128)S(1)} collective-permute-done((f32[3,128,128]{2,1,0:T(8,128)}, f32[3,128,128]{2,1,0:T(8,128)S(1)}, u32[]{:S(2)}, u32[]{:S(2)}) %collective-permute-start.1) | collective-permute-done | bytes 196640 | tf_op jit(solution)/shard_map/ppermute | solution.py:540
  93.1 0.3 collective-permute-done.2
  93.4 0.0 copy-done.11
  93.4 0.4 copy-done.12
  93.7 0.7 copy-done.13
  94.4 0.0 collective-permute-done.3
  94.4 0.0 all-to-all-done.1
  94.4 3.3 %collective-permute-start.9 = (f32[12,128,128]{2,1,0:T(8,128)S(1)}, f32[12,128,128]{2,1,0:T(8,128)S(1)}, u32[]{:S(2)}, u32[]{:S(2)}) collective-permute-start(f32[12,128,128]{2,1,0:T(8,128)S(1)} %get-tuple-element.39.t0), channel_id=1, source_target_pairs={{0,2},{1,3},{2,0},{3,1},{4,6},{5,7},{6,4},{7,5},{8,10},{9,11},{10,... | collective-permute-start | bytes 2359304 | tf_op jit(solution)/shard_map/ppermute | solution.py:497
  97.7 1.3 pad_maximum_fusion.rest_0_
  99.0 0.1 collective-permute-start.4
  99.0 2.5 %collective-permute-start.6 = (f32[4,3,128,128]{3,2,1,0:T(8,128)S(1)}, f32[4,3,128,128]{3,2,1,0:T(8,128)S(1)}, u32[]{:S(2)}, u32[]{:S(2)}) collective-permute-start(f32[4,3,128,128]{3,2,1,0:T(8,128)S(1)} %pad_maximum_fusion.rest_0_), channel_id=1, source_target_pairs={{8,0},{16,8},{24,16},{28,24},{20,28},{12,20},{4,12},{0,4},{9,1},{1... | collective-permute-start | bytes 2359304 | tf_op jit(solution)/shard_map/ppermute | solution.py:550
  101.5 0.0 collective-permute-start.8
  101.5 14.6 %collective-permute-done.9.t2 = f32[12,128,128]{2,1,0:T(8,128)S(1)} collective-permute-done((f32[12,128,128]{2,1,0:T(8,128)S(1)}, f32[12,128,128]{2,1,0:T(8,128)S(1)}, u32[]{:S(2)}, u32[]{:S(2)}) %collective-permute-start.9) | collective-permute-done | bytes 786464 | tf_op jit(solution)/shard_map/ppermute | solution.py:497
  116.1 0.1 collective-permute-start.10
  116.2 2.5 %collective-permute-done.4.rest_0_ = f32[4,3,128,128]{3,2,1,0:T(8,128)S(1)} collective-permute-done((f32[4,3,128,128]{3,2,1,0:T(8,128)S(1)}, f32[4,3,128,128]{3,2,1,0:T(8,128)S(1)}, u32[]{:S(2)}, u32[]{:S(2)}) %collective-permute-start.4) | collective-permute-done | bytes 786464 | tf_op jit(solution)/shard_map/ppermute | solution.py:549
  118.7 0.4 collective-permute-start.5
  119.1 0.5 collective-permute-done.6.rest_1_
  119.6 1.1 collective-permute-start.7
  120.7 0.0 collective-permute-done.8.t1
  120.7 0.0 collective-permute-done.10.t3
  120.7 1.0 copy-done.2
  121.8 7.5 %row_panels.1 = (bf16[1536,1024]{1,0:T(8,128)(2,1)S(1)}, f32[12,1,24,1,128,128]{5,4,3,2,1,0:T(8,128)}, bf16[3,256,768]{2,1,0:T(8,128)(2,1)S(1)}, s32[64]{0:T(128)S(1)}, s32[25]{0:T(128)S(1)}) custom-call(s32[4]{0:T(128)S(1)} %copy-done.4, s32[32]{0:T(128)S(1)} %fusion.slot_in, f32[12,128,128]{2,1,0:T(8,128)S(1)} %get-tuple-element.39.t0, ...), custom_call_target="tpu_custom_call" | custom-call | tf_op jit(solution)/shard_map/row_panels/pallas_call | solution.py:288
  129.3 0.0 copy-done.5
  129.3 0.0 copy-done.6
  129.3 6.4 %trailing.5.rest_4_ = f32[12,1,24,1,128,128]{5,4,3,2,1,0:T(8,128)} custom-call(s32[4]{0:T(128)S(1)} %copy-done.4, s32[192]{0:T(256)S(1)} %copy-done.5, s32[256]{0:T(256)S(1)} %copy-done.6, s32[64]{0:T(128)S(1)} %get-tuple-element.46.order, s32[25]{0:T(128)S(1)} %get-tuple-element.47.starts, ...), custom_call_target="tpu_custom_call", output_to_operand_aliasing={{}: (10, {})} | custom-call | flops 4831838208 | bytes 4718592 | tf_op jit(solution)/shard_map/trailing/pallas_call | solution.py:447
  135.6 0.0 copy-done
  135.6 1.5 collective-permute-done.5.rest_0_
  137.1 2.0 %collective-permute-done.7.rest_1_ = f32[4,3,128,128]{3,2,1,0:T(8,128)S(1)} collective-permute-done((f32[4,3,128,128]{3,2,1,0:T(8,128)S(1)}, f32[4,3,128,128]{3,2,1,0:T(8,128)S(1)}, u32[]{:S(2)}, u32[]{:S(2)}) %collective-permute-start.7) | collective-permute-done | bytes 786464 | tf_op jit(solution)/shard_map/ppermute | solution.py:550
  139.1 0.5 collective-permute-start.11
  139.6 1.5 collective-permute-start.13
  141.1 9.8 %trailing.6.rest_4_ = f32[12,1,24,1,128,128]{5,4,3,2,1,0:T(8,128)} custom-call(s32[4]{0:T(128)S(1)} %copy-done.4, s32[192]{0:T(256)S(1)} %copy-done.5, s32[256]{0:T(256)S(1)} %copy-done.6, s32[64]{0:T(128)S(1)} %get-tuple-element.46.order, s32[25]{0:T(128)S(1)} %get-tuple-element.47.starts, ...), custom_call_target="tpu_custom_call", output_to_operand_aliasing={{}: (11, {})} | custom-call | flops 9663676416 | bytes 9437184 | tf_op jit(solution)/shard_map/trailing/pallas_call | solution.py:447
  151.0 9.7 %trailing.7.rest_4_ = f32[12,1,24,1,128,128]{5,4,3,2,1,0:T(8,128)} custom-call(s32[4]{0:T(128)S(1)} %copy-done.4, s32[192]{0:T(256)S(1)} %copy-done.5, s32[256]{0:T(256)S(1)} %copy-done.6, s32[64]{0:T(128)S(1)} %get-tuple-element.46.order, s32[25]{0:T(128)S(1)} %get-tuple-element.47.starts, ...), custom_call_target="tpu_custom_call", output_to_operand_aliasing={{}: (11, {})} | custom-call | flops 9663676416 | bytes 9437184 | tf_op jit(solution)/shard_map/trailing/pallas_call | solution.py:447
  160.7 0.0 collective-permute-done.11.rest_0_
  160.7 0.7 collective-permute-start.12
  161.4 0.0 collective-permute-done.13.rest_1_
  161.4 0.0 copy-start.1
  161.4 1.5 collective-permute-start.14
  162.9 10.1 %trailing.8.rest_4_ = f32[12,1,24,1,128,128]{5,4,3,2,1,0:T(8,128)} custom-call(s32[4]{0:T(128)S(1)} %copy-done.4, s32[192]{0:T(256)S(1)} %copy-done.5, s32[256]{0:T(256)S(1)} %copy-done.6, s32[64]{0:T(128)S(1)} %get-tuple-element.46.order, s32[25]{0:T(128)S(1)} %get-tuple-element.47.starts, ...), custom_call_target="tpu_custom_call", output_to_operand_aliasing={{}: (11, {})} | custom-call | flops 9663676416 | bytes 9437184 | tf_op jit(solution)/shard_map/trailing/pallas_call | solution.py:447
  173.0 0.0 collective-permute-done.12.rest_0_
  173.0 0.0 collective-permute-done.14.rest_1_
  173.0 0.0 copy-done.1
  173.0 6.2 %trailing.9 = f32[12,1,24,1,128,128]{5,4,3,2,1,0:T(8,128)} custom-call(s32[4]{0:T(128)S(1)} %copy-done.4, s32[192]{0:T(256)S(1)} %copy-done.5, s32[256]{0:T(256)S(1)} %copy-done.6, s32[64]{0:T(128)S(1)} %get-tuple-element.46.order, s32[25]{0:T(128)S(1)} %get-tuple-element.47.starts, ...), custom_call_target="tpu_custom_call", output_to_operand_aliasing={{}: (11, {})} | custom-call | flops 4831838208 | bytes 4718592 | tf_op jit(solution)/shard_map/trailing/pallas_call | solution.py:447
  (10 shorter events, 0.1 us)
Async XLA Ops:
  1.2 69.5 %copy-start.4 = (s32[4]{0:T(128)S(1)}, s32[4]{0:T(128)}, u32[]{:S(2)}) copy-start(s32[4]{0:T(128)} %pad_add_fusion.place) | copy-start | bytes 52
  4.5 124.8 %copy-start.5 = (s32[192]{0:T(256)S(1)}, s32[192]{0:T(256)}, u32[]{:S(2)}) copy-start(s32[192]{0:T(256)} %constant.17.clone.columns_table) | copy-start | bytes 2308
  4.5 124.8 %copy-start.6 = (s32[256]{0:T(256)S(1)}, s32[256]{0:T(256)}, u32[]{:S(2)}) copy-start(s32[256]{0:T(256)} %constant.18.clone.places_table) | copy-start | bytes 3076
  73.2 0.7 copy-start.3
  74.0 0.7 copy-start.7
  74.6 0.7 copy-start.8
  75.3 0.7 copy-start.9
  76.0 0.7 copy-start.10
  76.7 17.7 %all-to-all-start.1 = ((f32[32,16,128]{2,1,0:T(8,128)}), f32[32,16,128]{2,1,0:T(8,128)S(1)}, u32[]{:S(2)}, u32[]{:S(2)}) async-start(f32[32,16,128]{2,1,0:T(8,128)} %copy-done.3), calls=%async_computation.1 | async-start | bytes 524288 | tf_op jit(solution)/shard_map/all_to_all | solution.py:492
  79.3 7.8 %collective-permute-start = (f32[3,128,128]{2,1,0:T(8,128)}, f32[3,128,128]{2,1,0:T(8,128)S(1)}, u32[]{:S(2)}, u32[]{:S(2)}) collective-permute-start(f32[3,128,128]{2,1,0:T(8,128)} %copy-done.10), channel_id=1, source_target_pairs={{0,0},{1,4},{2,8},{3,12},{4,1},{5,5},{6,9},{7,13},{8,2},{9,6},{10,... | collective-permute-start | bytes 589832 | tf_op jit(solution)/shard_map/ppermute | solution.py:540
  80.9 12.2 %collective-permute-start.1 = (f32[3,128,128]{2,1,0:T(8,128)}, f32[3,128,128]{2,1,0:T(8,128)S(1)}, u32[]{:S(2)}, u32[]{:S(2)}) collective-permute-start(f32[3,128,128]{2,1,0:T(8,128)} %copy-done.9), channel_id=1, source_target_pairs={{0,4},{1,8},{2,12},{3,0},{4,5},{5,9},{6,13},{7,1},{8,6},{9,10},{10... | collective-permute-start | bytes 589832 | tf_op jit(solution)/shard_map/ppermute | solution.py:540
  83.0 10.4 %collective-permute-start.2 = (f32[3,128,128]{2,1,0:T(8,128)}, f32[3,128,128]{2,1,0:T(8,128)S(1)}, u32[]{:S(2)}, u32[]{:S(2)}) collective-permute-start(f32[3,128,128]{2,1,0:T(8,128)} %copy-done.8), channel_id=1, source_target_pairs={{0,8},{1,12},{2,0},{3,4},{4,9},{5,13},{6,1},{7,5},{8,10},{9,14},{1... | collective-permute-start | bytes 589832 | tf_op jit(solution)/shard_map/ppermute | solution.py:540
  86.5 7.9 %collective-permute-start.3 = (f32[3,128,128]{2,1,0:T(8,128)}, f32[3,128,128]{2,1,0:T(8,128)}, u32[]{:S(2)}, u32[]{:S(2)}) collective-permute-start(f32[3,128,128]{2,1,0:T(8,128)} %copy-done.7), channel_id=1, source_target_pairs={{0,12},{1,0},{2,4},{3,8},{4,13},{5,1},{6,5},{7,9},{8,14},{9,2},{10... | collective-permute-start | bytes 589832 | tf_op jit(solution)/shard_map/ppermute | solution.py:540
  87.1 6.3 %copy-start.11 = (f32[3,128,128]{2,1,0:T(8,128)}, f32[3,128,128]{2,1,0:T(8,128)S(1)}, u32[]{:S(2)}) copy-start(f32[3,128,128]{2,1,0:T(8,128)S(1)} %collective-permute-done) | copy-start | bytes 589828
  93.1 0.7 copy-start.12
  93.7 0.7 copy-start.13
  94.4 21.6 %collective-permute-start.9 = (f32[12,128,128]{2,1,0:T(8,128)S(1)}, f32[12,128,128]{2,1,0:T(8,128)S(1)}, u32[]{:S(2)}, u32[]{:S(2)}) collective-permute-start(f32[12,128,128]{2,1,0:T(8,128)S(1)} %get-tuple-element.39.t0), channel_id=1, source_target_pairs={{0,2},{1,3},{2,0},{3,1},{4,6},{5,7},{6,4},{7,5},{8,10},{9,11},{10,... | collective-permute-start | bytes 2359304 | tf_op jit(solution)/shard_map/ppermute | solution.py:497
  99.0 19.7 %collective-permute-start.4 = (f32[4,3,128,128]{3,2,1,0:T(8,128)S(1)}, f32[4,3,128,128]{3,2,1,0:T(8,128)S(1)}, u32[]{:S(2)}, u32[]{:S(2)}) collective-permute-start(f32[4,3,128,128]{3,2,1,0:T(8,128)S(1)} %pad_maximum_fusion.rest_0_), channel_id=1, source_target_pairs={{0,8},{8,16},{16,24},{24,28},{28,20},{20,12},{12,4},{4,0},{1,9},{9... | collective-permute-start | bytes 2359304 | tf_op jit(solution)/shard_map/ppermute | solution.py:549
  99.0 20.6 %collective-permute-start.6 = (f32[4,3,128,128]{3,2,1,0:T(8,128)S(1)}, f32[4,3,128,128]{3,2,1,0:T(8,128)S(1)}, u32[]{:S(2)}, u32[]{:S(2)}) collective-permute-start(f32[4,3,128,128]{3,2,1,0:T(8,128)S(1)} %pad_maximum_fusion.rest_0_), channel_id=1, source_target_pairs={{8,0},{16,8},{24,16},{28,24},{20,28},{12,20},{4,12},{0,4},{9,1},{1... | collective-permute-start | bytes 2359304 | tf_op jit(solution)/shard_map/ppermute | solution.py:550
  101.5 19.2 %collective-permute-start.8 = (f32[12,128,128]{2,1,0:T(8,128)S(1)}, f32[12,128,128]{2,1,0:T(8,128)S(1)}, u32[]{:S(2)}, u32[]{:S(2)}) collective-permute-start(f32[12,128,128]{2,1,0:T(8,128)S(1)} %get-tuple-element.39.t0), channel_id=1, source_target_pairs={{0,1},{1,0},{2,3},{3,2},{4,5},{5,4},{6,7},{7,6},{8,9},{9,8},{10,11... | collective-permute-start | bytes 2359304 | tf_op jit(solution)/shard_map/ppermute | solution.py:496
  116.1 4.7 %collective-permute-start.10 = (f32[12,128,128]{2,1,0:T(8,128)S(1)}, f32[12,128,128]{2,1,0:T(8,128)S(1)}, u32[]{:S(2)}, u32[]{:S(2)}) collective-permute-start(f32[12,128,128]{2,1,0:T(8,128)S(1)} %collective-permute-done.9.t2), channel_id=1, source_target_pairs={{0,1},{1,0},{2,3},{3,2},{4,5},{5,4},{6,7},{7,6},{8,9},{9,8},{10,11... | collective-permute-start | bytes 2359304 | tf_op jit(solution)/shard_map/ppermute | solution.py:498
  118.7 18.4 %collective-permute-start.5 = (f32[4,3,128,128]{3,2,1,0:T(8,128)S(1)}, f32[4,3,128,128]{3,2,1,0:T(8,128)S(1)}, u32[]{:S(2)}, u32[]{:S(2)}) collective-permute-start(f32[4,3,128,128]{3,2,1,0:T(8,128)S(1)} %collective-permute-done.4.rest_0_), channel_id=1, source_target_pairs={{0,8},{8,16},{16,24},{24,28},{28,20},{20,12},{12,4},{4,0},{1,9},{9... | collective-permute-start | bytes 2359304 | tf_op jit(solution)/shard_map/ppermute | solution.py:549
  119.6 19.5 %collective-permute-start.7 = (f32[4,3,128,128]{3,2,1,0:T(8,128)S(1)}, f32[4,3,128,128]{3,2,1,0:T(8,128)S(1)}, u32[]{:S(2)}, u32[]{:S(2)}) collective-permute-start(f32[4,3,128,128]{3,2,1,0:T(8,128)S(1)} %collective-permute-done.6.rest_1_), channel_id=1, source_target_pairs={{8,0},{16,8},{24,16},{28,24},{20,28},{12,20},{4,12},{0,4},{9,1},{1... | collective-permute-start | bytes 2359304 | tf_op jit(solution)/shard_map/ppermute | solution.py:550
  120.7 1.0 copy-start.2
  129.2 6.4 %copy-start = (bf16[1536,1024]{1,0:T(8,128)(2,1)}, bf16[1536,1024]{1,0:T(8,128)(2,1)S(1)}, u32[]{:S(2)}) copy-start(bf16[1536,1024]{1,0:T(8,128)(2,1)S(1)} %get-tuple-element.48.pair_ref) | copy-start | bytes 9437188
  139.1 21.6 %collective-permute-start.11 = (f32[4,3,128,128]{3,2,1,0:T(8,128)S(1)}, f32[4,3,128,128]{3,2,1,0:T(8,128)S(1)}, u32[]{:S(2)}, u32[]{:S(2)}) collective-permute-start(f32[4,3,128,128]{3,2,1,0:T(8,128)S(1)} %collective-permute-done.5.rest_0_), channel_id=1, source_target_pairs={{0,8},{8,16},{16,24},{24,28},{28,20},{20,12},{12,4},{4,0},{1,9},{9... | collective-permute-start | bytes 2359304 | tf_op jit(solution)/shard_map/ppermute | solution.py:549
  139.6 21.8 %collective-permute-start.13 = (f32[4,3,128,128]{3,2,1,0:T(8,128)S(1)}, f32[4,3,128,128]{3,2,1,0:T(8,128)S(1)}, u32[]{:S(2)}, u32[]{:S(2)}) collective-permute-start(f32[4,3,128,128]{3,2,1,0:T(8,128)S(1)} %collective-permute-done.7.rest_1_), channel_id=1, source_target_pairs={{8,0},{16,8},{24,16},{28,24},{20,28},{12,20},{4,12},{0,4},{9,1},{1... | collective-permute-start | bytes 2359304 | tf_op jit(solution)/shard_map/ppermute | solution.py:550
  160.7 12.3 %collective-permute-start.12 = (f32[2,3,128,128]{3,2,1,0:T(8,128)S(1)}, f32[2,3,128,128]{3,2,1,0:T(8,128)S(1)}, u32[]{:S(2)}, u32[]{:S(2)}) collective-permute-start(f32[2,3,128,128]{3,2,1,0:T(8,128)S(1)} %slice.13), channel_id=1, source_target_pairs={{0,8},{8,16},{16,24},{24,28},{28,20},{20,12},{12,4},{4,0},{1,9},{9... | collective-permute-start | bytes 1179656 | tf_op jit(solution)/shard_map/ppermute | solution.py:555
  161.4 11.6 %copy-start.1 = (bf16[1536,1024]{1,0:T(8,128)(2,1)S(1)}, bf16[1536,1024]{1,0:T(8,128)(2,1)}, u32[]{:S(2)}) copy-start(bf16[1536,1024]{1,0:T(8,128)(2,1)} %copy-done) | copy-start | bytes 9437188
  161.4 11.6 %collective-permute-start.14 = (f32[2,3,128,128]{3,2,1,0:T(8,128)S(1)}, f32[2,3,128,128]{3,2,1,0:T(8,128)S(1)}, u32[]{:S(2)}, u32[]{:S(2)}) collective-permute-start(f32[2,3,128,128]{3,2,1,0:T(8,128)S(1)} %slice.14), channel_id=1, source_target_pairs={{8,0},{16,8},{24,16},{28,24},{20,28},{12,20},{4,12},{0,4},{9,1},{1... | collective-permute-start | bytes 1179656 | tf_op jit(solution)/shard_map/ppermute | solution.py:555

commit v16 on v15

--- a/solution.py
+++ b/solution.py
@@ -179,7 +179,7 @@
     _, height = lead_slices(devices)
     shapes = [(rows, TILE, TILE), (devices, height, TILE)]
     shapes += [(rows // parts, TILE, TILE)] * parts
-    out_shape = [jax.ShapeDtypeStruct(shape, jnp.float32) for shape in shapes]
+    out_shape = [pltpu.HBM(shape, jnp.float32) for shape in shapes]
     return pl.pallas_call(
         columns_kernel,
         grid_spec=pltpu.PrefetchScalarGridSpec(
@@ -278,7 +278,7 @@
     group = rows // 3
     height = group * TILE
     out_shape = [
-        jax.ShapeDtypeStruct((rows * TILE, 2 * WIDTH), jnp.bfloat16),
+        pltpu.HBM((rows * TILE, 2 * WIDTH), jnp.bfloat16),
         jax.ShapeDtypeStruct(front.shape, jnp.float32),
         jax.ShapeDtypeStruct((3, PANEL, 3 * PANEL), jnp.bfloat16),
         jax.ShapeDtypeStruct((2 * slot_in.shape[0],), jnp.int32),
@@ -407,15 +407,11 @@
 
         start = jnp.minimum(2 * step, count - 2)
         lanes = pl.ds(pl.multiple_of(start * TILE, TILE), 2 * TILE)
-        block = rows // 3
-        for m in range(3):
-            left = pair_ref[m * block * TILE : (m + 1) * block * TILE]
-            update = dot(left, right_ref[: 2 * WIDTH, lanes])
-            update = update + dot(left[:, :WIDTH], right_ref[2 * WIDTH :, lanes])
-            span = slice(m * block, (m + 1) * block)
-            for j in range(2):
-                part = update[:, j * TILE : (j + 1) * TILE].reshape(block, TILE, TILE)
-                given[slot, j, span] = taken[slot, j, span] - part
+        update = dot(pair_ref[...], right_ref[: 2 * WIDTH, lanes])
+        update = update + dot(pair_ref[:, :WIDTH], right_ref[2 * WIDTH :, lanes])
+        for j in range(2):
+            part = update[:, j * TILE : (j + 1) * TILE].reshape(rows, TILE, TILE)
+            given[slot, j] = taken[slot, j] - part
 
         def add(copy, j, s, a):
             copy.wait()
@@ -549,12 +545,13 @@
             ahead = lax.ppermute(ahead, "row", up)
             behind = lax.ppermute(behind, "row", down)
             if step == 2:
-                panels = updated(rounds[0], panels, 0)
+                panels = updated([*rounds[0], rounds[1][0]], panels, 0)
                 ahead, behind, panels = lax.optimization_barrier((ahead, behind, panels))
             rounds.append([(ahead, -step), (behind, step)])
         last = [lax.ppermute(ahead[:2], "row", up), lax.ppermute(behind[2:], "row", down)]
-        rounds = [*rounds[1:], [(last, n_row // 2)]]
-        first = 1
+        late = [entry for entries in rounds for entry in entries][2:]
+        rounds = [late[:2], late[2:3], *rounds[3:], [(last, n_row // 2)]]
+        first = 2
 
     else:
         pairs = [

time: 180 us -> 175 us (0.972)
  local copies, waits for them, and re-layouts: 5.61 us -> 1.21 us
  waiting for transfers between devices: 27.3 us -> 23.8 us
  Pallas kernels: 55.3 us -> 58.4 us
    unnamed x28 -> x14, local copies, waits for them, and re-layouts: 5.55 us -> 1.16 us
    ppermute x3, waiting for transfers between devices: 2.52 us -> 0.01 us  [body(): behind = lax.ppermute(behind, 'row', down)]
  transfers between devices with their start and end apart: 16 -> 16, of which waited for: 7 -> 5; matrix products, arithmetic and copies ran while one was open for 1% -> 1% of each run, Pallas kernels for 24% -> 26%
where the time goes in v16:
time: 175 us
  blocking collectives  65.4 us (37%)
  Pallas kernels  58.4 us (33%)
  waiting for transfers between devices  23.8 us (14%)
  starting transfers between devices  23 us (13%)
  other arithmetic  2.5 us (1%)
    all_to_all x1, blocking collectives, body(): lax.all_to_all(outgoing, BOTH, split_axis=0, concat_axis=0, tiled=True)  65.4 us
    pallas_call x5, Pallas kernels, trailing(): pl.pallas_call(functools.partial(trailing_kernel, first, len(pieces), hal...  43.3 us
    ppermute x1, waiting for transfers between devices, exchange(): far = lax.ppermute(mine, 'col', [(c, c ^ 2) for c in range(n_col)])  14.9 us
    ppermute x4, starting transfers between devices, body(): arrived.append(lax.ppermute(part, BOTH, pairs))  7.86 us
    pallas_call x1, Pallas kernels, row_panels(): pl.pallas_call(row_panels_kernel, grid_spec=pltpu.PrefetchScalarGridSpec(...  7.83 us
    ppermute x4, waiting for transfers between devices, body(): arrived.append(lax.ppermute(part, BOTH, pairs))  6.64 us
    ppermute x3, starting transfers between devices, body(): behind = lax.ppermute(behind, 'row', down)  4.26 us
    ppermute x1, starting transfers between devices, exchange(): far = lax.ppermute(mine, 'col', [(c, c ^ 2) for c in range(n_col)])  3.92 us
  transfers between devices with their start and end apart: 16, of which 5 were waited for; matrix products, arithmetic and copies ran while one was open for 1% of the time, Pallas kernels for 26%

profile of v16, /device:TPU:0, one launch (start us, length us, event | category | flops | bytes accessed | tf_op | source)
XLA Modules:
  0.0 175.2 jit_solution(7109352601526446494)
XLA Ops:
  0.7 0.7 pad_add_fusion.place
  1.3 0.0 copy-start.4
  1.3 3.3 %pack.1 = f32[32,152,128]{2,1,0:T(8,128)} custom-call(s32[4]{0:T(128)} %pad_add_fusion.place, s32[16]{0:T(128)} %bitcast.11, s32[16]{0:T(128)} %slot.1, s32[1]{0:T(128)S(6)} %copy.19.count, f32[16,128,128]{2,1,0:T(8,128)} %child_ref.1, f32[12,1,24,1,128,128]{5,4,3,2,1,0:T(8,128)} %rest_2_.7), custom_call_target="tpu_custom_call" | custom-call | tf_op jit(solution)/shard_map/pack/pallas_call | solution.py:123
  4.7 0.0 copy-start.3
  4.7 0.0 copy-start.5
  4.7 0.0 copy-start.6
  4.7 65.4 %all_to_all.10.incoming_ref.rest_3_.rest_2_ = f32[32,152,128]{2,1,0:T(8,128)S(1)} all-to-all(f32[32,152,128]{2,1,0:T(8,128)} %pack.1), channel_id=1, replica_groups=mesh['row'=8,'col'=4] {'row','col'}, dimensions={0} | all-to-all | bytes 4980736 | tf_op jit(solution)/shard_map/all_to_all | solution.py:483
  70.1 0.7 fusion.slot_in
  70.7 0.0 copy-done.4
  70.7 3.9 %panel_columns.1 = (f32[12,128,128]{2,1,0:T(8,128)}, f32[32,16,128]{2,1,0:T(8,128)}, f32[3,128,128]{2,1,0:T(8,128)}, f32[3,128,128]{2,1,0:T(8,128)}, f32[3,128,128]{2,1,0:T(8,128)}, /*index=5*/f32[3,128,128]{2,1,0:T(8,128)}) custom-call(s32[4]{0:T(128)S(1)} %copy-done.4, s32[32]{0:T(128)S(1)} %fusion.slot_in, f32[12,1,24,1,128,128]{5,4,3,2,1,0:T(8,128)} %rest_2_.7, ...), custom_call_target="tpu_custom_call" | custom-call | tf_op jit(solution)/shard_map/panel_columns/pallas_call | solution.py:183
  74.6 2.7 %all-to-all-start.1 = ((f32[32,16,128]{2,1,0:T(8,128)}), f32[32,16,128]{2,1,0:T(8,128)S(1)}, u32[]{:S(2)}, u32[]{:S(2)}) async-start(f32[32,16,128]{2,1,0:T(8,128)} %get-tuple-element.34), calls=%async_computation.1 | async-start | bytes 524288 | tf_op jit(solution)/shard_map/all_to_all | solution.py:488
  77.4 1.6 collective-permute-start
  79.0 2.3 %collective-permute-start.1 = (f32[3,128,128]{2,1,0:T(8,128)}, f32[3,128,128]{2,1,0:T(8,128)}, u32[]{:S(2)}, u32[]{:S(2)}) collective-permute-start(f32[3,128,128]{2,1,0:T(8,128)} %get-tuple-element.30), channel_id=1, source_target_pairs={{0,4},{1,8},{2,12},{3,0},{4,5},{5,9},{6,13},{7,1},{8,6},{9,10},{10... | collective-permute-start | bytes 589832 | tf_op jit(solution)/shard_map/ppermute | solution.py:536
  81.2 3.5 %collective-permute-start.2 = (f32[3,128,128]{2,1,0:T(8,128)}, f32[3,128,128]{2,1,0:T(8,128)}, u32[]{:S(2)}, u32[]{:S(2)}) collective-permute-start(f32[3,128,128]{2,1,0:T(8,128)} %get-tuple-element.31), channel_id=1, source_target_pairs={{0,8},{1,12},{2,0},{3,4},{4,9},{5,13},{6,1},{7,5},{8,10},{9,14},{1... | collective-permute-start | bytes 589832 | tf_op jit(solution)/shard_map/ppermute | solution.py:536
  84.7 0.5 collective-permute-start.3
  85.2 0.0 collective-permute-done
  85.2 5.9 %collective-permute-done.1 = f32[3,128,128]{2,1,0:T(8,128)} collective-permute-done((f32[3,128,128]{2,1,0:T(8,128)}, f32[3,128,128]{2,1,0:T(8,128)}, u32[]{:S(2)}, u32[]{:S(2)}) %collective-permute-start.1) | collective-permute-done | bytes 196640 | tf_op jit(solution)/shard_map/ppermute | solution.py:536
  91.1 0.4 collective-permute-done.2
  91.5 0.3 collective-permute-done.3
  91.9 0.0 all-to-all-done.1
  91.9 3.9 %collective-permute-start.9 = (f32[12,128,128]{2,1,0:T(8,128)}, f32[12,128,128]{2,1,0:T(8,128)S(1)}, u32[]{:S(2)}, u32[]{:S(2)}) collective-permute-start(f32[12,128,128]{2,1,0:T(8,128)} %get-tuple-element.39.t0), channel_id=1, source_target_pairs={{0,2},{1,3},{2,0},{3,1},{4,6},{5,7},{6,4},{7,5},{8,10},{9,11},{10,... | collective-permute-start | bytes 2359304 | tf_op jit(solution)/shard_map/ppermute | solution.py:493
  95.8 1.2 pad_maximum_fusion.rest_0_
  97.0 0.1 collective-permute-start.4
  97.0 2.0 %collective-permute-start.6 = (f32[4,3,128,128]{3,2,1,0:T(8,128)S(1)}, f32[4,3,128,128]{3,2,1,0:T(8,128)S(1)}, u32[]{:S(2)}, u32[]{:S(2)}) collective-permute-start(f32[4,3,128,128]{3,2,1,0:T(8,128)S(1)} %pad_maximum_fusion.rest_0_), channel_id=1, source_target_pairs={{8,0},{16,8},{24,16},{28,24},{20,28},{12,20},{4,12},{0,4},{9,1},{1... | collective-permute-start | bytes 2359304 | tf_op jit(solution)/shard_map/ppermute | solution.py:546
  99.1 0.0 collective-permute-start.8
  99.1 14.9 %collective-permute-done.9.t2 = f32[12,128,128]{2,1,0:T(8,128)S(1)} collective-permute-done((f32[12,128,128]{2,1,0:T(8,128)}, f32[12,128,128]{2,1,0:T(8,128)S(1)}, u32[]{:S(2)}, u32[]{:S(2)}) %collective-permute-start.9) | collective-permute-done | bytes 786464 | tf_op jit(solution)/shard_map/ppermute | solution.py:493
  114.0 0.0 collective-permute-start.10
  114.0 2.2 %collective-permute-done.4.rest_1_ = f32[4,3,128,128]{3,2,1,0:T(8,128)S(1)} collective-permute-done((f32[4,3,128,128]{3,2,1,0:T(8,128)S(1)}, f32[4,3,128,128]{3,2,1,0:T(8,128)S(1)}, u32[]{:S(2)}, u32[]{:S(2)}) %collective-permute-start.4) | collective-permute-done | bytes 786464 | tf_op jit(solution)/shard_map/ppermute | solution.py:545
  116.2 1.0 collective-permute-start.5
  117.2 0.0 collective-permute-done.6.rest_0_
  117.2 1.0 collective-permute-start.7
  118.2 0.0 collective-permute-done.8.t1
  118.2 0.0 collective-permute-done.10.t3
  118.2 0.0 copy-done.3
  118.2 0.0 copy-start.2
  118.2 1.1 copy-done.2
  119.4 7.8 %row_panels.1 = (bf16[1536,1024]{1,0:T(8,128)(2,1)}, f32[12,1,24,1,128,128]{5,4,3,2,1,0:T(8,128)}, bf16[3,256,768]{2,1,0:T(8,128)(2,1)S(1)}, s32[64]{0:T(128)S(1)}, s32[25]{0:T(128)S(1)}) custom-call(s32[4]{0:T(128)S(1)} %copy-done.4, s32[32]{0:T(128)S(1)} %fusion.slot_in, f32[12,128,128]{2,1,0:T(8,128)S(1)} %copy-done.2, ...), custom_call_target="tpu_custom_call" | custom-call | tf_op jit(solution)/shard_map/row_panels/pallas_call | solution.py:288
  127.2 0.0 copy-done.5
  127.2 0.0 copy-done.6
  127.2 10.0 %trailing.5.rest_4_ = f32[12,1,24,1,128,128]{5,4,3,2,1,0:T(8,128)} custom-call(s32[4]{0:T(128)S(1)} %copy-done.4, s32[192]{0:T(256)S(1)} %copy-done.5, s32[256]{0:T(256)S(1)} %copy-done.6, s32[64]{0:T(128)S(1)} %get-tuple-element.46.order, s32[25]{0:T(128)S(1)} %get-tuple-element.47.starts, ...), custom_call_target="tpu_custom_call", output_to_operand_aliasing={{}: (11, {})} | custom-call | flops 9663676416 | bytes 9437184 | tf_op jit(solution)/shard_map/trailing/pallas_call | solution.py:443
  137.2 0.0 copy-start
  137.2 0.0 collective-permute-done.5.rest_1_
  137.3 0.0 collective-permute-done.7.rest_0_
  137.3 0.9 collective-permute-start.11
  138.1 1.2 collective-permute-start.13
  139.3 9.8 %trailing.6.rest_3_ = f32[12,1,24,1,128,128]{5,4,3,2,1,0:T(8,128)} custom-call(s32[4]{0:T(128)S(1)} %copy-done.4, s32[192]{0:T(256)S(1)} %copy-done.5, s32[256]{0:T(256)S(1)} %copy-done.6, s32[64]{0:T(128)S(1)} %get-tuple-element.46.order, s32[25]{0:T(128)S(1)} %get-tuple-element.47.starts, ...), custom_call_target="tpu_custom_call", output_to_operand_aliasing={{}: (11, {})} | custom-call | flops 9663676416 | bytes 9437184 | tf_op jit(solution)/shard_map/trailing/pallas_call | solution.py:443
  149.1 0.0 copy-done
  149.1 6.2 %trailing.7.rest_4_ = f32[12,1,24,1,128,128]{5,4,3,2,1,0:T(8,128)} custom-call(s32[4]{0:T(128)S(1)} %copy-done.4, s32[192]{0:T(256)S(1)} %copy-done.5, s32[256]{0:T(256)S(1)} %copy-done.6, s32[64]{0:T(128)S(1)} %get-tuple-element.46.order, s32[25]{0:T(128)S(1)} %get-tuple-element.47.starts, ...), custom_call_target="tpu_custom_call", output_to_operand_aliasing={{}: (10, {})} | custom-call | flops 4831838208 | bytes 4718592 | tf_op jit(solution)/shard_map/trailing/pallas_call | solution.py:443
  155.4 0.0 collective-permute-done.11.rest_0_
  155.4 1.3 collective-permute-start.12
  156.7 0.0 collective-permute-done.13.rest_1_
  156.8 0.0 copy-start.1
  156.8 1.0 collective-permute-start.14
  157.8 10.9 %trailing.8.rest_4_ = f32[12,1,24,1,128,128]{5,4,3,2,1,0:T(8,128)} custom-call(s32[4]{0:T(128)S(1)} %copy-done.4, s32[192]{0:T(256)S(1)} %copy-done.5, s32[256]{0:T(256)S(1)} %copy-done.6, s32[64]{0:T(128)S(1)} %get-tuple-element.46.order, s32[25]{0:T(128)S(1)} %get-tuple-element.47.starts, ...), custom_call_target="tpu_custom_call", output_to_operand_aliasing={{}: (11, {})} | custom-call | flops 9663676416 | bytes 9437184 | tf_op jit(solution)/shard_map/trailing/pallas_call | solution.py:443
  168.7 0.0 collective-permute-done.12.rest_0_
  168.7 0.0 collective-permute-done.14.rest_1_
  168.7 0.0 copy-done.1
  168.7 6.4 %trailing.9 = f32[12,1,24,1,128,128]{5,4,3,2,1,0:T(8,128)} custom-call(s32[4]{0:T(128)S(1)} %copy-done.4, s32[192]{0:T(256)S(1)} %copy-done.5, s32[256]{0:T(256)S(1)} %copy-done.6, s32[64]{0:T(128)S(1)} %get-tuple-element.46.order, s32[25]{0:T(128)S(1)} %get-tuple-element.47.starts, ...), custom_call_target="tpu_custom_call", output_to_operand_aliasing={{}: (11, {})} | custom-call | flops 4831838208 | bytes 4718592 | tf_op jit(solution)/shard_map/trailing/pallas_call | solution.py:443
  (2 shorter events, 0.1 us)
Async XLA Ops:
  1.3 69.4 %copy-start.4 = (s32[4]{0:T(128)S(1)}, s32[4]{0:T(128)}, u32[]{:S(2)}) copy-start(s32[4]{0:T(128)} %pad_add_fusion.place) | copy-start | bytes 52
  4.7 113.6 %copy-start.3 = (f32[2,256,256]{2,1,0:T(8,128)S(1)}, f32[2,256,256]{2,1,0:T(8,128)}, u32[]{:S(2)}) copy-start(f32[2,256,256]{2,1,0:T(8,128)} %diag_ref.1) | copy-start | bytes 1572868
  4.7 122.5 %copy-start.5 = (s32[192]{0:T(256)S(1)}, s32[192]{0:T(256)}, u32[]{:S(2)}) copy-start(s32[192]{0:T(256)} %constant.17.clone.columns_table) | copy-start | bytes 2308
  4.7 122.5 %copy-start.6 = (s32[256]{0:T(256)S(1)}, s32[256]{0:T(256)}, u32[]{:S(2)}) copy-start(s32[256]{0:T(256)} %constant.18.clone.places_table) | copy-start | bytes 3076
  74.6 17.3 %all-to-all-start.1 = ((f32[32,16,128]{2,1,0:T(8,128)}), f32[32,16,128]{2,1,0:T(8,128)S(1)}, u32[]{:S(2)}, u32[]{:S(2)}) async-start(f32[32,16,128]{2,1,0:T(8,128)} %get-tuple-element.34), calls=%async_computation.1 | async-start | bytes 524288 | tf_op jit(solution)/shard_map/all_to_all | solution.py:488
  77.4 7.9 %collective-permute-start = (f32[3,128,128]{2,1,0:T(8,128)}, f32[3,128,128]{2,1,0:T(8,128)S(1)}, u32[]{:S(2)}, u32[]{:S(2)}) collective-permute-start(f32[3,128,128]{2,1,0:T(8,128)} %get-tuple-element.29), channel_id=1, source_target_pairs={{0,0},{1,4},{2,8},{3,12},{4,1},{5,5},{6,9},{7,13},{8,2},{9,6},{10,... | collective-permute-start | bytes 589832 | tf_op jit(solution)/shard_map/ppermute | solution.py:536
  79.0 12.1 %collective-permute-start.1 = (f32[3,128,128]{2,1,0:T(8,128)}, f32[3,128,128]{2,1,0:T(8,128)}, u32[]{:S(2)}, u32[]{:S(2)}) collective-permute-start(f32[3,128,128]{2,1,0:T(8,128)} %get-tuple-element.30), channel_id=1, source_target_pairs={{0,4},{1,8},{2,12},{3,0},{4,5},{5,9},{6,13},{7,1},{8,6},{9,10},{10... | collective-permute-start | bytes 589832 | tf_op jit(solution)/shard_map/ppermute | solution.py:536
  81.2 10.3 %collective-permute-start.2 = (f32[3,128,128]{2,1,0:T(8,128)}, f32[3,128,128]{2,1,0:T(8,128)}, u32[]{:S(2)}, u32[]{:S(2)}) collective-permute-start(f32[3,128,128]{2,1,0:T(8,128)} %get-tuple-element.31), channel_id=1, source_target_pairs={{0,8},{1,12},{2,0},{3,4},{4,9},{5,13},{6,1},{7,5},{8,10},{9,14},{1... | collective-permute-start | bytes 589832 | tf_op jit(solution)/shard_map/ppermute | solution.py:536
  84.7 7.2 %collective-permute-start.3 = (f32[3,128,128]{2,1,0:T(8,128)}, f32[3,128,128]{2,1,0:T(8,128)}, u32[]{:S(2)}, u32[]{:S(2)}) collective-permute-start(f32[3,128,128]{2,1,0:T(8,128)} %get-tuple-element.32), channel_id=1, source_target_pairs={{0,12},{1,0},{2,4},{3,8},{4,13},{5,1},{6,5},{7,9},{8,14},{9,2},{10... | collective-permute-start | bytes 589832 | tf_op jit(solution)/shard_map/ppermute | solution.py:536
  91.9 22.1 %collective-permute-start.9 = (f32[12,128,128]{2,1,0:T(8,128)}, f32[12,128,128]{2,1,0:T(8,128)S(1)}, u32[]{:S(2)}, u32[]{:S(2)}) collective-permute-start(f32[12,128,128]{2,1,0:T(8,128)} %get-tuple-element.39.t0), channel_id=1, source_target_pairs={{0,2},{1,3},{2,0},{3,1},{4,6},{5,7},{6,4},{7,5},{8,10},{9,11},{10,... | collective-permute-start | bytes 2359304 | tf_op jit(solution)/shard_map/ppermute | solution.py:493
  97.0 19.2 %collective-permute-start.4 = (f32[4,3,128,128]{3,2,1,0:T(8,128)S(1)}, f32[4,3,128,128]{3,2,1,0:T(8,128)S(1)}, u32[]{:S(2)}, u32[]{:S(2)}) collective-permute-start(f32[4,3,128,128]{3,2,1,0:T(8,128)S(1)} %pad_maximum_fusion.rest_0_), channel_id=1, source_target_pairs={{0,8},{8,16},{16,24},{24,28},{28,20},{20,12},{12,4},{4,0},{1,9},{9... | collective-permute-start | bytes 2359304 | tf_op jit(solution)/shard_map/ppermute | solution.py:545
  97.0 20.1 %collective-permute-start.6 = (f32[4,3,128,128]{3,2,1,0:T(8,128)S(1)}, f32[4,3,128,128]{3,2,1,0:T(8,128)S(1)}, u32[]{:S(2)}, u32[]{:S(2)}) collective-permute-start(f32[4,3,128,128]{3,2,1,0:T(8,128)S(1)} %pad_maximum_fusion.rest_0_), channel_id=1, source_target_pairs={{8,0},{16,8},{24,16},{28,24},{20,28},{12,20},{4,12},{0,4},{9,1},{1... | collective-permute-start | bytes 2359304 | tf_op jit(solution)/shard_map/ppermute | solution.py:546
  99.1 19.2 %collective-permute-start.8 = (f32[12,128,128]{2,1,0:T(8,128)}, f32[12,128,128]{2,1,0:T(8,128)S(1)}, u32[]{:S(2)}, u32[]{:S(2)}) collective-permute-start(f32[12,128,128]{2,1,0:T(8,128)} %get-tuple-element.39.t0), channel_id=1, source_target_pairs={{0,1},{1,0},{2,3},{3,2},{4,5},{5,4},{6,7},{7,6},{8,9},{9,8},{10,11... | collective-permute-start | bytes 2359304 | tf_op jit(solution)/shard_map/ppermute | solution.py:492
  114.0 4.3 %collective-permute-start.10 = (f32[12,128,128]{2,1,0:T(8,128)S(1)}, f32[12,128,128]{2,1,0:T(8,128)S(1)}, u32[]{:S(2)}, u32[]{:S(2)}) collective-permute-start(f32[12,128,128]{2,1,0:T(8,128)S(1)} %collective-permute-done.9.t2), channel_id=1, source_target_pairs={{0,1},{1,0},{2,3},{3,2},{4,5},{5,4},{6,7},{7,6},{8,9},{9,8},{10,11... | collective-permute-start | bytes 2359304 | tf_op jit(solution)/shard_map/ppermute | solution.py:494
  116.2 21.1 %collective-permute-start.5 = (f32[4,3,128,128]{3,2,1,0:T(8,128)S(1)}, f32[4,3,128,128]{3,2,1,0:T(8,128)S(1)}, u32[]{:S(2)}, u32[]{:S(2)}) collective-permute-start(f32[4,3,128,128]{3,2,1,0:T(8,128)S(1)} %collective-permute-done.4.rest_1_), channel_id=1, source_target_pairs={{0,8},{8,16},{16,24},{24,28},{28,20},{20,12},{12,4},{4,0},{1,9},{9... | collective-permute-start | bytes 2359304 | tf_op jit(solution)/shard_map/ppermute | solution.py:545
  117.2 20.1 %collective-permute-start.7 = (f32[4,3,128,128]{3,2,1,0:T(8,128)S(1)}, f32[4,3,128,128]{3,2,1,0:T(8,128)S(1)}, u32[]{:S(2)}, u32[]{:S(2)}) collective-permute-start(f32[4,3,128,128]{3,2,1,0:T(8,128)S(1)} %collective-permute-done.6.rest_0_), channel_id=1, source_target_pairs={{8,0},{16,8},{24,16},{28,24},{20,28},{12,20},{4,12},{0,4},{9,1},{1... | collective-permute-start | bytes 2359304 | tf_op jit(solution)/shard_map/ppermute | solution.py:546
  118.2 1.1 copy-start.2
  137.2 11.9 %copy-start = (bf16[1536,1024]{1,0:T(8,128)(2,1)S(1)}, bf16[1536,1024]{1,0:T(8,128)(2,1)}, u32[]{:S(2)}) copy-start(bf16[1536,1024]{1,0:T(8,128)(2,1)} %get-tuple-element.48.pair_ref) | copy-start | bytes 9437188
  137.3 18.1 %collective-permute-start.11 = (f32[4,3,128,128]{3,2,1,0:T(8,128)S(1)}, f32[4,3,128,128]{3,2,1,0:T(8,128)S(1)}, u32[]{:S(2)}, u32[]{:S(2)}) collective-permute-start(f32[4,3,128,128]{3,2,1,0:T(8,128)S(1)} %collective-permute-done.5.rest_1_), channel_id=1, source_target_pairs={{0,8},{8,16},{16,24},{24,28},{28,20},{20,12},{12,4},{4,0},{1,9},{9... | collective-permute-start | bytes 2359304 | tf_op jit(solution)/shard_map/ppermute | solution.py:545
  138.1 18.6 %collective-permute-start.13 = (f32[4,3,128,128]{3,2,1,0:T(8,128)S(1)}, f32[4,3,128,128]{3,2,1,0:T(8,128)S(1)}, u32[]{:S(2)}, u32[]{:S(2)}) collective-permute-start(f32[4,3,128,128]{3,2,1,0:T(8,128)S(1)} %collective-permute-done.7.rest_0_), channel_id=1, source_target_pairs={{8,0},{16,8},{24,16},{28,24},{20,28},{12,20},{4,12},{0,4},{9,1},{1... | collective-permute-start | bytes 2359304 | tf_op jit(solution)/shard_map/ppermute | solution.py:546
  155.4 13.3 %collective-permute-start.12 = (f32[2,3,128,128]{3,2,1,0:T(8,128)S(1)}, f32[2,3,128,128]{3,2,1,0:T(8,128)S(1)}, u32[]{:S(2)}, u32[]{:S(2)}) collective-permute-start(f32[2,3,128,128]{3,2,1,0:T(8,128)S(1)} %slice.13), channel_id=1, source_target_pairs={{0,8},{8,16},{16,24},{24,28},{28,20},{20,12},{12,4},{4,0},{1,9},{9... | collective-permute-start | bytes 1179656 | tf_op jit(solution)/shard_map/ppermute | solution.py:551
  156.8 11.9 %copy-start.1 = (bf16[1536,1024]{1,0:T(8,128)(2,1)S(1)}, bf16[1536,1024]{1,0:T(8,128)(2,1)}, u32[]{:S(2)}) copy-start(bf16[1536,1024]{1,0:T(8,128)(2,1)} %get-tuple-element.48.pair_ref) | copy-start | bytes 9437188
  156.8 11.9 %collective-permute-start.14 = (f32[2,3,128,128]{3,2,1,0:T(8,128)S(1)}, f32[2,3,128,128]{3,2,1,0:T(8,128)S(1)}, u32[]{:S(2)}, u32[]{:S(2)}) collective-permute-start(f32[2,3,128,128]{3,2,1,0:T(8,128)S(1)} %slice.14), channel_id=1, source_target_pairs={{8,0},{16,8},{24,16},{28,24},{20,28},{12,20},{4,12},{0,4},{9,1},{1... | collective-permute-start | bytes 1179656 | tf_op jit(solution)/shard_map/ppermute | solution.py:551

commit v17 on v16

--- a/solution.py
+++ b/solution.py
@@ -200,9 +200,47 @@
     )(place, slot_in, front, incoming)
 
 
+def square(tiles_ref):
+    return jnp.concatenate(
+        [jnp.concatenate([tiles_ref[i, 0], tiles_ref[i, 1]], axis=1) for i in range(2)], axis=0
+    )
+
+
+def piece_panels_kernel(rolled, place, t0, t1, t2, t3, lead_ref, diag_ref, out_ref, tiles_ref):
+    group = t0.shape[0]
+    for i, tile_ref in enumerate((t0, t1, t2, t3)):
+        tiles_ref[i] = tile_ref[...]
+    lead = dot(deep(square(lead_ref)), stacked(diag_ref[0]))
+    small = [deep(diag_ref[0].T), deep(lead), deep(diag_ref[1].T)]
+    columns = []
+    for c in range(4):
+        at = lax.rem(place[0] + 4 - c, 4) if rolled else c
+        columns.append(jnp.concatenate([tiles_ref[at, t] for t in range(group)], axis=1))
+    for i, panel in enumerate(two_panels_across(columns, small)):
+        for j in range(2):
+            for t in range(group):
+                out_ref[2 * i + j, t] = panel[
+                    j * TILE : (j + 1) * TILE, t * TILE : (t + 1) * TILE
+                ]
+
+
+def piece_panels(parts, lead, diag, place, rolled):
+    shape = (4, *parts[0].shape)
+    return pl.pallas_call(
+        functools.partial(piece_panels_kernel, rolled),
+        in_specs=[pl.BlockSpec(memory_space=pltpu.SMEM)]
+        + [pl.BlockSpec(memory_space=pltpu.VMEM)] * 6,
+        out_specs=pl.BlockSpec(memory_space=pltpu.VMEM),
+        scratch_shapes=[pltpu.VMEM(shape, jnp.float32)],
+        out_shape=jax.ShapeDtypeStruct(shape, jnp.float32),
+        compiler_params=pltpu.CompilerParams(vmem_limit_bytes=VMEM),
+        name="piece_panels",
+    )(place, *parts, lead, diag)
+
+
 def row_panels_kernel(
-    place, slot_in, t0, t1, t2, t3, lead_ref, diag_ref, pair_ref, out_ref, across_ref, order,
-    starts, small_ref, tiles_ref, cursor,
+    place, slot_in, t0, t1, t2, t3, lead_ref, diag_ref, pair_ref, out_ref, order, starts,
+    small_ref, tiles_ref, cursor,
 ):
     step = pl.program_id(0)
     cols = starts.shape[0] - 1
@@ -213,15 +251,9 @@
     @pl.when(step == 0)
     def _():
         small_ref[0] = stacked(diag_ref[0])
-        lead = jnp.concatenate(
-            [jnp.concatenate([lead_ref[i, 0], lead_ref[i, 1]], axis=1) for i in range(2)], axis=0
-        )
-        lead = dot(deep(lead), small_ref[0])
+        lead = dot(deep(square(lead_ref)), small_ref[0])
         small_ref[1] = stacked(lead.T)
         small_ref[2] = stacked(diag_ref[1])
-        across_ref[0] = deep(diag_ref[0].T)
-        across_ref[1] = deep(lead)
-        across_ref[2] = deep(diag_ref[1].T)
 
         @pl.loop(0, cols + 1)
         def _(b):
@@ -280,7 +312,6 @@
     out_shape = [
         pltpu.HBM((rows * TILE, 2 * WIDTH), jnp.bfloat16),
         jax.ShapeDtypeStruct(front.shape, jnp.float32),
-        jax.ShapeDtypeStruct((3, PANEL, 3 * PANEL), jnp.bfloat16),
         jax.ShapeDtypeStruct((2 * slot_in.shape[0],), jnp.int32),
         jax.ShapeDtypeStruct((cols + 1,), jnp.int32),
     ]
@@ -294,7 +325,6 @@
             out_specs=[
                 pl.BlockSpec((height, 2 * WIDTH), lambda i, *_: (i, 0)),
                 pl.BlockSpec((group, 1, 1, 1, TILE, TILE), lambda i, *_: (i, 0, 0, 0, 0, 0)),
-                whole_spec(out_shape[2]),
                 pl.BlockSpec(memory_space=pltpu.SMEM),
                 pl.BlockSpec(memory_space=pltpu.SMEM),
             ],
@@ -311,8 +341,7 @@
 
 
 def trailing_kernel(
-    first, n_held, halved, place, columns_table, places_table, order, starts, pair_ref, small_ref,
-    *rest,
+    first, n_held, halved, place, columns_table, order, starts, pair_ref, *rest
 ):
     piece_refs = rest[:n_held]
     front_ref, incoming_ref, _, out_ref, right_ref, taken, given, child_ref, *rest = rest[n_held:]
@@ -327,7 +356,6 @@
     steps = (count + 1) // 2
     rows, cols = front_ref.shape[0], front_ref.shape[2]
     columns_base = place[0] * cols + first * group
-    places_base = (place[0] * (cols // group) + first) * 4
 
     def columns_of(step):
         for j in range(2):
@@ -380,21 +408,11 @@
     for step in range(steps):
         each_child(step, lambda copy, *_: copy.start())
 
-    tile_columns = [
-        jnp.concatenate(
-            [
-                piece[places_table[places_base + 4 * p + c], t]
-                for p, piece in enumerate(piece_refs)
-                for t in range(group)
-            ],
-            axis=1,
-        )
-        for c in range(4)
-    ]
-    for i, panel in enumerate(two_panels_across(tile_columns, small_ref)):
-        high, low = halves(panel)
+    for c in range(4):
+        tiles = [piece[c, t] for piece in piece_refs for t in range(group)]
+        high, low = halves(jnp.concatenate(tiles, axis=1))
         for k, half in enumerate((high, high, low)):
-            right_ref[k * WIDTH + i * PANEL : k * WIDTH + (i + 1) * PANEL] = half
+            right_ref[k * WIDTH + c * TILE : k * WIDTH + (c + 1) * TILE] = half
 
     @pl.loop(0, steps)
     def _(step):
@@ -428,21 +446,21 @@
         each_give(step, lambda copy: copy.wait())
 
 
-def trailing(front, pieces, first, place, tables, panels, incoming):
+def trailing(front, pieces, first, place, table, panels, incoming):
     rows = front.shape[0]
-    pair, out, small, order, starts = panels
+    pair, out, order, starts = panels
     group = pieces[0].shape[1]
     halved = pieces[0].shape[0] == 2
     count = group if halved else len(pieces) * group
-    scalars = [place, *tables, order, starts]
-    held = [pair, small, *pieces]
+    scalars = [place, table, order, starts]
+    held = [pair, *pieces]
     distant = [front, incoming, out]
     spec = lambda space, n: [pl.BlockSpec(memory_space=space)] * n
     height = rows * TILE
     devices = incoming.shape[0]
     return pl.pallas_call(
         functools.partial(trailing_kernel, first, len(pieces), halved),
-        in_specs=spec(pltpu.SMEM, 5) + spec(pltpu.VMEM, len(held)) + spec(pltpu.HBM, 3),
+        in_specs=spec(pltpu.SMEM, 4) + spec(pltpu.VMEM, len(held)) + spec(pltpu.HBM, 3),
         out_specs=pl.BlockSpec(memory_space=pltpu.HBM),
         scratch_shapes=[
             pltpu.VMEM((3 * WIDTH, count * TILE), jnp.bfloat16),
@@ -455,7 +473,7 @@
         ]
         + [pltpu.VMEM((4, group, TILE, TILE), jnp.float32)] * halved,
         out_shape=jax.ShapeDtypeStruct(front.shape, jnp.float32),
-        input_output_aliases={len(held) + 7: 0},
+        input_output_aliases={len(held) + 6: 0},
         compiler_params=pltpu.CompilerParams(vmem_limit_bytes=VMEM),
         cost_estimate=pl.CostEstimate(
             flops=8 * count * 2 * height * TILE * WIDTH,
@@ -503,25 +521,19 @@
 
     def described(row, shift):
         if not ring:
-            return [a * sets + shift for a in range(rows_here)], list(range(n_col))
+            return [a * sets + shift for a in range(rows_here)]
         origin = circle[(circle.index(row) + shift) % n_row]
         part, group = origin % n_col, rows_here // n_col
-        columns = [(part * group + t) * sets + origin // n_col for t in range(group)]
-        return columns, [(part - c) % n_col for c in range(n_col)]
-
-    tables = [
-        jnp.asarray(
-            np.concatenate([described(row, shift)[k] for row in range(n_row) for shift in shifts]),
-            jnp.int32,
-        )
-        for k in range(2)
-    ]
+        return [(part * group + t) * sets + origin // n_col for t in range(group)]
+
+    table = np.concatenate([described(row, shift) for row in range(n_row) for shift in shifts])
+    table = jnp.asarray(table, jnp.int32)
 
     def updated(entries, panels, first):
         assert [shift for _, shift in entries] == shifts[first : first + len(entries)]
         pieces = [piece for piece, _ in entries]
         pieces = pieces[0] if isinstance(pieces[0], list) else pieces
-        out = trailing(front, pieces, first, place, tables, panels, incoming)
+        out = trailing(front, pieces, first, place, table, panels, incoming)
         return [panels[0], out, *panels[2:]]
 
     first = 0
@@ -535,7 +547,7 @@
             ]
             arrived.append(lax.ppermute(part, BOTH, pairs))
         arrived, mine, lead = lax.optimization_barrier((arrived, mine, lead))
-        piece = jnp.stack(arrived)
+        piece = piece_panels(arrived, lead, diag_inverses, place, True)
         up = [(circle[i], circle[(i + 1) % n_row]) for i in range(n_row)]
         down = [(b, a) for a, b in up]
         rounds = [[(piece, 0)]]
@@ -560,7 +572,11 @@
             for c in range(n_col)
         ]
         moved = lax.all_gather(lax.ppermute(parts[0], BOTH, pairs), "row", axis=0, tiled=False)
-        rounds = [[(moved[h * n_col : (h + 1) * n_col], h)] for h in range(sets)]
+        whole = [[moved[h * n_col + c] for c in range(n_col)] for h in range(sets)]
+        rounds = [
+            [(piece_panels(raw, lead, diag_inverses, place, False), h)]
+            for h, raw in enumerate(whole)
+        ]
         panels = own_panels(mine, lead)
 
     for entries in rounds:

time: 175 us -> 179 us (1.023)
  local copies, waits for them, and re-layouts: 1.21 us -> 7.9 us
  Pallas kernels: 58.4 us -> 52.6 us
  waiting for transfers between devices: 23.8 us -> 26.2 us
    unnamed x14 -> x22, local copies, waits for them, and re-layouts: 1.16 us -> 7.84 us
    pallas_call x5, Pallas kernels: 43.3 us -> 36.8 us  [trailing(): pl.pallas_call(functools.partial(trailing_kernel, first, len(pieces), hal...]
    ppermute x3, waiting for transfers between devices: 2.23 us -> 7.35 us  [body(): ahead = lax.ppermute(ahead, 'row', up)]
    ppermute x1, waiting for transfers between devices: 14.9 us -> 11.2 us  [exchange(): far = lax.ppermute(mine, 'col', [(c, c ^ 2) for c in range(n_col)])]
  transfers between devices with their start and end apart: 16 -> 16, of which waited for: 5 -> 6; matrix products, arithmetic and copies ran while one was open for 1% -> 0% of each run, Pallas kernels for 26% -> 23%
where the time goes in v17:
time: 179 us; the launch traced here: 178 us
  blocking collectives  65.5 us (37%)
  Pallas kernels  52.6 us (29%)
  waiting for transfers between devices  26.2 us (15%)
  starting transfers between devices  23.7 us (13%)
  local copies, waits for them, and re-layouts  7.9 us (4%)
    all_to_all x1, blocking collectives, body(): lax.all_to_all(outgoing, BOTH, split_axis=0, concat_axis=0, tiled=True)  65.5 us
    pallas_call x5, Pallas kernels, trailing(): pl.pallas_call(functools.partial(trailing_kernel, first, len(pieces), hal...  36.8 us
    ppermute x1, waiting for transfers between devices, exchange(): far = lax.ppermute(mine, 'col', [(c, c ^ 2) for c in range(n_col)])  11.2 us
    ppermute x4, starting transfers between devices, body(): arrived.append(lax.ppermute(part, BOTH, pairs))  7.86 us
    unnamed x22, local copies, waits for them, and re-layouts  7.84 us
    pallas_call x1, Pallas kernels, row_panels(): pl.pallas_call(row_panels_kernel, grid_spec=pltpu.PrefetchScalarGridSpec(...  7.78 us
    ppermute x3, waiting for transfers between devices, body(): ahead = lax.ppermute(ahead, 'row', up)  7.35 us
    ppermute x4, waiting for transfers between devices, body(): arrived.append(lax.ppermute(part, BOTH, pairs))  5.76 us
  transfers between devices with their start and end apart: 16, of which 6 were waited for; matrix products, arithmetic and copies ran while one was open for 0% of the time, Pallas kernels for 23%

profile of v17, /device:TPU:0, one launch (start us, length us, event | category | flops | bytes accessed | tf_op | source)
XLA Modules:
  0.0 178.1 jit_solution(4319929023605429356)
XLA Ops:
  0.7 0.6 pad_add_fusion.place
  1.3 0.0 copy-start.9
  1.3 3.2 %pack.1 = f32[32,152,128]{2,1,0:T(8,128)} custom-call(s32[4]{0:T(128)} %pad_add_fusion.place, s32[16]{0:T(128)} %bitcast.7, s32[16]{0:T(128)} %slot.1, s32[1]{0:T(128)S(6)} %copy.18.count, f32[16,128,128]{2,1,0:T(8,128)} %child_ref.1, f32[12,1,24,1,128,128]{5,4,3,2,1,0:T(8,128)} %rest_2_.7), custom_call_target="tpu_custom_call" | custom-call | tf_op jit(solution)/shard_map/pack/pallas_call | solution.py:123
  4.4 0.0 copy-start.1
  4.4 0.0 copy-start.10
  4.5 65.5 %all_to_all.10.incoming_ref.rest_3_.rest_2_ = f32[32,152,128]{2,1,0:T(8,128)S(1)} all-to-all(f32[32,152,128]{2,1,0:T(8,128)} %pack.1), channel_id=1, replica_groups=mesh['row'=8,'col'=4] {'row','col'}, dimensions={0} | all-to-all | bytes 4980736 | tf_op jit(solution)/shard_map/all_to_all | solution.py:501
  69.9 0.7 fusion.slot_in
  70.6 0.0 copy-done.9
  70.6 3.2 %panel_columns.1 = (f32[12,128,128]{2,1,0:T(8,128)}, f32[32,16,128]{2,1,0:T(8,128)}, f32[3,128,128]{2,1,0:T(8,128)}, f32[3,128,128]{2,1,0:T(8,128)}, f32[3,128,128]{2,1,0:T(8,128)}, /*index=5*/f32[3,128,128]{2,1,0:T(8,128)}) custom-call(s32[4]{0:T(128)S(1)} %copy-done.9, s32[32]{0:T(128)S(1)} %fusion.slot_in, f32[12,1,24,1,128,128]{5,4,3,2,1,0:T(8,128)} %rest_2_.7, ...), custom_call_target="tpu_custom_call" | custom-call | tf_op jit(solution)/shard_map/panel_columns/pallas_call | solution.py:183
  73.8 3.4 %all-to-all-start.1 = ((f32[32,16,128]{2,1,0:T(8,128)}), f32[32,16,128]{2,1,0:T(8,128)S(1)}, u32[]{:S(2)}, u32[]{:S(2)}) async-start(f32[32,16,128]{2,1,0:T(8,128)} %get-tuple-element.32), calls=%async_computation.1 | async-start | bytes 524288 | tf_op jit(solution)/shard_map/all_to_all | solution.py:506
  77.3 1.6 collective-permute-start
  78.8 2.3 %collective-permute-start.1 = (f32[3,128,128]{2,1,0:T(8,128)}, f32[3,128,128]{2,1,0:T(8,128)S(1)}, u32[]{:S(2)}, u32[]{:S(2)}) collective-permute-start(f32[3,128,128]{2,1,0:T(8,128)} %get-tuple-element.28), channel_id=1, source_target_pairs={{0,4},{1,8},{2,12},{3,0},{4,5},{5,9},{6,13},{7,1},{8,6},{9,10},{10... | collective-permute-start | bytes 589832 | tf_op jit(solution)/shard_map/ppermute | solution.py:548
  81.1 3.5 %collective-permute-start.2 = (f32[3,128,128]{2,1,0:T(8,128)}, f32[3,128,128]{2,1,0:T(8,128)S(1)}, u32[]{:S(2)}, u32[]{:S(2)}) collective-permute-start(f32[3,128,128]{2,1,0:T(8,128)} %get-tuple-element.29), channel_id=1, source_target_pairs={{0,8},{1,12},{2,0},{3,4},{4,9},{5,13},{6,1},{7,5},{8,10},{9,14},{1... | collective-permute-start | bytes 589832 | tf_op jit(solution)/shard_map/ppermute | solution.py:548
  84.6 0.5 collective-permute-start.3
  85.1 0.0 collective-permute-done.t0
  85.1 5.8 %collective-permute-done.1.t1 = f32[3,128,128]{2,1,0:T(8,128)S(1)} collective-permute-done((f32[3,128,128]{2,1,0:T(8,128)}, f32[3,128,128]{2,1,0:T(8,128)S(1)}, u32[]{:S(2)}, u32[]{:S(2)}) %collective-permute-start.1) | collective-permute-done | bytes 196640 | tf_op jit(solution)/shard_map/ppermute | solution.py:548
  90.9 0.0 copy-start.3
  90.9 0.7 copy-done.3
  91.6 0.0 collective-permute-done.2.t2
  91.6 0.0 copy-start.5
  91.6 0.7 copy-done.5
  92.2 0.0 collective-permute-done.3.t3
  92.2 0.0 copy-start.7
  92.2 0.7 copy-done.7
  92.9 0.0 all-to-all-done.1
  92.9 3.3 %collective-permute-start.9 = (f32[12,128,128]{2,1,0:T(8,128)}, f32[12,128,128]{2,1,0:T(8,128)S(1)}, u32[]{:S(2)}, u32[]{:S(2)}) collective-permute-start(f32[12,128,128]{2,1,0:T(8,128)} %get-tuple-element.38.t0), channel_id=1, source_target_pairs={{0,2},{1,3},{2,0},{3,1},{4,6},{5,7},{6,4},{7,5},{8,10},{9,11},{10,... | collective-permute-start | bytes 2359304 | tf_op jit(solution)/shard_map/ppermute | solution.py:511
  96.3 0.0 copy-done.1
  96.3 0.9 copy-done.4
  97.2 0.0 copy-start.6
  97.2 0.9 copy-done.6
  98.1 0.0 copy-start.8
  98.1 0.9 copy-done.8
  99.0 1.7 piece_panels.1.rest_0_
  100.8 0.1 collective-permute-start.4
  100.8 2.6 %collective-permute-start.6 = (f32[4,3,128,128]{3,2,1,0:T(8,128)S(1)}, f32[4,3,128,128]{3,2,1,0:T(8,128)S(1)}, u32[]{:S(2)}, u32[]{:S(2)}) collective-permute-start(f32[4,3,128,128]{3,2,1,0:T(8,128)S(1)} %piece_panels.1.rest_0_), channel_id=1, source_target_pairs={{8,0},{16,8},{24,16},{28,24},{20,28},{12,20},{4,12},{0,4},{9,1},{1... | collective-permute-start | bytes 2359304 | tf_op jit(solution)/shard_map/ppermute | solution.py:558
  103.4 0.0 collective-permute-start.8
  103.4 11.2 %collective-permute-done.9.t2 = f32[12,128,128]{2,1,0:T(8,128)S(1)} collective-permute-done((f32[12,128,128]{2,1,0:T(8,128)}, f32[12,128,128]{2,1,0:T(8,128)S(1)}, u32[]{:S(2)}, u32[]{:S(2)}) %collective-permute-start.9) | collective-permute-done | bytes 786464 | tf_op jit(solution)/shard_map/ppermute | solution.py:511
  114.6 0.3 collective-permute-start.10
  115.0 5.6 %collective-permute-done.4.rest_1_ = f32[4,3,128,128]{3,2,1,0:T(8,128)S(1)} collective-permute-done((f32[4,3,128,128]{3,2,1,0:T(8,128)S(1)}, f32[4,3,128,128]{3,2,1,0:T(8,128)S(1)}, u32[]{:S(2)}, u32[]{:S(2)}) %collective-permute-start.4) | collective-permute-done | bytes 786464 | tf_op jit(solution)/shard_map/ppermute | solution.py:557
  120.6 0.3 collective-permute-start.5
  120.9 0.5 collective-permute-done.6.rest_0_
  121.4 1.2 collective-permute-start.7
  122.6 0.0 collective-permute-done.8.t1
  122.6 0.0 collective-permute-done.10.t3
  122.6 0.0 copy-start.2
  122.6 1.1 copy-done.2
  123.7 7.8 %row_panels.1 = (bf16[1536,1024]{1,0:T(8,128)(2,1)}, f32[12,1,24,1,128,128]{5,4,3,2,1,0:T(8,128)}, s32[64]{0:T(128)S(1)}, s32[25]{0:T(128)S(1)}) custom-call(s32[4]{0:T(128)S(1)} %copy-done.9, s32[32]{0:T(128)S(1)} %fusion.slot_in, f32[12,128,128]{2,1,0:T(8,128)S(1)} %copy-done.2, f32[12,128,128]{2,1,0:T(8,128)S(1)} %collective-permute-done.8.t1, ...), custom_call_target="tpu_custom_call" | custom-call | tf_op jit(solution)/shard_map/row_panels/pallas_call | solution.py:319
  131.5 0.0 copy-done.10
  131.5 1.9 %copy-done = bf16[1536,1024]{1,0:T(8,128)(2,1)S(1)} copy-done((bf16[1536,1024]{1,0:T(8,128)(2,1)S(1)}, bf16[1536,1024]{1,0:T(8,128)(2,1)}, u32[]{:S(2)}) %copy-start) | copy-done | bytes 3145752
  133.4 7.8 %trailing.5.rest_4_ = f32[12,1,24,1,128,128]{5,4,3,2,1,0:T(8,128)} custom-call(s32[4]{0:T(128)S(1)} %copy-done.9, s32[192]{0:T(256)S(1)} %copy-done.10, s32[64]{0:T(128)S(1)} %get-tuple-element.43.order, s32[25]{0:T(128)S(1)} %get-tuple-element.44.starts, bf16[1536,1024]{1,0:T(8,128)(2,1)S(1)} %copy-done, ...), custom_call_target="tpu_custom_call", output_to_operand_aliasing={{}: (9, {})} | custom-call | flops 9663676416 | bytes 9437184 | tf_op jit(solution)/shard_map/trailing/pallas_call | solution.py:461
  141.2 0.0 collective-permute-done.5.rest_1_
  141.2 0.0 collective-permute-done.7.rest_0_
  141.3 1.4 collective-permute-start.11
  142.6 1.0 collective-permute-start.13
  143.6 8.3 %trailing.6.rest_3_ = f32[12,1,24,1,128,128]{5,4,3,2,1,0:T(8,128)} custom-call(s32[4]{0:T(128)S(1)} %copy-done.9, s32[192]{0:T(256)S(1)} %copy-done.10, s32[64]{0:T(128)S(1)} %get-tuple-element.43.order, s32[25]{0:T(128)S(1)} %get-tuple-element.44.starts, bf16[1536,1024]{1,0:T(8,128)(2,1)S(1)} %copy-done, ...), custom_call_target="tpu_custom_call", output_to_operand_aliasing={{}: (9, {})} | custom-call | flops 9663676416 | bytes 9437184 | tf_op jit(solution)/shard_map/trailing/pallas_call | solution.py:461
  152.0 6.2 %trailing.7.rest_4_ = f32[12,1,24,1,128,128]{5,4,3,2,1,0:T(8,128)} custom-call(s32[4]{0:T(128)S(1)} %copy-done.9, s32[192]{0:T(256)S(1)} %copy-done.10, s32[64]{0:T(128)S(1)} %get-tuple-element.43.order, s32[25]{0:T(128)S(1)} %get-tuple-element.44.starts, bf16[1536,1024]{1,0:T(8,128)(2,1)S(1)} %copy-done, ...), custom_call_target="tpu_custom_call", output_to_operand_aliasing={{}: (8, {})} | custom-call | flops 4831838208 | bytes 4718592 | tf_op jit(solution)/shard_map/trailing/pallas_call | solution.py:461
  158.1 1.7 collective-permute-done.11.rest_0_
  159.9 2.1 %collective-permute-start.12 = (f32[2,3,128,128]{3,2,1,0:T(8,128)S(1)}, f32[2,3,128,128]{3,2,1,0:T(8,128)S(1)}, u32[]{:S(2)}, u32[]{:S(2)}) collective-permute-start(f32[2,3,128,128]{3,2,1,0:T(8,128)S(1)} %slice.13), channel_id=1, source_target_pairs={{0,8},{8,16},{16,24},{24,28},{28,20},{20,12},{12,4},{4,0},{1,9},{9... | collective-permute-start | bytes 1179656 | tf_op jit(solution)/shard_map/ppermute | solution.py:563
  162.0 0.0 collective-permute-done.13.rest_1_
  162.0 0.1 collective-permute-start.14
  162.1 8.3 %trailing.8.rest_4_ = f32[12,1,24,1,128,128]{5,4,3,2,1,0:T(8,128)} custom-call(s32[4]{0:T(128)S(1)} %copy-done.9, s32[192]{0:T(256)S(1)} %copy-done.10, s32[64]{0:T(128)S(1)} %get-tuple-element.43.order, s32[25]{0:T(128)S(1)} %get-tuple-element.44.starts, bf16[1536,1024]{1,0:T(8,128)(2,1)S(1)} %copy-done, ...), custom_call_target="tpu_custom_call", output_to_operand_aliasing={{}: (9, {})} | custom-call | flops 9663676416 | bytes 9437184 | tf_op jit(solution)/shard_map/trailing/pallas_call | solution.py:461
  170.4 0.0 collective-permute-done.12.rest_0_
  170.4 1.4 collective-permute-done.14.rest_1_
  171.8 6.2 %trailing.9 = f32[12,1,24,1,128,128]{5,4,3,2,1,0:T(8,128)} custom-call(s32[4]{0:T(128)S(1)} %copy-done.9, s32[192]{0:T(256)S(1)} %copy-done.10, s32[64]{0:T(128)S(1)} %get-tuple-element.43.order, s32[25]{0:T(128)S(1)} %get-tuple-element.44.starts, bf16[1536,1024]{1,0:T(8,128)(2,1)S(1)} %copy-done, ...), custom_call_target="tpu_custom_call", output_to_operand_aliasing={{}: (9, {})} | custom-call | flops 4831838208 | bytes 4718592 | tf_op jit(solution)/shard_map/trailing/pallas_call | solution.py:461
  (4 shorter events, 0.1 us)
Async XLA Ops:
  1.3 69.3 %copy-start.9 = (s32[4]{0:T(128)S(1)}, s32[4]{0:T(128)}, u32[]{:S(2)}) copy-start(s32[4]{0:T(128)} %pad_add_fusion.place) | copy-start | bytes 52
  4.4 91.8 %copy-start.1 = (f32[2,256,256]{2,1,0:T(8,128)S(1)}, f32[2,256,256]{2,1,0:T(8,128)}, u32[]{:S(2)}) copy-start(f32[2,256,256]{2,1,0:T(8,128)} %diag_ref.3) | copy-start | bytes 1572868
  4.4 127.1 %copy-start.10 = (s32[192]{0:T(256)S(1)}, s32[192]{0:T(256)}, u32[]{:S(2)}) copy-start(s32[192]{0:T(256)} %constant.15.clone.columns_table) | copy-start | bytes 2308
  73.8 19.1 %all-to-all-start.1 = ((f32[32,16,128]{2,1,0:T(8,128)}), f32[32,16,128]{2,1,0:T(8,128)S(1)}, u32[]{:S(2)}, u32[]{:S(2)}) async-start(f32[32,16,128]{2,1,0:T(8,128)} %get-tuple-element.32), calls=%async_computation.1 | async-start | bytes 524288 | tf_op jit(solution)/shard_map/all_to_all | solution.py:506
  77.3 7.9 %collective-permute-start = (f32[3,128,128]{2,1,0:T(8,128)}, f32[3,128,128]{2,1,0:T(8,128)S(1)}, u32[]{:S(2)}, u32[]{:S(2)}) collective-permute-start(f32[3,128,128]{2,1,0:T(8,128)} %get-tuple-element.27), channel_id=1, source_target_pairs={{0,0},{1,4},{2,8},{3,12},{4,1},{5,5},{6,9},{7,13},{8,2},{9,6},{10,... | collective-permute-start | bytes 589832 | tf_op jit(solution)/shard_map/ppermute | solution.py:548
  78.8 12.0 %collective-permute-start.1 = (f32[3,128,128]{2,1,0:T(8,128)}, f32[3,128,128]{2,1,0:T(8,128)S(1)}, u32[]{:S(2)}, u32[]{:S(2)}) collective-permute-start(f32[3,128,128]{2,1,0:T(8,128)} %get-tuple-element.28), channel_id=1, source_target_pairs={{0,4},{1,8},{2,12},{3,0},{4,5},{5,9},{6,13},{7,1},{8,6},{9,10},{10... | collective-permute-start | bytes 589832 | tf_op jit(solution)/shard_map/ppermute | solution.py:548
  81.1 10.4 %collective-permute-start.2 = (f32[3,128,128]{2,1,0:T(8,128)}, f32[3,128,128]{2,1,0:T(8,128)S(1)}, u32[]{:S(2)}, u32[]{:S(2)}) collective-permute-start(f32[3,128,128]{2,1,0:T(8,128)} %get-tuple-element.29), channel_id=1, source_target_pairs={{0,8},{1,12},{2,0},{3,4},{4,9},{5,13},{6,1},{7,5},{8,10},{9,14},{1... | collective-permute-start | bytes 589832 | tf_op jit(solution)/shard_map/ppermute | solution.py:548
  84.6 7.7 %collective-permute-start.3 = (f32[3,128,128]{2,1,0:T(8,128)}, f32[3,128,128]{2,1,0:T(8,128)S(1)}, u32[]{:S(2)}, u32[]{:S(2)}) collective-permute-start(f32[3,128,128]{2,1,0:T(8,128)} %get-tuple-element.30), channel_id=1, source_target_pairs={{0,12},{1,0},{2,4},{3,8},{4,13},{5,1},{6,5},{7,9},{8,14},{9,2},{10... | collective-permute-start | bytes 589832 | tf_op jit(solution)/shard_map/ppermute | solution.py:548
  90.9 0.7 copy-start.3
  91.6 0.7 copy-start.5
  92.2 0.7 copy-start.7
  92.9 21.7 %collective-permute-start.9 = (f32[12,128,128]{2,1,0:T(8,128)}, f32[12,128,128]{2,1,0:T(8,128)S(1)}, u32[]{:S(2)}, u32[]{:S(2)}) collective-permute-start(f32[12,128,128]{2,1,0:T(8,128)} %get-tuple-element.38.t0), channel_id=1, source_target_pairs={{0,2},{1,3},{2,0},{3,1},{4,6},{5,7},{6,4},{7,5},{8,10},{9,11},{10,... | collective-permute-start | bytes 2359304 | tf_op jit(solution)/shard_map/ppermute | solution.py:511
  96.3 0.9 copy-start.4
  97.2 0.9 copy-start.6
  98.1 0.9 copy-start.8
  100.8 19.8 %collective-permute-start.4 = (f32[4,3,128,128]{3,2,1,0:T(8,128)S(1)}, f32[4,3,128,128]{3,2,1,0:T(8,128)S(1)}, u32[]{:S(2)}, u32[]{:S(2)}) collective-permute-start(f32[4,3,128,128]{3,2,1,0:T(8,128)S(1)} %piece_panels.1.rest_0_), channel_id=1, source_target_pairs={{0,8},{8,16},{16,24},{24,28},{28,20},{20,12},{12,4},{4,0},{1,9},{9... | collective-permute-start | bytes 2359304 | tf_op jit(solution)/shard_map/ppermute | solution.py:557
  100.8 20.6 %collective-permute-start.6 = (f32[4,3,128,128]{3,2,1,0:T(8,128)S(1)}, f32[4,3,128,128]{3,2,1,0:T(8,128)S(1)}, u32[]{:S(2)}, u32[]{:S(2)}) collective-permute-start(f32[4,3,128,128]{3,2,1,0:T(8,128)S(1)} %piece_panels.1.rest_0_), channel_id=1, source_target_pairs={{8,0},{16,8},{24,16},{28,24},{20,28},{12,20},{4,12},{0,4},{9,1},{1... | collective-permute-start | bytes 2359304 | tf_op jit(solution)/shard_map/ppermute | solution.py:558
  103.4 19.2 %collective-permute-start.8 = (f32[12,128,128]{2,1,0:T(8,128)}, f32[12,128,128]{2,1,0:T(8,128)S(1)}, u32[]{:S(2)}, u32[]{:S(2)}) collective-permute-start(f32[12,128,128]{2,1,0:T(8,128)} %get-tuple-element.38.t0), channel_id=1, source_target_pairs={{0,1},{1,0},{2,3},{3,2},{4,5},{5,4},{6,7},{7,6},{8,9},{9,8},{10,11... | collective-permute-start | bytes 2359304 | tf_op jit(solution)/shard_map/ppermute | solution.py:510
  114.6 8.0 %collective-permute-start.10 = (f32[12,128,128]{2,1,0:T(8,128)S(1)}, f32[12,128,128]{2,1,0:T(8,128)S(1)}, u32[]{:S(2)}, u32[]{:S(2)}) collective-permute-start(f32[12,128,128]{2,1,0:T(8,128)S(1)} %collective-permute-done.9.t2), channel_id=1, source_target_pairs={{0,1},{1,0},{2,3},{3,2},{4,5},{5,4},{6,7},{7,6},{8,9},{9,8},{10,11... | collective-permute-start | bytes 2359304 | tf_op jit(solution)/shard_map/ppermute | solution.py:512
  120.6 20.7 %collective-permute-start.5 = (f32[4,3,128,128]{3,2,1,0:T(8,128)S(1)}, f32[4,3,128,128]{3,2,1,0:T(8,128)S(1)}, u32[]{:S(2)}, u32[]{:S(2)}) collective-permute-start(f32[4,3,128,128]{3,2,1,0:T(8,128)S(1)} %collective-permute-done.4.rest_1_), channel_id=1, source_target_pairs={{0,8},{8,16},{16,24},{24,28},{28,20},{20,12},{12,4},{4,0},{1,9},{9... | collective-permute-start | bytes 2359304 | tf_op jit(solution)/shard_map/ppermute | solution.py:557
  121.4 19.9 %collective-permute-start.7 = (f32[4,3,128,128]{3,2,1,0:T(8,128)S(1)}, f32[4,3,128,128]{3,2,1,0:T(8,128)S(1)}, u32[]{:S(2)}, u32[]{:S(2)}) collective-permute-start(f32[4,3,128,128]{3,2,1,0:T(8,128)S(1)} %collective-permute-done.6.rest_0_), channel_id=1, source_target_pairs={{8,0},{16,8},{24,16},{28,24},{20,28},{12,20},{4,12},{0,4},{9,1},{1... | collective-permute-start | bytes 2359304 | tf_op jit(solution)/shard_map/ppermute | solution.py:558
  122.6 1.1 copy-start.2
  131.5 1.9 %copy-start = (bf16[1536,1024]{1,0:T(8,128)(2,1)S(1)}, bf16[1536,1024]{1,0:T(8,128)(2,1)}, u32[]{:S(2)}) copy-start(bf16[1536,1024]{1,0:T(8,128)(2,1)} %get-tuple-element.45.pair_ref) | copy-start | bytes 9437188
  141.3 18.6 %collective-permute-start.11 = (f32[4,3,128,128]{3,2,1,0:T(8,128)S(1)}, f32[4,3,128,128]{3,2,1,0:T(8,128)S(1)}, u32[]{:S(2)}, u32[]{:S(2)}) collective-permute-start(f32[4,3,128,128]{3,2,1,0:T(8,128)S(1)} %collective-permute-done.5.rest_1_), channel_id=1, source_target_pairs={{0,8},{8,16},{16,24},{24,28},{28,20},{20,12},{12,4},{4,0},{1,9},{9... | collective-permute-start | bytes 2359304 | tf_op jit(solution)/shard_map/ppermute | solution.py:557
  142.6 19.4 %collective-permute-start.13 = (f32[4,3,128,128]{3,2,1,0:T(8,128)S(1)}, f32[4,3,128,128]{3,2,1,0:T(8,128)S(1)}, u32[]{:S(2)}, u32[]{:S(2)}) collective-permute-start(f32[4,3,128,128]{3,2,1,0:T(8,128)S(1)} %collective-permute-done.7.rest_0_), channel_id=1, source_target_pairs={{8,0},{16,8},{24,16},{28,24},{20,28},{12,20},{4,12},{0,4},{9,1},{1... | collective-permute-start | bytes 2359304 | tf_op jit(solution)/shard_map/ppermute | solution.py:558
  159.9 10.5 %collective-permute-start.12 = (f32[2,3,128,128]{3,2,1,0:T(8,128)S(1)}, f32[2,3,128,128]{3,2,1,0:T(8,128)S(1)}, u32[]{:S(2)}, u32[]{:S(2)}) collective-permute-start(f32[2,3,128,128]{3,2,1,0:T(8,128)S(1)} %slice.13), channel_id=1, source_target_pairs={{0,8},{8,16},{16,24},{24,28},{28,20},{20,12},{12,4},{4,0},{1,9},{9... | collective-permute-start | bytes 1179656 | tf_op jit(solution)/shard_map/ppermute | solution.py:563
  162.0 9.8 %collective-permute-start.14 = (f32[2,3,128,128]{3,2,1,0:T(8,128)S(1)}, f32[2,3,128,128]{3,2,1,0:T(8,128)S(1)}, u32[]{:S(2)}, u32[]{:S(2)}) collective-permute-start(f32[2,3,128,128]{3,2,1,0:T(8,128)S(1)} %slice.14), channel_id=1, source_target_pairs={{8,0},{16,8},{24,16},{28,24},{20,28},{12,20},{4,12},{0,4},{9,1},{1... | collective-permute-start | bytes 1179656 | tf_op jit(solution)/shard_map/ppermute | solution.py:563

commit v18 on v17

--- a/solution.py
+++ b/solution.py
@@ -206,10 +206,8 @@
     )
 
 
-def piece_panels_kernel(rolled, place, t0, t1, t2, t3, lead_ref, diag_ref, out_ref, tiles_ref):
-    group = t0.shape[0]
-    for i, tile_ref in enumerate((t0, t1, t2, t3)):
-        tiles_ref[i] = tile_ref[...]
+def piece_panels_kernel(rolled, place, tiles_ref, lead_ref, diag_ref, out_ref):
+    group = tiles_ref.shape[1]
     lead = dot(deep(square(lead_ref)), stacked(diag_ref[0]))
     small = [deep(diag_ref[0].T), deep(lead), deep(diag_ref[1].T)]
     columns = []
@@ -224,18 +222,16 @@
                 ]
 
 
-def piece_panels(parts, lead, diag, place, rolled):
-    shape = (4, *parts[0].shape)
+def piece_panels(piece, lead, diag, place, rolled):
     return pl.pallas_call(
         functools.partial(piece_panels_kernel, rolled),
         in_specs=[pl.BlockSpec(memory_space=pltpu.SMEM)]
-        + [pl.BlockSpec(memory_space=pltpu.VMEM)] * 6,
+        + [pl.BlockSpec(memory_space=pltpu.VMEM)] * 3,
         out_specs=pl.BlockSpec(memory_space=pltpu.VMEM),
-        scratch_shapes=[pltpu.VMEM(shape, jnp.float32)],
-        out_shape=jax.ShapeDtypeStruct(shape, jnp.float32),
+        out_shape=jax.ShapeDtypeStruct(piece.shape, jnp.float32),
         compiler_params=pltpu.CompilerParams(vmem_limit_bytes=VMEM),
         name="piece_panels",
-    )(place, *parts, lead, diag)
+    )(place, piece, lead, diag)
 
 
 def row_panels_kernel(
@@ -547,7 +543,7 @@
             ]
             arrived.append(lax.ppermute(part, BOTH, pairs))
         arrived, mine, lead = lax.optimization_barrier((arrived, mine, lead))
-        piece = piece_panels(arrived, lead, diag_inverses, place, True)
+        piece = piece_panels(jnp.stack(arrived), lead, diag_inverses, place, True)
         up = [(circle[i], circle[(i + 1) % n_row]) for i in range(n_row)]
         down = [(b, a) for a, b in up]
         rounds = [[(piece, 0)]]
@@ -557,13 +553,12 @@
             ahead = lax.ppermute(ahead, "row", up)
             behind = lax.ppermute(behind, "row", down)
             if step == 2:
-                panels = updated([*rounds[0], rounds[1][0]], panels, 0)
+                panels = updated(rounds[0], panels, 0)
                 ahead, behind, panels = lax.optimization_barrier((ahead, behind, panels))
             rounds.append([(ahead, -step), (behind, step)])
         last = [lax.ppermute(ahead[:2], "row", up), lax.ppermute(behind[2:], "row", down)]
-        late = [entry for entries in rounds for entry in entries][2:]
-        rounds = [late[:2], late[2:3], *rounds[3:], [(last, n_row // 2)]]
-        first = 2
+        rounds = [*rounds[1:], [(last, n_row // 2)]]
+        first = 1
 
     else:
         pairs = [
@@ -572,10 +567,10 @@
             for c in range(n_col)
         ]
         moved = lax.all_gather(lax.ppermute(parts[0], BOTH, pairs), "row", axis=0, tiled=False)
-        whole = [[moved[h * n_col + c] for c in range(n_col)] for h in range(sets)]
+        raw = [moved[h * n_col : (h + 1) * n_col] for h in range(sets)]
         rounds = [
-            [(piece_panels(raw, lead, diag_inverses, place, False), h)]
-            for h, raw in enumerate(whole)
+            [(piece_panels(piece, lead, diag_inverses, place, False), h)]
+            for h, piece in enumerate(raw)
         ]
         panels = own_panels(mine, lead)
 

time: 179 us -> 174 us (0.972)
  local copies, waits for them, and re-layouts: 7.9 us -> 3.78 us
    unnamed x22 -> x12, local copies, waits for them, and re-layouts: 7.84 us -> 3.73 us
    ppermute x3, waiting for transfers between devices: 7.35 us -> 3.67 us  [body(): ahead = lax.ppermute(ahead, 'row', up)]
    ppermute x1, waiting for transfers between devices: 11.2 us -> 13.5 us  [exchange(): far = lax.ppermute(mine, 'col', [(c, c ^ 2) for c in range(n_col)])]
  transfers between devices with their start and end apart: 16 -> 16, of which waited for: 6 -> 6; matrix products, arithmetic and copies ran while one was open for 0% -> 1% of each run, Pallas kernels for 23% -> 23%
where the time goes in v18:
time: 174 us
  blocking collectives  65.3 us (38%)
  Pallas kernels  53.1 us (31%)
  waiting for transfers between devices  25.3 us (15%)
  starting transfers between devices  22.9 us (13%)
  local copies, waits for them, and re-layouts  3.78 us (2%)
  other arithmetic  2.43 us (1%)
    all_to_all x1, blocking collectives, body(): lax.all_to_all(outgoing, BOTH, split_axis=0, concat_axis=0, tiled=True)  65.3 us
    pallas_call x5, Pallas kernels, trailing(): pl.pallas_call(functools.partial(trailing_kernel, first, len(pieces), hal...  37 us
    ppermute x1, waiting for transfers between devices, exchange(): far = lax.ppermute(mine, 'col', [(c, c ^ 2) for c in range(n_col)])  13.5 us
    ppermute x4, starting transfers between devices, body(): arrived.append(lax.ppermute(part, BOTH, pairs))  7.86 us
    pallas_call x1, Pallas kernels, row_panels(): pl.pallas_call(row_panels_kernel, grid_spec=pltpu.PrefetchScalarGridSpec(...  7.78 us
    ppermute x4, waiting for transfers between devices, body(): arrived.append(lax.ppermute(part, BOTH, pairs))  6.19 us
    ppermute x3, starting transfers between devices, body(): behind = lax.ppermute(behind, 'row', down)  4.25 us
    unnamed x12, local copies, waits for them, and re-layouts  3.73 us
  transfers between devices with their start and end apart: 16, of which 6 were waited for; matrix products, arithmetic and copies ran while one was open for 1% of the time, Pallas kernels for 23%

profile of v18, /device:TPU:0, one launch (start us, length us, event | category | flops | bytes accessed | tf_op | source)
XLA Modules:
  0.0 173.9 jit_solution(1500884968715210313)
XLA Ops:
  0.7 0.6 pad_add_fusion.place
  1.3 0.0 copy-start.3
  1.3 3.4 %pack.1 = f32[32,152,128]{2,1,0:T(8,128)} custom-call(s32[4]{0:T(128)} %pad_add_fusion.place, s32[16]{0:T(128)} %bitcast.13, s32[16]{0:T(128)} %slot.1, s32[1]{0:T(128)S(6)} %copy.18.count, f32[16,128,128]{2,1,0:T(8,128)} %child_ref.1, f32[12,1,24,1,128,128]{5,4,3,2,1,0:T(8,128)} %rest_2_.7), custom_call_target="tpu_custom_call" | custom-call | tf_op jit(solution)/shard_map/pack/pallas_call | solution.py:123
  4.6 0.0 copy-start.1
  4.7 0.0 copy-start.4
  4.7 65.3 %all_to_all.10.incoming_ref.rest_2_.rest_3_ = f32[32,152,128]{2,1,0:T(8,128)S(1)} all-to-all(f32[32,152,128]{2,1,0:T(8,128)} %pack.1), channel_id=1, replica_groups=mesh['row'=8,'col'=4] {'row','col'}, dimensions={0} | all-to-all | bytes 4980736 | tf_op jit(solution)/shard_map/all_to_all | solution.py:497
  70.0 0.7 fusion.slot_in
  70.6 0.0 copy-done.3
  70.7 3.2 %panel_columns.1 = (f32[12,128,128]{2,1,0:T(8,128)}, f32[32,16,128]{2,1,0:T(8,128)}, f32[3,128,128]{2,1,0:T(8,128)}, f32[3,128,128]{2,1,0:T(8,128)}, f32[3,128,128]{2,1,0:T(8,128)}, /*index=5*/f32[3,128,128]{2,1,0:T(8,128)}) custom-call(s32[4]{0:T(128)S(1)} %copy-done.3, s32[32]{0:T(128)S(1)} %fusion.slot_in, f32[12,1,24,1,128,128]{5,4,3,2,1,0:T(8,128)} %rest_2_.7, ...), custom_call_target="tpu_custom_call" | custom-call | tf_op jit(solution)/shard_map/panel_columns/pallas_call | solution.py:183
  73.9 3.2 %all-to-all-start.1 = ((f32[32,16,128]{2,1,0:T(8,128)}), f32[32,16,128]{2,1,0:T(8,128)S(1)}, u32[]{:S(2)}, u32[]{:S(2)}) async-start(f32[32,16,128]{2,1,0:T(8,128)} %get-tuple-element.32), calls=%async_computation.1 | async-start | bytes 524288 | tf_op jit(solution)/shard_map/all_to_all | solution.py:502
  77.1 1.6 collective-permute-start
  78.7 2.3 %collective-permute-start.1 = (f32[3,128,128]{2,1,0:T(8,128)}, f32[3,128,128]{2,1,0:T(8,128)}, u32[]{:S(2)}, u32[]{:S(2)}) collective-permute-start(f32[3,128,128]{2,1,0:T(8,128)} %get-tuple-element.28), channel_id=1, source_target_pairs={{0,4},{1,8},{2,12},{3,0},{4,5},{5,9},{6,13},{7,1},{8,6},{9,10},{10... | collective-permute-start | bytes 589832 | tf_op jit(solution)/shard_map/ppermute | solution.py:544
  80.9 3.5 %collective-permute-start.2 = (f32[3,128,128]{2,1,0:T(8,128)}, f32[3,128,128]{2,1,0:T(8,128)S(1)}, u32[]{:S(2)}, u32[]{:S(2)}) collective-permute-start(f32[3,128,128]{2,1,0:T(8,128)} %get-tuple-element.29), channel_id=1, source_target_pairs={{0,8},{1,12},{2,0},{3,4},{4,9},{5,13},{6,1},{7,5},{8,10},{9,14},{1... | collective-permute-start | bytes 589832 | tf_op jit(solution)/shard_map/ppermute | solution.py:544
  84.4 0.5 collective-permute-start.3
  84.9 0.0 collective-permute-done
  84.9 5.9 %collective-permute-done.1 = f32[3,128,128]{2,1,0:T(8,128)} collective-permute-done((f32[3,128,128]{2,1,0:T(8,128)}, f32[3,128,128]{2,1,0:T(8,128)}, u32[]{:S(2)}, u32[]{:S(2)}) %collective-permute-start.1) | collective-permute-done | bytes 196640 | tf_op jit(solution)/shard_map/ppermute | solution.py:544
  90.8 0.3 collective-permute-done.2
  91.1 0.0 copy-start.5
  91.1 0.7 copy-done.5
  91.8 0.0 collective-permute-done.3
  91.8 0.0 all-to-all-done.1
  91.8 3.7 %collective-permute-start.9 = (f32[12,128,128]{2,1,0:T(8,128)}, f32[12,128,128]{2,1,0:T(8,128)S(1)}, u32[]{:S(2)}, u32[]{:S(2)}) collective-permute-start(f32[12,128,128]{2,1,0:T(8,128)} %get-tuple-element.38.t0), channel_id=1, source_target_pairs={{0,2},{1,3},{2,0},{3,1},{4,6},{5,7},{6,4},{7,5},{8,10},{9,11},{10,... | collective-permute-start | bytes 2359304 | tf_op jit(solution)/shard_map/ppermute | solution.py:507
  95.5 1.2 pad_maximum_fusion.tiles_ref
  96.7 0.0 copy-done.1
  96.7 1.7 piece_panels.1.rest_0_
  98.4 0.1 collective-permute-start.4
  98.4 2.0 %collective-permute-start.6 = (f32[4,3,128,128]{3,2,1,0:T(8,128)S(1)}, f32[4,3,128,128]{3,2,1,0:T(8,128)S(1)}, u32[]{:S(2)}, u32[]{:S(2)}) collective-permute-start(f32[4,3,128,128]{3,2,1,0:T(8,128)S(1)} %piece_panels.1.rest_0_), channel_id=1, source_target_pairs={{8,0},{16,8},{24,16},{28,24},{20,28},{12,20},{4,12},{0,4},{9,1},{1... | collective-permute-start | bytes 2359304 | tf_op jit(solution)/shard_map/ppermute | solution.py:554
  100.5 0.0 collective-permute-start.8
  100.5 13.5 %collective-permute-done.9.t2 = f32[12,128,128]{2,1,0:T(8,128)S(1)} collective-permute-done((f32[12,128,128]{2,1,0:T(8,128)}, f32[12,128,128]{2,1,0:T(8,128)S(1)}, u32[]{:S(2)}, u32[]{:S(2)}) %collective-permute-start.9) | collective-permute-done | bytes 786464 | tf_op jit(solution)/shard_map/ppermute | solution.py:507
  114.0 0.2 collective-permute-start.10
  114.2 3.7 %collective-permute-done.4.rest_0_ = f32[4,3,128,128]{3,2,1,0:T(8,128)S(1)} collective-permute-done((f32[4,3,128,128]{3,2,1,0:T(8,128)S(1)}, f32[4,3,128,128]{3,2,1,0:T(8,128)S(1)}, u32[]{:S(2)}, u32[]{:S(2)}) %collective-permute-start.4) | collective-permute-done | bytes 786464 | tf_op jit(solution)/shard_map/ppermute | solution.py:553
  117.9 0.7 collective-permute-start.5
  118.6 0.3 collective-permute-done.6.rest_1_
  118.9 1.0 collective-permute-start.7
  119.9 0.0 collective-permute-done.8.t1
  119.9 0.0 collective-permute-done.10.t3
  119.9 0.0 copy-start.2
  119.9 1.1 copy-done.2
  121.0 7.8 %row_panels.1 = (bf16[1536,1024]{1,0:T(8,128)(2,1)}, f32[12,1,24,1,128,128]{5,4,3,2,1,0:T(8,128)}, s32[64]{0:T(128)S(1)}, s32[25]{0:T(128)S(1)}) custom-call(s32[4]{0:T(128)S(1)} %copy-done.3, s32[32]{0:T(128)S(1)} %fusion.slot_in, f32[12,128,128]{2,1,0:T(8,128)S(1)} %copy-done.2, f32[12,128,128]{2,1,0:T(8,128)S(1)} %collective-permute-done.8.t1, ...), custom_call_target="tpu_custom_call" | custom-call | tf_op jit(solution)/shard_map/row_panels/pallas_call | solution.py:315
  128.8 0.0 copy-done.4
  128.8 0.0 copy-start
  128.8 1.9 %copy-done = bf16[1536,1024]{1,0:T(8,128)(2,1)S(1)} copy-done((bf16[1536,1024]{1,0:T(8,128)(2,1)S(1)}, bf16[1536,1024]{1,0:T(8,128)(2,1)}, u32[]{:S(2)}) %copy-start) | copy-done | bytes 3145752
  130.7 5.9 %trailing.5.rest_4_ = f32[12,1,24,1,128,128]{5,4,3,2,1,0:T(8,128)} custom-call(s32[4]{0:T(128)S(1)} %copy-done.3, s32[192]{0:T(256)S(1)} %copy-done.4, s32[64]{0:T(128)S(1)} %get-tuple-element.43.order, s32[25]{0:T(128)S(1)} %get-tuple-element.44.starts, bf16[1536,1024]{1,0:T(8,128)(2,1)S(1)} %copy-done, ...), custom_call_target="tpu_custom_call", output_to_operand_aliasing={{}: (8, {})} | custom-call | flops 4831838208 | bytes 4718592 | tf_op jit(solution)/shard_map/trailing/pallas_call | solution.py:457
  136.6 0.0 collective-permute-done.5.rest_0_
  136.6 1.6 collective-permute-done.7.rest_1_
  138.3 0.8 collective-permute-start.11
  139.1 1.2 collective-permute-start.13
  140.3 8.3 %trailing.6.rest_4_ = f32[12,1,24,1,128,128]{5,4,3,2,1,0:T(8,128)} custom-call(s32[4]{0:T(128)S(1)} %copy-done.3, s32[192]{0:T(256)S(1)} %copy-done.4, s32[64]{0:T(128)S(1)} %get-tuple-element.43.order, s32[25]{0:T(128)S(1)} %get-tuple-element.44.starts, bf16[1536,1024]{1,0:T(8,128)(2,1)S(1)} %copy-done, ...), custom_call_target="tpu_custom_call", output_to_operand_aliasing={{}: (9, {})} | custom-call | flops 9663676416 | bytes 9437184 | tf_op jit(solution)/shard_map/trailing/pallas_call | solution.py:457
  148.7 8.3 %trailing.7.rest_4_ = f32[12,1,24,1,128,128]{5,4,3,2,1,0:T(8,128)} custom-call(s32[4]{0:T(128)S(1)} %copy-done.3, s32[192]{0:T(256)S(1)} %copy-done.4, s32[64]{0:T(128)S(1)} %get-tuple-element.43.order, s32[25]{0:T(128)S(1)} %get-tuple-element.44.starts, bf16[1536,1024]{1,0:T(8,128)(2,1)S(1)} %copy-done, ...), custom_call_target="tpu_custom_call", output_to_operand_aliasing={{}: (9, {})} | custom-call | flops 9663676416 | bytes 9437184 | tf_op jit(solution)/shard_map/trailing/pallas_call | solution.py:457
  157.0 0.0 collective-permute-done.11.rest_0_
  157.0 0.6 collective-permute-start.12
  157.6 0.0 collective-permute-done.13.rest_1_
  157.6 1.6 collective-permute-start.14
  159.2 8.3 %trailing.8.rest_4_ = f32[12,1,24,1,128,128]{5,4,3,2,1,0:T(8,128)} custom-call(s32[4]{0:T(128)S(1)} %copy-done.3, s32[192]{0:T(256)S(1)} %copy-done.4, s32[64]{0:T(128)S(1)} %get-tuple-element.43.order, s32[25]{0:T(128)S(1)} %get-tuple-element.44.starts, bf16[1536,1024]{1,0:T(8,128)(2,1)S(1)} %copy-done, ...), custom_call_target="tpu_custom_call", output_to_operand_aliasing={{}: (9, {})} | custom-call | flops 9663676416 | bytes 9437184 | tf_op jit(solution)/shard_map/trailing/pallas_call | solution.py:457
  167.5 0.0 collective-permute-done.12.rest_0_
  167.5 0.0 collective-permute-done.14.rest_1_
  167.6 6.2 %trailing.9 = f32[12,1,24,1,128,128]{5,4,3,2,1,0:T(8,128)} custom-call(s32[4]{0:T(128)S(1)} %copy-done.3, s32[192]{0:T(256)S(1)} %copy-done.4, s32[64]{0:T(128)S(1)} %get-tuple-element.43.order, s32[25]{0:T(128)S(1)} %get-tuple-element.44.starts, bf16[1536,1024]{1,0:T(8,128)(2,1)S(1)} %copy-done, ...), custom_call_target="tpu_custom_call", output_to_operand_aliasing={{}: (9, {})} | custom-call | flops 4831838208 | bytes 4718592 | tf_op jit(solution)/shard_map/trailing/pallas_call | solution.py:457
  (2 shorter events, 0.1 us)
Async XLA Ops:
  1.3 69.4 %copy-start.3 = (s32[4]{0:T(128)S(1)}, s32[4]{0:T(128)}, u32[]{:S(2)}) copy-start(s32[4]{0:T(128)} %pad_add_fusion.place) | copy-start | bytes 52
  4.6 92.0 %copy-start.1 = (f32[2,256,256]{2,1,0:T(8,128)S(1)}, f32[2,256,256]{2,1,0:T(8,128)}, u32[]{:S(2)}) copy-start(f32[2,256,256]{2,1,0:T(8,128)} %diag_ref.3) | copy-start | bytes 1572868
  4.7 124.2 %copy-start.4 = (s32[192]{0:T(256)S(1)}, s32[192]{0:T(256)}, u32[]{:S(2)}) copy-start(s32[192]{0:T(256)} %constant.15.clone.columns_table) | copy-start | bytes 2308
  73.9 18.0 %all-to-all-start.1 = ((f32[32,16,128]{2,1,0:T(8,128)}), f32[32,16,128]{2,1,0:T(8,128)S(1)}, u32[]{:S(2)}, u32[]{:S(2)}) async-start(f32[32,16,128]{2,1,0:T(8,128)} %get-tuple-element.32), calls=%async_computation.1 | async-start | bytes 524288 | tf_op jit(solution)/shard_map/all_to_all | solution.py:502
  77.1 7.9 %collective-permute-start = (f32[3,128,128]{2,1,0:T(8,128)}, f32[3,128,128]{2,1,0:T(8,128)S(1)}, u32[]{:S(2)}, u32[]{:S(2)}) collective-permute-start(f32[3,128,128]{2,1,0:T(8,128)} %get-tuple-element.27), channel_id=1, source_target_pairs={{0,0},{1,4},{2,8},{3,12},{4,1},{5,5},{6,9},{7,13},{8,2},{9,6},{10,... | collective-permute-start | bytes 589832 | tf_op jit(solution)/shard_map/ppermute | solution.py:544
  78.7 12.1 %collective-permute-start.1 = (f32[3,128,128]{2,1,0:T(8,128)}, f32[3,128,128]{2,1,0:T(8,128)}, u32[]{:S(2)}, u32[]{:S(2)}) collective-permute-start(f32[3,128,128]{2,1,0:T(8,128)} %get-tuple-element.28), channel_id=1, source_target_pairs={{0,4},{1,8},{2,12},{3,0},{4,5},{5,9},{6,13},{7,1},{8,6},{9,10},{10... | collective-permute-start | bytes 589832 | tf_op jit(solution)/shard_map/ppermute | solution.py:544
  80.9 10.2 %collective-permute-start.2 = (f32[3,128,128]{2,1,0:T(8,128)}, f32[3,128,128]{2,1,0:T(8,128)S(1)}, u32[]{:S(2)}, u32[]{:S(2)}) collective-permute-start(f32[3,128,128]{2,1,0:T(8,128)} %get-tuple-element.29), channel_id=1, source_target_pairs={{0,8},{1,12},{2,0},{3,4},{4,9},{5,13},{6,1},{7,5},{8,10},{9,14},{1... | collective-permute-start | bytes 589832 | tf_op jit(solution)/shard_map/ppermute | solution.py:544
  84.4 7.4 %collective-permute-start.3 = (f32[3,128,128]{2,1,0:T(8,128)}, f32[3,128,128]{2,1,0:T(8,128)}, u32[]{:S(2)}, u32[]{:S(2)}) collective-permute-start(f32[3,128,128]{2,1,0:T(8,128)} %get-tuple-element.30), channel_id=1, source_target_pairs={{0,12},{1,0},{2,4},{3,8},{4,13},{5,1},{6,5},{7,9},{8,14},{9,2},{10... | collective-permute-start | bytes 589832 | tf_op jit(solution)/shard_map/ppermute | solution.py:544
  91.1 0.7 copy-start.5
  91.8 22.2 %collective-permute-start.9 = (f32[12,128,128]{2,1,0:T(8,128)}, f32[12,128,128]{2,1,0:T(8,128)S(1)}, u32[]{:S(2)}, u32[]{:S(2)}) collective-permute-start(f32[12,128,128]{2,1,0:T(8,128)} %get-tuple-element.38.t0), channel_id=1, source_target_pairs={{0,2},{1,3},{2,0},{3,1},{4,6},{5,7},{6,4},{7,5},{8,10},{9,11},{10,... | collective-permute-start | bytes 2359304 | tf_op jit(solution)/shard_map/ppermute | solution.py:507
  98.4 19.5 %collective-permute-start.4 = (f32[4,3,128,128]{3,2,1,0:T(8,128)S(1)}, f32[4,3,128,128]{3,2,1,0:T(8,128)S(1)}, u32[]{:S(2)}, u32[]{:S(2)}) collective-permute-start(f32[4,3,128,128]{3,2,1,0:T(8,128)S(1)} %piece_panels.1.rest_0_), channel_id=1, source_target_pairs={{0,8},{8,16},{16,24},{24,28},{28,20},{20,12},{12,4},{4,0},{1,9},{9... | collective-permute-start | bytes 2359304 | tf_op jit(solution)/shard_map/ppermute | solution.py:553
  98.4 20.4 %collective-permute-start.6 = (f32[4,3,128,128]{3,2,1,0:T(8,128)S(1)}, f32[4,3,128,128]{3,2,1,0:T(8,128)S(1)}, u32[]{:S(2)}, u32[]{:S(2)}) collective-permute-start(f32[4,3,128,128]{3,2,1,0:T(8,128)S(1)} %piece_panels.1.rest_0_), channel_id=1, source_target_pairs={{8,0},{16,8},{24,16},{28,24},{20,28},{12,20},{4,12},{0,4},{9,1},{1... | collective-permute-start | bytes 2359304 | tf_op jit(solution)/shard_map/ppermute | solution.py:554
  100.5 19.5 %collective-permute-start.8 = (f32[12,128,128]{2,1,0:T(8,128)}, f32[12,128,128]{2,1,0:T(8,128)S(1)}, u32[]{:S(2)}, u32[]{:S(2)}) collective-permute-start(f32[12,128,128]{2,1,0:T(8,128)} %get-tuple-element.38.t0), channel_id=1, source_target_pairs={{0,1},{1,0},{2,3},{3,2},{4,5},{5,4},{6,7},{7,6},{8,9},{9,8},{10,11... | collective-permute-start | bytes 2359304 | tf_op jit(solution)/shard_map/ppermute | solution.py:506
  114.0 5.9 %collective-permute-start.10 = (f32[12,128,128]{2,1,0:T(8,128)S(1)}, f32[12,128,128]{2,1,0:T(8,128)S(1)}, u32[]{:S(2)}, u32[]{:S(2)}) collective-permute-start(f32[12,128,128]{2,1,0:T(8,128)S(1)} %collective-permute-done.9.t2), channel_id=1, source_target_pairs={{0,1},{1,0},{2,3},{3,2},{4,5},{5,4},{6,7},{7,6},{8,9},{9,8},{10,11... | collective-permute-start | bytes 2359304 | tf_op jit(solution)/shard_map/ppermute | solution.py:508
  117.9 18.8 %collective-permute-start.5 = (f32[4,3,128,128]{3,2,1,0:T(8,128)S(1)}, f32[4,3,128,128]{3,2,1,0:T(8,128)S(1)}, u32[]{:S(2)}, u32[]{:S(2)}) collective-permute-start(f32[4,3,128,128]{3,2,1,0:T(8,128)S(1)} %collective-permute-done.4.rest_0_), channel_id=1, source_target_pairs={{0,8},{8,16},{16,24},{24,28},{28,20},{20,12},{12,4},{4,0},{1,9},{9... | collective-permute-start | bytes 2359304 | tf_op jit(solution)/shard_map/ppermute | solution.py:553
  118.9 19.4 %collective-permute-start.7 = (f32[4,3,128,128]{3,2,1,0:T(8,128)S(1)}, f32[4,3,128,128]{3,2,1,0:T(8,128)S(1)}, u32[]{:S(2)}, u32[]{:S(2)}) collective-permute-start(f32[4,3,128,128]{3,2,1,0:T(8,128)S(1)} %collective-permute-done.6.rest_1_), channel_id=1, source_target_pairs={{8,0},{16,8},{24,16},{28,24},{20,28},{12,20},{4,12},{0,4},{9,1},{1... | collective-permute-start | bytes 2359304 | tf_op jit(solution)/shard_map/ppermute | solution.py:554
  119.9 1.1 copy-start.2
  128.8 1.9 %copy-start = (bf16[1536,1024]{1,0:T(8,128)(2,1)S(1)}, bf16[1536,1024]{1,0:T(8,128)(2,1)}, u32[]{:S(2)}) copy-start(bf16[1536,1024]{1,0:T(8,128)(2,1)} %get-tuple-element.45.pair_ref) | copy-start | bytes 9437188
  138.3 18.7 %collective-permute-start.11 = (f32[4,3,128,128]{3,2,1,0:T(8,128)S(1)}, f32[4,3,128,128]{3,2,1,0:T(8,128)S(1)}, u32[]{:S(2)}, u32[]{:S(2)}) collective-permute-start(f32[4,3,128,128]{3,2,1,0:T(8,128)S(1)} %collective-permute-done.5.rest_0_), channel_id=1, source_target_pairs={{0,8},{8,16},{16,24},{24,28},{28,20},{20,12},{12,4},{4,0},{1,9},{9... | collective-permute-start | bytes 2359304 | tf_op jit(solution)/shard_map/ppermute | solution.py:553
  139.1 18.5 %collective-permute-start.13 = (f32[4,3,128,128]{3,2,1,0:T(8,128)S(1)}, f32[4,3,128,128]{3,2,1,0:T(8,128)S(1)}, u32[]{:S(2)}, u32[]{:S(2)}) collective-permute-start(f32[4,3,128,128]{3,2,1,0:T(8,128)S(1)} %collective-permute-done.7.rest_1_), channel_id=1, source_target_pairs={{8,0},{16,8},{24,16},{28,24},{20,28},{12,20},{4,12},{0,4},{9,1},{1... | collective-permute-start | bytes 2359304 | tf_op jit(solution)/shard_map/ppermute | solution.py:554
  157.0 10.5 %collective-permute-start.12 = (f32[2,3,128,128]{3,2,1,0:T(8,128)S(1)}, f32[2,3,128,128]{3,2,1,0:T(8,128)S(1)}, u32[]{:S(2)}, u32[]{:S(2)}) collective-permute-start(f32[2,3,128,128]{3,2,1,0:T(8,128)S(1)} %slice.13), channel_id=1, source_target_pairs={{0,8},{8,16},{16,24},{24,28},{28,20},{20,12},{12,4},{4,0},{1,9},{9... | collective-permute-start | bytes 1179656 | tf_op jit(solution)/shard_map/ppermute | solution.py:559
  157.6 9.9 %collective-permute-start.14 = (f32[2,3,128,128]{3,2,1,0:T(8,128)S(1)}, f32[2,3,128,128]{3,2,1,0:T(8,128)S(1)}, u32[]{:S(2)}, u32[]{:S(2)}) collective-permute-start(f32[2,3,128,128]{3,2,1,0:T(8,128)S(1)} %slice.14), channel_id=1, source_target_pairs={{8,0},{16,8},{24,16},{28,24},{20,28},{12,20},{4,12},{0,4},{9,1},{1... | collective-permute-start | bytes 1179656 | tf_op jit(solution)/shard_map/ppermute | solution.py:559
